TPU v7x, 32 devices: a whole 2x2x4 slice. The times are simulated.
32 devices in a mesh: dp: 8 (over y, x, core), branch: 4 (over z).
Axes of the slice: x: 2, y: 2, z: 4, core: 2. Of those that a mesh axis runs over, the one named last changes fastest.
Arguments:
- frames: bfloat16 [8, 16, 14, 14, 832], P('dp', None, None, None, 'branch'), may hold values from -200 to 200
- lengths: int32 [8], P('dp'), may hold values from 2 to 16, as said below
- cotangent: bfloat16 [8, 8, 7, 7, 832], P('dp'), may hold values from -6 to 6
- pointwise: bfloat16 [2, 832, 576], replicated, may hold values from -0.21875 to 0.21875
- conv_mid: bfloat16 [2, 27, 160, 320], replicated, may hold values from -0.09375 to 0.09375
- conv_small: bfloat16 [2, 27, 32, 128], replicated, may hold values from -0.21875 to 0.21875
- gains: float32 [2, 1024], replicated, may hold values from 0.5 to 1.5
- shifts: float32 [2, 1024], replicated, may hold values from -2 to 2
Outputs:
- activations: bfloat16 [8, 8, 7, 7, 832], P('dp')
- input_grad: bfloat16 [8, 16, 14, 14, 832], P('dp', None, None, None, 'branch')
- pointwise_grad: float32 [2, 832, 576], replicated
- mid_grad: float32 [2, 27, 160, 320], replicated
- small_grad: float32 [2, 27, 32, 128], replicated
- gain_grad: float32 [2, 1024], replicated
- shift_grad: float32 [2, 1024], replicated
Inputs may be any that keep to these rules, and one draw needn't show every extreme that they name: `lengths`: every length is even; some clip has all 16 frames.
All inputs are finite; a program needn't handle non-finite values.
Results may differ from a plain program's by a relative error of at most 0.013.
Values may be sent and summed in bfloat16 or wider, within the bound.
No kernel may reach another device: no remote copies, remote signals or barrier semaphores. Data moves between devices by JAX's collectives and lax.ppermute only.
A program may use at most 384 MiB of HBM per device.

v0:
```python
import functools

import jax
import jax.numpy as jnp
from jax import lax
from jax.experimental import pallas as pl
from jax.experimental.pallas import tpu as pltpu
from jax.sharding import PartitionSpec as P

DIRECT = 256
MID_IN = 160
MID_OUT = 320
SMALL_IN = 32
SMALL_OUT = 128
TAPS = 27
CHANNELS = 832
SQUEEZED = 576
PITCH = 16
REDUCED = 256
POOLED = 128
FIRST = 640
SECOND = 512
OUTER = 896
TAP_ROWS = 432
EPSILON = 1e-05
F32 = jnp.float32
BF16 = jnp.bfloat16
VMEM_BYTES = 58 * 2**20
LARGE = 2200 * 2**10


def call(body, out_shape, scratch=(), scalars=0, cost=5, aliases=None, far=(), far_out=()):
    aliases = aliases or {}

    def large(values):
        size = values.dtype.itemsize
        for extent in values.shape:
            size = size * extent
        return size > LARGE

    def placed(out):
        return pltpu.HBM(out.shape, out.dtype) if large(out) else out

    def run(*operands):
        specs = [
            pl.BlockSpec(
                memory_space=pl.ANY
                if number in aliases or number in far
                else pltpu.SMEM
                if number < scalars
                else pltpu.VMEM
            )
            for number in range(len(operands))
        ]
        operands = [
            pltpu.with_memory_space_constraint(operand, pltpu.HBM) if large(operand) else operand
            for operand in operands
        ]
        if isinstance(out_shape, tuple):
            out_specs = tuple(
                pl.BlockSpec(memory_space=pl.ANY if number in far_out else pltpu.VMEM)
                for number in range(len(out_shape))
            )
        else:
            out_specs = pl.BlockSpec(memory_space=pl.ANY if 0 in far_out else pltpu.VMEM)
        return pl.pallas_call(
            body,
            out_shape=jax.tree.map(placed, out_shape),
            in_specs=specs,
            out_specs=out_specs,
            input_output_aliases=aliases,
            scratch_shapes=list(scratch),
            compiler_params=pltpu.CompilerParams(vmem_limit_bytes=VMEM_BYTES),
            cost_estimate=pl.CostEstimate(
                flops=0, bytes_accessed=int(cost * 3 * 10**6), transcendentals=0
            ),
        )(*operands)

    return run


def shape(dims, dtype):
    return jax.ShapeDtypeStruct(tuple(dims), dtype)


def rows_at(start, size):
    return pl.ds(pl.multiple_of(start, 16), size)


def frames_of(rows, width=128):
    return lax.broadcasted_iota(jnp.int32, (rows, width), 0) & (PITCH - 1)


def frame_mask(rows, length, width=128):
    mask = jnp.where(frames_of(rows) < length, 1.0, 0.0)
    return jnp.concatenate([mask] * (width // 128), axis=1) if width > 128 else mask


def earlier(values):
    return jnp.where(frames_of(*values.shape) > 0, pltpu.roll(values, 1, 0), 0.0)


def later(values):
    rows = values.shape[0]
    return jnp.where(frames_of(*values.shape) < PITCH - 1, pltpu.roll(values, rows - 1, 0), 0.0)


def plane_box(values):
    across = values + earlier(values) + later(values)
    edge = jnp.zeros((PITCH, values.shape[1]), values.dtype)
    return (
        across
        + jnp.concatenate([across[PITCH:], edge], axis=0)
        + jnp.concatenate([edge, across[:-PITCH]], axis=0)
    )


def box_window(side, length):
    frame = frames_of(side * PITCH)
    place = lax.broadcasted_iota(jnp.int32, (side * PITCH, 128), 0) >> 4

    def one(condition):
        return jnp.where(condition, 1.0, 0.0)

    count = one(frame < length) + one(frame + 1 < length) + one((frame > 0) & (frame - 1 < length))
    return count * (3.0 - one(place == 0) - one(place == side - 1))


def box_scale(line, side, window):
    lines = 3.0 - jnp.where(line == 0, 1.0, 0.0) - jnp.where(line == side - 1, 1.0, 0.0)
    return 1.0 / jnp.maximum(window * lines, 1.0)


def sigmoid(value):
    return 0.5 * jnp.tanh(0.5 * value) + 0.5


def silu(value):
    return value * sigmoid(value)


def silu_slope(value):
    gate = sigmoid(value)
    return gate * (1.0 + value * (1.0 - gate))


def partial_sum(values):
    rows, width = values.shape
    return jnp.sum(values.reshape(rows // 8, 8, width), axis=0)


def moments(total, square, count):
    center = total / count
    return (center, lax.rsqrt(square / count - center * center + EPSILON))


def total_of(gathered):
    count = len(gathered) if isinstance(gathered, (list, tuple)) else gathered.shape[0]
    total = gathered[0][...]
    for number in range(1, count):
        total = total + gathered[number][...]
    return total


def pool_matrix(side, transposed):
    line = 2 * side * PITCH
    few, many = (side * PITCH, 2 * line)
    dims = (many, few) if transposed else (few, many)
    coarse = lax.broadcasted_iota(jnp.int32, dims, 1 if transposed else 0)
    fine = lax.broadcasted_iota(jnp.int32, dims, 0 if transposed else 1)
    fine = jnp.where(fine >= line, fine - line, fine)
    same = (fine >> 5 == coarse >> 4) & ((fine & (PITCH - 1)) >> 1 == coarse & (PITCH - 1))
    return jnp.where(same, 0.125, 0.0).astype(BF16)


class Grid:
    def __init__(self, side):
        self.side = side
        self.line_rows = side * PITCH
        self.rows = side * self.line_rows
        self.pitch = (side + 1) * PITCH
        self.lead = self.pitch + PITCH
        self.padded = (side + 2) * self.pitch + 2 * PITCH
        self.group = 2 if side % 2 == 0 else side


class Slots:
    def __init__(self, grid, parts):
        self.pairs = grid.side // 2
        self.parts = parts
        self.each = -(-self.pairs // parts)
        self.empty = parts * self.each - self.pairs
        self.gap = parts * self.each // 2 - 1
        self.pair_rows = 2 * grid.line_rows
        self.rows = self.each * self.pair_rows

    def slot_of(self, pair):
        return pair + jnp.where(pair >= self.gap, self.empty, 0)

    def pair_of(self, slot):
        return slot - jnp.where(slot >= self.gap, self.empty, 0)

    def used(self, slot):
        return (slot < self.gap) | (slot >= self.gap + self.empty)

    def held(self, place):
        count = jnp.zeros((), jnp.int32)
        for number in range(self.each):
            count = count + jnp.where(self.used(place * self.each + number), 1, 0)
        return count


def clear_empty(grid, ref):
    width = ref.shape[1]
    ref[0 : grid.lead, :] = jnp.zeros((grid.lead, width), ref.dtype)
    end = grid.lead + grid.side * grid.pitch
    ref[end:, :] = jnp.zeros((ref.shape[0] - end, width), ref.dtype)

    @pl.loop(0, grid.side)
    def _(line):
        at = rows_at(grid.lead + line * grid.pitch + grid.line_rows, PITCH)
        ref[at, :] = jnp.zeros((PITCH, width), ref.dtype)


def store_taps(mid_ref, small_ref, at, act):
    before, after_ = (earlier(act), later(act))
    mid_ref[at, 0:128] = before[:, :128].astype(BF16)
    mid_ref[at, 128:256] = act[:, :128].astype(BF16)
    mid_ref[at, 256:384] = after_[:, :128].astype(BF16)
    before, act, after_ = (before[:, 128:], act[:, 128:], after_[:, 128:])
    lane = lax.broadcasted_iota(jnp.int32, act.shape, 1)
    mid_ref[at, 384:512] = jnp.where(
        lane < 32, before, jnp.where(lane < 64, pltpu.roll(act, 32, 1), pltpu.roll(after_, 64, 1))
    ).astype(BF16)
    small_ref[at, :] = jnp.where(
        lane < 32, pltpu.roll(before, 96, 1), jnp.where(lane < 64, act, pltpu.roll(after_, 32, 1))
    ).astype(BF16)


def tap_start(grid, base, tap, sign):
    return base + sign * ((tap // 3 - 1) * grid.pitch + (tap % 3 - 1) * PITCH)


def convolve(grid, taps, kernels, rest_ref, acc_ref, stage_ref, e_ref, stage_sem, sums_ref, length):
    mid_ref, small_ref = taps
    main_ref, last_ref, small_kernel_ref = kernels
    group_rows = grid.group * grid.pitch
    stage_rows = grid.group * grid.line_rows
    groups = grid.side // grid.group
    sums_ref[...] = jnp.zeros_like(sums_ref)
    mask = frame_mask(grid.line_rows, length, SECOND)
    edge = jnp.zeros((grid.pitch, 256), F32)
    rest_ref[PITCH : grid.lead, :] = edge
    end = grid.lead + grid.side * grid.pitch
    rest_ref[end : end + grid.pitch, :] = edge

    @pl.loop(0, groups)
    def _(group):
        base = grid.lead + group * group_rows
        total = None
        for place in range(3):
            part = jnp.dot(
                mid_ref[rows_at(base + (place - 1) * PITCH, group_rows), :],
                last_ref[place],
                preferred_element_type=F32,
            )
            total = part if total is None else total + part
        rest_ref[rows_at(base, group_rows), :] = total

    lane = lax.broadcasted_iota(jnp.int32, (grid.line_rows, 128), 1)

    def staged(group, slot):
        return pltpu.make_async_copy(
            stage_ref.at[slot],
            e_ref.at[rows_at(group * stage_rows, stage_rows), :],
            stage_sem.at[slot],
        )

    @pl.loop(0, groups)
    def _(group):
        base = grid.lead + group * group_rows
        slot = lax.rem(group, 2)
        for tap in range(9):
            part = jnp.dot(
                mid_ref[rows_at(tap_start(grid, base, tap, 1), group_rows), :],
                main_ref[tap],
                preferred_element_type=F32,
            )
            acc_ref[:, 0:256] = part if tap == 0 else acc_ref[:, 0:256] + part
        near = [small_ref[rows_at(tap_start(grid, base, tap, 1), group_rows), :] for tap in range(9)]
        acc_ref[:, 256:384] = jnp.dot(
            jnp.concatenate(near, axis=1), small_kernel_ref[...], preferred_element_type=F32
        )

        @pl.when(group >= 2)
        def _():
            staged(group - 2, slot).wait()

        for number in range(grid.group):
            rows = grid.line_rows
            start = base + number * grid.pitch
            last = (
                rest_ref[rows_at(start - grid.pitch, rows), 0:128]
                + pltpu.roll(rest_ref[rows_at(start, rows), 0:128], 64, 1)
                + rest_ref[rows_at(start + grid.pitch, rows), 128:256]
            )
            lines = slice(number * grid.pitch, number * grid.pitch + rows)
            values = jnp.concatenate(
                [acc_ref[lines, 0:256], jnp.where(lane < 64, last, 0.0), acc_ref[lines, 256:384]],
                axis=1,
            )
            stage_ref[slot, number * rows : (number + 1) * rows, :] = values
            masked = values * mask
            sums_ref[0:8] += partial_sum(masked)
            sums_ref[8:16] += partial_sum(masked * values)
        staged(group, slot).start()

    for group in range(max(groups - 2, 0), groups):
        staged(group, group % 2).wait()


def conv_scratch(grid):
    group_rows = grid.group * grid.pitch
    return [
        pltpu.VMEM((9, 512, 256), BF16),
        pltpu.VMEM((3, 512, 256), BF16),
        pltpu.VMEM((1152, 128), BF16),
        pltpu.VMEM((grid.padded, 512), BF16),
        pltpu.VMEM((grid.padded, 128), BF16),
        pltpu.VMEM((grid.rows, REDUCED), BF16),
        pltpu.VMEM((grid.padded, 256), F32),
        pltpu.VMEM((group_rows, 384), F32),
        pltpu.VMEM((2, grid.group * grid.line_rows, SECOND), F32),
        pltpu.VMEM((16, SECOND), F32),
        pltpu.SemaphoreType.DMA((3,)),
        pltpu.SemaphoreType.DMA((3,)),
        pltpu.SemaphoreType.DMA((2,)),
    ]


def conv_outputs(grid, *clips):
    return (
        shape((grid.rows, REDUCED), BF16),
        shape((grid.padded, 512), BF16),
        shape((grid.padded, 128), BF16),
        shape((grid.rows, SECOND), F32),
        shape((*clips, 2, SECOND), F32),
    )


def copies(sources, targets, sem_ref):
    return [
        pltpu.make_async_copy(source, target, sem_ref.at[number])
        for number, (source, target) in enumerate(zip(sources, targets))
    ]


def run_convolution(grid, length, far_kernels, outputs, scratch, fill):
    h_out, mid_out, small_out, e_out, sums_out = outputs
    kernels, (mid_ref, small_ref, h_ref), rest = (scratch[:3], scratch[3:6], scratch[6:])
    rest_ref, acc_ref, stage_ref, sums_ref, in_sem, out_sem, stage_sem = rest
    arriving = copies(far_kernels, kernels, in_sem)
    for copy in arriving:
        copy.start()
    clear_empty(grid, mid_ref)
    clear_empty(grid, small_ref)
    fill(h_ref, mid_ref, small_ref)
    leaving = copies((mid_ref, small_ref, h_ref), (mid_out, small_out, h_out), out_sem)
    for copy in leaving:
        copy.start()
    for copy in arriving:
        copy.wait()
    convolve(
        grid, (mid_ref, small_ref), kernels, rest_ref, acc_ref, stage_ref, e_out, stage_sem, sums_ref, length
    )
    write_sums(sums_out, sums_ref, 0, SECOND)
    for copy in leaving:
        copy.wait()


def write_row(out_ref, row, lo, hi, values):
    if len(out_ref.shape) == 2:
        out_ref[row : row + 1, lo:hi] = values
    else:
        for clip in range(out_ref.shape[0]):
            out_ref[clip, row : row + 1, lo:hi] = values


def write_sums(out_ref, sums_ref, lo, hi):
    for number in range(2):
        values = jnp.sum(sums_ref[8 * number : 8 * number + 8], axis=0, keepdims=True)
        write_row(out_ref, number, lo, hi, values)


def turn(slots, x_ref, out_ref):
    for slot in range(slots.parts * slots.each):
        part, number = divmod(slot, slots.each)
        lanes = slice(number * slots.pair_rows, (number + 1) * slots.pair_rows)
        if slots.gap <= slot < slots.gap + slots.empty:
            out_ref[part, :, lanes] = jnp.zeros((out_ref.shape[1], slots.pair_rows), BF16)
            continue
        pair = slot - (slots.empty if slot >= slots.gap else 0)
        rows = slice(pair * slots.pair_rows, (pair + 1) * slots.pair_rows)
        out_ref[part, :, lanes] = x_ref[rows, :].T


def first_pointwise(slots, length_ref, count_ref, x_ref, p_ref, mid_ref, pool_ref, direct_ref, sums_ref, u_ref):
    rows, step = (slots.rows, 112)
    length, count = (length_ref[0], count_ref[0])
    for part in range(slots.parts):
        product = lax.dot_general(
            x_ref[part], p_ref[part], (((0,), (1,)), ((), ())), preferred_element_type=F32
        )
        u_ref[...] = product if part == 0 else u_ref[...] + product
    mask = frame_mask(step, length, FIRST)

    def summed(number, carry):
        values = u_ref[rows_at(number * step, step), :] * mask
        u_ref[rows_at(number * step, step), :] = values
        few = values[:, :SECOND]
        return (carry[0] + partial_sum(values), carry[1] + partial_sum(few * few))

    zero = (jnp.zeros((8, FIRST), F32), jnp.zeros((8, SECOND), F32))
    total, square = lax.fori_loop(0, rows // step, summed, zero)
    total = jnp.sum(total, axis=0, keepdims=True)
    write_row(sums_ref, 0, 0, SECOND, total[:, :SECOND])
    write_row(sums_ref, 1, 0, SECOND, jnp.sum(square, axis=0, keepdims=True))
    write_row(sums_ref, 2, 0, SECOND, jnp.full((1, SECOND), count, F32))
    offset = (total / jnp.full((1, FIRST), jnp.maximum(count, 1.0), F32)).astype(BF16)
    wide_offset = offset.astype(F32)
    tail = jnp.broadcast_to(wide_offset, (PITCH, FIRST)).astype(BF16)
    pool_ref[rows : rows + PITCH, :] = tail[:, SECOND:]
    shared = mid_ref.shape[0] - 2 * PITCH
    mid_ref[shared : shared + PITCH, :] = tail[:, 256:384]
    mid_ref[shared + PITCH :, :] = tail[:, 384:512]

    @pl.loop(0, rows // step)
    def _(number):
        at = rows_at(number * step, step)
        values = u_ref[at, :]
        direct_ref[at, :] = values[:, :DIRECT]
        values = values[:, DIRECT:] - wide_offset[:, DIRECT:]
        mid_ref[at, :] = values[:, :128].astype(BF16)
        pool_ref[at, :] = values[:, 256:].astype(BF16)

    lane = lax.broadcasted_iota(jnp.int32, (step, 128), 1)
    for couple in range(0, slots.each, 2):

        @pl.loop(0, slots.pair_rows // step)
        def _(number):
            start = couple * slots.pair_rows + number * step
            values = u_ref[rows_at(start, step), 384:512] - wide_offset[:, 384:512]
            if couple + 1 < slots.each:
                other = u_ref[rows_at(start + slots.pair_rows, step), 384:512]
                other = pltpu.roll(other - wide_offset[:, 384:512], 64, 1)
                values = jnp.where(lane < 64, values, other)
            place = rows + couple // 2 * slots.pair_rows + number * step
            mid_ref[rows_at(place, step), :] = values.astype(BF16)


def mid_rows(slots):
    return slots.rows + -(-slots.each // 2) * slots.pair_rows + 2 * PITCH


def each_pair(slots, place, refs, visit):
    for step, ref in enumerate(refs):
        source = lax.rem(place - step + slots.parts, slots.parts)
        for number in range(slots.each):
            slot = source * slots.each + number

            @pl.when(slots.used(slot))
            def _():
                visit(slots.pair_of(slot), ref, number)


def set_moments(total, moment_ref):
    count = total[2:3]
    center, inverse = moments(total[0:1], total[1:2], count)
    moment_ref[0:1, :] = center
    moment_ref[1:2, :] = inverse
    moment_ref[2:3, :] = count
    return (center, inverse)


def first_convolve(grid, slots, block, length_ref, place_ref, *refs):
    parts = slots.parts
    mids, (moment_ref, gain_ref, shift_ref), refs = (refs[:parts], refs[parts : parts + 3], refs[parts + 3 :])
    far_kernels, outputs, scratch = (refs[:3], refs[3:8], refs[8:])
    length = length_ref[0]
    center, inverse = (moment_ref[0:1, DIRECT:], moment_ref[1:2, DIRECT:])
    gain, shift = (gain_ref[block : block + 1], shift_ref[block : block + 1])
    step = 112
    mask = frame_mask(step, length, REDUCED)
    lane = lax.broadcasted_iota(jnp.int32, (step, 128), 1)

    def fill(h_ref, mid_ref, small_ref):
        def visit(pair, ref, number):
            shared = ref.shape[0] - 2 * PITCH
            offset = jnp.concatenate(
                [
                    ref[at : at + PITCH, :].astype(F32)[0:1]
                    for at in (shared, shared + PITCH)
                ],
                axis=1,
            )
            other = slots.rows + number // 2 * slots.pair_rows

            @pl.loop(0, slots.pair_rows // step)
            def _(chunk):
                values = ref[rows_at(number * slots.pair_rows + chunk * step, step), :].astype(F32)
                few = ref[rows_at(other + chunk * step, step), :].astype(F32)
                if number % 2 == 1:
                    few = pltpu.roll(few, 64, 1)
                few = jnp.where(lane < 64, few, 0.0)
                values = jnp.concatenate([values, few], axis=1) + offset
                scaled = (values - center) * inverse
                row = pair * slots.pair_rows + chunk * step
                h_ref[rows_at(row, step), :] = scaled.astype(BF16)
                act = silu(gain * scaled + shift) * mask
                line = row // grid.line_rows
                at = grid.lead + line * grid.pitch + row - line * grid.line_rows
                store_taps(mid_ref, small_ref, rows_at(at, step), act)

        each_pair(slots, place_ref[0], mids, visit)

    run_convolution(grid, length, far_kernels, outputs, scratch, fill)


def pool_planes(grid, plane_ref, q_ref, lo, sums_ref, length, window):
    rows = grid.line_rows
    mask = frame_mask(rows, length)
    sums_ref[...] = jnp.zeros_like(sums_ref)

    @pl.loop(0, grid.side)
    def _(line):
        start = line * rows
        values = (
            plane_ref[rows_at(start, rows), :]
            + plane_ref[rows_at(start + rows, rows), :]
            + plane_ref[rows_at(start + 2 * rows, rows), :]
        ) * box_scale(line, grid.side, window)
        q_ref[rows_at(start, rows), lo : lo + POOLED] = values
        masked = values * mask
        sums_ref[0:8] += partial_sum(masked)
        sums_ref[8:16] += partial_sum(masked * values)


def clear_edges(grid, plane_ref):
    rows = grid.line_rows
    plane_ref[0:rows] = jnp.zeros((rows, POOLED), F32)
    plane_ref[grid.rows + rows : grid.rows + 2 * rows] = jnp.zeros((rows, POOLED), F32)


def first_pool(grid, slots, length_ref, place_ref, *refs):
    pools, refs = (refs[: slots.parts], refs[slots.parts :])
    e_sums_ref, q_ref, out_sums_ref, plane_ref, sums_ref = refs
    length = length_ref[0]
    rows = grid.line_rows
    for row in range(2):
        write_row(out_sums_ref, row, 0, SECOND, e_sums_ref[row : row + 1, :])
    clear_edges(grid, plane_ref)

    def visit(pair, ref, number):
        offset = ref[slots.rows : slots.rows + PITCH, :].astype(F32)[0:1]
        for line in range(2):
            at = rows_at(number * slots.pair_rows + line * rows, rows)
            plane_ref[rows_at((2 * pair + line + 1) * rows, rows), :] = plane_box(
                ref[at, :].astype(F32) + offset
            )

    each_pair(slots, place_ref[0], pools, visit)
    pool_planes(grid, plane_ref, q_ref, 0, sums_ref, length, box_window(grid.side, length))
    write_sums(out_sums_ref, sums_ref, SECOND, FIRST)


def normalize(values, center, inverse, gain, shift, mask):
    scaled = (values - center) * inverse
    shifted = gain * scaled + shift
    gate = sigmoid(shifted)
    gate_mask = gate * mask
    act = shifted * gate_mask
    return (scaled, act, gate_mask + act * (1.0 - gate))


def pool_pieces(matrix, pieces):
    return jnp.dot(
        matrix, jnp.concatenate(pieces, axis=0), preferred_element_type=F32
    ).astype(BF16)


def first_direct(grid, small, slots, block, length_ref, u_ref, gain_ref, shift_ref, *refs):
    sums, (pooled_ref, kept_ref, moment_ref) = (refs[: slots.parts], refs[slots.parts :])
    rows = grid.line_rows
    mask = frame_mask(rows, length_ref[0], DIRECT)
    center, inverse = set_moments(total_of(sums), moment_ref)
    center, inverse = (center[:, :DIRECT], inverse[:, :DIRECT])
    gain, shift = (gain_ref[block : block + 1, :DIRECT], shift_ref[block : block + 1, :DIRECT])
    matrix = pool_matrix(small.side, False)

    @pl.loop(0, slots.each)
    def _(number):
        acts, slopes, products = ([], [], [])
        for line in range(2):
            at = rows_at(number * slots.pair_rows + line * rows, rows)
            scaled, act, slope = normalize(u_ref[at, :], center, inverse, gain, shift, mask)
            kept_ref[at, 0:DIRECT] = scaled.astype(BF16)
            kept_ref[at, DIRECT : 2 * DIRECT] = slope.astype(BF16)
            acts.append(act.astype(BF16))
            slopes.append(slope.astype(BF16))
            products.append((slope * scaled).astype(BF16))
        size = small.line_rows
        pooled_ref[rows_at(number * size, size), :] = pool_pieces(matrix, acts)
        at = rows_at(slots.rows + number * size, size)
        kept_ref[at, 0:DIRECT] = pool_pieces(matrix, slopes)
        kept_ref[at, DIRECT : 2 * DIRECT] = pool_pieces(matrix, products)


def outer_moments(center, inverse, count, outer_ref):
    outer_ref[0:1, :] = center
    outer_ref[1:2, :] = inverse
    outer_ref[2:3, :] = jnp.concatenate([count[:, 0:128]] * (OUTER // 128), axis=1)


def first_output(grid, small, block, length_ref, q_far, e_far, moment_ref, sums_in_ref, gain_ref, shift_ref, *refs):
    pooled_ref, h_far, slope_far, outer_ref, pooled_slope_ref, pooled_product_ref, *refs = refs
    q_ref, e_ref, h_ref, slope_ref, q_sem, e_sem, h_sem, slope_sem = refs
    rows = grid.line_rows
    wide = 2 * rows
    pairs = grid.side // 2

    def arriving(pair, slot):
        at = rows_at(pair * wide, wide)
        return [
            pltpu.make_async_copy(q_far.at[at, :], q_ref.at[slot], q_sem.at[slot]),
            pltpu.make_async_copy(e_far.at[at, :], e_ref.at[slot], e_sem.at[slot]),
        ]

    def leaving(pair, slot):
        at = rows_at(pair * wide, wide)
        return [
            pltpu.make_async_copy(h_ref.at[slot], h_far.at[at, :], h_sem.at[slot]),
            pltpu.make_async_copy(slope_ref.at[slot], slope_far.at[at, :], slope_sem.at[slot]),
        ]

    for copy in arriving(0, 0):
        copy.start()
    mask = frame_mask(rows, length_ref[0], FIRST)
    total = total_of(sums_in_ref)
    count = jnp.concatenate([moment_ref[2:3, 0:128]] * (FIRST // 128), axis=1)
    center, inverse = moments(total[0:1], total[1:2], count)
    outer_moments(
        jnp.concatenate([moment_ref[0:1, :DIRECT], center], axis=1),
        jnp.concatenate([moment_ref[1:2, :DIRECT], inverse], axis=1),
        count,
        outer_ref,
    )
    matrix = pool_matrix(small.side, False)
    gain, shift = (gain_ref[block : block + 1, DIRECT:], shift_ref[block : block + 1, DIRECT:])

    @pl.loop(0, pairs)
    def _(pair):
        slot = lax.rem(pair, 2)

        @pl.when(pair + 1 < pairs)
        def _():
            for copy in arriving(pair + 1, 1 - slot):
                copy.start()

        for copy in arriving(pair, slot):
            copy.wait()

        @pl.when(pair >= 2)
        def _():
            for copy in leaving(pair - 2, slot):
                copy.wait()

        acts, slopes, products = ([], [], [])
        for number in range(2):
            lines = slice(number * rows, (number + 1) * rows)
            values = jnp.concatenate([e_ref[slot, lines, :], q_ref[slot, lines, :]], axis=1)
            scaled, act, slope = normalize(values, center, inverse, gain, shift, mask)
            h_ref[slot, lines, :] = scaled.astype(BF16)
            low_slope = slope.astype(BF16)
            slope_ref[slot, lines, :] = low_slope
            acts.append(act.astype(BF16))
            slopes.append(low_slope)
            products.append((slope * scaled).astype(BF16))
        for copy in leaving(pair, slot):
            copy.start()
        at = rows_at(pair * small.line_rows, small.line_rows)
        pooled_ref[at, :] = pool_pieces(matrix, acts)
        pooled_slope_ref[at, :] = pool_pieces(matrix, slopes)
        pooled_product_ref[at, :] = pool_pieces(matrix, products)

    for pair in range(max(pairs - 2, 0), pairs):
        for copy in leaving(pair, pair % 2):
            copy.wait()


def second_pointwise(grid, slots, length_ref, place_ref, count_ref, *refs):
    directs, refs = (refs[: slots.parts], refs[slots.parts :])
    rest_ref, p_ref, q_ref, out_sums_ref, x_ref, plane_ref, sums_ref, pool_sums_ref = refs
    length = length_ref[0]
    rows = grid.line_rows
    sums_ref[...] = jnp.zeros_like(sums_ref)
    clear_edges(grid, plane_ref)
    x_ref[:, DIRECT:] = rest_ref[...]

    def visit(pair, ref, number):
        x_ref[rows_at(pair * rows, rows), 0:DIRECT] = ref[number * rows : (number + 1) * rows, :]

    each_pair(slots, place_ref[0], directs, visit)
    q_ref[...] = lax.dot_general(
        x_ref[...], p_ref[...], (((1,), (1,)), ((), ())), preferred_element_type=F32
    )

    @pl.loop(0, grid.side)
    def _(line):
        values = q_ref[rows_at(line * rows, rows), :]
        sums_ref[0:8] += partial_sum(values[:, :SECOND])
        sums_ref[8:16] += partial_sum(values[:, :SECOND] * values[:, :SECOND])
        plane_ref[rows_at((line + 1) * rows, rows), :] = plane_box(values[:, SECOND:])

    pool_planes(grid, plane_ref, q_ref, SECOND, pool_sums_ref, length, box_window(grid.side, length))
    write_sums(out_sums_ref, sums_ref, 0, SECOND)
    write_sums(out_sums_ref, pool_sums_ref, SECOND, FIRST)
    write_row(out_sums_ref, 2, 0, FIRST, jnp.full((1, FIRST), count_ref[0], F32))


def second_convolve(grid, block, length_ref, q_ref, sums_in_ref, gain_ref, shift_ref, *refs):
    far_kernels, outputs, moment_ref, scratch = (refs[:3], refs[3:8], refs[8], refs[9:])
    length = length_ref[0]
    center, inverse = set_moments(total_of(sums_in_ref), moment_ref)
    center, inverse = (center[:, DIRECT:SECOND], inverse[:, DIRECT:SECOND])
    gain, shift = (gain_ref[block : block + 1], shift_ref[block : block + 1])
    mask = frame_mask(grid.line_rows, length, REDUCED)

    def fill(h_ref, mid_ref, small_ref):
        @pl.loop(0, grid.side)
        def _(line):
            at = rows_at(line * grid.line_rows, grid.line_rows)
            scaled = (q_ref[at, DIRECT:SECOND] - center) * inverse
            h_ref[at, :] = scaled.astype(BF16)
            act = silu(gain * scaled + shift) * mask
            store_taps(
                mid_ref, small_ref, rows_at(grid.lead + line * grid.pitch, grid.line_rows), act
            )

    run_convolution(grid, length, far_kernels, outputs, scratch, fill)


def second_output(grid, block, length_ref, q_ref, e_ref, moment_ref, sums_in_ref, gain_ref, shift_ref, cot_ref, act_ref, h_ref, error_ref, outer_ref, out_sums_ref, sums_ref):
    rows = grid.line_rows
    side, frames = (grid.side, cot_ref.shape[1])
    mask = frame_mask(rows, length_ref[0], OUTER)
    total = total_of(sums_in_ref)
    count = moment_ref[2:3, 0:SECOND]
    center, inverse = moments(total[0:1], total[1:2], count)
    center = jnp.concatenate([moment_ref[0:1, :DIRECT], center, moment_ref[0:1, SECOND:]], axis=1)
    inverse = jnp.concatenate([moment_ref[1:2, :DIRECT], inverse, moment_ref[1:2, SECOND:]], axis=1)
    outer_moments(center, inverse, count, outer_ref)
    sums_ref[...] = jnp.zeros_like(sums_ref)
    gain, shift = (gain_ref[block : block + 1], shift_ref[block : block + 1])
    gap = jnp.zeros((rows, 64), F32)
    unused = jnp.zeros((side, PITCH - frames, CHANNELS), F32)

    @pl.loop(0, side)
    def _(line):
        at = rows_at(line * rows, rows)
        places = pl.ds(line * side, side)
        values = jnp.concatenate([q_ref[at, :DIRECT], e_ref[at, :], q_ref[at, SECOND:]], axis=1)
        scaled = (values - center) * inverse
        h_ref[at, :] = scaled.astype(BF16)
        shifted = gain * scaled + shift
        gate = sigmoid(shifted)
        act = (shifted * gate * mask).reshape(side, PITCH, OUTER)[:, :frames].astype(BF16)
        act_ref[places, :, 0:576] = act[:, :, 0:576]
        act_ref[places, :, 576:CHANNELS] = act[:, :, 640:OUTER]
        slope = gate * (1.0 + shifted * (1.0 - gate))
        grad = jnp.concatenate([cot_ref[places].astype(F32), unused], axis=1)
        grad = grad.reshape(rows, CHANNELS)
        grad = jnp.concatenate([grad[:, :576], gap, grad[:, 576:]], axis=1)
        error = grad * slope * mask
        error_ref[at, :] = error.astype(BF16)
        sums_ref[0:8] += partial_sum(error)
        sums_ref[8:16] += partial_sum(error * scaled)

    write_sums(out_sums_ref, sums_ref, 0, OUTER)


def spread_matrix(grid, small):
    return None if small is None else pool_matrix(small.side, True)[: grid.line_rows]


def outer_error(slopes, small, grad_ref, matrix, line, lo, hi):
    values = slopes.astype(F32)
    if small is None:
        return values
    coarse = grad_ref[rows_at((line // 2) * small.line_rows, small.line_rows), lo:hi]
    return values * jnp.dot(matrix, coarse, preferred_element_type=F32)


class Lines:
    def __init__(self, grid, sources, buffers, sem_ref):
        self.step = 2 if grid.side % 2 == 0 else 1
        self.size = self.step * grid.line_rows
        self.steps = grid.side // self.step
        self.sources, self.buffers, self.sem = (sources, buffers, sem_ref)

    def copies(self, step):
        at = rows_at(step * self.size, self.size)
        copies = []
        for number, ((ref, lo, hi), (buffer, place)) in enumerate(zip(self.sources, self.buffers)):
            source = ref(step, lo, hi) if callable(ref) else ref.at[at, pl.ds(lo, hi - lo)]
            target = buffer.at[at, pl.ds(place, hi - lo)]
            copies.append(pltpu.make_async_copy(source, target, self.sem.at[number, step]))
        return copies

    def first(self):
        @pl.loop(0, self.steps)
        def _(step):
            for copy in self.copies(step):
                copy.start()

    def run(self, visit):
        @pl.loop(0, self.steps)
        def _(step):
            for copy in self.copies(step):
                copy.wait()
            visit(step)

    @staticmethod
    def semaphores(grid, count):
        return pltpu.SemaphoreType.DMA((count, grid.side // 2 if grid.side % 2 == 0 else grid.side))


def second_back(grid, small, block, slots, length_ref, first_ref, h_far, outer_ref, sums_in_ref, gain_ref, slope_far, *refs):
    first = small is not None
    (grad_ref, carried_ref), refs = (refs[:2], refs[2:]) if first else ((None, None), refs)
    mid_far, few_far, d_far, total_ref, out_ref, *refs = refs
    d_ref, h_ref, slope_ref, mid_ref, few_ref, mid_acc_ref, small_acc_ref, turned_ref, sem_ref, in_sem, out_sem = refs
    lo, hi = (DIRECT, DIRECT + SECOND)
    at = 0 if first else DIRECT
    lines = Lines(
        grid,
        ((h_far, at, at + SECOND), (slope_far, at, at + SECOND)),
        ((h_ref, 0), (slope_ref, 0)),
        sem_ref,
    )
    lines.first()
    arriving = copies((mid_far, few_far), (mid_ref, few_ref), in_sem)
    for copy in arriving:
        copy.start()
    total = total_of(sums_in_ref)
    total_ref[...] = total
    a, b, c = before_norm(
        gain_ref[block : block + 1, lo:hi], outer_ref[1:2, lo:hi], total[:, lo:hi], outer_ref[2:3, lo:hi]
    )
    mask = frame_mask(grid.line_rows, length_ref[0], SECOND)
    matrix = spread_matrix(grid, small)
    clear_empty(grid, d_ref)
    rows = grid.line_rows
    if first:
        share = out_ref.shape[1] - carried_ref.shape[1]
        for clip in range(out_ref.shape[0]):
            out_ref[clip, share:, :] = carried_ref[clip]

    def visit(step):
        for number in range(lines.step):
            line = step * lines.step + number
            here = rows_at(line * rows, rows)
            scaled = h_ref[here, :].astype(F32)
            error = outer_error(slope_ref[here, :], small, grad_ref, matrix, line, lo, hi)
            back = (a * error - b - c * scaled) * mask
            d_ref[rows_at(grid.lead + line * grid.pitch, rows), :] = back.astype(BF16)

    lines.run(visit)
    leaving = pltpu.make_async_copy(d_ref, d_far, out_sem.at[0])
    leaving.start()
    for copy in arriving:
        copy.wait()
    kernel_grads(grid, slots, first_ref, mid_ref, few_ref, d_ref, out_ref, mid_acc_ref, small_acc_ref, turned_ref)
    leaving.wait()


def before_norm(gain, inverse, sums, count):
    factor = gain * inverse
    return (factor, factor * sums[0:1] / count, factor * sums[1:2] / count)


def second_back_scratch(grid, slots):
    return [
        pltpu.VMEM((grid.padded, SECOND), BF16),
        pltpu.VMEM((grid.rows, SECOND), BF16),
        pltpu.VMEM((grid.rows, SECOND), BF16),
        pltpu.VMEM((grid.padded, 512), BF16),
        pltpu.VMEM((grid.padded, 128), BF16),
        pltpu.VMEM((slots, 384, 256), F32),
        pltpu.VMEM((slots, 128, 128), F32),
        pltpu.VMEM((MID_IN + 128, 128), F32),
        Lines.semaphores(grid, 2),
        pltpu.SemaphoreType.DMA((2,)),
        pltpu.SemaphoreType.DMA((1,)),
    ]


def conv_back(grid, slots, block, length_ref, d_ref, reduced_ref, reduced_gain_ref, reduced_shift_ref, *refs):
    far_kernels, refs = (refs[:3], refs[3:])
    first = len(refs) > 9
    (x_far, rest_product_ref), refs = (refs[:2], refs[2:]) if first else ((None, None), refs)
    r_ref, out_sums_ref, *refs = refs
    product_out, refs = (refs[0], refs[1:]) if first else (None, refs)
    kernels, (last_ref, acc_ref, sums_ref, in_sem, *refs) = (refs[:3], refs[3:])
    if first:
        x_ref, product_ref, x_sem = refs
        x_copy = pltpu.make_async_copy(x_far, x_ref, x_sem.at[0])
        x_copy.start()
    main_ref, rest_ref, small_ref = kernels
    arriving = copies(far_kernels, kernels, in_sem)
    for copy in arriving:
        copy.start()
    rows = grid.line_rows
    group_rows = grid.group * grid.pitch
    sums_ref[...] = jnp.zeros_like(sums_ref)
    mask = frame_mask(rows, length_ref[0], REDUCED)
    gain, shift = (reduced_gain_ref[block : block + 1], reduced_shift_ref[block : block + 1])
    turned = (((1,), (1,)), ((), ()))
    lane = lax.broadcasted_iota(jnp.int32, (rows, 128), 1)
    wide_lane = lax.broadcasted_iota(jnp.int32, (grid.pitch, 128), 1)

    @pl.loop(0, grid.side)
    def _(line):
        place = grid.lead + line * grid.pitch
        here = d_ref[rows_at(place, grid.pitch), 256:384].astype(F32)
        further = d_ref[rows_at(place + grid.pitch, grid.pitch), 256:384].astype(F32)
        at = rows_at(place, grid.pitch)
        last_ref[at, 0:128] = jnp.where(wide_lane < 64, further, pltpu.roll(here, 64, 1)).astype(
            BF16
        )
        last_ref[at, 128:256] = d_ref[rows_at(place - grid.pitch, grid.pitch), 256:384]

    last_ref[grid.lead - PITCH : grid.lead, :] = jnp.zeros((PITCH, 256), BF16)
    end = grid.lead + grid.side * grid.pitch
    last_ref[end : end + PITCH, :] = jnp.zeros((PITCH, 256), BF16)
    for copy in arriving:
        copy.wait()

    @pl.loop(0, grid.side // grid.group)
    def _(group):
        base = grid.lead + group * group_rows
        for tap in range(9):
            part = lax.dot_general(
                d_ref[rows_at(tap_start(grid, base, tap, -1), group_rows), 0:256],
                main_ref[tap],
                turned,
                preferred_element_type=F32,
            )
            acc_ref[:, 0:512] = part if tap == 0 else acc_ref[:, 0:512] + part
        for place in range(3):
            acc_ref[:, 0:512] += lax.dot_general(
                last_ref[rows_at(base - (place - 1) * PITCH, group_rows), :],
                rest_ref[place],
                turned,
                preferred_element_type=F32,
            )
        near = [
            d_ref[rows_at(tap_start(grid, base, tap, -1), group_rows), 384:512] for tap in range(9)
        ]
        acc_ref[:, 512:640] = jnp.dot(
            jnp.concatenate(near, axis=1), small_ref[...], preferred_element_type=F32
        )
        for number in range(grid.group):
            line = group * grid.group + number
            lines = slice(number * grid.pitch, number * grid.pitch + rows)
            rest, small = (acc_ref[lines, 384:512], acc_ref[lines, 512:640])
            one = jnp.where(lane < 32, rest, pltpu.roll(small, 32, 1))
            two = jnp.where(lane < 32, pltpu.roll(rest, 96, 1), small)
            three = jnp.where(lane < 32, pltpu.roll(rest, 64, 1), pltpu.roll(small, 96, 1))
            wide = later(acc_ref[lines, 0:128]) + acc_ref[lines, 128:256]
            wide = wide + earlier(acc_ref[lines, 256:384])
            narrow = jnp.where(lane < 64, later(one) + two + earlier(three), 0.0)
            back = jnp.concatenate([wide, narrow], axis=1)
            at = rows_at(line * rows, rows)
            scaled = reduced_ref[at, :].astype(F32)
            error = back * silu_slope(gain * scaled + shift) * mask
            r_ref[at, :] = error.astype(BF16)
            sums_ref[0:8] += partial_sum(error)
            sums_ref[8:16] += partial_sum(error * scaled)

    write_sums(out_sums_ref, sums_ref, 0, REDUCED)
    if first:
        x_copy.wait()
        ones = frame_mask(slots.rows, length_ref[0])
        low_ones = ones.astype(BF16)
        two_ones = jnp.concatenate([ones, ones], axis=1)

        def right_of(start, size):
            at = slice(start, start + size)
            scaled = (reduced_ref[at, :].astype(F32) * two_ones).astype(BF16)
            return jnp.concatenate([r_ref[at, :], scaled, low_ones], axis=1)

        channels = x_ref.shape[1]
        product_ref[0:channels, :] = channel_products(slots, x_ref, right_of)
        product_ref[channels:, :] = jnp.zeros((product_ref.shape[0] - channels, FIRST), F32)
        clips, _, size, _ = product_out.shape
        for clip in range(clips):
            at = slice(clip * size, (clip + 1) * size)
            for tile in range(3):
                product_out[clip, tile] = rest_product_ref[at, 128 * tile : 128 * (tile + 1)]
            for tile in range(5):
                product_out[clip, 3 + tile] = product_ref[at, 128 * tile : 128 * (tile + 1)]


def kernel_grads(grid, slots, first_ref, mid_ref, small_ref, d_ref, out_ref, mid_acc_ref, small_acc_ref, turned_ref):
    group_rows = grid.group * grid.pitch
    mid_acc_ref[...] = jnp.zeros_like(mid_acc_ref)
    small_acc_ref[...] = jnp.zeros_like(small_acc_ref)

    def neighbour(slot):
        return jnp.minimum(first_ref[0] + slot, TAPS - 1) // 9

    @pl.loop(0, grid.side // grid.group)
    def _(group):
        base = grid.lead + group * group_rows
        left = d_ref[rows_at(base, group_rows), :].T
        for slot in range(slots):
            tap = lax.rem(jnp.minimum(first_ref[0] + slot, TAPS - 1), 9)
            at = rows_at(
                base + (tap // 3 - 1) * grid.pitch + (lax.rem(tap, 3) - 1) * PITCH, group_rows
            )
            lanes = pl.ds(pl.multiple_of(neighbour(slot) * 128, 128), 128)
            right = jnp.concatenate([mid_ref[at, lanes], mid_ref[at, 384:512]], axis=1)
            mid_acc_ref[slot] += jnp.dot(left[0:384], right, preferred_element_type=F32)
            small_acc_ref[slot] += jnp.dot(
                left[384:512], small_ref[at, :], preferred_element_type=F32
            )

    share = round_up(slots * TAP_ROWS, 16 * out_ref.shape[0]) // out_ref.shape[0]

    def put(start, values):
        done = 0
        while done < values.shape[0]:
            clip, at = divmod(start + done, share)
            size = min(values.shape[0] - done, share - at)
            out_ref[clip, at : at + size, :] = values[done : done + size].astype(BF16)
            done = done + size

    half = MID_IN // 2
    for slot in range(slots):
        base = slot * TAP_ROWS
        rest = pl.ds(pl.multiple_of(neighbour(slot) * 32, 32), 32)
        for tile in range(3):
            lines = slice(128 * tile, 128 * (tile + 1))
            turned_ref[0:128, :] = mid_acc_ref[slot, lines, 0:128].T
            turned_ref[MID_IN : MID_IN + 128, :] = mid_acc_ref[slot, lines, 128:256].T
            turned_ref[128:MID_IN, :] = turned_ref[
                pl.ds(pl.multiple_of(MID_IN + neighbour(slot) * 32, 32), 32), :
            ]
            if tile < 2:
                put(base + MID_IN * tile, turned_ref[0:MID_IN, :])
            else:
                folded = turned_ref[0:half, :] + pltpu.roll(turned_ref[half:MID_IN, :], 64, 1)
                put(base + 2 * MID_IN, folded)
        turned_ref[0:128, :] = small_acc_ref[slot].T
        put(base + 2 * MID_IN + half, turned_ref[rest, :])
    used = slots * TAP_ROWS
    put(used, jnp.zeros((share * out_ref.shape[0] - used, 128), F32))


class Spread:
    def __init__(self, grid, plane_ref, across_ref, scale_ref, length):
        self.grid, self.plane, self.across, self.scale = (grid, plane_ref, across_ref, scale_ref)
        clear_edges(grid, plane_ref)
        window = box_window(grid.side, length)
        scale_ref[0] = box_scale(0, grid.side, window)
        scale_ref[1] = box_scale(1, grid.side, window)
        edge = jnp.zeros((PITCH, POOLED), F32)
        across_ref[0:PITCH, :] = edge
        across_ref[PITCH + grid.line_rows :, :] = edge

    def put(self, line, values):
        rows = self.grid.line_rows
        inner = jnp.where((line == 0) | (line == self.grid.side - 1), 0, 1)
        values = values * self.scale[inner]
        across = self.across
        across[PITCH : PITCH + rows, :] = values + earlier(values) + later(values)
        self.plane[rows_at((line + 1) * rows, rows), :] = (
            across[0:rows, :] + across[PITCH : PITCH + rows, :] + across[2 * PITCH :, :]
        )

    def get(self, start, size):
        rows = self.grid.line_rows
        return (
            self.plane[rows_at(start, size), :]
            + self.plane[rows_at(start + rows, size), :]
            + self.plane[rows_at(start + 2 * rows, size), :]
        )

    @staticmethod
    def scratch(grid):
        return [
            pltpu.VMEM((grid.rows + 2 * grid.line_rows, POOLED), F32),
            pltpu.VMEM((grid.line_rows + 2 * PITCH, POOLED), F32),
            pltpu.VMEM((2, grid.line_rows, POOLED), F32),
        ]


def channel_products(slots, x_ref, right_of):
    total = None
    for part in range(slots.parts):
        slot = part * slots.each
        pair = slot - (slots.empty if slot >= slots.gap + slots.empty else 0)
        pair = min(pair, slots.pairs - slots.each)
        product = jnp.dot(
            x_ref[part], right_of(pair * slots.pair_rows, slots.rows), preferred_element_type=F32
        )
        total = product if total is None else total + product
    return total


def rest_constants(outer_ref, total_ref, gain_ref, block):
    pool = OUTER - POOLED

    def pick(ref, lo, hi):
        return jnp.concatenate([ref[lo:hi, 0:DIRECT], ref[lo:hi, pool:]], axis=1)

    return before_norm(
        pick(gain_ref, block, block + 1), pick(outer_ref, 1, 2), pick(total_ref, 0, 2), pick(outer_ref, 2, 3)
    )


def point_back(grid, slots, block, kept, length_ref, place_ref, h_far, outer_ref, total_ref, gain_ref, error_far, reduced_far, r_far, moment_ref, sums_in_ref, reduced_gain_ref, x_far, p_far, *refs):
    pooled_slope_in, pooled_product_in, kept_far, *refs = refs
    dx_ref, dp_ref, reduced_total_ref, outer_sums_ref, *refs = refs
    h_ref, error_ref, reduced_ref, r_ref, x_ref, p_ref, du_ref, acc_ref, *refs = refs
    plane_ref, across_ref, scale_ref, sums_ref, pooled_slope_ref, pooled_product_ref, kept_ref, *refs = refs
    sem_ref, in_sem = refs
    rows = grid.line_rows
    pool = OUTER - POOLED
    lines = Lines(
        grid,
        (
            (h_far, 0, DIRECT),
            (h_far, pool, OUTER),
            (error_far, 0, DIRECT),
            (error_far, pool, OUTER),
            (reduced_far, 0, REDUCED),
            (r_far, 0, REDUCED),
        ),
        ((h_ref, 0), (h_ref, DIRECT), (error_ref, 0), (error_ref, DIRECT), (reduced_ref, 0), (r_ref, 0)),
        sem_ref,
    )
    lines.first()
    kept_rows = kept_ref.shape[1]
    arriving = copies(
        (x_far, p_far, kept_far.at[:, pl.ds(slots.rows, kept_rows), :]), (x_ref, p_ref, kept_ref), in_sem
    )
    for copy in arriving:
        copy.start()
    length = length_ref[0]
    total = total_of(sums_in_ref)
    reduced_total_ref[...] = total
    mid = before_norm(
        reduced_gain_ref[block : block + 1],
        moment_ref[1:2, DIRECT:SECOND],
        total,
        outer_ref[2:3, 0:REDUCED],
    )
    rest = rest_constants(outer_ref, total_ref, gain_ref, block)
    mask = frame_mask(rows, length, DIRECT + POOLED)
    spread = Spread(grid, plane_ref, across_ref, scale_ref, length)

    def visit(line):
        at = rows_at(line * rows, rows)
        back = rest[0] * error_ref[at, :].astype(F32) - rest[1] - rest[2] * h_ref[at, :].astype(F32)
        back = back * mask
        du_ref[at, 0:DIRECT] = back[:, :DIRECT].astype(BF16)
        spread.put(line, back[:, DIRECT:])
        back = mid[0] * r_ref[at, :].astype(F32) - mid[1] - mid[2] * reduced_ref[at, :].astype(F32)
        du_ref[at, DIRECT:SECOND] = (back * mask[:, :REDUCED]).astype(BF16)

    lines.run(visit)
    for copy in arriving:
        copy.wait()
    sums_ref[...] = jnp.zeros_like(sums_ref)
    pooled_slope_ref[:, DIRECT:] = pooled_slope_in[...]
    pooled_product_ref[:, DIRECT:] = pooled_product_in[...]
    for pair in range(slots.pairs):
        slot = pair + (slots.empty if pair >= slots.gap else 0)
        at = slice(pair * rows, (pair + 1) * rows)
        start = slot % slots.each * rows
        values = kept_ref[slot // slots.each, start : start + rows, :]
        pooled_slope_ref[at, 0:DIRECT] = values[:, :DIRECT]
        pooled_product_ref[at, 0:DIRECT] = values[:, DIRECT:]

    @pl.loop(0, grid.side)
    def _(line):
        at = rows_at(line * rows, rows)
        du_ref[at, SECOND:] = (spread.get(line * rows, rows) * mask[:, :POOLED]).astype(BF16)
        dx = jnp.dot(du_ref[at, :], p_ref[...], preferred_element_type=F32).astype(BF16)
        dx_ref[at, :] = dx
        for number, ref in enumerate((pooled_slope_ref, pooled_product_ref)):
            sums_ref[8 * number : 8 * number + 8] += partial_sum(
                dx.astype(F32) * ref[at, :].astype(F32)
            )

    write_sums(outer_sums_ref, sums_ref, 0, OUTER)
    acc_ref[...] = lax.dot_general(
        x_ref[...], du_ref[...], (((0,), (0,)), ((), ())), preferred_element_type=F32
    )
    start = pl.multiple_of(place_ref[0] * kept, 16) if kept < acc_ref.shape[0] else 0
    clips, size, _ = dp_ref.shape
    for tile in range(FIRST // 128):
        values = acc_ref[pl.ds(start, kept), 128 * tile : 128 * (tile + 1)].astype(BF16)
        done = 0
        while done < kept:
            clip, at = divmod(kept * tile + done, size)
            few = min(kept - done, size - at)
            dp_ref[clip, at : at + few, :] = values[done : done + few]
            done = done + few
    used = (FIRST // 128) * kept
    while used < clips * size:
        clip, at = divmod(used, size)
        dp_ref[clip, at:, :] = jnp.zeros((size - at, 128), BF16)
        used = used + size - at


def rest_back(grid, small, slots, block, length_ref, outer_ref, total_ref, gain_ref, grad_ref, h_far, slope_far, kept_far, x_far, du_far, product_ref, *refs):
    h_ref, slope_ref, x_ref, du_ref, plane_ref, across_ref, scale_ref, sem_ref, x_sem, du_sem = refs
    rows = grid.line_rows
    pool = OUTER - POOLED

    def direct(step, lo, hi):
        slot = slots.slot_of(step)
        at = rows_at(lax.rem(slot, slots.each) * slots.pair_rows, slots.pair_rows)
        return kept_far.at[slot // slots.each, at, pl.ds(lo, hi - lo)]

    lines = Lines(
        grid,
        (
            (direct, 0, DIRECT),
            (h_far, SECOND, FIRST),
            (direct, DIRECT, 2 * DIRECT),
            (slope_far, SECOND, FIRST),
        ),
        ((h_ref, 0), (h_ref, DIRECT), (slope_ref, 0), (slope_ref, DIRECT)),
        sem_ref,
    )
    lines.first()
    x_copy = pltpu.make_async_copy(x_far, x_ref, x_sem.at[0])
    x_copy.start()
    length = length_ref[0]
    matrix = spread_matrix(grid, small)
    a, b, c = rest_constants(outer_ref, total_ref, gain_ref, block)
    mask = frame_mask(rows, length, DIRECT + POOLED)
    spread = Spread(grid, plane_ref, across_ref, scale_ref, length)

    def visit(step):
        for number in range(lines.step):
            line = step * lines.step + number
            at = rows_at(line * rows, rows)
            coarse = grad_ref[rows_at((line // 2) * small.line_rows, small.line_rows), :]
            grad = jnp.dot(
                matrix,
                jnp.concatenate([coarse[:, :DIRECT], coarse[:, pool:]], axis=1),
                preferred_element_type=F32,
            )
            back = a * (grad * slope_ref[at, :].astype(F32)) - b - c * h_ref[at, :].astype(F32)
            back = back * mask
            du_ref[at, 0:DIRECT] = back[:, :DIRECT].astype(BF16)
            spread.put(line, back[:, DIRECT:])

    lines.run(visit)
    x_copy.wait()
    wide = lines.size
    pool_mask = frame_mask(wide, length)

    def leaving(step):
        at = rows_at(step * wide, wide)
        return pltpu.make_async_copy(du_ref.at[at, :], du_far.at[at, :], du_sem.at[0])

    @pl.loop(0, lines.steps)
    def _(step):
        at = rows_at(step * wide, wide)
        du_ref[at, DIRECT:] = (spread.get(step * wide, wide) * pool_mask).astype(BF16)
        leaving(step).start()

    channels = x_ref.shape[1]
    product_ref[0:channels, :] = channel_products(
        slots, x_ref, lambda start, size: du_ref[start : start + size, :]
    )
    product_ref[channels:, :] = jnp.zeros((product_ref.shape[0] - channels, DIRECT + POOLED), F32)
    pltpu.make_async_copy(du_ref, du_far, du_sem.at[0]).wait()


def mid_back(grid, block, length_ref, place_ref, moment_ref, sums_in_ref, gain_ref, du_far, h_far, r_far, p_far, dx_far, total_ref, *refs):
    du_ref, h_ref, r_ref, p_ref, dx_ref, sem_ref, p_sem, dx_sem = refs
    lines = Lines(
        grid,
        ((du_far, 0, DIRECT + POOLED), (h_far, 0, REDUCED), (r_far, 0, REDUCED)),
        ((du_ref, 0), (h_ref, 0), (r_ref, 0)),
        sem_ref,
    )
    lines.first()
    p_copy = pltpu.make_async_copy(p_far.at[place_ref[0]], p_ref, p_sem.at[0])
    p_copy.start()
    total = total_of(sums_in_ref)
    total_ref[...] = total
    a, b, c = before_norm(
        gain_ref[block : block + 1], moment_ref[1:2, DIRECT:], total, moment_ref[2:3, DIRECT:]
    )
    mask = frame_mask(lines.size, length_ref[0], REDUCED)
    p_copy.wait()

    def leaving(step):
        at = rows_at(step * lines.size, lines.size)
        return pltpu.make_async_copy(dx_ref.at[at, :], dx_far.at[at, :], dx_sem.at[0])

    def visit(step):
        at = rows_at(step * lines.size, lines.size)
        back = a * r_ref[at, :].astype(F32) - b - c * h_ref[at, :].astype(F32)
        du = jnp.concatenate(
            [du_ref[at, :DIRECT], (back * mask).astype(BF16), du_ref[at, DIRECT:]], axis=1
        )
        dx_ref[at, :] = jnp.dot(du, p_ref[...], preferred_element_type=F32).astype(BF16)
        leaving(step).start()

    lines.run(visit)
    pltpu.make_async_copy(dx_ref, dx_far, dx_sem.at[0]).wait()


def combine(block, pieces_ref, moment_ref, sums_in_ref, gain_ref, out_ref):
    total = total_of(sums_in_ref)
    a, b, c = before_norm(
        gain_ref[block : block + 1], moment_ref[1:2, DIRECT:], total, moment_ref[2:3, DIRECT:]
    )
    size = out_ref.shape[0] // 5
    products = total_of(pieces_ref)
    for tile in range(2):
        out_ref[size * tile : size * (tile + 1), :] = products[tile].astype(BF16)
        lanes = slice(128 * tile, 128 * (tile + 1))
        mid = a[:, lanes] * products[3 + tile] - b[:, lanes] * products[7] - c[:, lanes] * products[5 + tile]
        out_ref[size * (2 + tile) : size * (3 + tile), :] = mid.astype(BF16)
    out_ref[4 * size :, :] = products[2].astype(BF16)


def write_taps(read, slots, mid_ref, small_ref, mid_out, small_out, sem_ref):
    half = MID_IN // 2

    def leaving(tap):
        return (
            pltpu.make_async_copy(mid_ref.at[tap], mid_out.at[tap], sem_ref.at[0]),
            pltpu.make_async_copy(small_ref.at[tap], small_out.at[tap], sem_ref.at[1]),
        )

    for tap in range(TAPS):
        part, slot = divmod(tap, slots)
        base = slot * TAP_ROWS
        folded = read(part, base + 2 * MID_IN, half)
        mid_ref[tap, :, 0:128] = read(part, base, MID_IN)
        mid_ref[tap, :, 128:256] = read(part, base + MID_IN, MID_IN)
        mid_ref[tap, 0:half, 256:320] = folded[:, 0:64]
        mid_ref[tap, half:MID_IN, 256:320] = pltpu.roll(folded, 64, 1)[:, 0:64]
        small_ref[tap] = read(part, base + 2 * MID_IN + half, SMALL_IN)
        for copy in leaving(tap):
            copy.start()
    pltpu.make_async_copy(mid_ref, mid_out, sem_ref.at[0]).wait()
    pltpu.make_async_copy(small_ref, small_out, sem_ref.at[1]).wait()


def write_point(read, parts, kept, point_ref, wide_ref):
    for tile in range(FIRST // 128):
        for part in range(parts):
            start, stop = (kept * part, kept * (part + 1))
            values = read(part, kept * tile, kept)
            if kept * parts == CHANNELS:
                wide_ref[start:stop, :] = values
                continue
            for lo, hi, moved in ((0, 576, 0), (640, OUTER, 64)):
                lo, hi = (max(lo, start), min(hi, stop))
                if lo < hi:
                    wide_ref[lo - moved : hi - moved, :] = values[lo - start : hi - start]
        turned = wide_ref[...].T
        if tile < 3:
            point_ref[128 * tile : 128 * (tile + 1), :] = turned
        elif tile == 3:
            point_ref[384:448, :] = turned[0:64]
        else:
            point_ref[448:576, :] = turned


def copy_out(pairs, sem_ref):
    copies = [
        pltpu.make_async_copy(source, target, sem_ref.at[number])
        for number, (source, target) in enumerate(pairs)
    ]
    for copy in copies:
        copy.start()
    for copy in copies:
        copy.wait()


def share_reader(ref, clips, lo, share):
    def read(part, start, size):
        pieces, done = ([], 0)
        while done < size:
            clip, at = divmod(start + done, share)
            few = min(size - done, share - at)
            pieces.append(ref[part * clips + clip, lo + at : lo + at + few, :].astype(F32))
            done = done + few
        return pieces[0] if len(pieces) == 1 else jnp.concatenate(pieces, axis=0)

    return read


def unpack_second(clips, slots, shares_ref, mid_out, small_out, mid_ref, small_ref, sem_ref):
    read = share_reader(shares_ref, clips, 0, shares_ref.shape[1])
    write_taps(read, slots, mid_ref, small_ref, mid_out.at[1], small_out.at[1], sem_ref)


def unpack_first(parts, clips, slots, share, shares_ref, *refs):
    totals, refs = (refs[:4], refs[4:])
    mid_in, small_in, mid_out, small_out, point_out, gain_out, shift_out, *refs = refs
    mid_ref, small_ref, point_ref, wide_ref, sem_ref = refs
    for block in range(2):
        outer_ref, reduced_ref = totals[2 * block : 2 * block + 2]
        for row, out in enumerate((shift_out, gain_out)):
            at, line = (slice(block, block + 1), slice(row, row + 1))
            out[at, 0:256] = outer_ref[line, 0:256]
            out[at, 256:448] = reduced_ref[line, 0:192]
            out[at, 448:576] = outer_ref[line, 768:896]
            out[at, 576:896] = outer_ref[line, 256:576]
            out[at, 896:1024] = outer_ref[line, 640:768]
    read = share_reader(shares_ref, clips, share, shares_ref.shape[1] - share)
    write_point(read, parts, OUTER // parts, point_ref, wide_ref)
    last = pltpu.make_async_copy(point_ref, point_out.at[1], sem_ref.at[2])
    last.start()
    read = share_reader(shares_ref, clips, 0, share)
    write_taps(read, slots, mid_ref, small_ref, mid_out.at[0], small_out.at[0], sem_ref)
    last.wait()


def unpack_point(parts, clips, kept, place_ref, clip_ref, mine_ref, other_ref, point_in, point_out, buffer_ref, point_ref, wide_ref, sem_ref):
    tiles = FIRST // 128
    size = buffer_ref.shape[2] // clips
    for chip in range(clips // 2):
        for step in range(parts):
            part = lax.rem(place_ref[0] - step + parts, parts)
            for swapped, ref in enumerate((mine_ref, other_ref)):
                owner = clip_ref[0] ^ (2 * chip) ^ swapped
                source = (chip * parts + step) * tiles * size
                for tile in range(tiles):
                    buffer_ref[part, tile, rows_at(owner * size, size), :] = ref[
                        source + tile * size : source + (tile + 1) * size, :
                    ]

    def read(part, start, size):
        tile, at = divmod(start, kept)
        return buffer_ref[part, tile, at : at + size, :].astype(F32)

    write_point(read, parts, kept, point_ref, wide_ref)
    last = pltpu.make_async_copy(point_ref, point_out.at[0], sem_ref.at[0])
    last.start()
    last.wait()


def prepare(parts, mid_in, small_in, point_in, gain_in, shift_in, *refs):
    kernels, (point_ref, second_ref, *vectors) = (refs[:8], refs[8:14])
    for block in range(2):
        main_ref, last_ref, few_ref, back_ref = kernels[4 * block : 4 * block + 4]

        @pl.loop(0, 9)
        def _(tap):
            for number in range(3):
                source = 9 * number + tap
                main_ref[tap, 128 * number : 128 * (number + 1), :] = mid_in[block, source, 0:128, 0:256]
                main_ref[tap, 384 + 32 * number : 416 + 32 * number, :] = mid_in[
                    block, source, 128:MID_IN, 0:256
                ]
            main_ref[tap, 480:512, :] = jnp.zeros((32, 256), BF16)
            small = jnp.concatenate(
                [small_in[block, 9 * number + tap] for number in range(3)]
                + [jnp.zeros((32, 128), BF16)],
                axis=0,
            )
            at = pl.ds(pl.multiple_of(tap * 128, 128), 128)
            few_ref[at, :] = small
            back_ref[at, :] = small.astype(F32).T.astype(BF16)

        @pl.loop(0, 3)
        def _(place):
            for number in range(3):
                for rows, start, size in (
                    (slice(0, 128), 128 * number, 128),
                    (slice(128, MID_IN), 384 + 32 * number, 32),
                ):
                    pieces = [
                        mid_in[block, 9 * number + 3 * line + place, rows, 256:MID_OUT].astype(F32)
                        for line in range(3)
                    ]
                    pieces.append(jnp.zeros((size, 64), F32))
                    last_ref[place, start : start + size, :] = jnp.concatenate(
                        pieces, axis=1
                    ).astype(BF16)
            last_ref[place, 480:512, :] = jnp.zeros((32, 256), BF16)

    own = point_ref.shape[2]
    for lo, hi, at in ((0, 448, 0), (448, SQUEEZED, SECOND)):
        values = point_in[0, lo:hi, :].astype(F32)
        for part in range(parts):
            point_ref[part, at : at + hi - lo, :] = values[:, own * part : own * (part + 1)].astype(
                BF16
            )
        values = point_in[1, lo:hi, :].astype(F32)
        gap = jnp.zeros((hi - lo, 64), F32)
        second_ref[at : at + hi - lo, :] = jnp.concatenate(
            [values[:, :576], gap, values[:, 576:]], axis=1
        ).astype(BF16)
    for part in range(parts):
        point_ref[part, 448:SECOND, :] = jnp.zeros((64, own), BF16)
    second_ref[448:SECOND, :] = jnp.zeros((64, OUTER), BF16)
    for source, outer, reduced in ((gain_in, vectors[0], vectors[1]), (shift_in, vectors[2], vectors[3])):
        outer[:, 0:256] = source[:, 0:256]
        outer[:, 256:576] = source[:, 576:896]
        outer[:, 576:640] = jnp.zeros((2, 64), F32)
        outer[:, 640:768] = source[:, 896:1024]
        outer[:, 768:896] = source[:, 448:576]
        reduced[:, 0:192] = source[:, 256:448]
        reduced[:, 192:256] = jnp.zeros((2, 64), F32)


def round_up(value, unit):
    return -(-value // unit) * unit


def spread_over(values, axis, size):
    received = [values]
    for step in range(1, size):
        perm = [(source, (source + step) % size) for source in range(size)]
        received.append(lax.ppermute(values, axis, perm))
    return received


def after(values, earlier):
    return lax.optimization_barrier((values, earlier))[0]


def exchange(values):
    return lax.all_to_all(values, "dp", 0, 0, tiled=True)


def summed(pieces):
    pieces = exchange(pieces)
    return jnp.sum(pieces.astype(F32), axis=0).astype(BF16)


def gather_chips(column, clips, work=None):
    columns = [column]
    for chip in range(1, clips // 2):
        perm = [(source, source ^ (2 * chip)) for source in range(clips)]
        columns.append(lax.ppermute(column, "dp", perm))
    if work is not None:
        columns = after(columns, work)
    mine = jnp.concatenate(columns, axis=0)
    other = lax.ppermute(mine, "dp", [(source, source ^ 1) for source in range(clips)])
    return (mine, other)


def on_device(frames, lengths, cotangent, pointwise, conv_mid, conv_small, gains, shifts):
    parts = lax.axis_size("branch")
    clips = lax.axis_size("dp")
    place = lax.axis_index("branch").astype(jnp.int32)
    side = frames.shape[2]
    grid, small = (Grid(side), Grid(side // 2))
    slots = Slots(grid, parts)
    cells = side * side
    own_channels = frames.shape[-1]
    length = lengths.astype(jnp.int32)
    half_length = length // 2
    place_one = place.reshape(1)

    own = frames[0].transpose(1, 2, 0, 3).reshape(grid.rows, own_channels)
    turned = call(functools.partial(turn, slots), shape((parts, own_channels, slots.rows), BF16))(own)
    by_pairs = lax.all_to_all(turned, "branch", 0, 0, tiled=True)
    kernel_shapes = (
        shape((9, 512, 256), BF16),
        shape((3, 512, 256), BF16),
        shape((1152, 128), BF16),
        shape((1152, 128), BF16),
    )
    prepared = call(
        functools.partial(prepare, parts),
        (
            *kernel_shapes,
            *kernel_shapes,
            shape((parts, FIRST, own_channels), BF16),
            shape((FIRST, OUTER), BF16),
            shape((2, OUTER), F32),
            shape((2, REDUCED), F32),
            shape((2, OUTER), F32),
            shape((2, REDUCED), F32),
        ),
    )(conv_mid, conv_small, pointwise.swapaxes(1, 2), gains, shifts)
    kernels = (prepared[0:4], prepared[4:8])
    point_first, point_second, outer_gain, reduced_gain, outer_shift, reduced_shift = prepared[8:]

    local_count = (length * (slots.held(place) * 2 * side)).astype(F32)
    mid, pool, direct, sums = call(
        functools.partial(first_pointwise, slots),
        (
            shape((mid_rows(slots), 128), BF16),
            shape((slots.rows + PITCH, POOLED), BF16),
            shape((slots.rows, DIRECT), F32),
            shape((clips, 3, SECOND), F32),
        ),
        [pltpu.VMEM((slots.rows, FIRST), F32)],
        scalars=2,
    )(length, local_count, by_pairs, point_first)
    mids = spread_over(mid, "branch", parts)
    sums = spread_over(jnp.sum(exchange(sums), axis=0), "branch", parts)
    pooled_direct, kept_direct, moment = call(
        functools.partial(first_direct, grid, small, slots, 0),
        (
            shape((slots.each * small.line_rows, DIRECT), BF16),
            shape((slots.rows + slots.each * small.line_rows, 2 * DIRECT), BF16),
            shape((3, SECOND), F32),
        ),
        scalars=1,
        cost=3,
    )(length, direct, outer_gain, outer_shift, *sums)
    pool, pooled_direct = after((pool, pooled_direct), mids)
    pools = spread_over(pool, "branch", parts)
    h_reduced, taps_mid, taps_few, e, e_sums = call(
        functools.partial(first_convolve, grid, slots, 0),
        conv_outputs(grid),
        conv_scratch(grid),
        scalars=2,
        cost=40,
        far=range(5 + parts, 8 + parts),
        far_out=range(4),
    )(length, place_one, *mids, moment, reduced_gain, reduced_shift, *kernels[0][:3])
    pooled_directs = spread_over(after(pooled_direct, (pools, e_sums)), "branch", parts)
    kept_direct = lax.all_gather(after(kept_direct, pooled_directs), "branch", axis=0)
    q_pool, second_sums = call(
        functools.partial(first_pool, grid, slots),
        (shape((grid.rows, POOLED), F32), shape((clips, 2, FIRST), F32)),
        [
            pltpu.VMEM((grid.rows + 2 * grid.line_rows, POOLED), F32),
            pltpu.VMEM((16, POOLED), F32),
        ],
        scalars=2,
    )(length, place_one, *pools, e_sums)
    second_sums = exchange(second_sums)
    pair = 2 * grid.line_rows
    pooled, h_outer, slope, outer, pooled_slope, pooled_product = call(
        functools.partial(first_output, grid, small, 0),
        (
            shape((small.rows, FIRST), BF16),
            shape((grid.rows, FIRST), BF16),
            shape((grid.rows, FIRST), BF16),
            shape((3, OUTER), F32),
            shape((small.rows, FIRST), BF16),
            shape((small.rows, FIRST), BF16),
        ),
        [
            pltpu.VMEM((2, pair, POOLED), F32),
            pltpu.VMEM((2, pair, SECOND), F32),
            pltpu.VMEM((2, pair, FIRST), BF16),
            pltpu.VMEM((2, pair, FIRST), BF16),
            *[pltpu.SemaphoreType.DMA((2,))] * 4,
        ],
        scalars=1,
        far=(1, 2),
        far_out=(1, 2),
    )(
        length,
        q_pool,
        e,
        moment,
        second_sums,
        outer_gain,
        outer_shift,
    )

    small_count = half_length.astype(F32) * float(small.side * small.side)
    q_small, sums_small, pooled = call(
        functools.partial(second_pointwise, small, slots),
        (
            shape((small.rows, FIRST), F32),
            shape((clips, 3, FIRST), F32),
            shape((small.rows, OUTER), BF16),
        ),
        [
            pltpu.VMEM((small.rows + 2 * small.line_rows, POOLED), F32),
            pltpu.VMEM((16, SECOND), F32),
            pltpu.VMEM((16, POOLED), F32),
        ],
        scalars=3,
    )(half_length, place_one, small_count, *pooled_directs, pooled, point_second)
    sums_small = exchange(sums_small)
    h_reduced_small, taps_mid_small, taps_few_small, e_small, e_sums_small, moment_small = call(
        functools.partial(second_convolve, small, 1),
        (*conv_outputs(small, clips), shape((3, FIRST), F32)),
        conv_scratch(small),
        scalars=1,
        far=range(5, 8),
        far_out=range(4),
    )(half_length, q_small, sums_small, reduced_gain, reduced_shift, *kernels[1][:3])
    e_sums_small = exchange(e_sums_small)
    cot = cotangent[0].transpose(1, 2, 0, 3).reshape(small.side**2, cotangent.shape[1], CHANNELS)
    act, h_outer_small, error_small, outer_small, outer_sums_small = call(
        functools.partial(second_output, small, 1),
        (
            shape(cot.shape, BF16),
            shape((small.rows, OUTER), BF16),
            shape((small.rows, OUTER), BF16),
            shape((3, OUTER), F32),
            shape((clips, 2, OUTER), F32),
        ),
        [pltpu.VMEM((16, OUTER), F32)],
        scalars=1,
    )(half_length, q_small, e_small, moment_small, e_sums_small, outer_gain, outer_shift, cot)

    taps_each = -(-TAPS // parts)
    tap_share = round_up(taps_each * TAP_ROWS, 16 * clips) // clips
    first_tap = place_one * taps_each

    def conv_back_scratch(at):
        return [
            pltpu.VMEM((9, 512, 256), BF16),
            pltpu.VMEM((3, 512, 256), BF16),
            pltpu.VMEM((1152, 128), BF16),
            pltpu.VMEM((at.padded, 256), BF16),
            pltpu.VMEM((at.group * at.pitch, FIRST), F32),
            pltpu.VMEM((16, REDUCED), F32),
            pltpu.SemaphoreType.DMA((3,)),
        ]

    gathered = exchange(outer_sums_small)
    d_low, total_small, packed_small = call(
        functools.partial(second_back, small, None, 1, taps_each),
        (
            shape((small.padded, SECOND), BF16),
            shape((2, OUTER), F32),
            shape((clips, tap_share, 128), BF16),
        ),
        second_back_scratch(small, taps_each),
        scalars=2,
        cost=8,
        far=(2, 6, 7, 8),
        far_out=(0,),
    )(
        half_length,
        first_tap,
        h_outer_small,
        outer_small,
        gathered,
        outer_gain,
        error_small,
        taps_mid_small,
        taps_few_small,
    )
    r_low, sums_low = call(
        functools.partial(conv_back, small, None, 1),
        (shape((small.rows, REDUCED), BF16), shape((clips, 2, REDUCED), F32)),
        conv_back_scratch(small),
        scalars=1,
        cost=8,
        far=(5, 6, 7),
    )(
        half_length,
        d_low,
        h_reduced_small,
        reduced_gain,
        reduced_shift,
        *kernels[1][:2],
        kernels[1][3],
    )
    share_small = summed(packed_small)
    sums_low, share_small = lax.optimization_barrier((sums_low, share_small))
    gathered = exchange(sums_low)
    kept = OUTER // parts
    point_share = round_up(kept * (FIRST // 128), 16 * clips) // clips
    coarse_rows = slots.each * small.line_rows
    dx_small, point_packed, reduced_total_small, outer_sums = call(
        functools.partial(point_back, small, slots, 1, kept),
        (
            shape((small.rows, OUTER), BF16),
            shape((clips, point_share, 128), BF16),
            shape((2, REDUCED), F32),
            shape((clips, 2, OUTER), F32),
        ),
        [
            pltpu.VMEM((small.rows, DIRECT + POOLED), BF16),
            pltpu.VMEM((small.rows, DIRECT + POOLED), BF16),
            pltpu.VMEM((small.rows, REDUCED), BF16),
            pltpu.VMEM((small.rows, REDUCED), BF16),
            pltpu.VMEM((small.rows, OUTER), BF16),
            pltpu.VMEM((FIRST, OUTER), BF16),
            pltpu.VMEM((small.rows, FIRST), BF16),
            pltpu.VMEM((OUTER, FIRST), F32),
            *Spread.scratch(small),
            pltpu.VMEM((16, OUTER), F32),
            pltpu.VMEM((small.rows, OUTER), BF16),
            pltpu.VMEM((small.rows, OUTER), BF16),
            pltpu.VMEM((parts, coarse_rows, 2 * DIRECT), BF16),
            Lines.semaphores(small, 6),
            pltpu.SemaphoreType.DMA((3,)),
        ],
        scalars=2,
        cost=10,
        far=(2, 6, 7, 8, 12, 13, 16),
    )(
        half_length,
        place_one,
        h_outer_small,
        outer_small,
        total_small,
        outer_gain,
        error_small,
        h_reduced_small,
        r_low,
        moment_small,
        gathered,
        reduced_gain,
        pooled,
        point_second,
        pooled_slope,
        pooled_product,
        kept_direct,
    )
    whole_small = lax.all_gather(share_small, ("branch", "dp"), axis=0)

    gathered = exchange(outer_sums)
    d_low, total, packed = call(
        functools.partial(second_back, grid, small, 0, taps_each),
        (
            shape((grid.padded, SECOND), BF16),
            shape((2, OUTER), F32),
            shape((clips, tap_share + point_share, 128), BF16),
        ),
        second_back_scratch(grid, taps_each),
        scalars=2,
        cost=18,
        far=(2, 6, 9, 10),
        far_out=(0,),
    )(length, first_tap, h_outer, outer, gathered, outer_gain, slope, dx_small, point_packed, taps_mid, taps_few)
    product_rows = round_up(own_channels, 16 * clips)
    du_rest, rest_product = call(
        functools.partial(rest_back, grid, small, slots, 0),
        (shape((grid.rows, DIRECT + POOLED), BF16), shape((product_rows, DIRECT + POOLED), F32)),
        [
            pltpu.VMEM((grid.rows, DIRECT + POOLED), BF16),
            pltpu.VMEM((grid.rows, DIRECT + POOLED), BF16),
            pltpu.VMEM(turned.shape, BF16),
            pltpu.VMEM((grid.rows, DIRECT + POOLED), BF16),
            *Spread.scratch(grid),
            Lines.semaphores(grid, 4),
            pltpu.SemaphoreType.DMA((1,)),
            pltpu.SemaphoreType.DMA((1,)),
        ],
        scalars=1,
        cost=8,
        far=(5, 6, 7, 8),
        far_out=(0,),
    )(length, outer, after(total, packed), outer_gain, dx_small, h_outer, slope, kept_direct, turned)
    share = summed(packed)
    d_low, share = lax.optimization_barrier((after(d_low, rest_product), share))
    r_low, sums_low, products = call(
        functools.partial(conv_back, grid, slots, 0),
        (
            shape((grid.rows, REDUCED), BF16),
            shape((clips, 2, REDUCED), F32),
            shape((clips, 8, product_rows // clips, 128), F32),
        ),
        [
            *conv_back_scratch(grid),
            pltpu.VMEM(turned.shape, BF16),
            pltpu.VMEM((product_rows, FIRST), F32),
            pltpu.SemaphoreType.DMA((1,)),
        ],
        scalars=1,
        cost=22,
        far=(5, 6, 7, 8),
    )(
        length,
        d_low,
        h_reduced,
        reduced_gain,
        reduced_shift,
        *kernels[0][:2],
        kernels[0][3],
        turned,
        rest_product,
    )
    whole = lax.all_gather(share, ("branch", "dp"), axis=0)
    gathered = exchange(sums_low)
    pieces = exchange(products)
    dx, reduced_total = call(
        functools.partial(mid_back, grid, 0),
        (shape((grid.rows, own_channels), BF16), shape((2, REDUCED), F32)),
        [
            pltpu.VMEM((grid.rows, DIRECT + POOLED), BF16),
            pltpu.VMEM((grid.rows, REDUCED), BF16),
            pltpu.VMEM((grid.rows, REDUCED), BF16),
            pltpu.VMEM((FIRST, own_channels), BF16),
            pltpu.VMEM((grid.rows, own_channels), BF16),
            Lines.semaphores(grid, 3),
            pltpu.SemaphoreType.DMA((1,)),
            pltpu.SemaphoreType.DMA((1,)),
        ],
        scalars=2,
        cost=8,
        far=(5, 6, 7, 8),
        far_out=(0,),
    )(length, place_one, moment, gathered, reduced_gain, du_rest, h_reduced, r_low, point_first)
    pieces, dx = lax.optimization_barrier((pieces, dx))
    point_sum = call(
        functools.partial(combine, 0),
        shape((5 * product_rows // clips, 128), BF16),
        cost=1,
    )(pieces, moment, gathered, reduced_gain)
    received = spread_over(point_sum, "branch", parts)

    outs = (
        shape((2, TAPS, MID_IN, MID_OUT), F32),
        shape((2, TAPS, SMALL_IN, SMALL_OUT), F32),
        shape((2, SQUEEZED, CHANNELS), F32),
    )
    tap_scratch = [
        pltpu.VMEM((TAPS, MID_IN, MID_OUT), F32),
        pltpu.VMEM((TAPS, SMALL_IN, SMALL_OUT), F32),
    ]
    point_scratch = [pltpu.VMEM((SQUEEZED, CHANNELS), F32), pltpu.VMEM((CHANNELS, 128), F32)]
    mid_grad, small_grad = call(
        functools.partial(unpack_second, clips, taps_each),
        outs[:2],
        [*tap_scratch, pltpu.SemaphoreType.DMA((2,))],
        far_out=(0, 1),
        cost=5,
    )(whole_small)
    received, mid_grad, small_grad = lax.optimization_barrier((received, mid_grad, small_grad))
    norms = shape((2, 1024), F32)
    mid_grad, small_grad, point_grad, gain_grad, shift_grad = call(
        functools.partial(unpack_first, parts, clips, taps_each, tap_share),
        (*outs, norms, norms),
        [*tap_scratch, *point_scratch, pltpu.SemaphoreType.DMA((3,))],
        far_out=(0, 1, 2),
        aliases={5: 0, 6: 1},
        cost=6,
    )(whole, total, reduced_total, total_small, reduced_total_small, mid_grad, small_grad)
    point_mine, point_other = gather_chips(
        jnp.concatenate(received, axis=0), clips, (mid_grad, small_grad)
    )
    clip_one = lax.axis_index("dp").astype(jnp.int32).reshape(1)
    point_grad = call(
        functools.partial(unpack_point, parts, clips, own_channels),
        outs[2],
        [
            pltpu.VMEM((parts, FIRST // 128, product_rows, 128), BF16),
            *point_scratch,
            pltpu.SemaphoreType.DMA((1,)),
        ],
        scalars=2,
        far_out=(0,),
        aliases={4: 0},
        cost=3,
    )(place_one, clip_one, point_mine, point_other, point_grad)
    act = act.reshape(small.side, small.side, cotangent.shape[1], CHANNELS).transpose(2, 0, 1, 3)
    input_grad = dx.reshape(side, side, PITCH, own_channels).transpose(2, 0, 1, 3)
    return (
        act[None],
        input_grad[None],
        point_grad.swapaxes(1, 2),
        mid_grad,
        small_grad,
        gain_grad,
        shift_grad,
    )


def solution(mesh):
    split = P("dp", None, None, None, "branch")
    whole = P("dp", None, None, None, None)
    return jax.shard_map(
        on_device,
        mesh=mesh,
        in_specs=(split, P("dp"), whole, P(), P(), P(), P(), P()),
        out_specs=(whole, split, P(), P(), P(), P(), P()),
        check_vma=False,
    )
```

profile of v0, /device:TPU:0, one launch (start us, length us, event | category | flops | bytes accessed | tf_op | source)
XLA Modules:
  0.0 388.5 jit_solution(3648249246734092509)
XLA Ops:
  7.2 3.2 shard_map.135.x_far.refs_3_
  10.4 6.3 %all-to-all-start = ((bf16[4,208,896]{2,1,0:T(8,128)(2,1)}), bf16[4,208,896]{2,1,0:T(8,128)(2,1)S(1)}, u32[]{:S(2)}, u32[]{:S(2)}) async-start(bf16[4,208,896]{2,1,0:T(8,128)(2,1)} %shard_map.135.x_far.refs_3_), calls=%async_computation | async-start | bytes 2981888 | tf_op jit(solution)/shard_map/all_to_all | solution.py:1584
  17.4 10.3 %shard_map.136 = (bf16[9,512,256]{2,1,0:T(8,128)(2,1)}, bf16[3,512,256]{2,1,0:T(8,128)(2,1)}, bf16[1152,128]{1,0:T(8,128)(2,1)}, bf16[1152,128]{1,0:T(8,128)(2,1...) custom-call(bf16[2,27,160,320]{3,2,1,0:T(8,128)(2,1)} %mid_in.1, ...), custom_call_target="tpu_custom_call" | custom-call | bytes 15000000 | tf_op jit(solution)/shard_map/pallas_call | solution.py:66
  27.7 24.3 %all-to-all-done.x_ref = bf16[4,208,896]{2,1,0:T(8,128)(2,1)S(1)} async-done(((bf16[4,208,896]{2,1,0:T(8,128)(2,1)}), bf16[4,208,896]{2,1,0:T(8,128)(2,1)S(1)}, u32[]{:S(2)}, u32[]{:S(2)}) %all-to-all-start) | async-done | bytes 1490976 | tf_op jit(solution)/shard_map/all_to_all | solution.py:1584
  53.0 5.3 %shard_map.137 = (bf16[1376,128]{1,0:T(8,128)(2,1)}, bf16[912,128]{1,0:T(8,128)(2,1)}, f32[896,256]{1,0:T(8,128)}, f32[8,3,512]{2,1,0:T(4,128)}) custom-call(s32[1]{0:T(128)S(6)} %copy.27.length_ref, f32[1]{0:T(128)S(6)} %convert_element_type.5.count_ref, bf16[4,208,896]{2,1,0:T(8,128)(2,1)} %copy-done, bf16[4,640,208]{2,1,0:T(8,128)(2,1)} %get-tuple-element.103.p_ref.p_far), custom_call_target="tpu_custom_call" | custom-call | bytes 15000000 | tf_op jit(solution)/shard_map/pallas_call | solution.py:66
  58.3 2.0 collective-permute-start.4
  62.2 8.7 %all_to_all.60 = f32[8,3,512]{2,1,0:T(4,128)S(1)} all-to-all(f32[8,3,512]{2,1,0:T(4,128)} %get-tuple-element.108), channel_id=1, replica_groups=mesh['dp'=8,'branch'=4] {'dp'}, dimensions={0} | all-to-all | bytes 98304 | tf_op jit(solution)/shard_map/all_to_all | solution.py:1549
  73.1 12.0 %collective-permute-done.refs_1_ = f32[3,512]{1,0:T(4,128)S(1)} collective-permute-done((f32[3,512]{1,0:T(4,128)S(1)}, f32[3,512]{1,0:T(4,128)S(1)}, u32[]{:S(2)}, u32[]{:S(2)}) %collective-permute-start) | collective-permute-done | bytes 6176 | tf_op jit(solution)/shard_map/ppermute | solution.py:1540
  85.1 6.9 %collective-permute-done.1.refs_2_ = f32[3,512]{1,0:T(4,128)S(1)} collective-permute-done((f32[3,512]{1,0:T(4,128)S(1)}, f32[3,512]{1,0:T(4,128)S(1)}, u32[]{:S(2)}, u32[]{:S(2)}) %collective-permute-start.1) | collective-permute-done | bytes 6176 | tf_op jit(solution)/shard_map/ppermute | solution.py:1540
  92.6 3.2 shard_map.138
  98.3 2.8 collective-permute-start.8
  101.2 24.9 %shard_map.139 = (bf16[3136,256]{1,0:T(8,128)(2,1)}, bf16[3872,512]{1,0:T(8,128)(2,1)}, bf16[3872,128]{1,0:T(8,128)(2,1)}, f32[3136,512]{1,0:T(8,128)}, f32[2,512]{1,0:T(2,128)}) custom-call(s32[1]{0:T(128)S(6)} %copy.27.length_ref, s32[1]{0:T(128)} %bitcast.place_ref, bf16[1376,128]{1,0:T(8,128)(2,1)} %get-tuple-element.110.refs_0_, ...), custom_call_target="tpu_custom_call" | custom-call | bytes 120000000 | tf_op jit(solution)/shard_map/pallas_call | solution.py:66
  126.9 3.2 collective-permute-start.11
  130.0 2.9 collective-permute-done.9.refs_1_
  133.0 2.3 collective-permute-done.10.refs_2_
  135.3 4.0 %shard_map.140 = (f32[3136,128]{1,0:T(8,128)}, f32[8,2,640]{2,1,0:T(2,128)}) custom-call(s32[1]{0:T(128)S(6)} %copy.27.length_ref, s32[1]{0:T(128)} %bitcast.place_ref, bf16[912,128]{1,0:T(8,128)(2,1)} %get-tuple-element.112.refs_0_, bf16[912,128]{1,0:T(8,128)(2,1)} %copy-done.7, bf16[912,128]{1,0:T(8,128)(2,1)} %copy-done.8, bf16[912,128]{1,0:T(8,128)(2,1)} %copy-done.9, ...), custom_call_target="tpu_custom_call" | custom-call | bytes 15000000 | tf_op jit(solution)/shard_map/pallas_call | solution.py:66
  139.3 3.7 all-to-all-start.2
  143.0 4.9 %all-to-all-done.2.sums_in_ref = f32[8,2,640]{2,1,0:T(2,128)S(1)} async-done(((f32[8,2,640]{2,1,0:T(2,128)}), f32[8,2,640]{2,1,0:T(2,128)S(1)}, u32[]{:S(2)}, u32[]{:S(2)}) %all-to-all-start.2) | async-done | bytes 40992 | tf_op jit(solution)/shard_map/all_to_all | solution.py:1549
  148.5 12.0 %shard_map.141 = (bf16[784,640]{1,0:T(8,128)(2,1)}, bf16[3136,640]{1,0:T(8,128)(2,1)}, bf16[3136,640]{1,0:T(8,128)(2,1)}, f32[3,896]{1,0:T(4,128)}, bf16[784,640]{1,0:T(8,128)(2,1)}, /*index=5*/bf16[784,640]{1,0:T(8,128)(2,1)}) custom-call(s32[1]{0:T(128)S(6)} %copy.27.length_ref, f32[3136,128]{1,0:T(8,128)} %get-tuple-element.121.q_far, ...), custom_call_target="tpu_custom_call" | custom-call | bytes 15000000 | tf_op jit(solution)/shard_map/pallas_call | solution.py:66
  160.5 5.9 %shard_map.142 = (f32[784,640]{1,0:T(8,128)}, f32[8,3,640]{2,1,0:T(4,128)}, bf16[784,896]{1,0:T(8,128)(2,1)}) custom-call(s32[1]{0:T(128)S(6)} %select_n.12.length_ref, s32[1]{0:T(128)} %bitcast.place_ref, f32[1]{0:T(128)S(6)} %mul.20.count_ref, bf16[224,256]{1,0:T(8,128)(2,1)} %get-tuple-element.120.refs_0_, bf16[224,256]{1,0:T(8,128)(2,1)} %copy-done.14, ...), custom_call_target="tpu_custom_call" | custom-call | bytes 15000000 | tf_op jit(solution)/shard_map/pallas_call | solution.py:66
  166.4 9.1 %all_to_all.61.sums_in_ref = f32[8,3,640]{2,1,0:T(4,128)} all-to-all(f32[8,3,640]{2,1,0:T(4,128)} %get-tuple-element.127), channel_id=1, replica_groups=mesh['dp'=8,'branch'=4] {'dp'}, dimensions={0} | all-to-all | bytes 122880 | tf_op jit(solution)/shard_map/all_to_all | solution.py:1549
  175.5 9.0 %shard_map.143 = (bf16[784,256]{1,0:T(8,128)(2,1)}, bf16[1184,512]{1,0:T(8,128)(2,1)}, bf16[1184,128]{1,0:T(8,128)(2,1)}, f32[784,512]{1,0:T(8,128)}, f32[8,2,512]{2,1,0:T(2,128)}, /*index=5*/f32[3,640]{1,0:T(4,128)}) custom-call(s32[1]{0:T(128)S(6)} %select_n.12.length_ref, f32[784,640]{1,0:T(8,128)} %get-tuple-element.126.q_ref, ...), custom_call_target="tpu_custom_call" | custom-call | bytes 15000000 | tf_op jit(solution)/shard_map/pallas_call | solution.py:66
  184.4 8.8 %all_to_all.62.sums_in_ref = f32[8,2,512]{2,1,0:T(2,128)} all-to-all(f32[8,2,512]{2,1,0:T(2,128)} %get-tuple-element.133), channel_id=1, replica_groups=mesh['dp'=8,'branch'=4] {'dp'}, dimensions={0} | all-to-all | bytes 65536 | tf_op jit(solution)/shard_map/all_to_all | solution.py:1549
  193.2 6.8 %shard_map.144 = (bf16[49,8,832]{2,1,0:T(8,128)(2,1)}, bf16[784,896]{1,0:T(8,128)(2,1)}, bf16[784,896]{1,0:T(8,128)(2,1)}, f32[3,896]{1,0:T(4,128)}, f32[8,2,896]{2,1,0:T(2,128)}) custom-call(s32[1]{0:T(128)S(6)} %select_n.12.length_ref, f32[784,640]{1,0:T(8,128)} %get-tuple-element.126.q_ref, f32[784,512]{1,0:T(8,128)} %get-tuple-element.131.e_ref, ...), custom_call_target="tpu_custom_call" | custom-call | bytes 15000000 | tf_op jit(solution)/shard_map/pallas_call | solution.py:66
  200.0 3.3 all-to-all-start.5
  203.4 4.9 %all-to-all-done.5.sums_in_ref = f32[8,2,896]{2,1,0:T(2,128)S(1)} async-done(((f32[8,2,896]{2,1,0:T(2,128)}), f32[8,2,896]{2,1,0:T(2,128)S(1)}, u32[]{:S(2)}, u32[]{:S(2)}) %all-to-all-start.5) | async-done | bytes 57376 | tf_op jit(solution)/shard_map/all_to_all | solution.py:1549
  208.9 6.1 %shard_map.145 = (bf16[1184,512]{1,0:T(8,128)(2,1)}, f32[2,896]{1,0:T(2,128)}, bf16[8,384,128]{2,1,0:T(8,128)(2,1)}) custom-call(s32[1]{0:T(128)S(6)} %select_n.12.length_ref, s32[1]{0:T(128)S(6)} %mul.25.first_ref, bf16[784,896]{1,0:T(8,128)(2,1)} %get-tuple-element.137.h_far, f32[3,896]{1,0:T(4,128)} %get-tuple-element.138.outer_ref, ...), custom_call_target="tpu_custom_call" | custom-call | bytes 24000000 | tf_op jit(solution)/shard_map/pallas_call | solution.py:66
  215.0 3.6 all-to-all-start.6
  218.6 8.0 %shard_map.146 = (bf16[784,256]{1,0:T(8,128)(2,1)}, f32[8,2,256]{2,1,0:T(2,128)}) custom-call(s32[1]{0:T(128)S(6)} %select_n.12.length_ref, bf16[1184,512]{1,0:T(8,128)(2,1)} %get-tuple-element.145.d_ref, bf16[784,256]{1,0:T(8,128)(2,1)} %get-tuple-element.144.reduced_ref.reduced_far, f32[2,256]{1,0:T(2,128)} %get-tuple-element.114.refs_5_.gain_ref.reduced_gain_ref, ...), custom_call_target="tpu_custom_call" | custom-call | bytes 24000000 | tf_op jit(solution)/shard_map/pallas_call | solution.py:66
  226.7 4.4 %all-to-all-done.6 = bf16[8,384,128]{2,1,0:T(8,128)(2,1)S(1)} async-done(((bf16[8,384,128]{2,1,0:T(8,128)(2,1)}), bf16[8,384,128]{2,1,0:T(8,128)(2,1)S(1)}, u32[]{:S(2)}, u32[]{:S(2)}) %all-to-all-start.6) | async-done | bytes 786464 | tf_op jit(solution)/shard_map/all_to_all | solution.py:1549
  231.9 8.6 %all_to_all.63.sums_in_ref = f32[8,2,256]{2,1,0:T(2,128)} all-to-all(f32[8,2,256]{2,1,0:T(2,128)} %get-tuple-element.150), channel_id=1, replica_groups=mesh['dp'=8,'branch'=4] {'dp'}, dimensions={0} | all-to-all | bytes 32768 | tf_op jit(solution)/shard_map/all_to_all | solution.py:1549
  240.5 10.0 %shard_map.147 = (bf16[784,896]{1,0:T(8,128)(2,1)}, bf16[8,144,128]{2,1,0:T(8,128)(2,1)}, f32[2,256]{1,0:T(2,128)}, f32[8,2,896]{2,1,0:T(2,128)}) custom-call(s32[1]{0:T(128)S(6)} %select_n.12.length_ref, s32[1]{0:T(128)} %bitcast.place_ref, bf16[784,896]{1,0:T(8,128)(2,1)} %get-tuple-element.137.h_far, f32[3,896]{1,0:T(4,128)} %get-tuple-element.138.outer_ref, ...), custom_call_target="tpu_custom_call" | custom-call | bytes 30000000 | tf_op jit(solution)/shard_map/pallas_call | solution.py:66
  250.4 9.3 %all_to_all.64.sums_in_ref = f32[8,2,896]{2,1,0:T(2,128)} all-to-all(f32[8,2,896]{2,1,0:T(2,128)} %get-tuple-element.156), channel_id=1, replica_groups=mesh['dp'=8,'branch'=4] {'dp'}, dimensions={0} | all-to-all | bytes 114688 | tf_op jit(solution)/shard_map/all_to_all | solution.py:1549
  259.8 16.4 %shard_map.148 = (bf16[3872,512]{1,0:T(8,128)(2,1)}, f32[2,896]{1,0:T(2,128)}, bf16[8,528,128]{2,1,0:T(8,128)(2,1)}) custom-call(s32[1]{0:T(128)S(6)} %copy.27.length_ref, s32[1]{0:T(128)S(6)} %mul.25.first_ref, bf16[3136,640]{1,0:T(8,128)(2,1)} %get-tuple-element.135.h_far, f32[3,896]{1,0:T(4,128)} %get-tuple-element.136.outer_ref, ...), custom_call_target="tpu_custom_call" | custom-call | bytes 54000000 | tf_op jit(solution)/shard_map/pallas_call | solution.py:66
  276.2 3.6 all-to-all-start.9
  279.8 8.1 %shard_map.149 = (bf16[3136,384]{1,0:T(8,128)(2,1)}, f32[256,384]{1,0:T(8,128)}) custom-call(s32[1]{0:T(128)S(6)} %copy.27.length_ref, f32[3,896]{1,0:T(4,128)} %get-tuple-element.136.outer_ref, f32[2,896]{1,0:T(2,128)} %get-tuple-element.165.total_ref.refs_0_, f32[2,896]{1,0:T(2,128)} %get-tuple-element.106.gain_ref, ...), custom_call_target="tpu_custom_call" | custom-call | bytes 24000000 | tf_op jit(solution)/shard_map/pallas_call | solution.py:66
  287.9 7.6 %all-to-all-done.9 = bf16[8,528,128]{2,1,0:T(8,128)(2,1)S(1)} async-done(((bf16[8,528,128]{2,1,0:T(8,128)(2,1)}), bf16[8,528,128]{2,1,0:T(8,128)(2,1)S(1)}, u32[]{:S(2)}, u32[]{:S(2)}) %all-to-all-start.9) | async-done | bytes 1081376 | tf_op jit(solution)/shard_map/all_to_all | solution.py:1549
  296.3 23.5 %shard_map.150 = (bf16[3136,256]{1,0:T(8,128)(2,1)}, f32[8,2,256]{2,1,0:T(2,128)}, f32[8,8,32,128]{3,2,1,0:T(8,128)}) custom-call(s32[1]{0:T(128)S(6)} %copy.27.length_ref, bf16[3872,512]{1,0:T(8,128)(2,1)} %get-tuple-element.168.d_ref, bf16[3136,256]{1,0:T(8,128)(2,1)} %get-tuple-element.169.reduced_ref.h_far, ...), custom_call_target="tpu_custom_call" | custom-call | bytes 66000000 | tf_op jit(solution)/shard_map/pallas_call | solution.py:66
  319.8 8.5 %all_to_all.65.sums_in_ref = f32[8,2,256]{2,1,0:T(2,128)} all-to-all(f32[8,2,256]{2,1,0:T(2,128)} %get-tuple-element.172), channel_id=1, replica_groups=mesh['dp'=8,'branch'=4] {'dp'}, dimensions={0} | all-to-all | bytes 32768 | tf_op jit(solution)/shard_map/all_to_all | solution.py:1549
  328.3 3.6 all-to-all-start.10
  331.9 7.4 %shard_map.151 = (bf16[3136,208]{1,0:T(8,128)(2,1)}, f32[2,256]{1,0:T(2,128)}) custom-call(s32[1]{0:T(128)S(6)} %copy.27.length_ref, s32[1]{0:T(128)} %bitcast.place_ref, f32[3,512]{1,0:T(4,128)} %get-tuple-element.113.refs_4_.moment_ref, f32[8,2,256]{2,1,0:T(2,128)} %all_to_all.65.sums_in_ref, ...), custom_call_target="tpu_custom_call" | custom-call | bytes 24000000 | tf_op jit(solution)/shard_map/pallas_call | solution.py:66
  339.3 14.0 %all-to-all-done.10.pieces_ref = f32[8,8,32,128]{3,2,1,0:T(8,128)S(1)} async-done(((f32[8,8,32,128]{3,2,1,0:T(8,128)}), f32[8,8,32,128]{3,2,1,0:T(8,128)S(1)}, u32[]{:S(2)}, u32[]{:S(2)}) %all-to-all-start.10) | async-done | bytes 1048608 | tf_op jit(solution)/shard_map/all_to_all | solution.py:1549
  354.2 1.9 shard_map.152
  360.4 4.9 %shard_map.153 = (f32[2,27,160,320]{3,2,1,0:T(8,128)}, f32[2,27,32,128]{3,2,1,0:T(8,128)}) custom-call(bf16[32,384,128]{2,1,0:T(8,128)(2,1)} %bitcast.32), custom_call_target="tpu_custom_call" | custom-call | bytes 15000000 | tf_op jit(solution)/shard_map/pallas_call | solution.py:66
  366.5 2.4 collective-permute-start.17
  369.0 6.8 %shard_map.154 = (f32[2,27,160,320]{3,2,1,0:T(8,128)}, f32[2,27,32,128]{3,2,1,0:T(8,128)}, f32[2,576,832]{2,1,0:T(8,128)}, f32[2,1024]{1,0:T(2,128)}, f32[2,1024]{1,0:T(2,128)}) custom-call(bf16[32,528,128]{2,1,0:T(8,128)(2,1)} %bitcast.30, f32[2,896]{1,0:T(2,128)} %get-tuple-element.165.total_ref.refs_0_, ...), custom_call_target="tpu_custom_call", output_to_operand_aliasing={{0}: (5, {}), {1}: (6, {})} | custom-call | bytes 18000000 | tf_op jit(solution)/shard_map/pallas_call | solution.py:66
  376.0 2.1 collective-permute-done.18.other_ref
  378.9 3.1 shard_map.155
  (91 shorter events, 19.3 us)
Async XLA Ops:
  10.4 41.5 %all-to-all-start = ((bf16[4,208,896]{2,1,0:T(8,128)(2,1)}), bf16[4,208,896]{2,1,0:T(8,128)(2,1)S(1)}, u32[]{:S(2)}, u32[]{:S(2)}) async-start(bf16[4,208,896]{2,1,0:T(8,128)(2,1)} %shard_map.135.x_far.refs_3_), calls=%async_computation | async-start | bytes 2981888 | tf_op jit(solution)/shard_map/all_to_all | solution.py:1584
  16.7 223.8 %all-gather.7.cloned.1.call-start = ((), (), s32[]{:S(2)}) async-start(), calls=%async_computation.12 | async-start | bytes 5734400 | tf_op jit(solution)/shard_map/all_gather | solution.py:1643
  51.9 1.1 copy-start
  58.3 37.5 %collective-permute-start.3 = (bf16[1376,128]{1,0:T(8,128)(2,1)}, bf16[1376,128]{1,0:T(8,128)(2,1)S(1)}, u32[]{:S(2)}, u32[]{:S(2)}) collective-permute-start(bf16[1376,128]{1,0:T(8,128)(2,1)} %get-tuple-element.110.refs_0_), channel_id=1, source_target_pairs={{0,1},{1,2},{2,3},{3,0},{4,5},{5,6},{6,7},{7,4},{8,9},{9,10},{10,1... | collective-permute-start | bytes 1056776 | tf_op jit(solution)/shard_map/ppermute | solution.py:1540
  58.3 37.5 %collective-permute-start.4 = (bf16[1376,128]{1,0:T(8,128)(2,1)}, bf16[1376,128]{1,0:T(8,128)(2,1)S(1)}, u32[]{:S(2)}, u32[]{:S(2)}) collective-permute-start(bf16[1376,128]{1,0:T(8,128)(2,1)} %get-tuple-element.110.refs_0_), channel_id=1, source_target_pairs={{0,2},{1,3},{2,0},{3,1},{4,6},{5,7},{6,4},{7,5},{8,10},{9,11},{10,... | collective-permute-start | bytes 1056776 | tf_op jit(solution)/shard_map/ppermute | solution.py:1540
  60.4 35.4 %collective-permute-start.5 = (bf16[1376,128]{1,0:T(8,128)(2,1)}, bf16[1376,128]{1,0:T(8,128)(2,1)S(1)}, u32[]{:S(2)}, u32[]{:S(2)}) collective-permute-start(bf16[1376,128]{1,0:T(8,128)(2,1)} %get-tuple-element.110.refs_0_), channel_id=1, source_target_pairs={{0,3},{1,0},{2,1},{3,2},{4,7},{5,4},{6,5},{7,6},{8,11},{9,8},{10,9... | collective-permute-start | bytes 1056776 | tf_op jit(solution)/shard_map/ppermute | solution.py:1540
  70.9 21.0 %copy-start.17 = (f32[3,512]{1,0:T(4,128)}, f32[3,512]{1,0:T(4,128)S(1)}, u32[]{:S(2)}) copy-start(f32[3,512]{1,0:T(4,128)S(1)} %reduce_sum.33.refs_0_) | copy-start | bytes 18436
  70.9 14.2 %collective-permute-start = (f32[3,512]{1,0:T(4,128)S(1)}, f32[3,512]{1,0:T(4,128)S(1)}, u32[]{:S(2)}, u32[]{:S(2)}) collective-permute-start(f32[3,512]{1,0:T(4,128)S(1)} %reduce_sum.33.refs_0_), channel_id=1, source_target_pairs={{0,1},{1,2},{2,3},{3,0},{4,5},{5,6},{6,7},{7,4},{8,9},{9,10},{10,1... | collective-permute-start | bytes 18440 | tf_op jit(solution)/shard_map/ppermute | solution.py:1540
  71.6 20.4 %collective-permute-start.1 = (f32[3,512]{1,0:T(4,128)S(1)}, f32[3,512]{1,0:T(4,128)S(1)}, u32[]{:S(2)}, u32[]{:S(2)}) collective-permute-start(f32[3,512]{1,0:T(4,128)S(1)} %reduce_sum.33.refs_0_), channel_id=1, source_target_pairs={{0,2},{1,3},{2,0},{3,1},{4,6},{5,7},{6,4},{7,5},{8,10},{9,11},{10,... | collective-permute-start | bytes 18440 | tf_op jit(solution)/shard_map/ppermute | solution.py:1540
  85.1 6.9 %copy-start.18 = (f32[3,512]{1,0:T(4,128)}, f32[3,512]{1,0:T(4,128)S(1)}, u32[]{:S(2)}) copy-start(f32[3,512]{1,0:T(4,128)S(1)} %collective-permute-done.refs_1_) | copy-start | bytes 18436
  85.1 6.9 %collective-permute-start.2 = (f32[3,512]{1,0:T(4,128)S(1)}, f32[3,512]{1,0:T(4,128)S(1)}, u32[]{:S(2)}, u32[]{:S(2)}) collective-permute-start(f32[3,512]{1,0:T(4,128)S(1)} %reduce_sum.33.refs_0_), channel_id=1, source_target_pairs={{0,3},{1,0},{2,1},{3,2},{4,7},{5,4},{6,5},{7,6},{8,11},{9,8},{10,9... | collective-permute-start | bytes 18440 | tf_op jit(solution)/shard_map/ppermute | solution.py:1540
  92.0 0.6 copy-start.20
  95.8 5.4 %copy-start.4 = (bf16[1376,128]{1,0:T(8,128)(2,1)}, bf16[1376,128]{1,0:T(8,128)(2,1)S(1)}, u32[]{:S(2)}) copy-start(bf16[1376,128]{1,0:T(8,128)(2,1)S(1)} %collective-permute-done.3.refs_1_) | copy-start | bytes 1056772
  95.8 5.4 %copy-start.5 = (bf16[1376,128]{1,0:T(8,128)(2,1)}, bf16[1376,128]{1,0:T(8,128)(2,1)S(1)}, u32[]{:S(2)}) copy-start(bf16[1376,128]{1,0:T(8,128)(2,1)S(1)} %collective-permute-done.4.refs_2_) | copy-start | bytes 1056772
  95.8 5.4 %copy-start.6 = (bf16[1376,128]{1,0:T(8,128)(2,1)}, bf16[1376,128]{1,0:T(8,128)(2,1)S(1)}, u32[]{:S(2)}) copy-start(bf16[1376,128]{1,0:T(8,128)(2,1)S(1)} %collective-permute-done.5.refs_3_) | copy-start | bytes 1056772
  95.8 30.2 %collective-permute-start.6 = (bf16[912,128]{1,0:T(8,128)(2,1)}, bf16[912,128]{1,0:T(8,128)(2,1)S(1)}, u32[]{:S(2)}, u32[]{:S(2)}) collective-permute-start(bf16[912,128]{1,0:T(8,128)(2,1)} %get-tuple-element.112.refs_0_), channel_id=1, source_target_pairs={{0,1},{1,2},{2,3},{3,0},{4,5},{5,6},{6,7},{7,4},{8,9},{9,10},{10,1... | collective-permute-start | bytes 700424 | tf_op jit(solution)/shard_map/ppermute | solution.py:1540
  96.8 29.3 %collective-permute-start.7 = (bf16[912,128]{1,0:T(8,128)(2,1)}, bf16[912,128]{1,0:T(8,128)(2,1)S(1)}, u32[]{:S(2)}, u32[]{:S(2)}) collective-permute-start(bf16[912,128]{1,0:T(8,128)(2,1)} %get-tuple-element.112.refs_0_), channel_id=1, source_target_pairs={{0,2},{1,3},{2,0},{3,1},{4,6},{5,7},{6,4},{7,5},{8,10},{9,11},{10,... | collective-permute-start | bytes 700424 | tf_op jit(solution)/shard_map/ppermute | solution.py:1540
  98.3 27.8 %collective-permute-start.8 = (bf16[912,128]{1,0:T(8,128)(2,1)}, bf16[912,128]{1,0:T(8,128)(2,1)S(1)}, u32[]{:S(2)}, u32[]{:S(2)}) collective-permute-start(bf16[912,128]{1,0:T(8,128)(2,1)} %get-tuple-element.112.refs_0_), channel_id=1, source_target_pairs={{0,3},{1,0},{2,1},{3,2},{4,7},{5,4},{6,5},{7,6},{8,11},{9,8},{10,9... | collective-permute-start | bytes 700424 | tf_op jit(solution)/shard_map/ppermute | solution.py:1540
  101.2 25.0 %copy-start.13 = (bf16[224,256]{1,0:T(8,128)(2,1)S(1)}, bf16[224,256]{1,0:T(8,128)(2,1)}, u32[]{:S(2)}) copy-start(bf16[224,256]{1,0:T(8,128)(2,1)} %get-tuple-element.120.refs_0_) | copy-start | bytes 344068
  126.1 9.2 %copy-start.7 = (bf16[912,128]{1,0:T(8,128)(2,1)}, bf16[912,128]{1,0:T(8,128)(2,1)S(1)}, u32[]{:S(2)}) copy-start(bf16[912,128]{1,0:T(8,128)(2,1)S(1)} %collective-permute-done.6.refs_1_) | copy-start | bytes 700420
  126.1 9.2 %copy-start.8 = (bf16[912,128]{1,0:T(8,128)(2,1)}, bf16[912,128]{1,0:T(8,128)(2,1)S(1)}, u32[]{:S(2)}) copy-start(bf16[912,128]{1,0:T(8,128)(2,1)S(1)} %collective-permute-done.7.refs_2_) | copy-start | bytes 700420
  126.1 9.2 %copy-start.9 = (bf16[912,128]{1,0:T(8,128)(2,1)}, bf16[912,128]{1,0:T(8,128)(2,1)S(1)}, u32[]{:S(2)}) copy-start(bf16[912,128]{1,0:T(8,128)(2,1)S(1)} %collective-permute-done.8.refs_3_) | copy-start | bytes 700420
  126.1 6.8 %collective-permute-start.9 = (bf16[224,256]{1,0:T(8,128)(2,1)S(1)}, bf16[224,256]{1,0:T(8,128)(2,1)S(1)}, u32[]{:S(2)}, u32[]{:S(2)}) collective-permute-start(bf16[224,256]{1,0:T(8,128)(2,1)S(1)} %copy-done.13), channel_id=1, source_target_pairs={{0,1},{1,2},{2,3},{3,0},{4,5},{5,6},{6,7},{7,4},{8,9},{9,10},{10,1... | collective-permute-start | bytes 344072 | tf_op jit(solution)/shard_map/ppermute | solution.py:1540
  126.2 9.0 %collective-permute-start.10 = (bf16[224,256]{1,0:T(8,128)(2,1)S(1)}, bf16[224,256]{1,0:T(8,128)(2,1)S(1)}, u32[]{:S(2)}, u32[]{:S(2)}) collective-permute-start(bf16[224,256]{1,0:T(8,128)(2,1)S(1)} %copy-done.13), channel_id=1, source_target_pairs={{0,2},{1,3},{2,0},{3,1},{4,6},{5,7},{6,4},{7,5},{8,10},{9,11},{10,... | collective-permute-start | bytes 344072 | tf_op jit(solution)/shard_map/ppermute | solution.py:1540
  126.9 8.4 %collective-permute-start.11 = (bf16[224,256]{1,0:T(8,128)(2,1)S(1)}, bf16[224,256]{1,0:T(8,128)(2,1)S(1)}, u32[]{:S(2)}, u32[]{:S(2)}) collective-permute-start(bf16[224,256]{1,0:T(8,128)(2,1)S(1)} %copy-done.13), channel_id=1, source_target_pairs={{0,3},{1,0},{2,1},{3,2},{4,7},{5,4},{6,5},{7,6},{8,11},{9,8},{10,9... | collective-permute-start | bytes 344072 | tf_op jit(solution)/shard_map/ppermute | solution.py:1540
  133.0 27.5 %copy-start.14 = (bf16[224,256]{1,0:T(8,128)(2,1)}, bf16[224,256]{1,0:T(8,128)(2,1)S(1)}, u32[]{:S(2)}) copy-start(bf16[224,256]{1,0:T(8,128)(2,1)S(1)} %collective-permute-done.9.refs_1_) | copy-start | bytes 344068
  135.3 25.3 %copy-start.15 = (bf16[224,256]{1,0:T(8,128)(2,1)}, bf16[224,256]{1,0:T(8,128)(2,1)S(1)}, u32[]{:S(2)}) copy-start(bf16[224,256]{1,0:T(8,128)(2,1)S(1)} %collective-permute-done.10.refs_2_) | copy-start | bytes 344068
  135.3 25.3 %copy-start.16 = (bf16[224,256]{1,0:T(8,128)(2,1)}, bf16[224,256]{1,0:T(8,128)(2,1)S(1)}, u32[]{:S(2)}) copy-start(bf16[224,256]{1,0:T(8,128)(2,1)S(1)} %collective-permute-done.11.refs_3_) | copy-start | bytes 344068
  139.3 8.6 %all-to-all-start.2 = ((f32[8,2,640]{2,1,0:T(2,128)}), f32[8,2,640]{2,1,0:T(2,128)S(1)}, u32[]{:S(2)}, u32[]{:S(2)}) async-start(f32[8,2,640]{2,1,0:T(2,128)} %get-tuple-element.123), calls=%async_computation.2 | async-start | bytes 81920 | tf_op jit(solution)/shard_map/all_to_all | solution.py:1549
  147.9 0.6 copy-start.11
  200.0 8.3 %all-to-all-start.5 = ((f32[8,2,896]{2,1,0:T(2,128)}), f32[8,2,896]{2,1,0:T(2,128)S(1)}, u32[]{:S(2)}, u32[]{:S(2)}) async-start(f32[8,2,896]{2,1,0:T(2,128)} %get-tuple-element.139), calls=%async_computation.5 | async-start | bytes 114688 | tf_op jit(solution)/shard_map/all_to_all | solution.py:1549
  208.3 0.6 copy-start.10
  215.0 16.1 %all-to-all-start.6 = ((bf16[8,384,128]{2,1,0:T(8,128)(2,1)}), bf16[8,384,128]{2,1,0:T(8,128)(2,1)S(1)}, u32[]{:S(2)}, u32[]{:S(2)}) async-start(bf16[8,384,128]{2,1,0:T(8,128)(2,1)} %get-tuple-element.149), calls=%async_computation.6 | async-start | bytes 1572864 | tf_op jit(solution)/shard_map/all_to_all | solution.py:1549
  218.6 141.8 %all-gather.9.cloned.1.call-start = ((), (), s32[]{:S(2)}) async-start(), calls=%async_computation.13 | async-start | bytes 3244032 | tf_op jit(solution)/shard_map/all_gather | solution.py:1832
  276.2 19.3 %all-to-all-start.9 = ((bf16[8,528,128]{2,1,0:T(8,128)(2,1)}), bf16[8,528,128]{2,1,0:T(8,128)(2,1)S(1)}, u32[]{:S(2)}, u32[]{:S(2)}) async-start(bf16[8,528,128]{2,1,0:T(8,128)(2,1)} %get-tuple-element.164), calls=%async_computation.9 | async-start | bytes 2162688 | tf_op jit(solution)/shard_map/all_to_all | solution.py:1549
  279.8 89.2 %all-gather.11.cloned.1.call-start = ((), (), s32[]{:S(2)}) async-start(), calls=%async_computation.14 | async-start | bytes 4460544 | tf_op jit(solution)/shard_map/all_gather | solution.py:1896
  328.3 25.0 %all-to-all-start.10 = ((f32[8,8,32,128]{3,2,1,0:T(8,128)}), f32[8,8,32,128]{3,2,1,0:T(8,128)S(1)}, u32[]{:S(2)}, u32[]{:S(2)}) async-start(f32[8,8,32,128]{3,2,1,0:T(8,128)} %get-tuple-element.171), calls=%async_computation.10 | async-start | bytes 2097152 | tf_op jit(solution)/shard_map/all_to_all | solution.py:1549
  353.3 1.0 copy-start.1
  356.1 9.2 %copy-start.12 = (bf16[160,128]{1,0:T(8,128)(2,1)S(1)}, bf16[160,128]{1,0:T(8,128)(2,1)}, u32[]{:S(2)}) copy-start(bf16[160,128]{1,0:T(8,128)(2,1)} %shard_map.152) | copy-start | bytes 122884
  356.1 9.2 %collective-permute-start.12 = (bf16[160,128]{1,0:T(8,128)(2,1)}, bf16[160,128]{1,0:T(8,128)(2,1)S(1)}, u32[]{:S(2)}, u32[]{:S(2)}) collective-permute-start(bf16[160,128]{1,0:T(8,128)(2,1)} %shard_map.152), channel_id=1, source_target_pairs={{0,1},{1,2},{2,3},{3,0},{4,5},{5,6},{6,7},{7,4},{8,9},{9,10},{10,1... | collective-permute-start | bytes 122888 | tf_op jit(solution)/shard_map/ppermute | solution.py:1540
  358.0 7.3 %collective-permute-start.13 = (bf16[160,128]{1,0:T(8,128)(2,1)}, bf16[160,128]{1,0:T(8,128)(2,1)S(1)}, u32[]{:S(2)}, u32[]{:S(2)}) collective-permute-start(bf16[160,128]{1,0:T(8,128)(2,1)} %shard_map.152), channel_id=1, source_target_pairs={{0,2},{1,3},{2,0},{3,1},{4,6},{5,7},{6,4},{7,5},{8,10},{9,11},{10,... | collective-permute-start | bytes 122888 | tf_op jit(solution)/shard_map/ppermute | solution.py:1540
  358.7 6.7 %collective-permute-start.14 = (bf16[160,128]{1,0:T(8,128)(2,1)}, bf16[160,128]{1,0:T(8,128)(2,1)S(1)}, u32[]{:S(2)}, u32[]{:S(2)}) collective-permute-start(bf16[160,128]{1,0:T(8,128)(2,1)} %shard_map.152), channel_id=1, source_target_pairs={{0,3},{1,0},{2,1},{3,2},{4,7},{5,4},{6,5},{7,6},{8,11},{9,8},{10,9... | collective-permute-start | bytes 122888 | tf_op jit(solution)/shard_map/ppermute | solution.py:1540
  365.4 10.3 %collective-permute-start.15 = (bf16[640,128]{1,0:T(8,128)(2,1)S(1)}, bf16[640,128]{1,0:T(8,128)(2,1)S(1)}, u32[]{:S(2)}, u32[]{:S(2)}) collective-permute-start(bf16[640,128]{1,0:T(8,128)(2,1)S(1)} %constant_dynamic-update-slice_fusion), channel_id=1, source_target_pairs={{0,8},{4,12},{8,0},{12,4},{16,24},{20,28},{24,16},{28,20},{1,9},{5... | collective-permute-start | bytes 491528 | tf_op jit(solution)/shard_map/ppermute | solution.py:1561
  365.5 10.3 %collective-permute-start.16 = (bf16[640,128]{1,0:T(8,128)(2,1)S(1)}, bf16[640,128]{1,0:T(8,128)(2,1)S(1)}, u32[]{:S(2)}, u32[]{:S(2)}) collective-permute-start(bf16[640,128]{1,0:T(8,128)(2,1)S(1)} %constant_dynamic-update-slice_fusion), channel_id=1, source_target_pairs={{0,16},{4,20},{8,24},{12,28},{16,0},{20,4},{24,8},{28,12},{1,17},{... | collective-permute-start | bytes 491528 | tf_op jit(solution)/shard_map/ppermute | solution.py:1561
  366.5 9.2 %collective-permute-start.17 = (bf16[640,128]{1,0:T(8,128)(2,1)S(1)}, bf16[640,128]{1,0:T(8,128)(2,1)S(1)}, u32[]{:S(2)}, u32[]{:S(2)}) collective-permute-start(bf16[640,128]{1,0:T(8,128)(2,1)S(1)} %constant_dynamic-update-slice_fusion), channel_id=1, source_target_pairs={{0,24},{4,28},{8,16},{12,20},{16,8},{20,12},{24,0},{28,4},{1,25},{... | collective-permute-start | bytes 491528 | tf_op jit(solution)/shard_map/ppermute | solution.py:1561
  375.9 2.2 copy-start.2
  375.9 2.2 collective-permute-start.18
  378.1 0.9 copy-start.3
  (1 other events, 0.6 us)
Sparse Core Ops, SparseCore 0:
  135.4 87.5 all-gather.6
  232.0 57.5 all-gather.8
  296.5 68.0 all-gather.10
where the time goes:
time: 390 us; the launch traced here: 389 us
  Pallas kernels  181 us (46%)
  waiting for transfers between devices  86.3 us (22%)
  blocking collectives  53 us (14%)
  starting transfers between devices  47.2 us (12%)
  between operations  14.9 us (4%)
  local copies, waits for them, and re-layouts  4.93 us (1%)
    pallas_call x21, Pallas kernels, run(): pl.pallas_call(body, out_shape=jax.tree.map(placed, out_shape), in_specs=...  181 us
    all_to_all x6, blocking collectives, exchange(): return lax.all_to_all(values, 'dp', 0, 0, tiled=True)  53 us
    all_to_all x5, waiting for transfers between devices, exchange(): return lax.all_to_all(values, 'dp', 0, 0, tiled=True)  35.8 us
    all_to_all x1, waiting for transfers between devices, on_device(): by_pairs = lax.all_to_all(turned, 'branch', 0, 0, tiled=True)  24.3 us
    ppermute x15, waiting for transfers between devices, spread_over(): received.append(lax.ppermute(values, axis, perm))  24.1 us
    ppermute x15, starting transfers between devices, spread_over(): received.append(lax.ppermute(values, axis, perm))  19.4 us
    all_to_all x5, starting transfers between devices, exchange(): return lax.all_to_all(values, 'dp', 0, 0, tiled=True)  17.8 us
  transfers between devices with their start and end apart: 28, of which 11 were waited for; matrix products, arithmetic and copies ran while one was open for 0% of the time, Pallas kernels for 44%

commit v1 on v0

--- a/solution.py
+++ b/solution.py
@@ -15,7 +15,7 @@
 TAPS = 27
 CHANNELS = 832
 SQUEEZED = 576
-PITCH = 16
+TILE = 16
 REDUCED = 256
 POOLED = 128
 FIRST = 640
@@ -87,43 +87,39 @@
     return pl.ds(pl.multiple_of(start, 16), size)
 
 
-def frames_of(rows, width=128):
-    return lax.broadcasted_iota(jnp.int32, (rows, width), 0) & (PITCH - 1)
-
-
-def frame_mask(rows, length, width=128):
-    mask = jnp.where(frames_of(rows) < length, 1.0, 0.0)
-    return jnp.concatenate([mask] * (width // 128), axis=1) if width > 128 else mask
-
-
-def earlier(values):
-    return jnp.where(frames_of(*values.shape) > 0, pltpu.roll(values, 1, 0), 0.0)
-
-
-def later(values):
+def frames_of(values_or_rows, unit):
+    dims = values_or_rows if isinstance(values_or_rows, tuple) else (values_or_rows, 128)
+    return lax.broadcasted_iota(jnp.int32, dims, 0) & (unit - 1)
+
+
+def earlier(values, unit):
+    return jnp.where(frames_of(values.shape, unit) > 0, pltpu.roll(values, 1, 0), 0.0)
+
+
+def later(values, unit):
     rows = values.shape[0]
-    return jnp.where(frames_of(*values.shape) < PITCH - 1, pltpu.roll(values, rows - 1, 0), 0.0)
-
-
-def plane_box(values):
-    across = values + earlier(values) + later(values)
-    edge = jnp.zeros((PITCH, values.shape[1]), values.dtype)
+    shifted = pltpu.roll(values, rows - 1, 0)
+    return jnp.where(frames_of(values.shape, unit) < unit - 1, shifted, 0.0)
+
+
+def plane_box(values, unit):
+    across = values + earlier(values, unit) + later(values, unit)
+    edge = jnp.zeros((unit, values.shape[1]), values.dtype)
     return (
         across
-        + jnp.concatenate([across[PITCH:], edge], axis=0)
-        + jnp.concatenate([edge, across[:-PITCH]], axis=0)
-    )
-
-
-def box_window(side, length):
-    frame = frames_of(side * PITCH)
-    place = lax.broadcasted_iota(jnp.int32, (side * PITCH, 128), 0) >> 4
+        + jnp.concatenate([across[unit:], edge], axis=0)
+        + jnp.concatenate([edge, across[:-unit]], axis=0)
+    )
+
+
+def box_window(grid, length):
+    frame, place = (frames_of(grid.line_rows, grid.unit), grid.places_of(grid.line_rows))
 
     def one(condition):
         return jnp.where(condition, 1.0, 0.0)
 
     count = one(frame < length) + one(frame + 1 < length) + one((frame > 0) & (frame - 1 < length))
-    return count * (3.0 - one(place == 0) - one(place == side - 1))
+    return count * (3.0 - one(place == 0) - one(place == grid.side - 1))
 
 
 def box_scale(line, side, window):
@@ -162,26 +158,49 @@
     return total
 
 
-def pool_matrix(side, transposed):
-    line = 2 * side * PITCH
-    few, many = (side * PITCH, 2 * line)
+def pool_matrix(grid, small, transposed):
+    line = grid.line_rows
+    few, many = (small.line_rows, 2 * line)
     dims = (many, few) if transposed else (few, many)
     coarse = lax.broadcasted_iota(jnp.int32, dims, 1 if transposed else 0)
     fine = lax.broadcasted_iota(jnp.int32, dims, 0 if transposed else 1)
     fine = jnp.where(fine >= line, fine - line, fine)
-    same = (fine >> 5 == coarse >> 4) & ((fine & (PITCH - 1)) >> 1 == coarse & (PITCH - 1))
+    same = (fine >> (grid.bits + 1) == coarse >> small.bits) & (
+        (fine & (grid.unit - 1)) >> 1 == coarse & (small.unit - 1)
+    )
     return jnp.where(same, 0.125, 0.0).astype(BF16)
 
 
 class Grid:
-    def __init__(self, side):
-        self.side = side
-        self.line_rows = side * PITCH
+    def __init__(self, side, unit):
+        self.side, self.unit = (side, unit)
+        self.bits = unit.bit_length() - 1
+        self.copies = TILE // unit
+        self.line_rows = side * unit if self.copies == 1 else (side + 1) * unit
         self.rows = side * self.line_rows
-        self.pitch = (side + 1) * PITCH
-        self.lead = self.pitch + PITCH
-        self.padded = (side + 2) * self.pitch + 2 * PITCH
+        self.pitch = (side + 1) * unit
+        margin = 1 if self.copies == 1 else 2
+        self.lead = margin * self.pitch + TILE
+        self.padded = (side + 2 * margin) * self.pitch + 2 * TILE
         self.group = 2 if side % 2 == 0 else side
+
+    def places_of(self, rows):
+        place = lax.broadcasted_iota(jnp.int32, (rows, 128), 0) >> self.bits
+        return place if self.copies == 1 else place & self.side
+
+    def mask(self, rows, length, width=128):
+        valid = frames_of(rows, self.unit) < length
+        if self.copies > 1:
+            valid = valid & (self.places_of(rows) < self.side)
+        mask = jnp.where(valid, 1.0, 0.0)
+        return jnp.concatenate([mask] * (width // 128), axis=1) if width > 128 else mask
+
+    def near(self, ref, base, lines, places, size, lanes=slice(None)):
+        start = base + lines * self.pitch
+        if self.copies == 1:
+            return ref[0, rows_at(start + places * TILE, size), lanes]
+        copy = 0 if places == 0 else 1
+        return ref[copy, rows_at(start - (TILE if places < 0 else 0), size), lanes]
 
 
 class Slots:
@@ -192,6 +211,7 @@
         self.empty = parts * self.each - self.pairs
         self.gap = parts * self.each // 2 - 1
         self.pair_rows = 2 * grid.line_rows
+        self.grid = grid
         self.rows = self.each * self.pair_rows
 
     def slot_of(self, pair):
@@ -211,34 +231,37 @@
 
 
 def clear_empty(grid, ref):
-    width = ref.shape[1]
-    ref[0 : grid.lead, :] = jnp.zeros((grid.lead, width), ref.dtype)
+    width = ref.shape[2]
+    if grid.copies > 1:
+        ref[...] = jnp.zeros_like(ref)
+        return
+    ref[0, 0 : grid.lead, :] = jnp.zeros((grid.lead, width), ref.dtype)
     end = grid.lead + grid.side * grid.pitch
-    ref[end:, :] = jnp.zeros((ref.shape[0] - end, width), ref.dtype)
+    ref[0, end:, :] = jnp.zeros((ref.shape[1] - end, width), ref.dtype)
 
     @pl.loop(0, grid.side)
     def _(line):
-        at = rows_at(grid.lead + line * grid.pitch + grid.line_rows, PITCH)
-        ref[at, :] = jnp.zeros((PITCH, width), ref.dtype)
-
-
-def store_taps(mid_ref, small_ref, at, act):
-    before, after_ = (earlier(act), later(act))
-    mid_ref[at, 0:128] = before[:, :128].astype(BF16)
-    mid_ref[at, 128:256] = act[:, :128].astype(BF16)
-    mid_ref[at, 256:384] = after_[:, :128].astype(BF16)
+        at = rows_at(grid.lead + line * grid.pitch + grid.line_rows, TILE)
+        ref[0, at, :] = jnp.zeros((TILE, width), ref.dtype)
+
+
+def store_taps(unit, mid_ref, small_ref, copy, at, act):
+    before, after_ = (earlier(act, unit), later(act, unit))
+    mid_ref[copy, at, 0:128] = before[:, :128].astype(BF16)
+    mid_ref[copy, at, 128:256] = act[:, :128].astype(BF16)
+    mid_ref[copy, at, 256:384] = after_[:, :128].astype(BF16)
     before, act, after_ = (before[:, 128:], act[:, 128:], after_[:, 128:])
     lane = lax.broadcasted_iota(jnp.int32, act.shape, 1)
-    mid_ref[at, 384:512] = jnp.where(
+    mid_ref[copy, at, 384:512] = jnp.where(
         lane < 32, before, jnp.where(lane < 64, pltpu.roll(act, 32, 1), pltpu.roll(after_, 64, 1))
     ).astype(BF16)
-    small_ref[at, :] = jnp.where(
+    small_ref[copy, at, :] = jnp.where(
         lane < 32, pltpu.roll(before, 96, 1), jnp.where(lane < 64, act, pltpu.roll(after_, 32, 1))
     ).astype(BF16)
 
 
-def tap_start(grid, base, tap, sign):
-    return base + sign * ((tap // 3 - 1) * grid.pitch + (tap % 3 - 1) * PITCH)
+def near_tap(grid, ref, base, tap, sign, size, lanes=slice(None)):
+    return grid.near(ref, base, sign * (tap // 3 - 1), sign * (tap % 3 - 1), size, lanes)
 
 
 def convolve(grid, taps, kernels, rest_ref, acc_ref, stage_ref, e_ref, stage_sem, sums_ref, length):
@@ -248,9 +271,9 @@
     stage_rows = grid.group * grid.line_rows
     groups = grid.side // grid.group
     sums_ref[...] = jnp.zeros_like(sums_ref)
-    mask = frame_mask(grid.line_rows, length, SECOND)
+    mask = grid.mask(grid.line_rows, length, SECOND)
     edge = jnp.zeros((grid.pitch, 256), F32)
-    rest_ref[PITCH : grid.lead, :] = edge
+    rest_ref[grid.lead - grid.pitch : grid.lead, :] = edge
     end = grid.lead + grid.side * grid.pitch
     rest_ref[end : end + grid.pitch, :] = edge
 
@@ -260,7 +283,7 @@
         total = None
         for place in range(3):
             part = jnp.dot(
-                mid_ref[rows_at(base + (place - 1) * PITCH, group_rows), :],
+                grid.near(mid_ref, base, 0, place - 1, group_rows),
                 last_ref[place],
                 preferred_element_type=F32,
             )
@@ -282,12 +305,12 @@
         slot = lax.rem(group, 2)
         for tap in range(9):
             part = jnp.dot(
-                mid_ref[rows_at(tap_start(grid, base, tap, 1), group_rows), :],
+                near_tap(grid, mid_ref, base, tap, 1, group_rows),
                 main_ref[tap],
                 preferred_element_type=F32,
             )
             acc_ref[:, 0:256] = part if tap == 0 else acc_ref[:, 0:256] + part
-        near = [small_ref[rows_at(tap_start(grid, base, tap, 1), group_rows), :] for tap in range(9)]
+        near = [near_tap(grid, small_ref, base, tap, 1, group_rows) for tap in range(9)]
         acc_ref[:, 256:384] = jnp.dot(
             jnp.concatenate(near, axis=1), small_kernel_ref[...], preferred_element_type=F32
         )
@@ -325,8 +348,8 @@
         pltpu.VMEM((9, 512, 256), BF16),
         pltpu.VMEM((3, 512, 256), BF16),
         pltpu.VMEM((1152, 128), BF16),
-        pltpu.VMEM((grid.padded, 512), BF16),
-        pltpu.VMEM((grid.padded, 128), BF16),
+        pltpu.VMEM((grid.copies, grid.padded, 512), BF16),
+        pltpu.VMEM((grid.copies, grid.padded, 128), BF16),
         pltpu.VMEM((grid.rows, REDUCED), BF16),
         pltpu.VMEM((grid.padded, 256), F32),
         pltpu.VMEM((group_rows, 384), F32),
@@ -341,8 +364,8 @@
 def conv_outputs(grid, *clips):
     return (
         shape((grid.rows, REDUCED), BF16),
-        shape((grid.padded, 512), BF16),
-        shape((grid.padded, 128), BF16),
+        shape((grid.copies, grid.padded, 512), BF16),
+        shape((grid.copies, grid.padded, 128), BF16),
         shape((grid.rows, SECOND), F32),
         shape((*clips, 2, SECOND), F32),
     )
@@ -412,7 +435,7 @@
             x_ref[part], p_ref[part], (((0,), (1,)), ((), ())), preferred_element_type=F32
         )
         u_ref[...] = product if part == 0 else u_ref[...] + product
-    mask = frame_mask(step, length, FIRST)
+    mask = slots.grid.mask(step, length, FIRST)
 
     def summed(number, carry):
         values = u_ref[rows_at(number * step, step), :] * mask
@@ -428,11 +451,11 @@
     write_row(sums_ref, 2, 0, SECOND, jnp.full((1, SECOND), count, F32))
     offset = (total / jnp.full((1, FIRST), jnp.maximum(count, 1.0), F32)).astype(BF16)
     wide_offset = offset.astype(F32)
-    tail = jnp.broadcast_to(wide_offset, (PITCH, FIRST)).astype(BF16)
-    pool_ref[rows : rows + PITCH, :] = tail[:, SECOND:]
-    shared = mid_ref.shape[0] - 2 * PITCH
-    mid_ref[shared : shared + PITCH, :] = tail[:, 256:384]
-    mid_ref[shared + PITCH :, :] = tail[:, 384:512]
+    tail = jnp.broadcast_to(wide_offset, (TILE, FIRST)).astype(BF16)
+    pool_ref[rows : rows + TILE, :] = tail[:, SECOND:]
+    shared = mid_ref.shape[0] - 2 * TILE
+    mid_ref[shared : shared + TILE, :] = tail[:, 256:384]
+    mid_ref[shared + TILE :, :] = tail[:, 384:512]
 
     @pl.loop(0, rows // step)
     def _(number):
@@ -459,7 +482,7 @@
 
 
 def mid_rows(slots):
-    return slots.rows + -(-slots.each // 2) * slots.pair_rows + 2 * PITCH
+    return slots.rows + -(-slots.each // 2) * slots.pair_rows + 2 * TILE
 
 
 def each_pair(slots, place, refs, visit):
@@ -490,16 +513,16 @@
     center, inverse = (moment_ref[0:1, DIRECT:], moment_ref[1:2, DIRECT:])
     gain, shift = (gain_ref[block : block + 1], shift_ref[block : block + 1])
     step = 112
-    mask = frame_mask(step, length, REDUCED)
+    mask = grid.mask(step, length, REDUCED)
     lane = lax.broadcasted_iota(jnp.int32, (step, 128), 1)
 
     def fill(h_ref, mid_ref, small_ref):
         def visit(pair, ref, number):
-            shared = ref.shape[0] - 2 * PITCH
+            shared = ref.shape[0] - 2 * TILE
             offset = jnp.concatenate(
                 [
-                    ref[at : at + PITCH, :].astype(F32)[0:1]
-                    for at in (shared, shared + PITCH)
+                    ref[at : at + TILE, :].astype(F32)[0:1]
+                    for at in (shared, shared + TILE)
                 ],
                 axis=1,
             )
@@ -519,7 +542,7 @@
                 act = silu(gain * scaled + shift) * mask
                 line = row // grid.line_rows
                 at = grid.lead + line * grid.pitch + row - line * grid.line_rows
-                store_taps(mid_ref, small_ref, rows_at(at, step), act)
+                store_taps(grid.unit, mid_ref, small_ref, 0, rows_at(at, step), act)
 
         each_pair(slots, place_ref[0], mids, visit)
 
@@ -528,7 +551,7 @@
 
 def pool_planes(grid, plane_ref, q_ref, lo, sums_ref, length, window):
     rows = grid.line_rows
-    mask = frame_mask(rows, length)
+    mask = grid.mask(rows, length)
     sums_ref[...] = jnp.zeros_like(sums_ref)
 
     @pl.loop(0, grid.side)
@@ -561,15 +584,15 @@
     clear_edges(grid, plane_ref)
 
     def visit(pair, ref, number):
-        offset = ref[slots.rows : slots.rows + PITCH, :].astype(F32)[0:1]
+        offset = ref[slots.rows : slots.rows + TILE, :].astype(F32)[0:1]
         for line in range(2):
             at = rows_at(number * slots.pair_rows + line * rows, rows)
             plane_ref[rows_at((2 * pair + line + 1) * rows, rows), :] = plane_box(
-                ref[at, :].astype(F32) + offset
+                ref[at, :].astype(F32) + offset, grid.unit
             )
 
     each_pair(slots, place_ref[0], pools, visit)
-    pool_planes(grid, plane_ref, q_ref, 0, sums_ref, length, box_window(grid.side, length))
+    pool_planes(grid, plane_ref, q_ref, 0, sums_ref, length, box_window(grid, length))
     write_sums(out_sums_ref, sums_ref, SECOND, FIRST)
 
 
@@ -591,11 +614,11 @@
 def first_direct(grid, small, slots, block, length_ref, u_ref, gain_ref, shift_ref, *refs):
     sums, (pooled_ref, kept_ref, moment_ref) = (refs[: slots.parts], refs[slots.parts :])
     rows = grid.line_rows
-    mask = frame_mask(rows, length_ref[0], DIRECT)
+    mask = grid.mask(rows, length_ref[0], DIRECT)
     center, inverse = set_moments(total_of(sums), moment_ref)
     center, inverse = (center[:, :DIRECT], inverse[:, :DIRECT])
     gain, shift = (gain_ref[block : block + 1, :DIRECT], shift_ref[block : block + 1, :DIRECT])
-    matrix = pool_matrix(small.side, False)
+    matrix = pool_matrix(grid, small, False)
 
     @pl.loop(0, slots.each)
     def _(number):
@@ -644,7 +667,7 @@
 
     for copy in arriving(0, 0):
         copy.start()
-    mask = frame_mask(rows, length_ref[0], FIRST)
+    mask = grid.mask(rows, length_ref[0], FIRST)
     total = total_of(sums_in_ref)
     count = jnp.concatenate([moment_ref[2:3, 0:128]] * (FIRST // 128), axis=1)
     center, inverse = moments(total[0:1], total[1:2], count)
@@ -654,7 +677,7 @@
         count,
         outer_ref,
     )
-    matrix = pool_matrix(small.side, False)
+    matrix = pool_matrix(grid, small, False)
     gain, shift = (gain_ref[block : block + 1, DIRECT:], shift_ref[block : block + 1, DIRECT:])
 
     @pl.loop(0, pairs)
@@ -719,12 +742,30 @@
         values = q_ref[rows_at(line * rows, rows), :]
         sums_ref[0:8] += partial_sum(values[:, :SECOND])
         sums_ref[8:16] += partial_sum(values[:, :SECOND] * values[:, :SECOND])
-        plane_ref[rows_at((line + 1) * rows, rows), :] = plane_box(values[:, SECOND:])
-
-    pool_planes(grid, plane_ref, q_ref, SECOND, pool_sums_ref, length, box_window(grid.side, length))
+        plane_ref[rows_at((line + 1) * rows, rows), :] = plane_box(
+            values[:, SECOND:], grid.unit
+        )
+
+    pool_planes(grid, plane_ref, q_ref, SECOND, pool_sums_ref, length, box_window(grid, length))
     write_sums(out_sums_ref, sums_ref, 0, SECOND)
     write_sums(out_sums_ref, pool_sums_ref, SECOND, FIRST)
     write_row(out_sums_ref, 2, 0, FIRST, jnp.full((1, FIRST), count_ref[0], F32))
+
+
+def clear_ends(grid, ref):
+    edge = jnp.zeros((grid.line_rows, ref.shape[1]), F32)
+    ref[0 : grid.line_rows, :] = edge
+    ref[grid.rows + grid.line_rows :, :] = edge
+
+
+def store_copies(grid, ref, store):
+    @pl.loop(0, grid.side + 1)
+    def _(number):
+        start = number * grid.line_rows
+        at = rows_at(grid.lead + (number - 1) * grid.pitch, grid.line_rows)
+        store(0, at, ref[rows_at(start, grid.line_rows), :])
+        moved = pl.ds(pl.multiple_of(start + grid.unit, grid.unit), grid.line_rows)
+        store(1, at, ref[moved, :])
 
 
 def second_convolve(grid, block, length_ref, q_ref, sums_in_ref, gain_ref, shift_ref, *refs):
@@ -733,18 +774,24 @@
     center, inverse = set_moments(total_of(sums_in_ref), moment_ref)
     center, inverse = (center[:, DIRECT:SECOND], inverse[:, DIRECT:SECOND])
     gain, shift = (gain_ref[block : block + 1], shift_ref[block : block + 1])
-    mask = frame_mask(grid.line_rows, length, REDUCED)
+    rows = grid.line_rows
+    mask = grid.mask(rows, length, REDUCED)
+    scratch, act_ref = (scratch[:-1], scratch[-1])
 
     def fill(h_ref, mid_ref, small_ref):
+        clear_ends(grid, act_ref)
+
         @pl.loop(0, grid.side)
         def _(line):
-            at = rows_at(line * grid.line_rows, grid.line_rows)
+            at = rows_at(line * rows, rows)
             scaled = (q_ref[at, DIRECT:SECOND] - center) * inverse
             h_ref[at, :] = scaled.astype(BF16)
-            act = silu(gain * scaled + shift) * mask
-            store_taps(
-                mid_ref, small_ref, rows_at(grid.lead + line * grid.pitch, grid.line_rows), act
-            )
+            act_ref[rows_at((line + 1) * rows, rows), :] = silu(gain * scaled + shift) * mask
+
+        def store(copy, at, values):
+            store_taps(grid.unit, mid_ref, small_ref, copy, at, values)
+
+        store_copies(grid, act_ref, store)
 
     run_convolution(grid, length, far_kernels, outputs, scratch, fill)
 
@@ -752,7 +799,7 @@
 def second_output(grid, block, length_ref, q_ref, e_ref, moment_ref, sums_in_ref, gain_ref, shift_ref, cot_ref, act_ref, h_ref, error_ref, outer_ref, out_sums_ref, sums_ref):
     rows = grid.line_rows
     side, frames = (grid.side, cot_ref.shape[1])
-    mask = frame_mask(rows, length_ref[0], OUTER)
+    mask = grid.mask(rows, length_ref[0], OUTER)
     total = total_of(sums_in_ref)
     count = moment_ref[2:3, 0:SECOND]
     center, inverse = moments(total[0:1], total[1:2], count)
@@ -762,7 +809,7 @@
     sums_ref[...] = jnp.zeros_like(sums_ref)
     gain, shift = (gain_ref[block : block + 1], shift_ref[block : block + 1])
     gap = jnp.zeros((rows, 64), F32)
-    unused = jnp.zeros((side, PITCH - frames, CHANNELS), F32)
+    unused = jnp.zeros((grid.unit, CHANNELS), F32)
 
     @pl.loop(0, side)
     def _(line):
@@ -773,12 +820,12 @@
         h_ref[at, :] = scaled.astype(BF16)
         shifted = gain * scaled + shift
         gate = sigmoid(shifted)
-        act = (shifted * gate * mask).reshape(side, PITCH, OUTER)[:, :frames].astype(BF16)
+        act = (shifted * gate * mask).reshape(side + 1, frames, OUTER)[:side].astype(BF16)
         act_ref[places, :, 0:576] = act[:, :, 0:576]
         act_ref[places, :, 576:CHANNELS] = act[:, :, 640:OUTER]
         slope = gate * (1.0 + shifted * (1.0 - gate))
-        grad = jnp.concatenate([cot_ref[places].astype(F32), unused], axis=1)
-        grad = grad.reshape(rows, CHANNELS)
+        grad = cot_ref[places].astype(F32).reshape(side * frames, CHANNELS)
+        grad = jnp.concatenate([grad, unused], axis=0)
         grad = jnp.concatenate([grad[:, :576], gap, grad[:, 576:]], axis=1)
         error = grad * slope * mask
         error_ref[at, :] = error.astype(BF16)
@@ -789,7 +836,7 @@
 
 
 def spread_matrix(grid, small):
-    return None if small is None else pool_matrix(small.side, True)[: grid.line_rows]
+    return None if small is None else pool_matrix(grid, small, True)[: grid.line_rows]
 
 
 def outer_error(slopes, small, grad_ref, matrix, line, lo, hi):
@@ -838,7 +885,7 @@
     first = small is not None
     (grad_ref, carried_ref), refs = (refs[:2], refs[2:]) if first else ((None, None), refs)
     mid_far, few_far, d_far, total_ref, out_ref, *refs = refs
-    d_ref, h_ref, slope_ref, mid_ref, few_ref, mid_acc_ref, small_acc_ref, turned_ref, sem_ref, in_sem, out_sem = refs
+    d_ref, h_ref, slope_ref, mid_ref, few_ref, mid_acc_ref, small_acc_ref, turned_ref, sem_ref, in_sem, out_sem, *refs = refs
     lo, hi = (DIRECT, DIRECT + SECOND)
     at = 0 if first else DIRECT
     lines = Lines(
@@ -856,7 +903,7 @@
     a, b, c = before_norm(
         gain_ref[block : block + 1, lo:hi], outer_ref[1:2, lo:hi], total[:, lo:hi], outer_ref[2:3, lo:hi]
     )
-    mask = frame_mask(grid.line_rows, length_ref[0], SECOND)
+    mask = grid.mask(grid.line_rows, length_ref[0], SECOND)
     matrix = spread_matrix(grid, small)
     clear_empty(grid, d_ref)
     rows = grid.line_rows
@@ -872,9 +919,19 @@
             scaled = h_ref[here, :].astype(F32)
             error = outer_error(slope_ref[here, :], small, grad_ref, matrix, line, lo, hi)
             back = (a * error - b - c * scaled) * mask
-            d_ref[rows_at(grid.lead + line * grid.pitch, rows), :] = back.astype(BF16)
+            if grid.copies == 1:
+                d_ref[0, rows_at(grid.lead + line * grid.pitch, rows), :] = back.astype(BF16)
+            else:
+                refs[0][rows_at((line + 1) * rows, rows), :] = back
 
     lines.run(visit)
+    if grid.copies > 1:
+        clear_ends(grid, refs[0])
+
+        def store(copy, at, values):
+            d_ref[copy, at, :] = values.astype(BF16)
+
+        store_copies(grid, refs[0], store)
     leaving = pltpu.make_async_copy(d_ref, d_far, out_sem.at[0])
     leaving.start()
     for copy in arriving:
@@ -890,17 +947,18 @@
 
 def second_back_scratch(grid, slots):
     return [
-        pltpu.VMEM((grid.padded, SECOND), BF16),
+        pltpu.VMEM((grid.copies, grid.padded, SECOND), BF16),
         pltpu.VMEM((grid.rows, SECOND), BF16),
         pltpu.VMEM((grid.rows, SECOND), BF16),
-        pltpu.VMEM((grid.padded, 512), BF16),
-        pltpu.VMEM((grid.padded, 128), BF16),
+        pltpu.VMEM((grid.copies, grid.padded, 512), BF16),
+        pltpu.VMEM((grid.copies, grid.padded, 128), BF16),
         pltpu.VMEM((slots, 384, 256), F32),
         pltpu.VMEM((slots, 128, 128), F32),
         pltpu.VMEM((MID_IN + 128, 128), F32),
         Lines.semaphores(grid, 2),
         pltpu.SemaphoreType.DMA((2,)),
         pltpu.SemaphoreType.DMA((1,)),
+        *([pltpu.VMEM((grid.rows + 2 * grid.line_rows, SECOND), F32)] if grid.copies > 1 else []),
     ]
 
 
@@ -922,26 +980,32 @@
     rows = grid.line_rows
     group_rows = grid.group * grid.pitch
     sums_ref[...] = jnp.zeros_like(sums_ref)
-    mask = frame_mask(rows, length_ref[0], REDUCED)
+    mask = grid.mask(rows, length_ref[0], REDUCED)
     gain, shift = (reduced_gain_ref[block : block + 1], reduced_shift_ref[block : block + 1])
     turned = (((1,), (1,)), ((), ()))
     lane = lax.broadcasted_iota(jnp.int32, (rows, 128), 1)
     wide_lane = lax.broadcasted_iota(jnp.int32, (grid.pitch, 128), 1)
 
-    @pl.loop(0, grid.side)
-    def _(line):
-        place = grid.lead + line * grid.pitch
-        here = d_ref[rows_at(place, grid.pitch), 256:384].astype(F32)
-        further = d_ref[rows_at(place + grid.pitch, grid.pitch), 256:384].astype(F32)
-        at = rows_at(place, grid.pitch)
-        last_ref[at, 0:128] = jnp.where(wide_lane < 64, further, pltpu.roll(here, 64, 1)).astype(
-            BF16
-        )
-        last_ref[at, 128:256] = d_ref[rows_at(place - grid.pitch, grid.pitch), 256:384]
-
-    last_ref[grid.lead - PITCH : grid.lead, :] = jnp.zeros((PITCH, 256), BF16)
-    end = grid.lead + grid.side * grid.pitch
-    last_ref[end : end + PITCH, :] = jnp.zeros((PITCH, 256), BF16)
+    for copy in range(grid.copies):
+
+        @pl.loop(1 - grid.copies, grid.side)
+        def _(line):
+            place = grid.lead + line * grid.pitch
+
+            def lanes(start):
+                return d_ref[copy, rows_at(start, grid.pitch), 256:384]
+
+            further, here = (lanes(place + grid.pitch).astype(F32), lanes(place).astype(F32))
+            at = rows_at(place, grid.pitch)
+            last_ref[copy, at, 0:128] = jnp.where(
+                wide_lane < 64, further, pltpu.roll(here, 64, 1)
+            ).astype(BF16)
+            last_ref[copy, at, 128:256] = lanes(place - grid.pitch)
+
+        if grid.copies == 1:
+            last_ref[copy, grid.lead - TILE : grid.lead, :] = jnp.zeros((TILE, 256), BF16)
+        end = grid.lead + grid.side * grid.pitch
+        last_ref[copy, end : end + TILE, :] = jnp.zeros((TILE, 256), BF16)
     for copy in arriving:
         copy.wait()
 
@@ -950,7 +1014,7 @@
         base = grid.lead + group * group_rows
         for tap in range(9):
             part = lax.dot_general(
-                d_ref[rows_at(tap_start(grid, base, tap, -1), group_rows), 0:256],
+                near_tap(grid, d_ref, base, tap, -1, group_rows, slice(0, 256)),
                 main_ref[tap],
                 turned,
                 preferred_element_type=F32,
@@ -958,13 +1022,13 @@
             acc_ref[:, 0:512] = part if tap == 0 else acc_ref[:, 0:512] + part
         for place in range(3):
             acc_ref[:, 0:512] += lax.dot_general(
-                last_ref[rows_at(base - (place - 1) * PITCH, group_rows), :],
+                grid.near(last_ref, base, 0, 1 - place, group_rows),
                 rest_ref[place],
                 turned,
                 preferred_element_type=F32,
             )
         near = [
-            d_ref[rows_at(tap_start(grid, base, tap, -1), group_rows), 384:512] for tap in range(9)
+            near_tap(grid, d_ref, base, tap, -1, group_rows, slice(384, 512)) for tap in range(9)
         ]
         acc_ref[:, 512:640] = jnp.dot(
             jnp.concatenate(near, axis=1), small_ref[...], preferred_element_type=F32
@@ -976,9 +1040,10 @@
             one = jnp.where(lane < 32, rest, pltpu.roll(small, 32, 1))
             two = jnp.where(lane < 32, pltpu.roll(rest, 96, 1), small)
             three = jnp.where(lane < 32, pltpu.roll(rest, 64, 1), pltpu.roll(small, 96, 1))
-            wide = later(acc_ref[lines, 0:128]) + acc_ref[lines, 128:256]
-            wide = wide + earlier(acc_ref[lines, 256:384])
-            narrow = jnp.where(lane < 64, later(one) + two + earlier(three), 0.0)
+            unit = grid.unit
+            wide = later(acc_ref[lines, 0:128], unit) + acc_ref[lines, 128:256]
+            wide = wide + earlier(acc_ref[lines, 256:384], unit)
+            narrow = jnp.where(lane < 64, later(one, unit) + two + earlier(three, unit), 0.0)
             back = jnp.concatenate([wide, narrow], axis=1)
             at = rows_at(line * rows, rows)
             scaled = reduced_ref[at, :].astype(F32)
@@ -990,7 +1055,7 @@
     write_sums(out_sums_ref, sums_ref, 0, REDUCED)
     if first:
         x_copy.wait()
-        ones = frame_mask(slots.rows, length_ref[0])
+        ones = grid.mask(slots.rows, length_ref[0])
         low_ones = ones.astype(BF16)
         two_ones = jnp.concatenate([ones, ones], axis=1)
 
@@ -1022,17 +1087,23 @@
     @pl.loop(0, grid.side // grid.group)
     def _(group):
         base = grid.lead + group * group_rows
-        left = d_ref[rows_at(base, group_rows), :].T
+        left = d_ref[0, rows_at(base, group_rows), :].T
         for slot in range(slots):
             tap = lax.rem(jnp.minimum(first_ref[0] + slot, TAPS - 1), 9)
-            at = rows_at(
-                base + (tap // 3 - 1) * grid.pitch + (lax.rem(tap, 3) - 1) * PITCH, group_rows
-            )
+            start = base + (tap // 3 - 1) * grid.pitch
+            place = lax.rem(tap, 3) - 1
+            copy = 0
+            if grid.copies == 1:
+                start = start + place * TILE
+            else:
+                copy = jnp.where(place == 0, 0, 1)
+                start = start - jnp.where(place < 0, TILE, 0)
+            at = rows_at(start, group_rows)
             lanes = pl.ds(pl.multiple_of(neighbour(slot) * 128, 128), 128)
-            right = jnp.concatenate([mid_ref[at, lanes], mid_ref[at, 384:512]], axis=1)
+            right = jnp.concatenate([mid_ref[copy, at, lanes], mid_ref[copy, at, 384:512]], axis=1)
             mid_acc_ref[slot] += jnp.dot(left[0:384], right, preferred_element_type=F32)
             small_acc_ref[slot] += jnp.dot(
-                left[384:512], small_ref[at, :], preferred_element_type=F32
+                left[384:512], small_ref[copy, at, :], preferred_element_type=F32
             )
 
     share = round_up(slots * TAP_ROWS, 16 * out_ref.shape[0]) // out_ref.shape[0]
@@ -1071,21 +1142,22 @@
     def __init__(self, grid, plane_ref, across_ref, scale_ref, length):
         self.grid, self.plane, self.across, self.scale = (grid, plane_ref, across_ref, scale_ref)
         clear_edges(grid, plane_ref)
-        window = box_window(grid.side, length)
+        window = box_window(grid, length)
         scale_ref[0] = box_scale(0, grid.side, window)
         scale_ref[1] = box_scale(1, grid.side, window)
-        edge = jnp.zeros((PITCH, POOLED), F32)
-        across_ref[0:PITCH, :] = edge
-        across_ref[PITCH + grid.line_rows :, :] = edge
+        unit = grid.unit
+        edge = jnp.zeros((unit, POOLED), F32)
+        across_ref[0:unit, :] = edge
+        across_ref[unit + grid.line_rows :, :] = edge
 
     def put(self, line, values):
         rows = self.grid.line_rows
         inner = jnp.where((line == 0) | (line == self.grid.side - 1), 0, 1)
         values = values * self.scale[inner]
-        across = self.across
-        across[PITCH : PITCH + rows, :] = values + earlier(values) + later(values)
+        across, unit = (self.across, self.grid.unit)
+        across[unit : unit + rows, :] = values + earlier(values, unit) + later(values, unit)
         self.plane[rows_at((line + 1) * rows, rows), :] = (
-            across[0:rows, :] + across[PITCH : PITCH + rows, :] + across[2 * PITCH :, :]
+            across[0:rows, :] + across[unit : unit + rows, :] + across[2 * unit :, :]
         )
 
     def get(self, start, size):
@@ -1100,7 +1172,7 @@
     def scratch(grid):
         return [
             pltpu.VMEM((grid.rows + 2 * grid.line_rows, POOLED), F32),
-            pltpu.VMEM((grid.line_rows + 2 * PITCH, POOLED), F32),
+            pltpu.VMEM((grid.line_rows + 2 * grid.unit, POOLED), F32),
             pltpu.VMEM((2, grid.line_rows, POOLED), F32),
         ]
 
@@ -1167,7 +1239,7 @@
         outer_ref[2:3, 0:REDUCED],
     )
     rest = rest_constants(outer_ref, total_ref, gain_ref, block)
-    mask = frame_mask(rows, length, DIRECT + POOLED)
+    mask = grid.mask(rows, length, DIRECT + POOLED)
     spread = Spread(grid, plane_ref, across_ref, scale_ref, length)
 
     def visit(line):
@@ -1252,7 +1324,7 @@
     length = length_ref[0]
     matrix = spread_matrix(grid, small)
     a, b, c = rest_constants(outer_ref, total_ref, gain_ref, block)
-    mask = frame_mask(rows, length, DIRECT + POOLED)
+    mask = grid.mask(rows, length, DIRECT + POOLED)
     spread = Spread(grid, plane_ref, across_ref, scale_ref, length)
 
     def visit(step):
@@ -1273,7 +1345,7 @@
     lines.run(visit)
     x_copy.wait()
     wide = lines.size
-    pool_mask = frame_mask(wide, length)
+    pool_mask = grid.mask(wide, length)
 
     def leaving(step):
         at = rows_at(step * wide, wide)
@@ -1309,7 +1381,7 @@
     a, b, c = before_norm(
         gain_ref[block : block + 1], moment_ref[1:2, DIRECT:], total, moment_ref[2:3, DIRECT:]
     )
-    mask = frame_mask(lines.size, length_ref[0], REDUCED)
+    mask = grid.mask(lines.size, length_ref[0], REDUCED)
     p_copy.wait()
 
     def leaving(step):
@@ -1571,7 +1643,7 @@
     clips = lax.axis_size("dp")
     place = lax.axis_index("branch").astype(jnp.int32)
     side = frames.shape[2]
-    grid, small = (Grid(side), Grid(side // 2))
+    grid, small = (Grid(side, frames.shape[1]), Grid(side // 2, frames.shape[1] // 2))
     slots = Slots(grid, parts)
     cells = side * side
     own_channels = frames.shape[-1]
@@ -1609,7 +1681,7 @@
         functools.partial(first_pointwise, slots),
         (
             shape((mid_rows(slots), 128), BF16),
-            shape((slots.rows + PITCH, POOLED), BF16),
+            shape((slots.rows + TILE, POOLED), BF16),
             shape((slots.rows, DIRECT), F32),
             shape((clips, 3, SECOND), F32),
         ),
@@ -1640,7 +1712,6 @@
         far_out=range(4),
     )(length, place_one, *mids, moment, reduced_gain, reduced_shift, *kernels[0][:3])
     pooled_directs = spread_over(after(pooled_direct, (pools, e_sums)), "branch", parts)
-    kept_direct = lax.all_gather(after(kept_direct, pooled_directs), "branch", axis=0)
     q_pool, second_sums = call(
         functools.partial(first_pool, grid, slots),
         (shape((grid.rows, POOLED), F32), shape((clips, 2, FIRST), F32)),
@@ -1651,6 +1722,7 @@
         scalars=2,
     )(length, place_one, *pools, e_sums)
     second_sums = exchange(second_sums)
+    kept_direct = lax.all_gather(after(kept_direct, second_sums), "branch", axis=0)
     pair = 2 * grid.line_rows
     pooled, h_outer, slope, outer, pooled_slope, pooled_product = call(
         functools.partial(first_output, grid, small, 0),
@@ -1701,7 +1773,7 @@
     h_reduced_small, taps_mid_small, taps_few_small, e_small, e_sums_small, moment_small = call(
         functools.partial(second_convolve, small, 1),
         (*conv_outputs(small, clips), shape((3, FIRST), F32)),
-        conv_scratch(small),
+        [*conv_scratch(small), pltpu.VMEM((small.rows + 2 * small.line_rows, REDUCED), F32)],
         scalars=1,
         far=range(5, 8),
         far_out=range(4),
@@ -1730,7 +1802,7 @@
             pltpu.VMEM((9, 512, 256), BF16),
             pltpu.VMEM((3, 512, 256), BF16),
             pltpu.VMEM((1152, 128), BF16),
-            pltpu.VMEM((at.padded, 256), BF16),
+            pltpu.VMEM((at.copies, at.padded, 256), BF16),
             pltpu.VMEM((at.group * at.pitch, FIRST), F32),
             pltpu.VMEM((16, REDUCED), F32),
             pltpu.SemaphoreType.DMA((3,)),
@@ -1740,7 +1812,7 @@
     d_low, total_small, packed_small = call(
         functools.partial(second_back, small, None, 1, taps_each),
         (
-            shape((small.padded, SECOND), BF16),
+            shape((small.copies, small.padded, SECOND), BF16),
             shape((2, OUTER), F32),
             shape((clips, tap_share, 128), BF16),
         ),
@@ -1835,7 +1907,7 @@
     d_low, total, packed = call(
         functools.partial(second_back, grid, small, 0, taps_each),
         (
-            shape((grid.padded, SECOND), BF16),
+            shape((grid.copies, grid.padded, SECOND), BF16),
             shape((2, OUTER), F32),
             shape((clips, tap_share + point_share, 128), BF16),
         ),
@@ -1914,14 +1986,6 @@
         far=(5, 6, 7, 8),
         far_out=(0,),
     )(length, place_one, moment, gathered, reduced_gain, du_rest, h_reduced, r_low, point_first)
-    pieces, dx = lax.optimization_barrier((pieces, dx))
-    point_sum = call(
-        functools.partial(combine, 0),
-        shape((5 * product_rows // clips, 128), BF16),
-        cost=1,
-    )(pieces, moment, gathered, reduced_gain)
-    received = spread_over(point_sum, "branch", parts)
-
     outs = (
         shape((2, TAPS, MID_IN, MID_OUT), F32),
         shape((2, TAPS, SMALL_IN, SMALL_OUT), F32),
@@ -1939,7 +2003,14 @@
         far_out=(0, 1),
         cost=5,
     )(whole_small)
-    received, mid_grad, small_grad = lax.optimization_barrier((received, mid_grad, small_grad))
+    pieces, mid_grad, small_grad, dx = lax.optimization_barrier((pieces, mid_grad, small_grad, dx))
+    point_sum = call(
+        functools.partial(combine, 0),
+        shape((5 * product_rows // clips, 128), BF16),
+        cost=1,
+    )(pieces, moment, gathered, reduced_gain)
+    received = spread_over(point_sum, "branch", parts)
+
     norms = shape((2, 1024), F32)
     mid_grad, small_grad, point_grad, gain_grad, shift_grad = call(
         functools.partial(unpack_first, parts, clips, taps_each, tap_share),
@@ -1967,7 +2038,7 @@
         cost=3,
     )(place_one, clip_one, point_mine, point_other, point_grad)
     act = act.reshape(small.side, small.side, cotangent.shape[1], CHANNELS).transpose(2, 0, 1, 3)
-    input_grad = dx.reshape(side, side, PITCH, own_channels).transpose(2, 0, 1, 3)
+    input_grad = dx.reshape(side, side, grid.unit, own_channels).transpose(2, 0, 1, 3)
     return (
         act[None],
         input_grad[None],

time: 390 us -> 376 us (0.964)
  Pallas kernels: 181 us -> 169 us
  waiting for transfers between devices: 86.3 us -> 76.3 us
  blocking collectives: 53 us -> 61.8 us
    pallas_call x21, Pallas kernels: 181 us -> 169 us  [run(): pl.pallas_call(body, out_shape=jax.tree.map(placed, out_shape), in_specs=...]
    all_to_all x5 -> x4, waiting for transfers between devices: 35.8 us -> 26.3 us  [exchange(): return lax.all_to_all(values, 'dp', 0, 0, tiled=True)]
    all_to_all x6 -> x7, blocking collectives: 53 us -> 61.8 us  [exchange(): return lax.all_to_all(values, 'dp', 0, 0, tiled=True)]
    all_to_all x5 -> x4, starting transfers between devices: 17.8 us -> 14 us  [exchange(): return lax.all_to_all(values, 'dp', 0, 0, tiled=True)]
  transfers between devices with their start and end apart: 28 -> 27, of which waited for: 11 -> 10; matrix products, arithmetic and copies ran while one was open for 0% -> 1% of each run, Pallas kernels for 44% -> 41%
where the time goes in v1:
time: 376 us; the launch traced here: 374 us
  Pallas kernels  169 us (45%)
  waiting for transfers between devices  76.3 us (20%)
  blocking collectives  61.8 us (16%)
  starting transfers between devices  44.1 us (12%)
  between operations  14.8 us (4%)
  local copies, waits for them, and re-layouts  5.68 us (2%)
    pallas_call x21, Pallas kernels, run(): pl.pallas_call(body, out_shape=jax.tree.map(placed, out_shape), in_specs=...  169 us
    all_to_all x7, blocking collectives, exchange(): return lax.all_to_all(values, 'dp', 0, 0, tiled=True)  61.8 us
    all_to_all x4, waiting for transfers between devices, exchange(): return lax.all_to_all(values, 'dp', 0, 0, tiled=True)  26.3 us
    all_to_all x1, waiting for transfers between devices, on_device(): by_pairs = lax.all_to_all(turned, 'branch', 0, 0, tiled=True)  24.4 us
    ppermute x15, waiting for transfers between devices, spread_over(): received.append(lax.ppermute(values, axis, perm))  23.4 us
    ppermute x15, starting transfers between devices, spread_over(): received.append(lax.ppermute(values, axis, perm))  19.8 us
    all_to_all x4, starting transfers between devices, exchange(): return lax.all_to_all(values, 'dp', 0, 0, tiled=True)  14 us
  transfers between devices with their start and end apart: 27, of which 10 were waited for; matrix products, arithmetic and copies ran while one was open for 1% of the time, Pallas kernels for 41%

profile of v1, /device:TPU:0, one launch (start us, length us, event | category | flops | bytes accessed | tf_op | source)
XLA Modules:
  0.0 374.5 jit_solution(15811065990234969699)
XLA Ops:
  7.2 3.2 shard_map.135.x_far.refs_3_
  10.4 6.3 %all-to-all-start = ((bf16[4,208,896]{2,1,0:T(8,128)(2,1)}), bf16[4,208,896]{2,1,0:T(8,128)(2,1)S(1)}, u32[]{:S(2)}, u32[]{:S(2)}) async-start(bf16[4,208,896]{2,1,0:T(8,128)(2,1)} %shard_map.135.x_far.refs_3_), calls=%async_computation | async-start | bytes 2981888 | tf_op jit(solution)/shard_map/all_to_all | solution.py:1656
  17.4 10.1 %shard_map.136 = (bf16[9,512,256]{2,1,0:T(8,128)(2,1)}, bf16[3,512,256]{2,1,0:T(8,128)(2,1)}, bf16[1152,128]{1,0:T(8,128)(2,1)}, bf16[1152,128]{1,0:T(8,128)(2,1...) custom-call(bf16[2,27,160,320]{3,2,1,0:T(8,128)(2,1)} %mid_in.1, ...), custom_call_target="tpu_custom_call" | custom-call | bytes 15000000 | tf_op jit(solution)/shard_map/pallas_call | solution.py:66
  27.5 24.4 %all-to-all-done.x_ref = bf16[4,208,896]{2,1,0:T(8,128)(2,1)S(1)} async-done(((bf16[4,208,896]{2,1,0:T(8,128)(2,1)}), bf16[4,208,896]{2,1,0:T(8,128)(2,1)S(1)}, u32[]{:S(2)}, u32[]{:S(2)}) %all-to-all-start) | async-done | bytes 1490976 | tf_op jit(solution)/shard_map/all_to_all | solution.py:1656
  53.0 5.3 %shard_map.137 = (bf16[1376,128]{1,0:T(8,128)(2,1)}, bf16[912,128]{1,0:T(8,128)(2,1)}, f32[896,256]{1,0:T(8,128)}, f32[8,3,512]{2,1,0:T(4,128)}) custom-call(s32[1]{0:T(128)S(6)} %copy.24.length_ref, f32[1]{0:T(128)S(6)} %convert_element_type.5.count_ref, bf16[4,208,896]{2,1,0:T(8,128)(2,1)} %copy-done, bf16[4,640,208]{2,1,0:T(8,128)(2,1)} %get-tuple-element.99.p_ref.p_far), custom_call_target="tpu_custom_call" | custom-call | bytes 15000000 | tf_op jit(solution)/shard_map/pallas_call | solution.py:66
  58.3 2.0 collective-permute-start.4
  60.4 1.8 collective-permute-start.5
  62.2 8.7 %all_to_all.60 = f32[8,3,512]{2,1,0:T(4,128)S(1)} all-to-all(f32[8,3,512]{2,1,0:T(4,128)} %get-tuple-element.104), channel_id=1, replica_groups=mesh['dp'=8,'branch'=4] {'dp'}, dimensions={0} | all-to-all | bytes 98304 | tf_op jit(solution)/shard_map/all_to_all | solution.py:1621
  73.1 12.0 %collective-permute-done.refs_1_ = f32[3,512]{1,0:T(4,128)S(1)} collective-permute-done((f32[3,512]{1,0:T(4,128)S(1)}, f32[3,512]{1,0:T(4,128)S(1)}, u32[]{:S(2)}, u32[]{:S(2)}) %collective-permute-start) | collective-permute-done | bytes 6176 | tf_op jit(solution)/shard_map/ppermute | solution.py:1612
  85.1 6.9 %collective-permute-done.1.refs_2_ = f32[3,512]{1,0:T(4,128)S(1)} collective-permute-done((f32[3,512]{1,0:T(4,128)S(1)}, f32[3,512]{1,0:T(4,128)S(1)}, u32[]{:S(2)}, u32[]{:S(2)}) %collective-permute-start.1) | collective-permute-done | bytes 6176 | tf_op jit(solution)/shard_map/ppermute | solution.py:1612
  92.6 3.2 shard_map.138
  98.3 2.8 collective-permute-start.8
  101.2 24.9 %shard_map.139 = (bf16[3136,256]{1,0:T(8,128)(2,1)}, bf16[1,3872,512]{2,1,0:T(8,128)(2,1)}, bf16[1,3872,128]{2,1,0:T(8,128)(2,1)}, f32[3136,512]{1,0:T(8,128)}, f32[2,512]{1,0:T(2,128)}) custom-call(s32[1]{0:T(128)S(6)} %copy.24.length_ref, s32[1]{0:T(128)} %bitcast.place_ref, bf16[1376,128]{1,0:T(8,128)(2,1)} %get-tuple-element.106.refs_0_, ...), custom_call_target="tpu_custom_call" | custom-call | bytes 120000000 | tf_op jit(solution)/shard_map/pallas_call | solution.py:66
  126.9 3.9 %shard_map.140 = (f32[3136,128]{1,0:T(8,128)}, f32[8,2,640]{2,1,0:T(2,128)}) custom-call(s32[1]{0:T(128)S(6)} %copy.24.length_ref, s32[1]{0:T(128)} %bitcast.place_ref, bf16[912,128]{1,0:T(8,128)(2,1)} %get-tuple-element.108.refs_0_, bf16[912,128]{1,0:T(8,128)(2,1)} %copy-done.7, bf16[912,128]{1,0:T(8,128)(2,1)} %copy-done.8, bf16[912,128]{1,0:T(8,128)(2,1)} %copy-done.9, ...), custom_call_target="tpu_custom_call" | custom-call | bytes 15000000 | tf_op jit(solution)/shard_map/pallas_call | solution.py:66
  130.8 8.8 %all_to_all.61.sums_in_ref = f32[8,2,640]{2,1,0:T(2,128)} all-to-all(f32[8,2,640]{2,1,0:T(2,128)} %get-tuple-element.119), channel_id=1, replica_groups=mesh['dp'=8,'branch'=4] {'dp'}, dimensions={0} | all-to-all | bytes 81920 | tf_op jit(solution)/shard_map/all_to_all | solution.py:1621
  140.4 3.2 collective-permute-start.11
  143.6 11.7 %shard_map.141 = (bf16[448,640]{1,0:T(8,128)(2,1)}, bf16[3136,640]{1,0:T(8,128)(2,1)}, bf16[3136,640]{1,0:T(8,128)(2,1)}, f32[3,896]{1,0:T(4,128)}, bf16[448,640]{1,0:T(8,128)(2,1)}, /*index=5*/bf16[448,640]{1,0:T(8,128)(2,1)}) custom-call(s32[1]{0:T(128)S(6)} %copy.24.length_ref, f32[3136,128]{1,0:T(8,128)} %get-tuple-element.117.q_far, ...), custom_call_target="tpu_custom_call" | custom-call | bytes 15000000 | tf_op jit(solution)/shard_map/pallas_call | solution.py:66
  156.0 4.3 %shard_map.142 = (f32[448,640]{1,0:T(8,128)}, f32[8,3,640]{2,1,0:T(4,128)}, bf16[448,896]{1,0:T(8,128)(2,1)}) custom-call(s32[1]{0:T(128)S(6)} %select_n.12.length_ref, s32[1]{0:T(128)} %bitcast.place_ref, f32[1]{0:T(128)S(6)} %mul.20.count_ref, bf16[128,256]{1,0:T(8,128)(2,1)} %get-tuple-element.116.refs_0_, bf16[128,256]{1,0:T(8,128)(2,1)} %copy-done.12, ...), custom_call_target="tpu_custom_call" | custom-call | bytes 15000000 | tf_op jit(solution)/shard_map/pallas_call | solution.py:66
  160.3 9.1 %all_to_all.62.sums_in_ref = f32[8,3,640]{2,1,0:T(4,128)} all-to-all(f32[8,3,640]{2,1,0:T(4,128)} %get-tuple-element.123), channel_id=1, replica_groups=mesh['dp'=8,'branch'=4] {'dp'}, dimensions={0} | all-to-all | bytes 122880 | tf_op jit(solution)/shard_map/all_to_all | solution.py:1621
  169.4 6.7 %shard_map.143 = (bf16[448,256]{1,0:T(8,128)(2,1)}, bf16[2,736,512]{2,1,0:T(8,128)(2,1)}, bf16[2,736,128]{2,1,0:T(8,128)(2,1)}, f32[448,512]{1,0:T(8,128)}, f32[8,2,512]{2,1,0:T(2,128)}, /*index=5*/f32[3,640]{1,0:T(4,128)}) custom-call(s32[1]{0:T(128)S(6)} %select_n.12.length_ref, f32[448,640]{1,0:T(8,128)} %get-tuple-element.122.q_ref, ...), custom_call_target="tpu_custom_call" | custom-call | bytes 15000000 | tf_op jit(solution)/shard_map/pallas_call | solution.py:66
  176.1 8.8 %all_to_all.63.sums_in_ref = f32[8,2,512]{2,1,0:T(2,128)} all-to-all(f32[8,2,512]{2,1,0:T(2,128)} %get-tuple-element.129), channel_id=1, replica_groups=mesh['dp'=8,'branch'=4] {'dp'}, dimensions={0} | all-to-all | bytes 65536 | tf_op jit(solution)/shard_map/all_to_all | solution.py:1621
  184.9 4.8 %shard_map.144 = (bf16[49,8,832]{2,1,0:T(8,128)(2,1)}, bf16[448,896]{1,0:T(8,128)(2,1)}, bf16[448,896]{1,0:T(8,128)(2,1)}, f32[3,896]{1,0:T(4,128)}, f32[8,2,896]{2,1,0:T(2,128)}) custom-call(s32[1]{0:T(128)S(6)} %select_n.12.length_ref, f32[448,640]{1,0:T(8,128)} %get-tuple-element.122.q_ref, f32[448,512]{1,0:T(8,128)} %get-tuple-element.127.e_ref, ...), custom_call_target="tpu_custom_call" | custom-call | bytes 15000000 | tf_op jit(solution)/shard_map/pallas_call | solution.py:66
  189.7 3.3 all-to-all-start.5
  193.1 4.9 %all-to-all-done.5.sums_in_ref = f32[8,2,896]{2,1,0:T(2,128)S(1)} async-done(((f32[8,2,896]{2,1,0:T(2,128)}), f32[8,2,896]{2,1,0:T(2,128)S(1)}, u32[]{:S(2)}, u32[]{:S(2)}) %all-to-all-start.5) | async-done | bytes 57376 | tf_op jit(solution)/shard_map/all_to_all | solution.py:1621
  198.6 5.3 %shard_map.145 = (bf16[2,736,512]{2,1,0:T(8,128)(2,1)}, f32[2,896]{1,0:T(2,128)}, bf16[8,384,128]{2,1,0:T(8,128)(2,1)}) custom-call(s32[1]{0:T(128)S(6)} %select_n.12.length_ref, s32[1]{0:T(128)S(6)} %mul.25.first_ref, bf16[448,896]{1,0:T(8,128)(2,1)} %get-tuple-element.133.h_far, f32[3,896]{1,0:T(4,128)} %get-tuple-element.134.outer_ref, ...), custom_call_target="tpu_custom_call" | custom-call | bytes 24000000 | tf_op jit(solution)/shard_map/pallas_call | solution.py:66
  203.9 3.6 all-to-all-start.6
  207.5 6.3 %shard_map.146 = (bf16[448,256]{1,0:T(8,128)(2,1)}, f32[8,2,256]{2,1,0:T(2,128)}) custom-call(s32[1]{0:T(128)S(6)} %select_n.12.length_ref, bf16[2,736,512]{2,1,0:T(8,128)(2,1)} %get-tuple-element.141.d_ref, bf16[448,256]{1,0:T(8,128)(2,1)} %get-tuple-element.140.reduced_ref.reduced_far, f32[2,256]{1,0:T(2,128)} %get-tuple-element.110.refs_5_.gain_ref.reduced_gain_ref, ...), custom_call_target="tpu_custom_call" | custom-call | bytes 24000000 | tf_op jit(solution)/shard_map/pallas_call | solution.py:66
  213.8 6.2 %all-to-all-done.6 = bf16[8,384,128]{2,1,0:T(8,128)(2,1)S(1)} async-done(((bf16[8,384,128]{2,1,0:T(8,128)(2,1)}), bf16[8,384,128]{2,1,0:T(8,128)(2,1)S(1)}, u32[]{:S(2)}, u32[]{:S(2)}) %all-to-all-start.6) | async-done | bytes 786464 | tf_op jit(solution)/shard_map/all_to_all | solution.py:1621
  220.8 8.6 %all_to_all.64.sums_in_ref = f32[8,2,256]{2,1,0:T(2,128)} all-to-all(f32[8,2,256]{2,1,0:T(2,128)} %get-tuple-element.146), channel_id=1, replica_groups=mesh['dp'=8,'branch'=4] {'dp'}, dimensions={0} | all-to-all | bytes 32768 | tf_op jit(solution)/shard_map/all_to_all | solution.py:1621
  229.4 7.8 %shard_map.147 = (bf16[448,896]{1,0:T(8,128)(2,1)}, bf16[8,144,128]{2,1,0:T(8,128)(2,1)}, f32[2,256]{1,0:T(2,128)}, f32[8,2,896]{2,1,0:T(2,128)}) custom-call(s32[1]{0:T(128)S(6)} %select_n.12.length_ref, s32[1]{0:T(128)} %bitcast.place_ref, bf16[448,896]{1,0:T(8,128)(2,1)} %get-tuple-element.133.h_far, f32[3,896]{1,0:T(4,128)} %get-tuple-element.134.outer_ref, ...), custom_call_target="tpu_custom_call" | custom-call | bytes 30000000 | tf_op jit(solution)/shard_map/pallas_call | solution.py:66
  237.2 8.9 %all_to_all.65.sums_in_ref = f32[8,2,896]{2,1,0:T(2,128)} all-to-all(f32[8,2,896]{2,1,0:T(2,128)} %get-tuple-element.152), channel_id=1, replica_groups=mesh['dp'=8,'branch'=4] {'dp'}, dimensions={0} | all-to-all | bytes 114688 | tf_op jit(solution)/shard_map/all_to_all | solution.py:1621
  246.2 16.2 %shard_map.148 = (bf16[1,3872,512]{2,1,0:T(8,128)(2,1)}, f32[2,896]{1,0:T(2,128)}, bf16[8,528,128]{2,1,0:T(8,128)(2,1)}) custom-call(s32[1]{0:T(128)S(6)} %copy.24.length_ref, s32[1]{0:T(128)S(6)} %mul.25.first_ref, bf16[3136,640]{1,0:T(8,128)(2,1)} %get-tuple-element.131.h_far, f32[3,896]{1,0:T(4,128)} %get-tuple-element.132.outer_ref, ...), custom_call_target="tpu_custom_call" | custom-call | bytes 54000000 | tf_op jit(solution)/shard_map/pallas_call | solution.py:66
  262.4 3.6 all-to-all-start.9
  266.2 7.7 %shard_map.149 = (bf16[3136,384]{1,0:T(8,128)(2,1)}, f32[256,384]{1,0:T(8,128)}) custom-call(s32[1]{0:T(128)S(6)} %copy.24.length_ref, f32[3,896]{1,0:T(4,128)} %get-tuple-element.132.outer_ref, f32[2,896]{1,0:T(2,128)} %get-tuple-element.161.total_ref.refs_0_, f32[2,896]{1,0:T(2,128)} %get-tuple-element.102.gain_ref, ...), custom_call_target="tpu_custom_call" | custom-call | bytes 24000000 | tf_op jit(solution)/shard_map/pallas_call | solution.py:66
  273.9 7.7 %all-to-all-done.9 = bf16[8,528,128]{2,1,0:T(8,128)(2,1)S(1)} async-done(((bf16[8,528,128]{2,1,0:T(8,128)(2,1)}), bf16[8,528,128]{2,1,0:T(8,128)(2,1)S(1)}, u32[]{:S(2)}, u32[]{:S(2)}) %all-to-all-start.9) | async-done | bytes 1081376 | tf_op jit(solution)/shard_map/all_to_all | solution.py:1621
  282.5 23.4 %shard_map.150 = (bf16[3136,256]{1,0:T(8,128)(2,1)}, f32[8,2,256]{2,1,0:T(2,128)}, f32[8,8,32,128]{3,2,1,0:T(8,128)}) custom-call(s32[1]{0:T(128)S(6)} %copy.24.length_ref, bf16[1,3872,512]{2,1,0:T(8,128)(2,1)} %get-tuple-element.164.d_ref, bf16[3136,256]{1,0:T(8,128)(2,1)} %get-tuple-element.165.reduced_ref.h_far, ...), custom_call_target="tpu_custom_call" | custom-call | bytes 66000000 | tf_op jit(solution)/shard_map/pallas_call | solution.py:66
  306.0 8.8 %all_to_all.66.sums_in_ref = f32[8,2,256]{2,1,0:T(2,128)} all-to-all(f32[8,2,256]{2,1,0:T(2,128)} %get-tuple-element.171), channel_id=1, replica_groups=mesh['dp'=8,'branch'=4] {'dp'}, dimensions={0} | all-to-all | bytes 32768 | tf_op jit(solution)/shard_map/all_to_all | solution.py:1621
  314.8 3.6 all-to-all-start.10
  318.4 4.8 %shard_map.151 = (f32[2,27,160,320]{3,2,1,0:T(8,128)}, f32[2,27,32,128]{3,2,1,0:T(8,128)}) custom-call(bf16[32,384,128]{2,1,0:T(8,128)(2,1)} %bitcast.32), custom_call_target="tpu_custom_call" | custom-call | bytes 15000000 | tf_op jit(solution)/shard_map/pallas_call | solution.py:66
  323.2 7.7 %shard_map.152 = (bf16[3136,208]{1,0:T(8,128)(2,1)}, f32[2,256]{1,0:T(2,128)}) custom-call(s32[1]{0:T(128)S(6)} %copy.24.length_ref, s32[1]{0:T(128)} %bitcast.place_ref, f32[3,512]{1,0:T(4,128)} %get-tuple-element.109.refs_4_.moment_ref, f32[8,2,256]{2,1,0:T(2,128)} %all_to_all.66.sums_in_ref, ...), custom_call_target="tpu_custom_call" | custom-call | bytes 24000000 | tf_op jit(solution)/shard_map/pallas_call | solution.py:66
  331.0 7.5 %all-to-all-done.10.pieces_ref = f32[8,8,32,128]{3,2,1,0:T(8,128)S(1)} async-done(((f32[8,8,32,128]{3,2,1,0:T(8,128)}), f32[8,8,32,128]{3,2,1,0:T(8,128)S(1)}, u32[]{:S(2)}, u32[]{:S(2)}) %all-to-all-start.10) | async-done | bytes 1048608 | tf_op jit(solution)/shard_map/all_to_all | solution.py:1621
  339.5 1.9 shard_map.153
  341.4 2.9 collective-permute-start.14
  344.3 1.7 collective-permute-start.12
  346.9 3.7 collective-permute-done.13
  354.9 6.8 %shard_map.154 = (f32[2,27,160,320]{3,2,1,0:T(8,128)}, f32[2,27,32,128]{3,2,1,0:T(8,128)}, f32[2,576,832]{2,1,0:T(8,128)}, f32[2,1024]{1,0:T(2,128)}, f32[2,1024]{1,0:T(2,128)}) custom-call(bf16[32,528,128]{2,1,0:T(8,128)(2,1)} %bitcast.30, f32[2,896]{1,0:T(2,128)} %get-tuple-element.161.total_ref.refs_0_, ...), custom_call_target="tpu_custom_call", output_to_operand_aliasing={{0}: (5, {}), {1}: (6, {})} | custom-call | bytes 18000000 | tf_op jit(solution)/shard_map/pallas_call | solution.py:66
  361.9 2.1 collective-permute-done.18.other_ref
  364.9 3.1 shard_map.155
  (83 shorter events, 18.3 us)
Async XLA Ops:
  10.4 41.5 %all-to-all-start = ((bf16[4,208,896]{2,1,0:T(8,128)(2,1)}), bf16[4,208,896]{2,1,0:T(8,128)(2,1)S(1)}, u32[]{:S(2)}, u32[]{:S(2)}) async-start(bf16[4,208,896]{2,1,0:T(8,128)(2,1)} %shard_map.135.x_far.refs_3_), calls=%async_computation | async-start | bytes 2981888 | tf_op jit(solution)/shard_map/all_to_all | solution.py:1656
  16.7 212.7 %all-gather.7.cloned.1.call-start = ((), (), s32[]{:S(2)}) async-start(), calls=%async_computation.12 | async-start | bytes 5242880 | tf_op jit(solution)/shard_map/all_gather | solution.py:1725
  51.9 1.1 copy-start
  58.3 37.4 %collective-permute-start.3 = (bf16[1376,128]{1,0:T(8,128)(2,1)}, bf16[1376,128]{1,0:T(8,128)(2,1)S(1)}, u32[]{:S(2)}, u32[]{:S(2)}) collective-permute-start(bf16[1376,128]{1,0:T(8,128)(2,1)} %get-tuple-element.106.refs_0_), channel_id=1, source_target_pairs={{0,1},{1,2},{2,3},{3,0},{4,5},{5,6},{6,7},{7,4},{8,9},{9,10},{10,1... | collective-permute-start | bytes 1056776 | tf_op jit(solution)/shard_map/ppermute | solution.py:1612
  58.3 37.4 %collective-permute-start.4 = (bf16[1376,128]{1,0:T(8,128)(2,1)}, bf16[1376,128]{1,0:T(8,128)(2,1)S(1)}, u32[]{:S(2)}, u32[]{:S(2)}) collective-permute-start(bf16[1376,128]{1,0:T(8,128)(2,1)} %get-tuple-element.106.refs_0_), channel_id=1, source_target_pairs={{0,2},{1,3},{2,0},{3,1},{4,6},{5,7},{6,4},{7,5},{8,10},{9,11},{10,... | collective-permute-start | bytes 1056776 | tf_op jit(solution)/shard_map/ppermute | solution.py:1612
  60.4 35.4 %collective-permute-start.5 = (bf16[1376,128]{1,0:T(8,128)(2,1)}, bf16[1376,128]{1,0:T(8,128)(2,1)S(1)}, u32[]{:S(2)}, u32[]{:S(2)}) collective-permute-start(bf16[1376,128]{1,0:T(8,128)(2,1)} %get-tuple-element.106.refs_0_), channel_id=1, source_target_pairs={{0,3},{1,0},{2,1},{3,2},{4,7},{5,4},{6,5},{7,6},{8,11},{9,8},{10,9... | collective-permute-start | bytes 1056776 | tf_op jit(solution)/shard_map/ppermute | solution.py:1612
  70.9 21.0 %copy-start.15 = (f32[3,512]{1,0:T(4,128)}, f32[3,512]{1,0:T(4,128)S(1)}, u32[]{:S(2)}) copy-start(f32[3,512]{1,0:T(4,128)S(1)} %reduce_sum.33.refs_0_) | copy-start | bytes 18436
  70.9 14.2 %collective-permute-start = (f32[3,512]{1,0:T(4,128)S(1)}, f32[3,512]{1,0:T(4,128)S(1)}, u32[]{:S(2)}, u32[]{:S(2)}) collective-permute-start(f32[3,512]{1,0:T(4,128)S(1)} %reduce_sum.33.refs_0_), channel_id=1, source_target_pairs={{0,1},{1,2},{2,3},{3,0},{4,5},{5,6},{6,7},{7,4},{8,9},{9,10},{10,1... | collective-permute-start | bytes 18440 | tf_op jit(solution)/shard_map/ppermute | solution.py:1612
  71.6 20.4 %collective-permute-start.1 = (f32[3,512]{1,0:T(4,128)S(1)}, f32[3,512]{1,0:T(4,128)S(1)}, u32[]{:S(2)}, u32[]{:S(2)}) collective-permute-start(f32[3,512]{1,0:T(4,128)S(1)} %reduce_sum.33.refs_0_), channel_id=1, source_target_pairs={{0,2},{1,3},{2,0},{3,1},{4,6},{5,7},{6,4},{7,5},{8,10},{9,11},{10,... | collective-permute-start | bytes 18440 | tf_op jit(solution)/shard_map/ppermute | solution.py:1612
  85.1 6.9 %copy-start.16 = (f32[3,512]{1,0:T(4,128)}, f32[3,512]{1,0:T(4,128)S(1)}, u32[]{:S(2)}) copy-start(f32[3,512]{1,0:T(4,128)S(1)} %collective-permute-done.refs_1_) | copy-start | bytes 18436
  85.1 6.9 %collective-permute-start.2 = (f32[3,512]{1,0:T(4,128)S(1)}, f32[3,512]{1,0:T(4,128)S(1)}, u32[]{:S(2)}, u32[]{:S(2)}) collective-permute-start(f32[3,512]{1,0:T(4,128)S(1)} %reduce_sum.33.refs_0_), channel_id=1, source_target_pairs={{0,3},{1,0},{2,1},{3,2},{4,7},{5,4},{6,5},{7,6},{8,11},{9,8},{10,9... | collective-permute-start | bytes 18440 | tf_op jit(solution)/shard_map/ppermute | solution.py:1612
  92.0 0.6 copy-start.17
  92.0 0.6 copy-start.18
  95.8 5.4 %copy-start.4 = (bf16[1376,128]{1,0:T(8,128)(2,1)}, bf16[1376,128]{1,0:T(8,128)(2,1)S(1)}, u32[]{:S(2)}) copy-start(bf16[1376,128]{1,0:T(8,128)(2,1)S(1)} %collective-permute-done.3.refs_1_) | copy-start | bytes 1056772
  95.8 5.4 %copy-start.5 = (bf16[1376,128]{1,0:T(8,128)(2,1)}, bf16[1376,128]{1,0:T(8,128)(2,1)S(1)}, u32[]{:S(2)}) copy-start(bf16[1376,128]{1,0:T(8,128)(2,1)S(1)} %collective-permute-done.4.refs_2_) | copy-start | bytes 1056772
  95.8 5.4 %copy-start.6 = (bf16[1376,128]{1,0:T(8,128)(2,1)}, bf16[1376,128]{1,0:T(8,128)(2,1)S(1)}, u32[]{:S(2)}) copy-start(bf16[1376,128]{1,0:T(8,128)(2,1)S(1)} %collective-permute-done.5.refs_3_) | copy-start | bytes 1056772
  95.8 30.2 %collective-permute-start.6 = (bf16[912,128]{1,0:T(8,128)(2,1)}, bf16[912,128]{1,0:T(8,128)(2,1)S(1)}, u32[]{:S(2)}, u32[]{:S(2)}) collective-permute-start(bf16[912,128]{1,0:T(8,128)(2,1)} %get-tuple-element.108.refs_0_), channel_id=1, source_target_pairs={{0,1},{1,2},{2,3},{3,0},{4,5},{5,6},{6,7},{7,4},{8,9},{9,10},{10,1... | collective-permute-start | bytes 700424 | tf_op jit(solution)/shard_map/ppermute | solution.py:1612
  96.8 29.3 %collective-permute-start.7 = (bf16[912,128]{1,0:T(8,128)(2,1)}, bf16[912,128]{1,0:T(8,128)(2,1)S(1)}, u32[]{:S(2)}, u32[]{:S(2)}) collective-permute-start(bf16[912,128]{1,0:T(8,128)(2,1)} %get-tuple-element.108.refs_0_), channel_id=1, source_target_pairs={{0,2},{1,3},{2,0},{3,1},{4,6},{5,7},{6,4},{7,5},{8,10},{9,11},{10,... | collective-permute-start | bytes 700424 | tf_op jit(solution)/shard_map/ppermute | solution.py:1612
  98.3 27.8 %collective-permute-start.8 = (bf16[912,128]{1,0:T(8,128)(2,1)}, bf16[912,128]{1,0:T(8,128)(2,1)S(1)}, u32[]{:S(2)}, u32[]{:S(2)}) collective-permute-start(bf16[912,128]{1,0:T(8,128)(2,1)} %get-tuple-element.108.refs_0_), channel_id=1, source_target_pairs={{0,3},{1,0},{2,1},{3,2},{4,7},{5,4},{6,5},{7,6},{8,11},{9,8},{10,9... | collective-permute-start | bytes 700424 | tf_op jit(solution)/shard_map/ppermute | solution.py:1612
  101.1 38.5 %copy-start.11 = (bf16[128,256]{1,0:T(8,128)(2,1)S(1)}, bf16[128,256]{1,0:T(8,128)(2,1)}, u32[]{:S(2)}) copy-start(bf16[128,256]{1,0:T(8,128)(2,1)} %get-tuple-element.116.refs_0_) | copy-start | bytes 196612
  126.1 0.7 copy-start.7
  126.1 0.7 copy-start.8
  126.1 0.8 copy-start.9
  139.7 15.6 %collective-permute-start.9 = (bf16[128,256]{1,0:T(8,128)(2,1)S(1)}, bf16[128,256]{1,0:T(8,128)(2,1)S(1)}, u32[]{:S(2)}, u32[]{:S(2)}) collective-permute-start(bf16[128,256]{1,0:T(8,128)(2,1)S(1)} %copy-done.11), channel_id=1, source_target_pairs={{0,1},{1,2},{2,3},{3,0},{4,5},{5,6},{6,7},{7,4},{8,9},{9,10},{10,1... | collective-permute-start | bytes 196616 | tf_op jit(solution)/shard_map/ppermute | solution.py:1612
  139.8 15.6 %collective-permute-start.10 = (bf16[128,256]{1,0:T(8,128)(2,1)S(1)}, bf16[128,256]{1,0:T(8,128)(2,1)S(1)}, u32[]{:S(2)}, u32[]{:S(2)}) collective-permute-start(bf16[128,256]{1,0:T(8,128)(2,1)S(1)} %copy-done.11), channel_id=1, source_target_pairs={{0,2},{1,3},{2,0},{3,1},{4,6},{5,7},{6,4},{7,5},{8,10},{9,11},{10,... | collective-permute-start | bytes 196616 | tf_op jit(solution)/shard_map/ppermute | solution.py:1612
  140.4 14.9 %collective-permute-start.11 = (bf16[128,256]{1,0:T(8,128)(2,1)S(1)}, bf16[128,256]{1,0:T(8,128)(2,1)S(1)}, u32[]{:S(2)}, u32[]{:S(2)}) collective-permute-start(bf16[128,256]{1,0:T(8,128)(2,1)S(1)} %copy-done.11), channel_id=1, source_target_pairs={{0,3},{1,0},{2,1},{3,2},{4,7},{5,4},{6,5},{7,6},{8,11},{9,8},{10,9... | collective-permute-start | bytes 196616 | tf_op jit(solution)/shard_map/ppermute | solution.py:1612
  155.3 0.6 copy-start.12
  155.3 0.6 copy-start.13
  155.4 0.6 copy-start.14
  189.7 8.3 %all-to-all-start.5 = ((f32[8,2,896]{2,1,0:T(2,128)}), f32[8,2,896]{2,1,0:T(2,128)S(1)}, u32[]{:S(2)}, u32[]{:S(2)}) async-start(f32[8,2,896]{2,1,0:T(2,128)} %get-tuple-element.135), calls=%async_computation.5 | async-start | bytes 114688 | tf_op jit(solution)/shard_map/all_to_all | solution.py:1621
  198.0 0.6 copy-start.10
  203.9 16.1 %all-to-all-start.6 = ((bf16[8,384,128]{2,1,0:T(8,128)(2,1)}), bf16[8,384,128]{2,1,0:T(8,128)(2,1)S(1)}, u32[]{:S(2)}, u32[]{:S(2)}) async-start(bf16[8,384,128]{2,1,0:T(8,128)(2,1)} %get-tuple-element.145), calls=%async_computation.6 | async-start | bytes 1572864 | tf_op jit(solution)/shard_map/all_to_all | solution.py:1621
  207.5 110.9 %all-gather.9.cloned.1.call-start = ((), (), s32[]{:S(2)}) async-start(), calls=%async_computation.13 | async-start | bytes 3244032 | tf_op jit(solution)/shard_map/all_gather | solution.py:1904
  262.4 19.3 %all-to-all-start.9 = ((bf16[8,528,128]{2,1,0:T(8,128)(2,1)}), bf16[8,528,128]{2,1,0:T(8,128)(2,1)S(1)}, u32[]{:S(2)}, u32[]{:S(2)}) async-start(bf16[8,528,128]{2,1,0:T(8,128)(2,1)} %get-tuple-element.160), calls=%async_computation.9 | async-start | bytes 2162688 | tf_op jit(solution)/shard_map/all_to_all | solution.py:1621
  266.0 89.0 %all-gather.11.cloned.1.call-start = ((), (), s32[]{:S(2)}) async-start(), calls=%async_computation.14 | async-start | bytes 4460544 | tf_op jit(solution)/shard_map/all_gather | solution.py:1968
  314.8 23.7 %all-to-all-start.10 = ((f32[8,8,32,128]{3,2,1,0:T(8,128)}), f32[8,8,32,128]{3,2,1,0:T(8,128)S(1)}, u32[]{:S(2)}, u32[]{:S(2)}) async-start(f32[8,8,32,128]{3,2,1,0:T(8,128)} %get-tuple-element.167), calls=%async_computation.10 | async-start | bytes 2097152 | tf_op jit(solution)/shard_map/all_to_all | solution.py:1621
  338.5 1.0 copy-start.1
  341.4 5.5 %collective-permute-start.14 = (bf16[160,128]{1,0:T(8,128)(2,1)}, bf16[160,128]{1,0:T(8,128)(2,1)S(1)}, u32[]{:S(2)}, u32[]{:S(2)}) collective-permute-start(bf16[160,128]{1,0:T(8,128)(2,1)} %shard_map.153), channel_id=1, source_target_pairs={{0,3},{1,0},{2,1},{3,2},{4,7},{5,4},{6,5},{7,6},{8,11},{9,8},{10,9... | collective-permute-start | bytes 122888 | tf_op jit(solution)/shard_map/ppermute | solution.py:1612
  344.3 6.3 %collective-permute-start.13 = (bf16[160,128]{1,0:T(8,128)(2,1)}, bf16[160,128]{1,0:T(8,128)(2,1)S(1)}, u32[]{:S(2)}, u32[]{:S(2)}) collective-permute-start(bf16[160,128]{1,0:T(8,128)(2,1)} %shard_map.153), channel_id=1, source_target_pairs={{0,2},{1,3},{2,0},{3,1},{4,6},{5,7},{6,4},{7,5},{8,10},{9,11},{10,... | collective-permute-start | bytes 122888 | tf_op jit(solution)/shard_map/ppermute | solution.py:1612
  344.3 6.3 %collective-permute-start.12 = (bf16[160,128]{1,0:T(8,128)(2,1)}, bf16[160,128]{1,0:T(8,128)(2,1)S(1)}, u32[]{:S(2)}, u32[]{:S(2)}) collective-permute-start(bf16[160,128]{1,0:T(8,128)(2,1)} %shard_map.153), channel_id=1, source_target_pairs={{0,1},{1,2},{2,3},{3,0},{4,5},{5,6},{6,7},{7,4},{8,9},{9,10},{10,1... | collective-permute-start | bytes 122888 | tf_op jit(solution)/shard_map/ppermute | solution.py:1612
  351.4 10.3 %collective-permute-start.15 = (bf16[640,128]{1,0:T(8,128)(2,1)S(1)}, bf16[640,128]{1,0:T(8,128)(2,1)S(1)}, u32[]{:S(2)}, u32[]{:S(2)}) collective-permute-start(bf16[640,128]{1,0:T(8,128)(2,1)S(1)} %pad_maximum_fusion), channel_id=1, source_target_pairs={{0,8},{4,12},{8,0},{12,4},{16,24},{20,28},{24,16},{28,20},{1,9},{5... | collective-permute-start | bytes 491528 | tf_op jit(solution)/shard_map/ppermute | solution.py:1633
  352.7 9.0 %collective-permute-start.16 = (bf16[640,128]{1,0:T(8,128)(2,1)S(1)}, bf16[640,128]{1,0:T(8,128)(2,1)S(1)}, u32[]{:S(2)}, u32[]{:S(2)}) collective-permute-start(bf16[640,128]{1,0:T(8,128)(2,1)S(1)} %pad_maximum_fusion), channel_id=1, source_target_pairs={{0,16},{4,20},{8,24},{12,28},{16,0},{20,4},{24,8},{28,12},{1,17},{... | collective-permute-start | bytes 491528 | tf_op jit(solution)/shard_map/ppermute | solution.py:1633
  354.0 7.7 %collective-permute-start.17 = (bf16[640,128]{1,0:T(8,128)(2,1)S(1)}, bf16[640,128]{1,0:T(8,128)(2,1)S(1)}, u32[]{:S(2)}, u32[]{:S(2)}) collective-permute-start(bf16[640,128]{1,0:T(8,128)(2,1)S(1)} %pad_maximum_fusion), channel_id=1, source_target_pairs={{0,24},{4,28},{8,16},{12,20},{16,8},{20,12},{24,0},{28,4},{1,25},{... | collective-permute-start | bytes 491528 | tf_op jit(solution)/shard_map/ppermute | solution.py:1633
  361.8 2.2 copy-start.2
  361.8 2.2 collective-permute-start.18
  364.0 0.9 copy-start.3
Sparse Core Ops, SparseCore 0:
  139.8 77.1 all-gather.6
  220.9 57.3 all-gather.8
  282.6 69.0 all-gather.10

commit v2 on v1

--- a/solution.py
+++ b/solution.py
@@ -507,10 +507,12 @@
 
 def first_convolve(grid, slots, block, length_ref, place_ref, *refs):
     parts = slots.parts
-    mids, (moment_ref, gain_ref, shift_ref), refs = (refs[:parts], refs[parts : parts + 3], refs[parts + 3 :])
+    mids, sums, refs = (refs[:parts], refs[parts : 2 * parts], refs[2 * parts :])
+    gain_ref, shift_ref, *refs = refs
     far_kernels, outputs, scratch = (refs[:3], refs[3:8], refs[8:])
     length = length_ref[0]
-    center, inverse = (moment_ref[0:1, DIRECT:], moment_ref[1:2, DIRECT:])
+    total = total_of(sums)[:, DIRECT:]
+    center, inverse = moments(total[0:1], total[1:2], total[2:3])
     gain, shift = (gain_ref[block : block + 1], shift_ref[block : block + 1])
     step = 112
     mask = grid.mask(step, length, REDUCED)
@@ -965,7 +967,7 @@
 def conv_back(grid, slots, block, length_ref, d_ref, reduced_ref, reduced_gain_ref, reduced_shift_ref, *refs):
     far_kernels, refs = (refs[:3], refs[3:])
     first = len(refs) > 9
-    (x_far, rest_product_ref), refs = (refs[:2], refs[2:]) if first else ((None, None), refs)
+    x_far, refs = (refs[0], refs[1:]) if first else (None, refs)
     r_ref, out_sums_ref, *refs = refs
     product_out, refs = (refs[0], refs[1:]) if first else (None, refs)
     kernels, (last_ref, acc_ref, sums_ref, in_sem, *refs) = (refs[:3], refs[3:])
@@ -1055,25 +1057,13 @@
     write_sums(out_sums_ref, sums_ref, 0, REDUCED)
     if first:
         x_copy.wait()
-        ones = grid.mask(slots.rows, length_ref[0])
-        low_ones = ones.astype(BF16)
-        two_ones = jnp.concatenate([ones, ones], axis=1)
-
-        def right_of(start, size):
-            at = slice(start, start + size)
-            scaled = (reduced_ref[at, :].astype(F32) * two_ones).astype(BF16)
-            return jnp.concatenate([r_ref[at, :], scaled, low_ones], axis=1)
-
-        channels = x_ref.shape[1]
-        product_ref[0:channels, :] = channel_products(slots, x_ref, right_of)
-        product_ref[channels:, :] = jnp.zeros((product_ref.shape[0] - channels, FIRST), F32)
-        clips, _, size, _ = product_out.shape
-        for clip in range(clips):
-            at = slice(clip * size, (clip + 1) * size)
-            for tile in range(3):
-                product_out[clip, tile] = rest_product_ref[at, 128 * tile : 128 * (tile + 1)]
-            for tile in range(5):
-                product_out[clip, 3 + tile] = product_ref[at, 128 * tile : 128 * (tile + 1)]
+        write_products(
+            slots,
+            x_ref,
+            lambda start, size: r_ref[start : start + size, :],
+            product_ref,
+            product_out,
+        )
 
 
 def kernel_grads(grid, slots, first_ref, mid_ref, small_ref, d_ref, out_ref, mid_acc_ref, small_acc_ref, turned_ref):
@@ -1190,6 +1180,18 @@
     return total
 
 
+def write_products(slots, x_ref, right_of, product_ref, product_out):
+    channels = x_ref.shape[1]
+    product_ref[0:channels, :] = channel_products(slots, x_ref, right_of)
+    product_ref[channels:, :] = jnp.zeros((product_ref.shape[0] - channels, product_ref.shape[1]), F32)
+    clips, tiles, size, _ = product_out.shape
+    for clip in range(clips):
+        for tile in range(tiles):
+            product_out[clip, tile] = product_ref[
+                clip * size : (clip + 1) * size, 128 * tile : 128 * (tile + 1)
+            ]
+
+
 def rest_constants(outer_ref, total_ref, gain_ref, block):
     pool = OUTER - POOLED
 
@@ -1297,8 +1299,8 @@
         used = used + size - at
 
 
-def rest_back(grid, small, slots, block, length_ref, outer_ref, total_ref, gain_ref, grad_ref, h_far, slope_far, kept_far, x_far, du_far, product_ref, *refs):
-    h_ref, slope_ref, x_ref, du_ref, plane_ref, across_ref, scale_ref, sem_ref, x_sem, du_sem = refs
+def rest_back(grid, small, slots, block, length_ref, outer_ref, total_ref, gain_ref, grad_ref, h_far, slope_far, kept_far, x_far, reduced_far, du_far, product_out, *refs):
+    h_ref, slope_ref, x_ref, reduced_ref, du_ref, plane_ref, across_ref, scale_ref, product_ref, sem_ref, in_sem, du_sem = refs
     rows = grid.line_rows
     pool = OUTER - POOLED
 
@@ -1319,8 +1321,9 @@
         sem_ref,
     )
     lines.first()
-    x_copy = pltpu.make_async_copy(x_far, x_ref, x_sem.at[0])
-    x_copy.start()
+    arriving = copies((x_far, reduced_far), (x_ref, reduced_ref), in_sem)
+    for copy in arriving:
+        copy.start()
     length = length_ref[0]
     matrix = spread_matrix(grid, small)
     a, b, c = rest_constants(outer_ref, total_ref, gain_ref, block)
@@ -1343,7 +1346,8 @@
             spread.put(line, back[:, DIRECT:])
 
     lines.run(visit)
-    x_copy.wait()
+    for copy in arriving:
+        copy.wait()
     wide = lines.size
     pool_mask = grid.mask(wide, length)
 
@@ -1357,11 +1361,15 @@
         du_ref[at, DIRECT:] = (spread.get(step * wide, wide) * pool_mask).astype(BF16)
         leaving(step).start()
 
-    channels = x_ref.shape[1]
-    product_ref[0:channels, :] = channel_products(
-        slots, x_ref, lambda start, size: du_ref[start : start + size, :]
-    )
-    product_ref[channels:, :] = jnp.zeros((product_ref.shape[0] - channels, DIRECT + POOLED), F32)
+    ones = grid.mask(slots.rows, length)
+    two_ones = jnp.concatenate([ones, ones], axis=1)
+
+    def right_of(start, size):
+        at = slice(start, start + size)
+        scaled = (reduced_ref[at, :].astype(F32) * two_ones).astype(BF16)
+        return jnp.concatenate([du_ref[at, :], scaled, ones.astype(BF16)], axis=1)
+
+    write_products(slots, x_ref, right_of, product_ref, product_out)
     pltpu.make_async_copy(du_ref, du_far, du_sem.at[0]).wait()
 
 
@@ -1401,19 +1409,19 @@
     pltpu.make_async_copy(dx_ref, dx_far, dx_sem.at[0]).wait()
 
 
-def combine(block, pieces_ref, moment_ref, sums_in_ref, gain_ref, out_ref):
+def combine(block, rest_ref, pieces_ref, moment_ref, sums_in_ref, gain_ref, out_ref):
     total = total_of(sums_in_ref)
     a, b, c = before_norm(
         gain_ref[block : block + 1], moment_ref[1:2, DIRECT:], total, moment_ref[2:3, DIRECT:]
     )
     size = out_ref.shape[0] // 5
-    products = total_of(pieces_ref)
+    rest, products = (total_of(rest_ref), total_of(pieces_ref))
     for tile in range(2):
-        out_ref[size * tile : size * (tile + 1), :] = products[tile].astype(BF16)
+        out_ref[size * tile : size * (tile + 1), :] = rest[tile].astype(BF16)
         lanes = slice(128 * tile, 128 * (tile + 1))
-        mid = a[:, lanes] * products[3 + tile] - b[:, lanes] * products[7] - c[:, lanes] * products[5 + tile]
+        mid = a[:, lanes] * products[tile] - b[:, lanes] * rest[5] - c[:, lanes] * rest[3 + tile]
         out_ref[size * (2 + tile) : size * (3 + tile), :] = mid.astype(BF16)
-    out_ref[4 * size :, :] = products[2].astype(BF16)
+    out_ref[4 * size :, :] = rest[2].astype(BF16)
 
 
 def write_taps(read, slots, mid_ref, small_ref, mid_out, small_out, sem_ref):
@@ -1621,8 +1629,7 @@
     return lax.all_to_all(values, "dp", 0, 0, tiled=True)
 
 
-def summed(pieces):
-    pieces = exchange(pieces)
+def add_up(pieces):
     return jnp.sum(pieces.astype(F32), axis=0).astype(BF16)
 
 
@@ -1690,6 +1697,26 @@
     )(length, local_count, by_pairs, point_first)
     mids = spread_over(mid, "branch", parts)
     sums = spread_over(jnp.sum(exchange(sums), axis=0), "branch", parts)
+    pools = spread_over(after(pool, (mids, sums)), "branch", parts)
+    h_reduced, taps_mid, taps_few, e, e_sums = call(
+        functools.partial(first_convolve, grid, slots, 0),
+        conv_outputs(grid),
+        conv_scratch(grid),
+        scalars=2,
+        cost=40,
+        far=range(4 + 2 * parts, 7 + 2 * parts),
+        far_out=range(4),
+    )(length, place_one, *mids, *sums, reduced_gain, reduced_shift, *kernels[0][:3])
+    q_pool, second_sums = call(
+        functools.partial(first_pool, grid, slots),
+        (shape((grid.rows, POOLED), F32), shape((clips, 2, FIRST), F32)),
+        [
+            pltpu.VMEM((grid.rows + 2 * grid.line_rows, POOLED), F32),
+            pltpu.VMEM((16, POOLED), F32),
+        ],
+        scalars=2,
+    )(length, place_one, *pools, e_sums)
+    second_sums = exchange(second_sums)
     pooled_direct, kept_direct, moment = call(
         functools.partial(first_direct, grid, small, slots, 0),
         (
@@ -1700,28 +1727,8 @@
         scalars=1,
         cost=3,
     )(length, direct, outer_gain, outer_shift, *sums)
-    pool, pooled_direct = after((pool, pooled_direct), mids)
-    pools = spread_over(pool, "branch", parts)
-    h_reduced, taps_mid, taps_few, e, e_sums = call(
-        functools.partial(first_convolve, grid, slots, 0),
-        conv_outputs(grid),
-        conv_scratch(grid),
-        scalars=2,
-        cost=40,
-        far=range(5 + parts, 8 + parts),
-        far_out=range(4),
-    )(length, place_one, *mids, moment, reduced_gain, reduced_shift, *kernels[0][:3])
-    pooled_directs = spread_over(after(pooled_direct, (pools, e_sums)), "branch", parts)
-    q_pool, second_sums = call(
-        functools.partial(first_pool, grid, slots),
-        (shape((grid.rows, POOLED), F32), shape((clips, 2, FIRST), F32)),
-        [
-            pltpu.VMEM((grid.rows + 2 * grid.line_rows, POOLED), F32),
-            pltpu.VMEM((16, POOLED), F32),
-        ],
-        scalars=2,
-    )(length, place_one, *pools, e_sums)
-    second_sums = exchange(second_sums)
+    second_sums, pooled_direct = lax.optimization_barrier((second_sums, pooled_direct))
+    pooled_directs = spread_over(pooled_direct, "branch", parts)
     kept_direct = lax.all_gather(after(kept_direct, second_sums), "branch", axis=0)
     pair = 2 * grid.line_rows
     pooled, h_outer, slope, outer, pooled_slope, pooled_product = call(
@@ -1848,7 +1855,7 @@
         *kernels[1][:2],
         kernels[1][3],
     )
-    share_small = summed(packed_small)
+    share_small = add_up(exchange(packed_small))
     sums_low, share_small = lax.optimization_barrier((sums_low, share_small))
     gathered = exchange(sums_low)
     kept = OUTER // parts
@@ -1920,35 +1927,41 @@
     product_rows = round_up(own_channels, 16 * clips)
     du_rest, rest_product = call(
         functools.partial(rest_back, grid, small, slots, 0),
-        (shape((grid.rows, DIRECT + POOLED), BF16), shape((product_rows, DIRECT + POOLED), F32)),
+        (
+            shape((grid.rows, DIRECT + POOLED), BF16),
+            shape((clips, 6, product_rows // clips, 128), F32),
+        ),
         [
             pltpu.VMEM((grid.rows, DIRECT + POOLED), BF16),
             pltpu.VMEM((grid.rows, DIRECT + POOLED), BF16),
             pltpu.VMEM(turned.shape, BF16),
+            pltpu.VMEM((grid.rows, REDUCED), BF16),
             pltpu.VMEM((grid.rows, DIRECT + POOLED), BF16),
             *Spread.scratch(grid),
+            pltpu.VMEM((product_rows, 768), F32),
             Lines.semaphores(grid, 4),
-            pltpu.SemaphoreType.DMA((1,)),
+            pltpu.SemaphoreType.DMA((2,)),
             pltpu.SemaphoreType.DMA((1,)),
         ],
         scalars=1,
         cost=8,
-        far=(5, 6, 7, 8),
+        far=(5, 6, 7, 8, 9),
         far_out=(0,),
-    )(length, outer, after(total, packed), outer_gain, dx_small, h_outer, slope, kept_direct, turned)
-    share = summed(packed)
+    )(length, outer, after(total, packed), outer_gain, dx_small, h_outer, slope, kept_direct, turned, h_reduced)
+    share = add_up(exchange(packed))
+    rest_pieces = exchange(rest_product)
     d_low, share = lax.optimization_barrier((after(d_low, rest_product), share))
     r_low, sums_low, products = call(
         functools.partial(conv_back, grid, slots, 0),
         (
             shape((grid.rows, REDUCED), BF16),
             shape((clips, 2, REDUCED), F32),
-            shape((clips, 8, product_rows // clips, 128), F32),
+            shape((clips, 2, product_rows // clips, 128), F32),
         ),
         [
             *conv_back_scratch(grid),
             pltpu.VMEM(turned.shape, BF16),
-            pltpu.VMEM((product_rows, FIRST), F32),
+            pltpu.VMEM((product_rows, REDUCED), F32),
             pltpu.SemaphoreType.DMA((1,)),
         ],
         scalars=1,
@@ -1963,9 +1976,9 @@
         *kernels[0][:2],
         kernels[0][3],
         turned,
-        rest_product,
     )
     whole = lax.all_gather(share, ("branch", "dp"), axis=0)
+    sums_low, rest_pieces = lax.optimization_barrier((sums_low, rest_pieces))
     gathered = exchange(sums_low)
     pieces = exchange(products)
     dx, reduced_total = call(
@@ -1986,6 +1999,14 @@
         far=(5, 6, 7, 8),
         far_out=(0,),
     )(length, place_one, moment, gathered, reduced_gain, du_rest, h_reduced, r_low, point_first)
+    pieces, dx = lax.optimization_barrier((pieces, dx))
+    point_sum = call(
+        functools.partial(combine, 0),
+        shape((5 * product_rows // clips, 128), BF16),
+        cost=1,
+    )(rest_pieces, pieces, moment, gathered, reduced_gain)
+    received = spread_over(point_sum, "branch", parts)
+
     outs = (
         shape((2, TAPS, MID_IN, MID_OUT), F32),
         shape((2, TAPS, SMALL_IN, SMALL_OUT), F32),
@@ -2003,14 +2024,7 @@
         far_out=(0, 1),
         cost=5,
     )(whole_small)
-    pieces, mid_grad, small_grad, dx = lax.optimization_barrier((pieces, mid_grad, small_grad, dx))
-    point_sum = call(
-        functools.partial(combine, 0),
-        shape((5 * product_rows // clips, 128), BF16),
-        cost=1,
-    )(pieces, moment, gathered, reduced_gain)
-    received = spread_over(point_sum, "branch", parts)
-
+    received, mid_grad, small_grad = lax.optimization_barrier((received, mid_grad, small_grad))
     norms = shape((2, 1024), F32)
     mid_grad, small_grad, point_grad, gain_grad, shift_grad = call(
         functools.partial(unpack_first, parts, clips, taps_each, tap_share),

time: 376 us -> 367 us (0.976)
  blocking collectives: 61.8 us -> 53 us
  starting transfers between devices: 44.1 us -> 52.3 us
  waiting for transfers between devices: 76.3 us -> 69.3 us
    all_to_all x7 -> x6, blocking collectives: 61.8 us -> 53 us  [exchange(): return lax.all_to_all(values, 'dp', 0, 0, tiled=True)]
    all_to_all x4 -> x6, starting transfers between devices: 14 us -> 21.2 us  [exchange(): return lax.all_to_all(values, 'dp', 0, 0, tiled=True)]
    all_to_all x4 -> x6, waiting for transfers between devices: 26.3 us -> 20 us  [exchange(): return lax.all_to_all(values, 'dp', 0, 0, tiled=True)]
    ppermute x15, waiting for transfers between devices: 23.4 us -> 18.9 us  [spread_over(): received.append(lax.ppermute(values, axis, perm))]
    all_gather x1, waiting for transfers between devices: 0.01 us -> 4.12 us  [on_device(): whole = lax.all_gather(share, ('branch', 'dp'), axis=0)]
  transfers between devices with their start and end apart: 27 -> 29, of which waited for: 10 -> 9; matrix products, arithmetic and copies ran while one was open for 1% -> 0% of each run, Pallas kernels for 41% -> 42%
where the time goes in v2:
time: 367 us; the launch traced here: 365 us
  Pallas kernels  169 us (46%)
  waiting for transfers between devices  69.3 us (19%)
  blocking collectives  53 us (14%)
  starting transfers between devices  52.3 us (14%)
  between operations  14.9 us (4%)
  local copies, waits for them, and re-layouts  4.87 us (1%)
    pallas_call x21, Pallas kernels, run(): pl.pallas_call(body, out_shape=jax.tree.map(placed, out_shape), in_specs=...  169 us
    all_to_all x6, blocking collectives, exchange(): return lax.all_to_all(values, 'dp', 0, 0, tiled=True)  53 us
    all_to_all x1, waiting for transfers between devices, on_device(): by_pairs = lax.all_to_all(turned, 'branch', 0, 0, tiled=True)  24.4 us
    all_to_all x6, starting transfers between devices, exchange(): return lax.all_to_all(values, 'dp', 0, 0, tiled=True)  21.2 us
    ppermute x15, starting transfers between devices, spread_over(): received.append(lax.ppermute(values, axis, perm))  20.5 us
    all_to_all x6, waiting for transfers between devices, exchange(): return lax.all_to_all(values, 'dp', 0, 0, tiled=True)  20 us
    ppermute x15, waiting for transfers between devices, spread_over(): received.append(lax.ppermute(values, axis, perm))  18.9 us
  transfers between devices with their start and end apart: 29, of which 9 were waited for; matrix products, arithmetic and copies ran while one was open for 0% of the time, Pallas kernels for 42%

profile of v2, /device:TPU:0, one launch (start us, length us, event | category | flops | bytes accessed | tf_op | source)
XLA Modules:
  0.0 364.6 jit_solution(15863966031935413392)
XLA Ops:
  7.2 3.2 shard_map.135.x_far.refs_3_
  10.4 6.3 %all-to-all-start = ((bf16[4,208,896]{2,1,0:T(8,128)(2,1)}), bf16[4,208,896]{2,1,0:T(8,128)(2,1)S(1)}, u32[]{:S(2)}, u32[]{:S(2)}) async-start(bf16[4,208,896]{2,1,0:T(8,128)(2,1)} %shard_map.135.x_far.refs_3_), calls=%async_computation | async-start | bytes 2981888 | tf_op jit(solution)/shard_map/all_to_all | solution.py:1663
  17.4 10.1 %shard_map.136 = (bf16[9,512,256]{2,1,0:T(8,128)(2,1)}, bf16[3,512,256]{2,1,0:T(8,128)(2,1)}, bf16[1152,128]{1,0:T(8,128)(2,1)}, bf16[1152,128]{1,0:T(8,128)(2,1...) custom-call(bf16[2,27,160,320]{3,2,1,0:T(8,128)(2,1)} %mid_in.1, ...), custom_call_target="tpu_custom_call" | custom-call | bytes 15000000 | tf_op jit(solution)/shard_map/pallas_call | solution.py:66
  27.5 24.4 %all-to-all-done.x_ref = bf16[4,208,896]{2,1,0:T(8,128)(2,1)S(1)} async-done(((bf16[4,208,896]{2,1,0:T(8,128)(2,1)}), bf16[4,208,896]{2,1,0:T(8,128)(2,1)S(1)}, u32[]{:S(2)}, u32[]{:S(2)}) %all-to-all-start) | async-done | bytes 1490976 | tf_op jit(solution)/shard_map/all_to_all | solution.py:1663
  53.1 5.3 %shard_map.137 = (bf16[1376,128]{1,0:T(8,128)(2,1)}, bf16[912,128]{1,0:T(8,128)(2,1)}, f32[896,256]{1,0:T(8,128)}, f32[8,3,512]{2,1,0:T(4,128)}) custom-call(s32[1]{0:T(128)S(6)} %copy.27.length_ref, f32[1]{0:T(128)S(6)} %convert_element_type.5.count_ref, bf16[4,208,896]{2,1,0:T(8,128)(2,1)} %copy-done, bf16[4,640,208]{2,1,0:T(8,128)(2,1)} %get-tuple-element.105.p_ref.p_far), custom_call_target="tpu_custom_call" | custom-call | bytes 15000000 | tf_op jit(solution)/shard_map/pallas_call | solution.py:66
  58.4 2.0 collective-permute-start.1
  60.4 1.8 collective-permute-start.2
  62.2 8.7 %all_to_all.65 = f32[8,3,512]{2,1,0:T(4,128)S(1)} all-to-all(f32[8,3,512]{2,1,0:T(4,128)} %get-tuple-element.108), channel_id=1, replica_groups=mesh['dp'=8,'branch'=4] {'dp'}, dimensions={0} | all-to-all | bytes 98304 | tf_op jit(solution)/shard_map/all_to_all | solution.py:1629
  73.1 12.0 %collective-permute-done.3.refs_5_.refs_1_ = f32[3,512]{1,0:T(4,128)S(1)} collective-permute-done((f32[3,512]{1,0:T(4,128)S(1)}, f32[3,512]{1,0:T(4,128)S(1)}, u32[]{:S(2)}, u32[]{:S(2)}) %collective-permute-start.3) | collective-permute-done | bytes 6176 | tf_op jit(solution)/shard_map/ppermute | solution.py:1620
  85.1 6.9 %collective-permute-done.4.refs_6_.refs_2_ = f32[3,512]{1,0:T(4,128)S(1)} collective-permute-done((f32[3,512]{1,0:T(4,128)S(1)}, f32[3,512]{1,0:T(4,128)S(1)}, u32[]{:S(2)}, u32[]{:S(2)}) %collective-permute-start.4) | collective-permute-done | bytes 6176 | tf_op jit(solution)/shard_map/ppermute | solution.py:1620
  94.5 2.8 collective-permute-start.8
  97.4 25.0 %shard_map.138 = (bf16[3136,256]{1,0:T(8,128)(2,1)}, bf16[1,3872,512]{2,1,0:T(8,128)(2,1)}, bf16[1,3872,128]{2,1,0:T(8,128)(2,1)}, f32[3136,512]{1,0:T(8,128)}, f32[2,512]{1,0:T(2,128)}) custom-call(s32[1]{0:T(128)S(6)} %copy.27.length_ref, s32[1]{0:T(128)} %bitcast.place_ref, bf16[1376,128]{1,0:T(8,128)(2,1)} %get-tuple-element.107.refs_0_, ...), custom_call_target="tpu_custom_call" | custom-call | bytes 120000000 | tf_op jit(solution)/shard_map/pallas_call | solution.py:66
  123.2 3.9 %shard_map.139 = (f32[3136,128]{1,0:T(8,128)}, f32[8,2,640]{2,1,0:T(2,128)}) custom-call(s32[1]{0:T(128)S(6)} %copy.27.length_ref, s32[1]{0:T(128)} %bitcast.place_ref, bf16[912,128]{1,0:T(8,128)(2,1)} %get-tuple-element.109.refs_0_, bf16[912,128]{1,0:T(8,128)(2,1)} %copy-done.8, bf16[912,128]{1,0:T(8,128)(2,1)} %copy-done.9, bf16[912,128]{1,0:T(8,128)(2,1)} %copy-done.10, ...), custom_call_target="tpu_custom_call" | custom-call | bytes 15000000 | tf_op jit(solution)/shard_map/pallas_call | solution.py:66
  127.2 3.7 %all-to-all-start.2 = ((f32[8,2,640]{2,1,0:T(2,128)}), f32[8,2,640]{2,1,0:T(2,128)S(1)}, u32[]{:S(2)}, u32[]{:S(2)}) async-start(f32[8,2,640]{2,1,0:T(2,128)} %get-tuple-element.116), calls=%async_computation.2 | async-start | bytes 81920 | tf_op jit(solution)/shard_map/all_to_all | solution.py:1629
  130.9 3.2 shard_map.140
  136.5 3.1 collective-permute-start.11
  139.7 11.9 %shard_map.141 = (bf16[448,640]{1,0:T(8,128)(2,1)}, bf16[3136,640]{1,0:T(8,128)(2,1)}, bf16[3136,640]{1,0:T(8,128)(2,1)}, f32[3,896]{1,0:T(4,128)}, bf16[448,640]{1,0:T(8,128)(2,1)}, /*index=5*/bf16[448,640]{1,0:T(8,128)(2,1)}) custom-call(s32[1]{0:T(128)S(6)} %copy.27.length_ref, f32[3136,128]{1,0:T(8,128)} %get-tuple-element.122.q_far, ...), custom_call_target="tpu_custom_call" | custom-call | bytes 15000000 | tf_op jit(solution)/shard_map/pallas_call | solution.py:66
  152.3 4.4 %shard_map.142 = (f32[448,640]{1,0:T(8,128)}, f32[8,3,640]{2,1,0:T(4,128)}, bf16[448,896]{1,0:T(8,128)(2,1)}) custom-call(s32[1]{0:T(128)S(6)} %select_n.12.length_ref, s32[1]{0:T(128)} %bitcast.place_ref, f32[1]{0:T(128)S(6)} %mul.20.count_ref, bf16[128,256]{1,0:T(8,128)(2,1)} %get-tuple-element.121.refs_0_, bf16[128,256]{1,0:T(8,128)(2,1)} %copy-done.15, ...), custom_call_target="tpu_custom_call" | custom-call | bytes 15000000 | tf_op jit(solution)/shard_map/pallas_call | solution.py:66
  156.6 9.1 %all_to_all.66.sums_in_ref = f32[8,3,640]{2,1,0:T(4,128)} all-to-all(f32[8,3,640]{2,1,0:T(4,128)} %get-tuple-element.129), channel_id=1, replica_groups=mesh['dp'=8,'branch'=4] {'dp'}, dimensions={0} | all-to-all | bytes 122880 | tf_op jit(solution)/shard_map/all_to_all | solution.py:1629
  165.7 6.7 %shard_map.143 = (bf16[448,256]{1,0:T(8,128)(2,1)}, bf16[2,736,512]{2,1,0:T(8,128)(2,1)}, bf16[2,736,128]{2,1,0:T(8,128)(2,1)}, f32[448,512]{1,0:T(8,128)}, f32[8,2,512]{2,1,0:T(2,128)}, /*index=5*/f32[3,640]{1,0:T(4,128)}) custom-call(s32[1]{0:T(128)S(6)} %select_n.12.length_ref, f32[448,640]{1,0:T(8,128)} %get-tuple-element.128.q_ref, ...), custom_call_target="tpu_custom_call" | custom-call | bytes 15000000 | tf_op jit(solution)/shard_map/pallas_call | solution.py:66
  172.4 8.8 %all_to_all.67.sums_in_ref = f32[8,2,512]{2,1,0:T(2,128)} all-to-all(f32[8,2,512]{2,1,0:T(2,128)} %get-tuple-element.135), channel_id=1, replica_groups=mesh['dp'=8,'branch'=4] {'dp'}, dimensions={0} | all-to-all | bytes 65536 | tf_op jit(solution)/shard_map/all_to_all | solution.py:1629
  181.2 4.8 %shard_map.144 = (bf16[49,8,832]{2,1,0:T(8,128)(2,1)}, bf16[448,896]{1,0:T(8,128)(2,1)}, bf16[448,896]{1,0:T(8,128)(2,1)}, f32[3,896]{1,0:T(4,128)}, f32[8,2,896]{2,1,0:T(2,128)}) custom-call(s32[1]{0:T(128)S(6)} %select_n.12.length_ref, f32[448,640]{1,0:T(8,128)} %get-tuple-element.128.q_ref, f32[448,512]{1,0:T(8,128)} %get-tuple-element.133.e_ref, ...), custom_call_target="tpu_custom_call" | custom-call | bytes 15000000 | tf_op jit(solution)/shard_map/pallas_call | solution.py:66
  186.0 3.3 all-to-all-start.5
  189.4 4.9 %all-to-all-done.5.sums_in_ref = f32[8,2,896]{2,1,0:T(2,128)S(1)} async-done(((f32[8,2,896]{2,1,0:T(2,128)}), f32[8,2,896]{2,1,0:T(2,128)S(1)}, u32[]{:S(2)}, u32[]{:S(2)}) %all-to-all-start.5) | async-done | bytes 57376 | tf_op jit(solution)/shard_map/all_to_all | solution.py:1629
  194.9 5.4 %shard_map.145 = (bf16[2,736,512]{2,1,0:T(8,128)(2,1)}, f32[2,896]{1,0:T(2,128)}, bf16[8,384,128]{2,1,0:T(8,128)(2,1)}) custom-call(s32[1]{0:T(128)S(6)} %select_n.12.length_ref, s32[1]{0:T(128)S(6)} %mul.25.first_ref, bf16[448,896]{1,0:T(8,128)(2,1)} %get-tuple-element.139.h_far, f32[3,896]{1,0:T(4,128)} %get-tuple-element.140.outer_ref, ...), custom_call_target="tpu_custom_call" | custom-call | bytes 24000000 | tf_op jit(solution)/shard_map/pallas_call | solution.py:66
  200.3 3.6 all-to-all-start.6
  203.9 6.3 %shard_map.146 = (bf16[448,256]{1,0:T(8,128)(2,1)}, f32[8,2,256]{2,1,0:T(2,128)}) custom-call(s32[1]{0:T(128)S(6)} %select_n.12.length_ref, bf16[2,736,512]{2,1,0:T(8,128)(2,1)} %get-tuple-element.147.d_ref, bf16[448,256]{1,0:T(8,128)(2,1)} %get-tuple-element.146.reduced_ref.reduced_far, f32[2,256]{1,0:T(2,128)} %get-tuple-element.110.refs_8_.gain_ref.reduced_gain_ref, ...), custom_call_target="tpu_custom_call" | custom-call | bytes 24000000 | tf_op jit(solution)/shard_map/pallas_call | solution.py:66
  210.1 6.2 %all-to-all-done.6 = bf16[8,384,128]{2,1,0:T(8,128)(2,1)S(1)} async-done(((bf16[8,384,128]{2,1,0:T(8,128)(2,1)}), bf16[8,384,128]{2,1,0:T(8,128)(2,1)S(1)}, u32[]{:S(2)}, u32[]{:S(2)}) %all-to-all-start.6) | async-done | bytes 786464 | tf_op jit(solution)/shard_map/all_to_all | solution.py:1629
  217.1 8.4 %all_to_all.68.sums_in_ref = f32[8,2,256]{2,1,0:T(2,128)} all-to-all(f32[8,2,256]{2,1,0:T(2,128)} %get-tuple-element.152), channel_id=1, replica_groups=mesh['dp'=8,'branch'=4] {'dp'}, dimensions={0} | all-to-all | bytes 32768 | tf_op jit(solution)/shard_map/all_to_all | solution.py:1629
  225.6 7.8 %shard_map.147 = (bf16[448,896]{1,0:T(8,128)(2,1)}, bf16[8,144,128]{2,1,0:T(8,128)(2,1)}, f32[2,256]{1,0:T(2,128)}, f32[8,2,896]{2,1,0:T(2,128)}) custom-call(s32[1]{0:T(128)S(6)} %select_n.12.length_ref, s32[1]{0:T(128)} %bitcast.place_ref, bf16[448,896]{1,0:T(8,128)(2,1)} %get-tuple-element.139.h_far, f32[3,896]{1,0:T(4,128)} %get-tuple-element.140.outer_ref, ...), custom_call_target="tpu_custom_call" | custom-call | bytes 30000000 | tf_op jit(solution)/shard_map/pallas_call | solution.py:66
  233.4 8.9 %all_to_all.69.sums_in_ref = f32[8,2,896]{2,1,0:T(2,128)} all-to-all(f32[8,2,896]{2,1,0:T(2,128)} %get-tuple-element.158), channel_id=1, replica_groups=mesh['dp'=8,'branch'=4] {'dp'}, dimensions={0} | all-to-all | bytes 114688 | tf_op jit(solution)/shard_map/all_to_all | solution.py:1629
  242.4 16.2 %shard_map.148 = (bf16[1,3872,512]{2,1,0:T(8,128)(2,1)}, f32[2,896]{1,0:T(2,128)}, bf16[8,528,128]{2,1,0:T(8,128)(2,1)}) custom-call(s32[1]{0:T(128)S(6)} %copy.27.length_ref, s32[1]{0:T(128)S(6)} %mul.25.first_ref, bf16[3136,640]{1,0:T(8,128)(2,1)} %get-tuple-element.137.h_far, f32[3,896]{1,0:T(4,128)} %get-tuple-element.138.outer_ref, ...), custom_call_target="tpu_custom_call" | custom-call | bytes 54000000 | tf_op jit(solution)/shard_map/pallas_call | solution.py:66
  258.6 3.6 all-to-all-start.9
  262.4 8.2 %shard_map.149 = (bf16[3136,384]{1,0:T(8,128)(2,1)}, f32[8,6,32,128]{3,2,1,0:T(8,128)}) custom-call(s32[1]{0:T(128)S(6)} %copy.27.length_ref, f32[3,896]{1,0:T(4,128)} %get-tuple-element.138.outer_ref, f32[2,896]{1,0:T(2,128)} %get-tuple-element.167.total_ref.refs_0_, f32[2,896]{1,0:T(2,128)} %get-tuple-element.118.gain_ref, ...), custom_call_target="tpu_custom_call" | custom-call | bytes 24000000 | tf_op jit(solution)/shard_map/pallas_call | solution.py:66
  270.6 7.3 %all-to-all-done.9 = bf16[8,528,128]{2,1,0:T(8,128)(2,1)S(1)} async-done(((bf16[8,528,128]{2,1,0:T(8,128)(2,1)}), bf16[8,528,128]{2,1,0:T(8,128)(2,1)S(1)}, u32[]{:S(2)}, u32[]{:S(2)}) %all-to-all-start.9) | async-done | bytes 1081376 | tf_op jit(solution)/shard_map/all_to_all | solution.py:1629
  278.7 3.6 all-to-all-start.11
  282.3 22.3 %shard_map.150 = (bf16[3136,256]{1,0:T(8,128)(2,1)}, f32[8,2,256]{2,1,0:T(2,128)}, f32[8,2,32,128]{3,2,1,0:T(8,128)}) custom-call(s32[1]{0:T(128)S(6)} %copy.27.length_ref, bf16[1,3872,512]{2,1,0:T(8,128)(2,1)} %get-tuple-element.171.d_ref, bf16[3136,256]{1,0:T(8,128)(2,1)} %get-tuple-element.168.reduced_far.reduced_ref.h_far, ...), custom_call_target="tpu_custom_call" | custom-call | bytes 66000000 | tf_op jit(solution)/shard_map/pallas_call | solution.py:66
  304.6 9.0 %all_to_all.70.sums_in_ref = f32[8,2,256]{2,1,0:T(2,128)} all-to-all(f32[8,2,256]{2,1,0:T(2,128)} %get-tuple-element.175), channel_id=1, replica_groups=mesh['dp'=8,'branch'=4] {'dp'}, dimensions={0} | all-to-all | bytes 32768 | tf_op jit(solution)/shard_map/all_to_all | solution.py:1629
  313.6 3.4 all-to-all-start.10
  317.0 7.4 %shard_map.151 = (bf16[3136,208]{1,0:T(8,128)(2,1)}, f32[2,256]{1,0:T(2,128)}) custom-call(s32[1]{0:T(128)S(6)} %copy.27.length_ref, s32[1]{0:T(128)} %bitcast.place_ref, f32[3,512]{1,0:T(4,128)} %get-tuple-element.124.moment_ref, f32[8,2,256]{2,1,0:T(2,128)} %all_to_all.70.sums_in_ref, f32[2,256]{1,0:T(2,128)} %get-tuple-element.110.refs_8_.gain_ref.reduced_gain_ref, ...), custom_call_target="tpu_custom_call" | custom-call | bytes 24000000 | tf_op jit(solution)/shard_map/pallas_call | solution.py:66
  325.1 1.9 shard_map.152
  328.4 2.4 collective-permute-start.13
  332.4 4.9 %shard_map.153 = (f32[2,27,160,320]{3,2,1,0:T(8,128)}, f32[2,27,32,128]{3,2,1,0:T(8,128)}) custom-call(bf16[32,384,128]{2,1,0:T(8,128)(2,1)} %bitcast.32), custom_call_target="tpu_custom_call" | custom-call | bytes 15000000 | tf_op jit(solution)/shard_map/pallas_call | solution.py:66
  337.4 2.0 collective-permute-start.15
  340.9 4.1 %all-gather.11.cloned.1.call-done = bf16[16896,128]{1,0:T(8,128)(2,1)} async-done(((bf16[528,128]{1,0:T(8,128)(2,1)}), bf16[16896,128]{1,0:T(8,128)(2,1)}) %all-gather.11.cloned.1.call-update) | async-done | bytes 4325392 | tf_op jit(solution)/shard_map/all_gather | solution.py:1980
  345.1 6.8 %shard_map.154 = (f32[2,27,160,320]{3,2,1,0:T(8,128)}, f32[2,27,32,128]{3,2,1,0:T(8,128)}, f32[2,576,832]{2,1,0:T(8,128)}, f32[2,1024]{1,0:T(2,128)}, f32[2,1024]{1,0:T(2,128)}) custom-call(bf16[32,528,128]{2,1,0:T(8,128)(2,1)} %bitcast.30, f32[2,896]{1,0:T(2,128)} %get-tuple-element.167.total_ref.refs_0_, ...), custom_call_target="tpu_custom_call", output_to_operand_aliasing={{0}: (5, {}), {1}: (6, {})} | custom-call | bytes 18000000 | tf_op jit(solution)/shard_map/pallas_call | solution.py:66
  352.3 1.8 collective-permute-done.18.other_ref
  355.0 3.1 shard_map.155
  (93 shorter events, 18.7 us)
Async XLA Ops:
  10.4 41.5 %all-to-all-start = ((bf16[4,208,896]{2,1,0:T(8,128)(2,1)}), bf16[4,208,896]{2,1,0:T(8,128)(2,1)S(1)}, u32[]{:S(2)}, u32[]{:S(2)}) async-start(bf16[4,208,896]{2,1,0:T(8,128)(2,1)} %shard_map.135.x_far.refs_3_), calls=%async_computation | async-start | bytes 2981888 | tf_op jit(solution)/shard_map/all_to_all | solution.py:1663
  51.9 1.1 copy-start
  58.4 33.6 %collective-permute-start = (bf16[1376,128]{1,0:T(8,128)(2,1)}, bf16[1376,128]{1,0:T(8,128)(2,1)S(1)}, u32[]{:S(2)}, u32[]{:S(2)}) collective-permute-start(bf16[1376,128]{1,0:T(8,128)(2,1)} %get-tuple-element.107.refs_0_), channel_id=1, source_target_pairs={{0,1},{1,2},{2,3},{3,0},{4,5},{5,6},{6,7},{7,4},{8,9},{9,10},{10,1... | collective-permute-start | bytes 1056776 | tf_op jit(solution)/shard_map/ppermute | solution.py:1620
  58.4 33.6 %collective-permute-start.1 = (bf16[1376,128]{1,0:T(8,128)(2,1)}, bf16[1376,128]{1,0:T(8,128)(2,1)S(1)}, u32[]{:S(2)}, u32[]{:S(2)}) collective-permute-start(bf16[1376,128]{1,0:T(8,128)(2,1)} %get-tuple-element.107.refs_0_), channel_id=1, source_target_pairs={{0,2},{1,3},{2,0},{3,1},{4,6},{5,7},{6,4},{7,5},{8,10},{9,11},{10,... | collective-permute-start | bytes 1056776 | tf_op jit(solution)/shard_map/ppermute | solution.py:1620
  60.4 31.6 %collective-permute-start.2 = (bf16[1376,128]{1,0:T(8,128)(2,1)}, bf16[1376,128]{1,0:T(8,128)(2,1)S(1)}, u32[]{:S(2)}, u32[]{:S(2)}) collective-permute-start(bf16[1376,128]{1,0:T(8,128)(2,1)} %get-tuple-element.107.refs_0_), channel_id=1, source_target_pairs={{0,3},{1,0},{2,1},{3,2},{4,7},{5,4},{6,5},{7,6},{8,11},{9,8},{10,9... | collective-permute-start | bytes 1056776 | tf_op jit(solution)/shard_map/ppermute | solution.py:1620
  70.9 26.4 %copy-start.14 = (f32[3,512]{1,0:T(4,128)}, f32[3,512]{1,0:T(4,128)S(1)}, u32[]{:S(2)}) copy-start(f32[3,512]{1,0:T(4,128)S(1)} %reduce_sum.33.refs_4_.refs_0_) | copy-start | bytes 18436
  71.0 14.2 %collective-permute-start.3 = (f32[3,512]{1,0:T(4,128)S(1)}, f32[3,512]{1,0:T(4,128)S(1)}, u32[]{:S(2)}, u32[]{:S(2)}) collective-permute-start(f32[3,512]{1,0:T(4,128)S(1)} %reduce_sum.33.refs_4_.refs_0_), channel_id=1, source_target_pairs={{0,1},{1,2},{2,3},{3,0},{4,5},{5,6},{6,7},{7,4},{8,9},{9,10},{10,1... | collective-permute-start | bytes 18440 | tf_op jit(solution)/shard_map/ppermute | solution.py:1620
  71.6 20.4 %collective-permute-start.4 = (f32[3,512]{1,0:T(4,128)S(1)}, f32[3,512]{1,0:T(4,128)S(1)}, u32[]{:S(2)}, u32[]{:S(2)}) collective-permute-start(f32[3,512]{1,0:T(4,128)S(1)} %reduce_sum.33.refs_4_.refs_0_), channel_id=1, source_target_pairs={{0,2},{1,3},{2,0},{3,1},{4,6},{5,7},{6,4},{7,5},{8,10},{9,11},{10,... | collective-permute-start | bytes 18440 | tf_op jit(solution)/shard_map/ppermute | solution.py:1620
  85.1 12.2 %copy-start.18 = (f32[3,512]{1,0:T(4,128)}, f32[3,512]{1,0:T(4,128)S(1)}, u32[]{:S(2)}) copy-start(f32[3,512]{1,0:T(4,128)S(1)} %collective-permute-done.3.refs_5_.refs_1_) | copy-start | bytes 18436
  85.1 6.9 %collective-permute-start.5 = (f32[3,512]{1,0:T(4,128)S(1)}, f32[3,512]{1,0:T(4,128)S(1)}, u32[]{:S(2)}, u32[]{:S(2)}) collective-permute-start(f32[3,512]{1,0:T(4,128)S(1)} %reduce_sum.33.refs_4_.refs_0_), channel_id=1, source_target_pairs={{0,3},{1,0},{2,1},{3,2},{4,7},{5,4},{6,5},{7,6},{8,11},{9,8},{10,9... | collective-permute-start | bytes 18440 | tf_op jit(solution)/shard_map/ppermute | solution.py:1620
  92.0 5.4 %copy-start.19 = (f32[3,512]{1,0:T(4,128)}, f32[3,512]{1,0:T(4,128)S(1)}, u32[]{:S(2)}) copy-start(f32[3,512]{1,0:T(4,128)S(1)} %collective-permute-done.4.refs_6_.refs_2_) | copy-start | bytes 18436
  92.0 5.4 %copy-start.20 = (f32[3,512]{1,0:T(4,128)}, f32[3,512]{1,0:T(4,128)S(1)}, u32[]{:S(2)}) copy-start(f32[3,512]{1,0:T(4,128)S(1)} %collective-permute-done.5.refs_7_.refs_3_) | copy-start | bytes 18436
  92.0 5.4 %copy-start.5 = (bf16[1376,128]{1,0:T(8,128)(2,1)}, bf16[1376,128]{1,0:T(8,128)(2,1)S(1)}, u32[]{:S(2)}) copy-start(bf16[1376,128]{1,0:T(8,128)(2,1)S(1)} %collective-permute-done.refs_1_) | copy-start | bytes 1056772
  92.0 5.4 %copy-start.6 = (bf16[1376,128]{1,0:T(8,128)(2,1)}, bf16[1376,128]{1,0:T(8,128)(2,1)S(1)}, u32[]{:S(2)}) copy-start(bf16[1376,128]{1,0:T(8,128)(2,1)S(1)} %collective-permute-done.1.refs_2_) | copy-start | bytes 1056772
  92.0 5.4 %copy-start.7 = (bf16[1376,128]{1,0:T(8,128)(2,1)}, bf16[1376,128]{1,0:T(8,128)(2,1)S(1)}, u32[]{:S(2)}) copy-start(bf16[1376,128]{1,0:T(8,128)(2,1)S(1)} %collective-permute-done.2.refs_3_) | copy-start | bytes 1056772
  92.1 30.3 %collective-permute-start.6 = (bf16[912,128]{1,0:T(8,128)(2,1)}, bf16[912,128]{1,0:T(8,128)(2,1)S(1)}, u32[]{:S(2)}, u32[]{:S(2)}) collective-permute-start(bf16[912,128]{1,0:T(8,128)(2,1)} %get-tuple-element.109.refs_0_), channel_id=1, source_target_pairs={{0,1},{1,2},{2,3},{3,0},{4,5},{5,6},{6,7},{7,4},{8,9},{9,10},{10,1... | collective-permute-start | bytes 700424 | tf_op jit(solution)/shard_map/ppermute | solution.py:1620
  93.0 29.4 %collective-permute-start.7 = (bf16[912,128]{1,0:T(8,128)(2,1)}, bf16[912,128]{1,0:T(8,128)(2,1)S(1)}, u32[]{:S(2)}, u32[]{:S(2)}) collective-permute-start(bf16[912,128]{1,0:T(8,128)(2,1)} %get-tuple-element.109.refs_0_), channel_id=1, source_target_pairs={{0,2},{1,3},{2,0},{3,1},{4,6},{5,7},{6,4},{7,5},{8,10},{9,11},{10,... | collective-permute-start | bytes 700424 | tf_op jit(solution)/shard_map/ppermute | solution.py:1620
  94.5 27.9 %collective-permute-start.8 = (bf16[912,128]{1,0:T(8,128)(2,1)}, bf16[912,128]{1,0:T(8,128)(2,1)S(1)}, u32[]{:S(2)}, u32[]{:S(2)}) collective-permute-start(bf16[912,128]{1,0:T(8,128)(2,1)} %get-tuple-element.109.refs_0_), channel_id=1, source_target_pairs={{0,3},{1,0},{2,1},{3,2},{4,7},{5,4},{6,5},{7,6},{8,11},{9,8},{10,9... | collective-permute-start | bytes 700424 | tf_op jit(solution)/shard_map/ppermute | solution.py:1620
  122.4 0.7 copy-start.8
  122.4 0.7 copy-start.9
  122.4 0.8 copy-start.10
  127.2 8.6 %all-to-all-start.2 = ((f32[8,2,640]{2,1,0:T(2,128)}), f32[8,2,640]{2,1,0:T(2,128)S(1)}, u32[]{:S(2)}, u32[]{:S(2)}) async-start(f32[8,2,640]{2,1,0:T(2,128)} %get-tuple-element.116), calls=%async_computation.2 | async-start | bytes 81920 | tf_op jit(solution)/shard_map/all_to_all | solution.py:1629
  130.9 94.7 %all-gather.7.cloned.1.call-start = ((), (), s32[]{:S(2)}) async-start(), calls=%async_computation.13 | async-start | bytes 5242880 | tf_op jit(solution)/shard_map/all_gather | solution.py:1732
  135.8 3.9 %copy-start.12 = (f32[8,2,640]{2,1,0:T(2,128)}, f32[8,2,640]{2,1,0:T(2,128)S(1)}, u32[]{:S(2)}) copy-start(f32[8,2,640]{2,1,0:T(2,128)S(1)} %all-to-all-done.2.sums_in_ref) | copy-start | bytes 122884
  135.8 15.8 %collective-permute-start.9 = (bf16[128,256]{1,0:T(8,128)(2,1)}, bf16[128,256]{1,0:T(8,128)(2,1)S(1)}, u32[]{:S(2)}, u32[]{:S(2)}) collective-permute-start(bf16[128,256]{1,0:T(8,128)(2,1)} %get-tuple-element.121.refs_0_), channel_id=1, source_target_pairs={{0,1},{1,2},{2,3},{3,0},{4,5},{5,6},{6,7},{7,4},{8,9},{9,10},{10,1... | collective-permute-start | bytes 196616 | tf_op jit(solution)/shard_map/ppermute | solution.py:1620
  135.9 15.8 %collective-permute-start.10 = (bf16[128,256]{1,0:T(8,128)(2,1)}, bf16[128,256]{1,0:T(8,128)(2,1)S(1)}, u32[]{:S(2)}, u32[]{:S(2)}) collective-permute-start(bf16[128,256]{1,0:T(8,128)(2,1)} %get-tuple-element.121.refs_0_), channel_id=1, source_target_pairs={{0,2},{1,3},{2,0},{3,1},{4,6},{5,7},{6,4},{7,5},{8,10},{9,11},{10,... | collective-permute-start | bytes 196616 | tf_op jit(solution)/shard_map/ppermute | solution.py:1620
  136.5 15.1 %collective-permute-start.11 = (bf16[128,256]{1,0:T(8,128)(2,1)}, bf16[128,256]{1,0:T(8,128)(2,1)S(1)}, u32[]{:S(2)}, u32[]{:S(2)}) collective-permute-start(bf16[128,256]{1,0:T(8,128)(2,1)} %get-tuple-element.121.refs_0_), channel_id=1, source_target_pairs={{0,3},{1,0},{2,1},{3,2},{4,7},{5,4},{6,5},{7,6},{8,11},{9,8},{10,9... | collective-permute-start | bytes 196616 | tf_op jit(solution)/shard_map/ppermute | solution.py:1620
  151.6 0.6 copy-start.16
  151.7 0.6 copy-start.17
  186.0 8.3 %all-to-all-start.5 = ((f32[8,2,896]{2,1,0:T(2,128)}), f32[8,2,896]{2,1,0:T(2,128)S(1)}, u32[]{:S(2)}, u32[]{:S(2)}) async-start(f32[8,2,896]{2,1,0:T(2,128)} %get-tuple-element.141), calls=%async_computation.5 | async-start | bytes 114688 | tf_op jit(solution)/shard_map/all_to_all | solution.py:1629
  200.3 16.1 %all-to-all-start.6 = ((bf16[8,384,128]{2,1,0:T(8,128)(2,1)}), bf16[8,384,128]{2,1,0:T(8,128)(2,1)S(1)}, u32[]{:S(2)}, u32[]{:S(2)}) async-start(bf16[8,384,128]{2,1,0:T(8,128)(2,1)} %get-tuple-element.151), calls=%async_computation.6 | async-start | bytes 1572864 | tf_op jit(solution)/shard_map/all_to_all | solution.py:1629
  203.8 128.6 %all-gather.9.cloned.1.call-start = ((), (), s32[]{:S(2)}) async-start(), calls=%async_computation.14 | async-start | bytes 3244032 | tf_op jit(solution)/shard_map/all_gather | solution.py:1911
  258.6 19.3 %all-to-all-start.9 = ((bf16[8,528,128]{2,1,0:T(8,128)(2,1)}), bf16[8,528,128]{2,1,0:T(8,128)(2,1)S(1)}, u32[]{:S(2)}, u32[]{:S(2)}) async-start(bf16[8,528,128]{2,1,0:T(8,128)(2,1)} %get-tuple-element.166), calls=%async_computation.9 | async-start | bytes 2162688 | tf_op jit(solution)/shard_map/all_to_all | solution.py:1629
  262.1 82.9 %all-gather.11.cloned.1.call-start = ((), (), s32[]{:S(2)}) async-start(), calls=%async_computation.15 | async-start | bytes 4460544 | tf_op jit(solution)/shard_map/all_gather | solution.py:1980
  278.7 25.9 %all-to-all-start.11 = ((f32[8,6,32,128]{3,2,1,0:T(8,128)}), f32[8,6,32,128]{3,2,1,0:T(8,128)S(1)}, u32[]{:S(2)}, u32[]{:S(2)}) async-start(f32[8,6,32,128]{3,2,1,0:T(8,128)} %get-tuple-element.169), calls=%async_computation.11 | async-start | bytes 1572864 | tf_op jit(solution)/shard_map/all_to_all | solution.py:1629
  304.6 19.9 %copy-start.1 = (f32[8,6,32,128]{3,2,1,0:T(8,128)}, f32[8,6,32,128]{3,2,1,0:T(8,128)S(1)}, u32[]{:S(2)}) copy-start(f32[8,6,32,128]{3,2,1,0:T(8,128)S(1)} %all-to-all-done.11.rest_ref) | copy-start | bytes 2359300
  313.6 10.9 %all-to-all-start.10 = ((f32[8,2,32,128]{3,2,1,0:T(8,128)}), f32[8,2,32,128]{3,2,1,0:T(8,128)S(1)}, u32[]{:S(2)}, u32[]{:S(2)}) async-start(f32[8,2,32,128]{3,2,1,0:T(8,128)} %get-tuple-element.173), calls=%async_computation.10 | async-start | bytes 524288 | tf_op jit(solution)/shard_map/all_to_all | solution.py:1629
  324.4 0.7 copy-start.2
  327.0 10.3 %copy-start.13 = (bf16[160,128]{1,0:T(8,128)(2,1)S(1)}, bf16[160,128]{1,0:T(8,128)(2,1)}, u32[]{:S(2)}) copy-start(bf16[160,128]{1,0:T(8,128)(2,1)} %shard_map.152) | copy-start | bytes 122884
  327.1 10.2 %collective-permute-start.12 = (bf16[160,128]{1,0:T(8,128)(2,1)}, bf16[160,128]{1,0:T(8,128)(2,1)S(1)}, u32[]{:S(2)}, u32[]{:S(2)}) collective-permute-start(bf16[160,128]{1,0:T(8,128)(2,1)} %shard_map.152), channel_id=1, source_target_pairs={{0,1},{1,2},{2,3},{3,0},{4,5},{5,6},{6,7},{7,4},{8,9},{9,10},{10,1... | collective-permute-start | bytes 122888 | tf_op jit(solution)/shard_map/ppermute | solution.py:1620
  328.4 8.9 %collective-permute-start.13 = (bf16[160,128]{1,0:T(8,128)(2,1)}, bf16[160,128]{1,0:T(8,128)(2,1)S(1)}, u32[]{:S(2)}, u32[]{:S(2)}) collective-permute-start(bf16[160,128]{1,0:T(8,128)(2,1)} %shard_map.152), channel_id=1, source_target_pairs={{0,2},{1,3},{2,0},{3,1},{4,6},{5,7},{6,4},{7,5},{8,10},{9,11},{10,... | collective-permute-start | bytes 122888 | tf_op jit(solution)/shard_map/ppermute | solution.py:1620
  330.9 6.5 %collective-permute-start.14 = (bf16[160,128]{1,0:T(8,128)(2,1)}, bf16[160,128]{1,0:T(8,128)(2,1)S(1)}, u32[]{:S(2)}, u32[]{:S(2)}) collective-permute-start(bf16[160,128]{1,0:T(8,128)(2,1)} %shard_map.152), channel_id=1, source_target_pairs={{0,3},{1,0},{2,1},{3,2},{4,7},{5,4},{6,5},{7,6},{8,11},{9,8},{10,9... | collective-permute-start | bytes 122888 | tf_op jit(solution)/shard_map/ppermute | solution.py:1620
  337.4 14.4 %collective-permute-start.15 = (bf16[640,128]{1,0:T(8,128)(2,1)S(1)}, bf16[640,128]{1,0:T(8,128)(2,1)S(1)}, u32[]{:S(2)}, u32[]{:S(2)}) collective-permute-start(bf16[640,128]{1,0:T(8,128)(2,1)S(1)} %constant_dynamic-update-slice_fusion), channel_id=1, source_target_pairs={{0,8},{4,12},{8,0},{12,4},{16,24},{20,28},{24,16},{28,20},{1,9},{5... | collective-permute-start | bytes 491528 | tf_op jit(solution)/shard_map/ppermute | solution.py:1640
  339.4 12.5 %collective-permute-start.16 = (bf16[640,128]{1,0:T(8,128)(2,1)S(1)}, bf16[640,128]{1,0:T(8,128)(2,1)S(1)}, u32[]{:S(2)}, u32[]{:S(2)}) collective-permute-start(bf16[640,128]{1,0:T(8,128)(2,1)S(1)} %constant_dynamic-update-slice_fusion), channel_id=1, source_target_pairs={{0,16},{4,20},{8,24},{12,28},{16,0},{20,4},{24,8},{28,12},{1,17},{... | collective-permute-start | bytes 491528 | tf_op jit(solution)/shard_map/ppermute | solution.py:1640
  340.8 11.0 %collective-permute-start.17 = (bf16[640,128]{1,0:T(8,128)(2,1)S(1)}, bf16[640,128]{1,0:T(8,128)(2,1)S(1)}, u32[]{:S(2)}, u32[]{:S(2)}) collective-permute-start(bf16[640,128]{1,0:T(8,128)(2,1)S(1)} %constant_dynamic-update-slice_fusion), channel_id=1, source_target_pairs={{0,24},{4,28},{8,16},{12,20},{16,8},{20,12},{24,0},{28,4},{1,25},{... | collective-permute-start | bytes 491528 | tf_op jit(solution)/shard_map/ppermute | solution.py:1640
  352.0 2.2 copy-start.3
  352.0 2.2 collective-permute-start.18
  354.1 0.8 copy-start.4
  (2 other events, 1.2 us)
Sparse Core Ops, SparseCore 0:
  135.9 77.8 all-gather.6
  217.3 57.3 all-gather.8
  278.8 66.2 all-gather.10

commit v3 on v2

--- a/solution.py
+++ b/solution.py
@@ -29,7 +29,7 @@
 LARGE = 2200 * 2**10
 
 
-def call(body, out_shape, scratch=(), scalars=0, cost=5, aliases=None, far=(), far_out=()):
+def call(body, out_shape, scratch=(), scalars=0, cost=5, vmem=VMEM_BYTES, aliases=None, far=(), far_out=()):
     aliases = aliases or {}
 
     def large(values):
@@ -70,7 +70,7 @@
             out_specs=out_specs,
             input_output_aliases=aliases,
             scratch_shapes=list(scratch),
-            compiler_params=pltpu.CompilerParams(vmem_limit_bytes=VMEM_BYTES),
+            compiler_params=pltpu.CompilerParams(vmem_limit_bytes=vmem),
             cost_estimate=pl.CostEstimate(
                 flops=0, bytes_accessed=int(cost * 3 * 10**6), transcendentals=0
             ),
@@ -92,14 +92,19 @@
     return lax.broadcasted_iota(jnp.int32, dims, 0) & (unit - 1)
 
 
+def keep_frames(values, unit, lo, hi):
+    rows, width = values.shape
+    frame = lax.broadcasted_iota(jnp.int32, (1, unit, width), 1)
+    kept = jnp.where((frame >= lo) & (frame < hi), 1.0, 0.0)
+    return (values.reshape(rows // unit, unit, width) * kept).reshape(rows, width)
+
+
 def earlier(values, unit):
-    return jnp.where(frames_of(values.shape, unit) > 0, pltpu.roll(values, 1, 0), 0.0)
+    return keep_frames(pltpu.roll(values, 1, 0), unit, 1, unit)
 
 
 def later(values, unit):
-    rows = values.shape[0]
-    shifted = pltpu.roll(values, rows - 1, 0)
-    return jnp.where(frames_of(values.shape, unit) < unit - 1, shifted, 0.0)
+    return keep_frames(pltpu.roll(values, values.shape[0] - 1, 0), unit, 0, unit - 1)
 
 
 def plane_box(values, unit):
@@ -1694,6 +1699,7 @@
         ),
         [pltpu.VMEM((slots.rows, FIRST), F32)],
         scalars=2,
+        vmem=VMEM_BYTES // 3,
     )(length, local_count, by_pairs, point_first)
     mids = spread_over(mid, "branch", parts)
     sums = spread_over(jnp.sum(exchange(sums), axis=0), "branch", parts)
@@ -2004,6 +2010,7 @@
         functools.partial(combine, 0),
         shape((5 * product_rows // clips, 128), BF16),
         cost=1,
+        vmem=VMEM_BYTES // 3,
     )(rest_pieces, pieces, moment, gathered, reduced_gain)
     received = spread_over(point_sum, "branch", parts)
 
@@ -2050,6 +2057,7 @@
         far_out=(0,),
         aliases={4: 0},
         cost=3,
+        vmem=VMEM_BYTES // 2,
     )(place_one, clip_one, point_mine, point_other, point_grad)
     act = act.reshape(small.side, small.side, cotangent.shape[1], CHANNELS).transpose(2, 0, 1, 3)
     input_grad = dx.reshape(side, side, grid.unit, own_channels).transpose(2, 0, 1, 3)

time: 367 us -> 362 us (0.986)
  Pallas kernels: 169 us -> 163 us
    pallas_call x21, Pallas kernels: 169 us -> 163 us  [run(): pl.pallas_call(body, out_shape=jax.tree.map(placed, out_shape), in_specs=...]
where the time goes in v3:
time: 362 us; the launch traced here: 360 us
  Pallas kernels  163 us (45%)
  waiting for transfers between devices  71.5 us (20%)
  blocking collectives  52.9 us (15%)
  starting transfers between devices  52.3 us (14%)
  between operations  15 us (4%)
  local copies, waits for them, and re-layouts  4.45 us (1%)
    pallas_call x21, Pallas kernels, run(): pl.pallas_call(body, out_shape=jax.tree.map(placed, out_shape), in_specs=...  163 us
    all_to_all x6, blocking collectives, exchange(): return lax.all_to_all(values, 'dp', 0, 0, tiled=True)  52.9 us
    all_to_all x1, waiting for transfers between devices, on_device(): by_pairs = lax.all_to_all(turned, 'branch', 0, 0, tiled=True)  24.4 us
    all_to_all x6, starting transfers between devices, exchange(): return lax.all_to_all(values, 'dp', 0, 0, tiled=True)  21.2 us
    ppermute x15, starting transfers between devices, spread_over(): received.append(lax.ppermute(values, axis, perm))  20.6 us
    all_to_all x6, waiting for transfers between devices, exchange(): return lax.all_to_all(values, 'dp', 0, 0, tiled=True)  20 us
    ppermute x15, waiting for transfers between devices, spread_over(): received.append(lax.ppermute(values, axis, perm))  18.9 us
  transfers between devices with their start and end apart: 29, of which 9 were waited for; matrix products, arithmetic and copies ran while one was open for 0% of the time, Pallas kernels for 42%

profile of v3, /device:TPU:0, one launch (start us, length us, event | category | flops | bytes accessed | tf_op | source)
XLA Modules:
  0.0 360.3 jit_solution(1336576104618604216)
XLA Ops:
  7.2 3.2 shard_map.135.x_far.refs_3_
  10.4 6.3 %all-to-all-start = ((bf16[4,208,896]{2,1,0:T(8,128)(2,1)}), bf16[4,208,896]{2,1,0:T(8,128)(2,1)S(1)}, u32[]{:S(2)}, u32[]{:S(2)}) async-start(bf16[4,208,896]{2,1,0:T(8,128)(2,1)} %shard_map.135.x_far.refs_3_), calls=%async_computation | async-start | bytes 2981888 | tf_op jit(solution)/shard_map/all_to_all | solution.py:1668
  17.4 10.1 %shard_map.136 = (bf16[9,512,256]{2,1,0:T(8,128)(2,1)}, bf16[3,512,256]{2,1,0:T(8,128)(2,1)}, bf16[1152,128]{1,0:T(8,128)(2,1)}, bf16[1152,128]{1,0:T(8,128)(2,1...) custom-call(bf16[2,27,160,320]{3,2,1,0:T(8,128)(2,1)} %mid_in.1, ...), custom_call_target="tpu_custom_call" | custom-call | bytes 15000000 | tf_op jit(solution)/shard_map/pallas_call | solution.py:66
  27.5 24.4 %all-to-all-done.x_ref = bf16[4,208,896]{2,1,0:T(8,128)(2,1)S(1)} async-done(((bf16[4,208,896]{2,1,0:T(8,128)(2,1)}), bf16[4,208,896]{2,1,0:T(8,128)(2,1)S(1)}, u32[]{:S(2)}, u32[]{:S(2)}) %all-to-all-start) | async-done | bytes 1490976 | tf_op jit(solution)/shard_map/all_to_all | solution.py:1668
  53.3 2.5 shard_map.137
  56.7 2.0 collective-permute-start.1
  58.7 1.8 collective-permute-start.2
  60.5 8.5 %all_to_all.65 = f32[8,3,512]{2,1,0:T(4,128)S(1)} all-to-all(f32[8,3,512]{2,1,0:T(4,128)S(1)} %get-tuple-element.108), channel_id=1, replica_groups=mesh['dp'=8,'branch'=4] {'dp'}, dimensions={0} | all-to-all | bytes 98304 | tf_op jit(solution)/shard_map/all_to_all | solution.py:1634
  71.2 12.0 %collective-permute-done.3.refs_5_.refs_1_ = f32[3,512]{1,0:T(4,128)S(1)} collective-permute-done((f32[3,512]{1,0:T(4,128)S(1)}, f32[3,512]{1,0:T(4,128)S(1)}, u32[]{:S(2)}, u32[]{:S(2)}) %collective-permute-start.3) | collective-permute-done | bytes 6176 | tf_op jit(solution)/shard_map/ppermute | solution.py:1625
  83.2 6.9 %collective-permute-done.4.refs_6_.refs_2_ = f32[3,512]{1,0:T(4,128)S(1)} collective-permute-done((f32[3,512]{1,0:T(4,128)S(1)}, f32[3,512]{1,0:T(4,128)S(1)}, u32[]{:S(2)}, u32[]{:S(2)}) %collective-permute-start.4) | collective-permute-done | bytes 6176 | tf_op jit(solution)/shard_map/ppermute | solution.py:1625
  92.6 2.8 collective-permute-start.8
  95.5 25.1 %shard_map.138 = (bf16[3136,256]{1,0:T(8,128)(2,1)}, bf16[1,3872,512]{2,1,0:T(8,128)(2,1)}, bf16[1,3872,128]{2,1,0:T(8,128)(2,1)}, f32[3136,512]{1,0:T(8,128)}, f32[2,512]{1,0:T(2,128)}) custom-call(s32[1]{0:T(128)S(6)} %copy.27.length_ref, s32[1]{0:T(128)} %bitcast.place_ref, bf16[1376,128]{1,0:T(8,128)(2,1)} %copy-done.2, bf16[1376,128]{1,0:T(8,128)(2,1)} %copy-done.7, ...), custom_call_target="tpu_custom_call" | custom-call | bytes 120000000 | tf_op jit(solution)/shard_map/pallas_call | solution.py:66
  121.5 3.9 %shard_map.139 = (f32[3136,128]{1,0:T(8,128)}, f32[8,2,640]{2,1,0:T(2,128)}) custom-call(s32[1]{0:T(128)S(6)} %copy.27.length_ref, s32[1]{0:T(128)} %bitcast.place_ref, bf16[912,128]{1,0:T(8,128)(2,1)} %copy-done.3, bf16[912,128]{1,0:T(8,128)(2,1)} %copy-done.10, bf16[912,128]{1,0:T(8,128)(2,1)} %copy-done.11, bf16[912,128]{1,0:T(8,128)(2,1)} %copy-done.12, ...), custom_call_target="tpu_custom_call" | custom-call | bytes 15000000 | tf_op jit(solution)/shard_map/pallas_call | solution.py:66
  125.4 3.7 %all-to-all-start.2 = ((f32[8,2,640]{2,1,0:T(2,128)}), f32[8,2,640]{2,1,0:T(2,128)S(1)}, u32[]{:S(2)}, u32[]{:S(2)}) async-start(f32[8,2,640]{2,1,0:T(2,128)} %get-tuple-element.116), calls=%async_computation.2 | async-start | bytes 81920 | tf_op jit(solution)/shard_map/all_to_all | solution.py:1634
  129.1 3.2 shard_map.140
  132.4 1.6 all-to-all-done.2.sums_in_ref
  134.7 3.2 collective-permute-start.11
  137.9 11.9 %shard_map.141 = (bf16[448,640]{1,0:T(8,128)(2,1)}, bf16[3136,640]{1,0:T(8,128)(2,1)}, bf16[3136,640]{1,0:T(8,128)(2,1)}, f32[3,896]{1,0:T(4,128)}, bf16[448,640]{1,0:T(8,128)(2,1)}, /*index=5*/bf16[448,640]{1,0:T(8,128)(2,1)}) custom-call(s32[1]{0:T(128)S(6)} %copy.27.length_ref, f32[3136,128]{1,0:T(8,128)} %get-tuple-element.122.q_far, ...), custom_call_target="tpu_custom_call" | custom-call | bytes 15000000 | tf_op jit(solution)/shard_map/pallas_call | solution.py:66
  150.5 4.3 %shard_map.142 = (f32[448,640]{1,0:T(8,128)}, f32[8,3,640]{2,1,0:T(4,128)}, bf16[448,896]{1,0:T(8,128)(2,1)}) custom-call(s32[1]{0:T(128)S(6)} %select_n.12.length_ref, s32[1]{0:T(128)} %bitcast.place_ref, f32[1]{0:T(128)S(6)} %mul.20.count_ref, bf16[128,256]{1,0:T(8,128)(2,1)} %get-tuple-element.121.refs_0_, bf16[128,256]{1,0:T(8,128)(2,1)} %copy-done.16, ...), custom_call_target="tpu_custom_call" | custom-call | bytes 15000000 | tf_op jit(solution)/shard_map/pallas_call | solution.py:66
  154.9 9.1 %all_to_all.66.sums_in_ref = f32[8,3,640]{2,1,0:T(4,128)} all-to-all(f32[8,3,640]{2,1,0:T(4,128)} %get-tuple-element.129), channel_id=1, replica_groups=mesh['dp'=8,'branch'=4] {'dp'}, dimensions={0} | all-to-all | bytes 122880 | tf_op jit(solution)/shard_map/all_to_all | solution.py:1634
  163.9 6.7 %shard_map.143 = (bf16[448,256]{1,0:T(8,128)(2,1)}, bf16[2,736,512]{2,1,0:T(8,128)(2,1)}, bf16[2,736,128]{2,1,0:T(8,128)(2,1)}, f32[448,512]{1,0:T(8,128)}, f32[8,2,512]{2,1,0:T(2,128)}, /*index=5*/f32[3,640]{1,0:T(4,128)}) custom-call(s32[1]{0:T(128)S(6)} %select_n.12.length_ref, f32[448,640]{1,0:T(8,128)} %get-tuple-element.128.q_ref, ...), custom_call_target="tpu_custom_call" | custom-call | bytes 15000000 | tf_op jit(solution)/shard_map/pallas_call | solution.py:66
  170.7 8.8 %all_to_all.67.sums_in_ref = f32[8,2,512]{2,1,0:T(2,128)} all-to-all(f32[8,2,512]{2,1,0:T(2,128)} %get-tuple-element.135), channel_id=1, replica_groups=mesh['dp'=8,'branch'=4] {'dp'}, dimensions={0} | all-to-all | bytes 65536 | tf_op jit(solution)/shard_map/all_to_all | solution.py:1634
  179.4 4.8 %shard_map.144 = (bf16[49,8,832]{2,1,0:T(8,128)(2,1)}, bf16[448,896]{1,0:T(8,128)(2,1)}, bf16[448,896]{1,0:T(8,128)(2,1)}, f32[3,896]{1,0:T(4,128)}, f32[8,2,896]{2,1,0:T(2,128)}) custom-call(s32[1]{0:T(128)S(6)} %select_n.12.length_ref, f32[448,640]{1,0:T(8,128)} %get-tuple-element.128.q_ref, f32[448,512]{1,0:T(8,128)} %get-tuple-element.133.e_ref, ...), custom_call_target="tpu_custom_call" | custom-call | bytes 15000000 | tf_op jit(solution)/shard_map/pallas_call | solution.py:66
  184.2 3.3 all-to-all-start.5
  187.6 4.9 %all-to-all-done.5.sums_in_ref = f32[8,2,896]{2,1,0:T(2,128)S(1)} async-done(((f32[8,2,896]{2,1,0:T(2,128)}), f32[8,2,896]{2,1,0:T(2,128)S(1)}, u32[]{:S(2)}, u32[]{:S(2)}) %all-to-all-start.5) | async-done | bytes 57376 | tf_op jit(solution)/shard_map/all_to_all | solution.py:1634
  193.1 5.3 %shard_map.145 = (bf16[2,736,512]{2,1,0:T(8,128)(2,1)}, f32[2,896]{1,0:T(2,128)}, bf16[8,384,128]{2,1,0:T(8,128)(2,1)}) custom-call(s32[1]{0:T(128)S(6)} %select_n.12.length_ref, s32[1]{0:T(128)S(6)} %mul.25.first_ref, bf16[448,896]{1,0:T(8,128)(2,1)} %get-tuple-element.139.h_far, f32[3,896]{1,0:T(4,128)} %get-tuple-element.140.outer_ref, ...), custom_call_target="tpu_custom_call" | custom-call | bytes 24000000 | tf_op jit(solution)/shard_map/pallas_call | solution.py:66
  198.5 3.6 all-to-all-start.6
  202.1 6.3 %shard_map.146 = (bf16[448,256]{1,0:T(8,128)(2,1)}, f32[8,2,256]{2,1,0:T(2,128)}) custom-call(s32[1]{0:T(128)S(6)} %select_n.12.length_ref, bf16[2,736,512]{2,1,0:T(8,128)(2,1)} %get-tuple-element.147.d_ref, bf16[448,256]{1,0:T(8,128)(2,1)} %get-tuple-element.146.reduced_ref.reduced_far, f32[2,256]{1,0:T(2,128)} %get-tuple-element.110.refs_8_.gain_ref.reduced_gain_ref, ...), custom_call_target="tpu_custom_call" | custom-call | bytes 24000000 | tf_op jit(solution)/shard_map/pallas_call | solution.py:66
  208.3 6.2 %all-to-all-done.6 = bf16[8,384,128]{2,1,0:T(8,128)(2,1)S(1)} async-done(((bf16[8,384,128]{2,1,0:T(8,128)(2,1)}), bf16[8,384,128]{2,1,0:T(8,128)(2,1)S(1)}, u32[]{:S(2)}, u32[]{:S(2)}) %all-to-all-start.6) | async-done | bytes 786464 | tf_op jit(solution)/shard_map/all_to_all | solution.py:1634
  215.3 8.5 %all_to_all.68.sums_in_ref = f32[8,2,256]{2,1,0:T(2,128)} all-to-all(f32[8,2,256]{2,1,0:T(2,128)} %get-tuple-element.152), channel_id=1, replica_groups=mesh['dp'=8,'branch'=4] {'dp'}, dimensions={0} | all-to-all | bytes 32768 | tf_op jit(solution)/shard_map/all_to_all | solution.py:1634
  223.8 7.8 %shard_map.147 = (bf16[448,896]{1,0:T(8,128)(2,1)}, bf16[8,144,128]{2,1,0:T(8,128)(2,1)}, f32[2,256]{1,0:T(2,128)}, f32[8,2,896]{2,1,0:T(2,128)}) custom-call(s32[1]{0:T(128)S(6)} %select_n.12.length_ref, s32[1]{0:T(128)} %bitcast.place_ref, bf16[448,896]{1,0:T(8,128)(2,1)} %get-tuple-element.139.h_far, f32[3,896]{1,0:T(4,128)} %get-tuple-element.140.outer_ref, ...), custom_call_target="tpu_custom_call" | custom-call | bytes 30000000 | tf_op jit(solution)/shard_map/pallas_call | solution.py:66
  231.6 8.9 %all_to_all.69.sums_in_ref = f32[8,2,896]{2,1,0:T(2,128)} all-to-all(f32[8,2,896]{2,1,0:T(2,128)} %get-tuple-element.158), channel_id=1, replica_groups=mesh['dp'=8,'branch'=4] {'dp'}, dimensions={0} | all-to-all | bytes 114688 | tf_op jit(solution)/shard_map/all_to_all | solution.py:1634
  240.6 16.2 %shard_map.148 = (bf16[1,3872,512]{2,1,0:T(8,128)(2,1)}, f32[2,896]{1,0:T(2,128)}, bf16[8,528,128]{2,1,0:T(8,128)(2,1)}) custom-call(s32[1]{0:T(128)S(6)} %copy.27.length_ref, s32[1]{0:T(128)S(6)} %mul.25.first_ref, bf16[3136,640]{1,0:T(8,128)(2,1)} %get-tuple-element.137.h_far, f32[3,896]{1,0:T(4,128)} %get-tuple-element.138.outer_ref, ...), custom_call_target="tpu_custom_call" | custom-call | bytes 54000000 | tf_op jit(solution)/shard_map/pallas_call | solution.py:66
  256.8 3.6 all-to-all-start.9
  260.6 8.2 %shard_map.149 = (bf16[3136,384]{1,0:T(8,128)(2,1)}, f32[8,6,32,128]{3,2,1,0:T(8,128)}) custom-call(s32[1]{0:T(128)S(6)} %copy.27.length_ref, f32[3,896]{1,0:T(4,128)} %get-tuple-element.138.outer_ref, f32[2,896]{1,0:T(2,128)} %get-tuple-element.167.total_ref.refs_0_, f32[2,896]{1,0:T(2,128)} %get-tuple-element.118.gain_ref, ...), custom_call_target="tpu_custom_call" | custom-call | bytes 24000000 | tf_op jit(solution)/shard_map/pallas_call | solution.py:66
  268.8 7.3 %all-to-all-done.9 = bf16[8,528,128]{2,1,0:T(8,128)(2,1)S(1)} async-done(((bf16[8,528,128]{2,1,0:T(8,128)(2,1)}), bf16[8,528,128]{2,1,0:T(8,128)(2,1)S(1)}, u32[]{:S(2)}, u32[]{:S(2)}) %all-to-all-start.9) | async-done | bytes 1081376 | tf_op jit(solution)/shard_map/all_to_all | solution.py:1634
  276.9 3.6 all-to-all-start.11
  280.5 22.0 %shard_map.150 = (bf16[3136,256]{1,0:T(8,128)(2,1)}, f32[8,2,256]{2,1,0:T(2,128)}, f32[8,2,32,128]{3,2,1,0:T(8,128)}) custom-call(s32[1]{0:T(128)S(6)} %copy.27.length_ref, bf16[1,3872,512]{2,1,0:T(8,128)(2,1)} %get-tuple-element.171.d_ref, bf16[3136,256]{1,0:T(8,128)(2,1)} %get-tuple-element.168.reduced_far.reduced_ref.h_far, ...), custom_call_target="tpu_custom_call" | custom-call | bytes 66000000 | tf_op jit(solution)/shard_map/pallas_call | solution.py:66
  302.6 9.1 %all_to_all.70.sums_in_ref = f32[8,2,256]{2,1,0:T(2,128)} all-to-all(f32[8,2,256]{2,1,0:T(2,128)} %get-tuple-element.175), channel_id=1, replica_groups=mesh['dp'=8,'branch'=4] {'dp'}, dimensions={0} | all-to-all | bytes 32768 | tf_op jit(solution)/shard_map/all_to_all | solution.py:1634
  311.6 3.4 all-to-all-start.10
  315.1 7.4 %shard_map.151 = (bf16[3136,208]{1,0:T(8,128)(2,1)}, f32[2,256]{1,0:T(2,128)}) custom-call(s32[1]{0:T(128)S(6)} %copy.27.length_ref, s32[1]{0:T(128)} %bitcast.place_ref, f32[3,512]{1,0:T(4,128)} %get-tuple-element.124.moment_ref, f32[8,2,256]{2,1,0:T(2,128)} %all_to_all.70.sums_in_ref, f32[2,256]{1,0:T(2,128)} %get-tuple-element.110.refs_8_.gain_ref.reduced_gain_ref, ...), custom_call_target="tpu_custom_call" | custom-call | bytes 24000000 | tf_op jit(solution)/shard_map/pallas_call | solution.py:66
  324.0 2.4 collective-permute-start.13
  328.0 4.8 %shard_map.153 = (f32[2,27,160,320]{3,2,1,0:T(8,128)}, f32[2,27,32,128]{3,2,1,0:T(8,128)}) custom-call(bf16[32,384,128]{2,1,0:T(8,128)(2,1)} %bitcast.32), custom_call_target="tpu_custom_call" | custom-call | bytes 15000000 | tf_op jit(solution)/shard_map/pallas_call | solution.py:66
  333.0 2.0 collective-permute-start.15
  336.5 6.3 %all-gather.11.cloned.1.call-done = bf16[16896,128]{1,0:T(8,128)(2,1)} async-done(((bf16[528,128]{1,0:T(8,128)(2,1)}), bf16[16896,128]{1,0:T(8,128)(2,1)}) %all-gather.11.cloned.1.call-update) | async-done | bytes 4325392 | tf_op jit(solution)/shard_map/all_gather | solution.py:1986
  342.9 6.8 %shard_map.154 = (f32[2,27,160,320]{3,2,1,0:T(8,128)}, f32[2,27,32,128]{3,2,1,0:T(8,128)}, f32[2,576,832]{2,1,0:T(8,128)}, f32[2,1024]{1,0:T(2,128)}, f32[2,1024]{1,0:T(2,128)}) custom-call(bf16[32,528,128]{2,1,0:T(8,128)(2,1)} %bitcast.30, f32[2,896]{1,0:T(2,128)} %get-tuple-element.167.total_ref.refs_0_, ...), custom_call_target="tpu_custom_call", output_to_operand_aliasing={{0}: (5, {}), {1}: (6, {})} | custom-call | bytes 18000000 | tf_op jit(solution)/shard_map/pallas_call | solution.py:66
  350.1 1.8 collective-permute-done.18.other_ref
  352.0 1.8 shard_map.155
  (95 shorter events, 16.9 us)
Async XLA Ops:
  10.4 41.5 %all-to-all-start = ((bf16[4,208,896]{2,1,0:T(8,128)(2,1)}), bf16[4,208,896]{2,1,0:T(8,128)(2,1)S(1)}, u32[]{:S(2)}, u32[]{:S(2)}) async-start(bf16[4,208,896]{2,1,0:T(8,128)(2,1)} %shard_map.135.x_far.refs_3_), calls=%async_computation | async-start | bytes 2981888 | tf_op jit(solution)/shard_map/all_to_all | solution.py:1668
  51.9 1.3 copy-start
  55.7 0.9 copy-start.1
  56.7 38.8 %copy-start.2 = (bf16[1376,128]{1,0:T(8,128)(2,1)}, bf16[1376,128]{1,0:T(8,128)(2,1)S(1)}, u32[]{:S(2)}) copy-start(bf16[1376,128]{1,0:T(8,128)(2,1)S(1)} %get-tuple-element.107.refs_0_) | copy-start | bytes 1056772
  56.7 64.0 %copy-start.3 = (bf16[912,128]{1,0:T(8,128)(2,1)}, bf16[912,128]{1,0:T(8,128)(2,1)S(1)}, u32[]{:S(2)}) copy-start(bf16[912,128]{1,0:T(8,128)(2,1)S(1)} %get-tuple-element.109.refs_0_) | copy-start | bytes 700420
  56.7 33.4 %collective-permute-start = (bf16[1376,128]{1,0:T(8,128)(2,1)S(1)}, bf16[1376,128]{1,0:T(8,128)(2,1)S(1)}, u32[]{:S(2)}, u32[]{:S(2)}) collective-permute-start(bf16[1376,128]{1,0:T(8,128)(2,1)S(1)} %get-tuple-element.107.refs_0_), channel_id=1, source_target_pairs={{0,1},{1,2},{2,3},{3,0},{4,5},{5,6},{6,7},{7,4},{8,9},{9,10},{10,1... | collective-permute-start | bytes 1056776 | tf_op jit(solution)/shard_map/ppermute | solution.py:1625
  56.7 33.4 %collective-permute-start.1 = (bf16[1376,128]{1,0:T(8,128)(2,1)S(1)}, bf16[1376,128]{1,0:T(8,128)(2,1)S(1)}, u32[]{:S(2)}, u32[]{:S(2)}) collective-permute-start(bf16[1376,128]{1,0:T(8,128)(2,1)S(1)} %get-tuple-element.107.refs_0_), channel_id=1, source_target_pairs={{0,2},{1,3},{2,0},{3,1},{4,6},{5,7},{6,4},{7,5},{8,10},{9,11},{10,... | collective-permute-start | bytes 1056776 | tf_op jit(solution)/shard_map/ppermute | solution.py:1625
  58.7 31.4 %collective-permute-start.2 = (bf16[1376,128]{1,0:T(8,128)(2,1)S(1)}, bf16[1376,128]{1,0:T(8,128)(2,1)S(1)}, u32[]{:S(2)}, u32[]{:S(2)}) collective-permute-start(bf16[1376,128]{1,0:T(8,128)(2,1)S(1)} %get-tuple-element.107.refs_0_), channel_id=1, source_target_pairs={{0,3},{1,0},{2,1},{3,2},{4,7},{5,4},{6,5},{7,6},{8,11},{9,8},{10,9... | collective-permute-start | bytes 1056776 | tf_op jit(solution)/shard_map/ppermute | solution.py:1625
  69.1 26.4 %copy-start.15 = (f32[3,512]{1,0:T(4,128)}, f32[3,512]{1,0:T(4,128)S(1)}, u32[]{:S(2)}) copy-start(f32[3,512]{1,0:T(4,128)S(1)} %reduce_sum.33.refs_4_.refs_0_) | copy-start | bytes 18436
  69.1 14.2 %collective-permute-start.3 = (f32[3,512]{1,0:T(4,128)S(1)}, f32[3,512]{1,0:T(4,128)S(1)}, u32[]{:S(2)}, u32[]{:S(2)}) collective-permute-start(f32[3,512]{1,0:T(4,128)S(1)} %reduce_sum.33.refs_4_.refs_0_), channel_id=1, source_target_pairs={{0,1},{1,2},{2,3},{3,0},{4,5},{5,6},{6,7},{7,4},{8,9},{9,10},{10,1... | collective-permute-start | bytes 18440 | tf_op jit(solution)/shard_map/ppermute | solution.py:1625
  69.7 20.4 %collective-permute-start.4 = (f32[3,512]{1,0:T(4,128)S(1)}, f32[3,512]{1,0:T(4,128)S(1)}, u32[]{:S(2)}, u32[]{:S(2)}) collective-permute-start(f32[3,512]{1,0:T(4,128)S(1)} %reduce_sum.33.refs_4_.refs_0_), channel_id=1, source_target_pairs={{0,2},{1,3},{2,0},{3,1},{4,6},{5,7},{6,4},{7,5},{8,10},{9,11},{10,... | collective-permute-start | bytes 18440 | tf_op jit(solution)/shard_map/ppermute | solution.py:1625
  83.2 12.2 %copy-start.19 = (f32[3,512]{1,0:T(4,128)}, f32[3,512]{1,0:T(4,128)S(1)}, u32[]{:S(2)}) copy-start(f32[3,512]{1,0:T(4,128)S(1)} %collective-permute-done.3.refs_5_.refs_1_) | copy-start | bytes 18436
  83.2 6.9 %collective-permute-start.5 = (f32[3,512]{1,0:T(4,128)S(1)}, f32[3,512]{1,0:T(4,128)S(1)}, u32[]{:S(2)}, u32[]{:S(2)}) collective-permute-start(f32[3,512]{1,0:T(4,128)S(1)} %reduce_sum.33.refs_4_.refs_0_), channel_id=1, source_target_pairs={{0,3},{1,0},{2,1},{3,2},{4,7},{5,4},{6,5},{7,6},{8,11},{9,8},{10,9... | collective-permute-start | bytes 18440 | tf_op jit(solution)/shard_map/ppermute | solution.py:1625
  90.1 5.4 %copy-start.20 = (f32[3,512]{1,0:T(4,128)}, f32[3,512]{1,0:T(4,128)S(1)}, u32[]{:S(2)}) copy-start(f32[3,512]{1,0:T(4,128)S(1)} %collective-permute-done.4.refs_6_.refs_2_) | copy-start | bytes 18436
  90.1 5.4 %copy-start.21 = (f32[3,512]{1,0:T(4,128)}, f32[3,512]{1,0:T(4,128)S(1)}, u32[]{:S(2)}) copy-start(f32[3,512]{1,0:T(4,128)S(1)} %collective-permute-done.5.refs_7_.refs_3_) | copy-start | bytes 18436
  90.1 5.4 %copy-start.7 = (bf16[1376,128]{1,0:T(8,128)(2,1)}, bf16[1376,128]{1,0:T(8,128)(2,1)S(1)}, u32[]{:S(2)}) copy-start(bf16[1376,128]{1,0:T(8,128)(2,1)S(1)} %collective-permute-done.refs_1_) | copy-start | bytes 1056772
  90.1 5.4 %copy-start.8 = (bf16[1376,128]{1,0:T(8,128)(2,1)}, bf16[1376,128]{1,0:T(8,128)(2,1)S(1)}, u32[]{:S(2)}) copy-start(bf16[1376,128]{1,0:T(8,128)(2,1)S(1)} %collective-permute-done.1.refs_2_) | copy-start | bytes 1056772
  90.1 5.4 %copy-start.9 = (bf16[1376,128]{1,0:T(8,128)(2,1)}, bf16[1376,128]{1,0:T(8,128)(2,1)S(1)}, u32[]{:S(2)}) copy-start(bf16[1376,128]{1,0:T(8,128)(2,1)S(1)} %collective-permute-done.2.refs_3_) | copy-start | bytes 1056772
  90.2 30.5 %collective-permute-start.6 = (bf16[912,128]{1,0:T(8,128)(2,1)S(1)}, bf16[912,128]{1,0:T(8,128)(2,1)S(1)}, u32[]{:S(2)}, u32[]{:S(2)}) collective-permute-start(bf16[912,128]{1,0:T(8,128)(2,1)S(1)} %get-tuple-element.109.refs_0_), channel_id=1, source_target_pairs={{0,1},{1,2},{2,3},{3,0},{4,5},{5,6},{6,7},{7,4},{8,9},{9,10},{10,1... | collective-permute-start | bytes 700424 | tf_op jit(solution)/shard_map/ppermute | solution.py:1625
  91.1 29.6 %collective-permute-start.7 = (bf16[912,128]{1,0:T(8,128)(2,1)S(1)}, bf16[912,128]{1,0:T(8,128)(2,1)S(1)}, u32[]{:S(2)}, u32[]{:S(2)}) collective-permute-start(bf16[912,128]{1,0:T(8,128)(2,1)S(1)} %get-tuple-element.109.refs_0_), channel_id=1, source_target_pairs={{0,2},{1,3},{2,0},{3,1},{4,6},{5,7},{6,4},{7,5},{8,10},{9,11},{10,... | collective-permute-start | bytes 700424 | tf_op jit(solution)/shard_map/ppermute | solution.py:1625
  92.6 28.1 %collective-permute-start.8 = (bf16[912,128]{1,0:T(8,128)(2,1)S(1)}, bf16[912,128]{1,0:T(8,128)(2,1)S(1)}, u32[]{:S(2)}, u32[]{:S(2)}) collective-permute-start(bf16[912,128]{1,0:T(8,128)(2,1)S(1)} %get-tuple-element.109.refs_0_), channel_id=1, source_target_pairs={{0,3},{1,0},{2,1},{3,2},{4,7},{5,4},{6,5},{7,6},{8,11},{9,8},{10,9... | collective-permute-start | bytes 700424 | tf_op jit(solution)/shard_map/ppermute | solution.py:1625
  120.7 0.7 copy-start.10
  120.7 0.7 copy-start.11
  120.7 0.8 copy-start.12
  125.4 8.6 %all-to-all-start.2 = ((f32[8,2,640]{2,1,0:T(2,128)}), f32[8,2,640]{2,1,0:T(2,128)S(1)}, u32[]{:S(2)}, u32[]{:S(2)}) async-start(f32[8,2,640]{2,1,0:T(2,128)} %get-tuple-element.116), calls=%async_computation.2 | async-start | bytes 81920 | tf_op jit(solution)/shard_map/all_to_all | solution.py:1634
  129.1 94.7 %all-gather.7.cloned.1.call-start = ((), (), s32[]{:S(2)}) async-start(), calls=%async_computation.13 | async-start | bytes 5242880 | tf_op jit(solution)/shard_map/all_gather | solution.py:1738
  134.0 3.9 %copy-start.14 = (f32[8,2,640]{2,1,0:T(2,128)}, f32[8,2,640]{2,1,0:T(2,128)S(1)}, u32[]{:S(2)}) copy-start(f32[8,2,640]{2,1,0:T(2,128)S(1)} %all-to-all-done.2.sums_in_ref) | copy-start | bytes 122884
  134.0 15.8 %collective-permute-start.9 = (bf16[128,256]{1,0:T(8,128)(2,1)}, bf16[128,256]{1,0:T(8,128)(2,1)S(1)}, u32[]{:S(2)}, u32[]{:S(2)}) collective-permute-start(bf16[128,256]{1,0:T(8,128)(2,1)} %get-tuple-element.121.refs_0_), channel_id=1, source_target_pairs={{0,1},{1,2},{2,3},{3,0},{4,5},{5,6},{6,7},{7,4},{8,9},{9,10},{10,1... | collective-permute-start | bytes 196616 | tf_op jit(solution)/shard_map/ppermute | solution.py:1625
  134.1 15.8 %collective-permute-start.10 = (bf16[128,256]{1,0:T(8,128)(2,1)}, bf16[128,256]{1,0:T(8,128)(2,1)S(1)}, u32[]{:S(2)}, u32[]{:S(2)}) collective-permute-start(bf16[128,256]{1,0:T(8,128)(2,1)} %get-tuple-element.121.refs_0_), channel_id=1, source_target_pairs={{0,2},{1,3},{2,0},{3,1},{4,6},{5,7},{6,4},{7,5},{8,10},{9,11},{10,... | collective-permute-start | bytes 196616 | tf_op jit(solution)/shard_map/ppermute | solution.py:1625
  134.7 15.1 %collective-permute-start.11 = (bf16[128,256]{1,0:T(8,128)(2,1)}, bf16[128,256]{1,0:T(8,128)(2,1)S(1)}, u32[]{:S(2)}, u32[]{:S(2)}) collective-permute-start(bf16[128,256]{1,0:T(8,128)(2,1)} %get-tuple-element.121.refs_0_), channel_id=1, source_target_pairs={{0,3},{1,0},{2,1},{3,2},{4,7},{5,4},{6,5},{7,6},{8,11},{9,8},{10,9... | collective-permute-start | bytes 196616 | tf_op jit(solution)/shard_map/ppermute | solution.py:1625
  149.9 0.6 copy-start.18
  184.2 8.3 %all-to-all-start.5 = ((f32[8,2,896]{2,1,0:T(2,128)}), f32[8,2,896]{2,1,0:T(2,128)S(1)}, u32[]{:S(2)}, u32[]{:S(2)}) async-start(f32[8,2,896]{2,1,0:T(2,128)} %get-tuple-element.141), calls=%async_computation.5 | async-start | bytes 114688 | tf_op jit(solution)/shard_map/all_to_all | solution.py:1634
  198.5 16.1 %all-to-all-start.6 = ((bf16[8,384,128]{2,1,0:T(8,128)(2,1)}), bf16[8,384,128]{2,1,0:T(8,128)(2,1)S(1)}, u32[]{:S(2)}, u32[]{:S(2)}) async-start(bf16[8,384,128]{2,1,0:T(8,128)(2,1)} %get-tuple-element.151), calls=%async_computation.6 | async-start | bytes 1572864 | tf_op jit(solution)/shard_map/all_to_all | solution.py:1634
  202.0 126.0 %all-gather.9.cloned.1.call-start = ((), (), s32[]{:S(2)}) async-start(), calls=%async_computation.14 | async-start | bytes 3244032 | tf_op jit(solution)/shard_map/all_gather | solution.py:1917
  256.8 19.3 %all-to-all-start.9 = ((bf16[8,528,128]{2,1,0:T(8,128)(2,1)}), bf16[8,528,128]{2,1,0:T(8,128)(2,1)S(1)}, u32[]{:S(2)}, u32[]{:S(2)}) async-start(bf16[8,528,128]{2,1,0:T(8,128)(2,1)} %get-tuple-element.166), calls=%async_computation.9 | async-start | bytes 2162688 | tf_op jit(solution)/shard_map/all_to_all | solution.py:1634
  260.4 82.5 %all-gather.11.cloned.1.call-start = ((), (), s32[]{:S(2)}) async-start(), calls=%async_computation.15 | async-start | bytes 4460544 | tf_op jit(solution)/shard_map/all_gather | solution.py:1986
  276.9 25.6 %all-to-all-start.11 = ((f32[8,6,32,128]{3,2,1,0:T(8,128)}), f32[8,6,32,128]{3,2,1,0:T(8,128)S(1)}, u32[]{:S(2)}, u32[]{:S(2)}) async-start(f32[8,6,32,128]{3,2,1,0:T(8,128)} %get-tuple-element.169), calls=%async_computation.11 | async-start | bytes 1572864 | tf_op jit(solution)/shard_map/all_to_all | solution.py:1634
  311.6 10.9 %all-to-all-start.10 = ((f32[8,2,32,128]{3,2,1,0:T(8,128)}), f32[8,2,32,128]{3,2,1,0:T(8,128)S(1)}, u32[]{:S(2)}, u32[]{:S(2)}) async-start(f32[8,2,32,128]{3,2,1,0:T(8,128)} %get-tuple-element.173), calls=%async_computation.10 | async-start | bytes 524288 | tf_op jit(solution)/shard_map/all_to_all | solution.py:1634
  315.0 7.4 %copy-start.4 = (f32[8,2,256]{2,1,0:T(2,128)S(1)}, f32[8,2,256]{2,1,0:T(2,128)}, u32[]{:S(2)}) copy-start(f32[8,2,256]{2,1,0:T(2,128)} %all_to_all.70.sums_in_ref) | copy-start | bytes 49156
  315.0 7.4 %copy-start.5 = (f32[2,256]{1,0:T(2,128)S(1)}, f32[2,256]{1,0:T(2,128)}, u32[]{:S(2)}) copy-start(f32[2,256]{1,0:T(2,128)} %get-tuple-element.110.refs_8_.gain_ref.reduced_gain_ref) | copy-start | bytes 6148
  315.1 7.4 %copy-start.6 = (f32[3,512]{1,0:T(4,128)S(1)}, f32[3,512]{1,0:T(4,128)}, u32[]{:S(2)}) copy-start(f32[3,512]{1,0:T(4,128)} %get-tuple-element.124.moment_ref) | copy-start | bytes 18436
  322.6 10.3 %collective-permute-start.12 = (bf16[160,128]{1,0:T(8,128)(2,1)S(1)}, bf16[160,128]{1,0:T(8,128)(2,1)S(1)}, u32[]{:S(2)}, u32[]{:S(2)}) collective-permute-start(bf16[160,128]{1,0:T(8,128)(2,1)S(1)} %shard_map.152), channel_id=1, source_target_pairs={{0,1},{1,2},{2,3},{3,0},{4,5},{5,6},{6,7},{7,4},{8,9},{9,10},{10,1... | collective-permute-start | bytes 122888 | tf_op jit(solution)/shard_map/ppermute | solution.py:1625
  324.0 8.9 %collective-permute-start.13 = (bf16[160,128]{1,0:T(8,128)(2,1)S(1)}, bf16[160,128]{1,0:T(8,128)(2,1)S(1)}, u32[]{:S(2)}, u32[]{:S(2)}) collective-permute-start(bf16[160,128]{1,0:T(8,128)(2,1)S(1)} %shard_map.152), channel_id=1, source_target_pairs={{0,2},{1,3},{2,0},{3,1},{4,6},{5,7},{6,4},{7,5},{8,10},{9,11},{10,... | collective-permute-start | bytes 122888 | tf_op jit(solution)/shard_map/ppermute | solution.py:1625
  326.4 6.5 %collective-permute-start.14 = (bf16[160,128]{1,0:T(8,128)(2,1)S(1)}, bf16[160,128]{1,0:T(8,128)(2,1)S(1)}, u32[]{:S(2)}, u32[]{:S(2)}) collective-permute-start(bf16[160,128]{1,0:T(8,128)(2,1)S(1)} %shard_map.152), channel_id=1, source_target_pairs={{0,3},{1,0},{2,1},{3,2},{4,7},{5,4},{6,5},{7,6},{8,11},{9,8},{10,9... | collective-permute-start | bytes 122888 | tf_op jit(solution)/shard_map/ppermute | solution.py:1625
  333.0 16.7 %collective-permute-start.15 = (bf16[640,128]{1,0:T(8,128)(2,1)S(1)}, bf16[640,128]{1,0:T(8,128)(2,1)S(1)}, u32[]{:S(2)}, u32[]{:S(2)}) collective-permute-start(bf16[640,128]{1,0:T(8,128)(2,1)S(1)} %constant_dynamic-update-slice_fusion), channel_id=1, source_target_pairs={{0,8},{4,12},{8,0},{12,4},{16,24},{20,28},{24,16},{28,20},{1,9},{5... | collective-permute-start | bytes 491528 | tf_op jit(solution)/shard_map/ppermute | solution.py:1645
  335.0 14.7 %collective-permute-start.16 = (bf16[640,128]{1,0:T(8,128)(2,1)S(1)}, bf16[640,128]{1,0:T(8,128)(2,1)S(1)}, u32[]{:S(2)}, u32[]{:S(2)}) collective-permute-start(bf16[640,128]{1,0:T(8,128)(2,1)S(1)} %constant_dynamic-update-slice_fusion), channel_id=1, source_target_pairs={{0,16},{4,20},{8,24},{12,28},{16,0},{20,4},{24,8},{28,12},{1,17},{... | collective-permute-start | bytes 491528 | tf_op jit(solution)/shard_map/ppermute | solution.py:1645
  336.5 13.2 %collective-permute-start.17 = (bf16[640,128]{1,0:T(8,128)(2,1)S(1)}, bf16[640,128]{1,0:T(8,128)(2,1)S(1)}, u32[]{:S(2)}, u32[]{:S(2)}) collective-permute-start(bf16[640,128]{1,0:T(8,128)(2,1)S(1)} %constant_dynamic-update-slice_fusion), channel_id=1, source_target_pairs={{0,24},{4,28},{8,16},{12,20},{16,8},{20,12},{24,0},{28,4},{1,25},{... | collective-permute-start | bytes 491528 | tf_op jit(solution)/shard_map/ppermute | solution.py:1645
  349.8 2.2 collective-permute-start.18
  (3 other events, 1.9 us)
Sparse Core Ops, SparseCore 0:
  134.1 77.8 all-gather.6
  215.4 57.2 all-gather.8
  277.0 65.7 all-gather.10

commit v4 on v3

--- a/solution.py
+++ b/solution.py
@@ -1429,7 +1429,7 @@
     out_ref[4 * size :, :] = rest[2].astype(BF16)
 
 
-def write_taps(read, slots, mid_ref, small_ref, mid_out, small_out, sem_ref):
+def write_taps(read, slots, arriving, mid_ref, small_ref, mid_out, small_out, sem_ref):
     half = MID_IN // 2
 
     def leaving(tap):
@@ -1440,6 +1440,8 @@
 
     for tap in range(TAPS):
         part, slot = divmod(tap, slots)
+        if slot == 0:
+            arriving[part].wait()
         base = slot * TAP_ROWS
         folded = read(part, base + 2 * MID_IN, half)
         mid_ref[tap, :, 0:128] = read(part, base, MID_IN)
@@ -1449,8 +1451,22 @@
         small_ref[tap] = read(part, base + 2 * MID_IN + half, SMALL_IN)
         for copy in leaving(tap):
             copy.start()
-    pltpu.make_async_copy(mid_ref, mid_out, sem_ref.at[0]).wait()
-    pltpu.make_async_copy(small_ref, small_out, sem_ref.at[1]).wait()
+    for copy in arriving[-(-TAPS // slots) :]:
+        copy.wait()
+    return [
+        pltpu.make_async_copy(mid_ref, mid_out, sem_ref.at[0]),
+        pltpu.make_async_copy(small_ref, small_out, sem_ref.at[1]),
+    ]
+
+
+def parts_of(clips, far, ref, sem_ref):
+    copies = []
+    for part in range(far.shape[0] // clips):
+        at = pl.ds(part * clips, clips)
+        copies.append(pltpu.make_async_copy(far.at[at], ref.at[at], sem_ref.at[part]))
+    for copy in copies:
+        copy.start()
+    return copies
 
 
 def write_point(read, parts, kept, point_ref, wide_ref):
@@ -1498,15 +1514,21 @@
     return read
 
 
-def unpack_second(clips, slots, shares_ref, mid_out, small_out, mid_ref, small_ref, sem_ref):
+def unpack_second(clips, slots, far, mid_out, small_out, shares_ref, mid_ref, small_ref, sem_ref, in_sem):
+    arriving = parts_of(clips, far, shares_ref, in_sem)
     read = share_reader(shares_ref, clips, 0, shares_ref.shape[1])
-    write_taps(read, slots, mid_ref, small_ref, mid_out.at[1], small_out.at[1], sem_ref)
-
-
-def unpack_first(parts, clips, slots, share, shares_ref, *refs):
+    leaving = write_taps(
+        read, slots, arriving, mid_ref, small_ref, mid_out.at[1], small_out.at[1], sem_ref
+    )
+    for copy in leaving:
+        copy.wait()
+
+
+def unpack_first(parts, clips, slots, share, far, *refs):
     totals, refs = (refs[:4], refs[4:])
     mid_in, small_in, mid_out, small_out, point_out, gain_out, shift_out, *refs = refs
-    mid_ref, small_ref, point_ref, wide_ref, sem_ref = refs
+    shares_ref, mid_ref, small_ref, point_ref, wide_ref, sem_ref, in_sem = refs
+    arriving = parts_of(clips, far, shares_ref, in_sem)
     for block in range(2):
         outer_ref, reduced_ref = totals[2 * block : 2 * block + 2]
         for row, out in enumerate((shift_out, gain_out)):
@@ -1516,13 +1538,16 @@
             out[at, 448:576] = outer_ref[line, 768:896]
             out[at, 576:896] = outer_ref[line, 256:576]
             out[at, 896:1024] = outer_ref[line, 640:768]
+    read = share_reader(shares_ref, clips, 0, share)
+    leaving = write_taps(
+        read, slots, arriving, mid_ref, small_ref, mid_out.at[0], small_out.at[0], sem_ref
+    )
     read = share_reader(shares_ref, clips, share, shares_ref.shape[1] - share)
     write_point(read, parts, OUTER // parts, point_ref, wide_ref)
     last = pltpu.make_async_copy(point_ref, point_out.at[1], sem_ref.at[2])
     last.start()
-    read = share_reader(shares_ref, clips, 0, share)
-    write_taps(read, slots, mid_ref, small_ref, mid_out.at[0], small_out.at[0], sem_ref)
-    last.wait()
+    for copy in (*leaving, last):
+        copy.wait()
 
 
 def unpack_point(parts, clips, kept, place_ref, clip_ref, mine_ref, other_ref, point_in, point_out, buffer_ref, point_ref, wide_ref, sem_ref):
@@ -2027,7 +2052,13 @@
     mid_grad, small_grad = call(
         functools.partial(unpack_second, clips, taps_each),
         outs[:2],
-        [*tap_scratch, pltpu.SemaphoreType.DMA((2,))],
+        [
+            pltpu.VMEM(whole_small.shape, BF16),
+            *tap_scratch,
+            pltpu.SemaphoreType.DMA((2,)),
+            pltpu.SemaphoreType.DMA((parts,)),
+        ],
+        far=(0,),
         far_out=(0, 1),
         cost=5,
     )(whole_small)
@@ -2036,7 +2067,14 @@
     mid_grad, small_grad, point_grad, gain_grad, shift_grad = call(
         functools.partial(unpack_first, parts, clips, taps_each, tap_share),
         (*outs, norms, norms),
-        [*tap_scratch, *point_scratch, pltpu.SemaphoreType.DMA((3,))],
+        [
+            pltpu.VMEM(whole.shape, BF16),
+            *tap_scratch,
+            *point_scratch,
+            pltpu.SemaphoreType.DMA((3,)),
+            pltpu.SemaphoreType.DMA((parts,)),
+        ],
+        far=(0,),
         far_out=(0, 1, 2),
         aliases={5: 0, 6: 1},
         cost=6,

time: 362 us -> 362 us (level)
  transfers between devices with their start and end apart: 29 -> 29, of which waited for: 9 -> 11; matrix products, arithmetic and copies ran while one was open for 0% -> 0% of each run, Pallas kernels for 42% -> 42%
where the time goes in v4:
time: 362 us; the launch traced here: 360 us
  Pallas kernels  161 us (44%)
  waiting for transfers between devices  72.3 us (20%)
  blocking collectives  52.9 us (15%)
  starting transfers between devices  52.3 us (14%)
  between operations  14.9 us (4%)
  local copies, waits for them, and re-layouts  4.44 us (1%)
    pallas_call x21, Pallas kernels, run(): pl.pallas_call(body, out_shape=jax.tree.map(placed, out_shape), in_specs=...  161 us
    all_to_all x6, blocking collectives, exchange(): return lax.all_to_all(values, 'dp', 0, 0, tiled=True)  52.9 us
    all_to_all x1, waiting for transfers between devices, on_device(): by_pairs = lax.all_to_all(turned, 'branch', 0, 0, tiled=True)  24.4 us
    all_to_all x6, starting transfers between devices, exchange(): return lax.all_to_all(values, 'dp', 0, 0, tiled=True)  21.2 us
    ppermute x15, starting transfers between devices, spread_over(): received.append(lax.ppermute(values, axis, perm))  20.6 us
    all_to_all x6, waiting for transfers between devices, exchange(): return lax.all_to_all(values, 'dp', 0, 0, tiled=True)  20 us
    ppermute x15, waiting for transfers between devices, spread_over(): received.append(lax.ppermute(values, axis, perm))  19.1 us
  transfers between devices with their start and end apart: 29, of which 11 were waited for; matrix products, arithmetic and copies ran while one was open for 0% of the time, Pallas kernels for 42%

profile of v4, /device:TPU:0, one launch (start us, length us, event | category | flops | bytes accessed | tf_op | source)
XLA Modules:
  0.0 359.8 jit_solution(4155919785060809797)
XLA Ops:
  7.2 3.2 shard_map.135.x_far.refs_3_
  10.4 6.3 %all-to-all-start = ((bf16[4,208,896]{2,1,0:T(8,128)(2,1)}), bf16[4,208,896]{2,1,0:T(8,128)(2,1)S(1)}, u32[]{:S(2)}, u32[]{:S(2)}) async-start(bf16[4,208,896]{2,1,0:T(8,128)(2,1)} %shard_map.135.x_far.refs_3_), calls=%async_computation | async-start | bytes 2981888 | tf_op jit(solution)/shard_map/all_to_all | solution.py:1693
  17.4 10.1 %shard_map.136 = (bf16[9,512,256]{2,1,0:T(8,128)(2,1)}, bf16[3,512,256]{2,1,0:T(8,128)(2,1)}, bf16[1152,128]{1,0:T(8,128)(2,1)}, bf16[1152,128]{1,0:T(8,128)(2,1...) custom-call(bf16[2,27,160,320]{3,2,1,0:T(8,128)(2,1)} %mid_in.1, ...), custom_call_target="tpu_custom_call" | custom-call | bytes 15000000 | tf_op jit(solution)/shard_map/pallas_call | solution.py:66
  27.5 24.4 %all-to-all-done.x_ref = bf16[4,208,896]{2,1,0:T(8,128)(2,1)S(1)} async-done(((bf16[4,208,896]{2,1,0:T(8,128)(2,1)}), bf16[4,208,896]{2,1,0:T(8,128)(2,1)S(1)}, u32[]{:S(2)}, u32[]{:S(2)}) %all-to-all-start) | async-done | bytes 1490976 | tf_op jit(solution)/shard_map/all_to_all | solution.py:1693
  53.3 2.5 shard_map.137
  56.7 2.0 collective-permute-start.1
  58.7 1.8 collective-permute-start.2
  60.5 8.5 %all_to_all.65 = f32[8,3,512]{2,1,0:T(4,128)S(1)} all-to-all(f32[8,3,512]{2,1,0:T(4,128)S(1)} %get-tuple-element.108), channel_id=1, replica_groups=mesh['dp'=8,'branch'=4] {'dp'}, dimensions={0} | all-to-all | bytes 98304 | tf_op jit(solution)/shard_map/all_to_all | solution.py:1659
  71.2 12.0 %collective-permute-done.3.refs_5_.refs_1_ = f32[3,512]{1,0:T(4,128)S(1)} collective-permute-done((f32[3,512]{1,0:T(4,128)S(1)}, f32[3,512]{1,0:T(4,128)S(1)}, u32[]{:S(2)}, u32[]{:S(2)}) %collective-permute-start.3) | collective-permute-done | bytes 6176 | tf_op jit(solution)/shard_map/ppermute | solution.py:1650
  83.2 6.9 %collective-permute-done.4.refs_6_.refs_2_ = f32[3,512]{1,0:T(4,128)S(1)} collective-permute-done((f32[3,512]{1,0:T(4,128)S(1)}, f32[3,512]{1,0:T(4,128)S(1)}, u32[]{:S(2)}, u32[]{:S(2)}) %collective-permute-start.4) | collective-permute-done | bytes 6176 | tf_op jit(solution)/shard_map/ppermute | solution.py:1650
  92.6 2.8 collective-permute-start.8
  95.5 25.1 %shard_map.138 = (bf16[3136,256]{1,0:T(8,128)(2,1)}, bf16[1,3872,512]{2,1,0:T(8,128)(2,1)}, bf16[1,3872,128]{2,1,0:T(8,128)(2,1)}, f32[3136,512]{1,0:T(8,128)}, f32[2,512]{1,0:T(2,128)}) custom-call(s32[1]{0:T(128)S(6)} %copy.27.length_ref, s32[1]{0:T(128)} %bitcast.place_ref, bf16[1376,128]{1,0:T(8,128)(2,1)} %copy-done.2, bf16[1376,128]{1,0:T(8,128)(2,1)} %copy-done.7, ...), custom_call_target="tpu_custom_call" | custom-call | bytes 120000000 | tf_op jit(solution)/shard_map/pallas_call | solution.py:66
  121.5 3.9 %shard_map.139 = (f32[3136,128]{1,0:T(8,128)}, f32[8,2,640]{2,1,0:T(2,128)}) custom-call(s32[1]{0:T(128)S(6)} %copy.27.length_ref, s32[1]{0:T(128)} %bitcast.place_ref, bf16[912,128]{1,0:T(8,128)(2,1)} %copy-done.3, bf16[912,128]{1,0:T(8,128)(2,1)} %copy-done.10, bf16[912,128]{1,0:T(8,128)(2,1)} %copy-done.11, bf16[912,128]{1,0:T(8,128)(2,1)} %copy-done.12, ...), custom_call_target="tpu_custom_call" | custom-call | bytes 15000000 | tf_op jit(solution)/shard_map/pallas_call | solution.py:66
  125.4 3.7 %all-to-all-start.2 = ((f32[8,2,640]{2,1,0:T(2,128)}), f32[8,2,640]{2,1,0:T(2,128)S(1)}, u32[]{:S(2)}, u32[]{:S(2)}) async-start(f32[8,2,640]{2,1,0:T(2,128)} %get-tuple-element.116), calls=%async_computation.2 | async-start | bytes 81920 | tf_op jit(solution)/shard_map/all_to_all | solution.py:1659
  129.1 3.2 shard_map.140
  132.4 1.6 all-to-all-done.2.sums_in_ref
  134.7 3.2 collective-permute-start.11
  137.9 11.9 %shard_map.141 = (bf16[448,640]{1,0:T(8,128)(2,1)}, bf16[3136,640]{1,0:T(8,128)(2,1)}, bf16[3136,640]{1,0:T(8,128)(2,1)}, f32[3,896]{1,0:T(4,128)}, bf16[448,640]{1,0:T(8,128)(2,1)}, /*index=5*/bf16[448,640]{1,0:T(8,128)(2,1)}) custom-call(s32[1]{0:T(128)S(6)} %copy.27.length_ref, f32[3136,128]{1,0:T(8,128)} %get-tuple-element.122.q_far, ...), custom_call_target="tpu_custom_call" | custom-call | bytes 15000000 | tf_op jit(solution)/shard_map/pallas_call | solution.py:66
  150.5 4.3 %shard_map.142 = (f32[448,640]{1,0:T(8,128)}, f32[8,3,640]{2,1,0:T(4,128)}, bf16[448,896]{1,0:T(8,128)(2,1)}) custom-call(s32[1]{0:T(128)S(6)} %select_n.12.length_ref, s32[1]{0:T(128)} %bitcast.place_ref, f32[1]{0:T(128)S(6)} %mul.20.count_ref, bf16[128,256]{1,0:T(8,128)(2,1)} %get-tuple-element.121.refs_0_, bf16[128,256]{1,0:T(8,128)(2,1)} %copy-done.16, ...), custom_call_target="tpu_custom_call" | custom-call | bytes 15000000 | tf_op jit(solution)/shard_map/pallas_call | solution.py:66
  154.9 9.1 %all_to_all.66.sums_in_ref = f32[8,3,640]{2,1,0:T(4,128)} all-to-all(f32[8,3,640]{2,1,0:T(4,128)} %get-tuple-element.129), channel_id=1, replica_groups=mesh['dp'=8,'branch'=4] {'dp'}, dimensions={0} | all-to-all | bytes 122880 | tf_op jit(solution)/shard_map/all_to_all | solution.py:1659
  163.9 6.7 %shard_map.143 = (bf16[448,256]{1,0:T(8,128)(2,1)}, bf16[2,736,512]{2,1,0:T(8,128)(2,1)}, bf16[2,736,128]{2,1,0:T(8,128)(2,1)}, f32[448,512]{1,0:T(8,128)}, f32[8,2,512]{2,1,0:T(2,128)}, /*index=5*/f32[3,640]{1,0:T(4,128)}) custom-call(s32[1]{0:T(128)S(6)} %select_n.12.length_ref, f32[448,640]{1,0:T(8,128)} %get-tuple-element.128.q_ref, ...), custom_call_target="tpu_custom_call" | custom-call | bytes 15000000 | tf_op jit(solution)/shard_map/pallas_call | solution.py:66
  170.7 8.8 %all_to_all.67.sums_in_ref = f32[8,2,512]{2,1,0:T(2,128)} all-to-all(f32[8,2,512]{2,1,0:T(2,128)} %get-tuple-element.135), channel_id=1, replica_groups=mesh['dp'=8,'branch'=4] {'dp'}, dimensions={0} | all-to-all | bytes 65536 | tf_op jit(solution)/shard_map/all_to_all | solution.py:1659
  179.4 4.8 %shard_map.144 = (bf16[49,8,832]{2,1,0:T(8,128)(2,1)}, bf16[448,896]{1,0:T(8,128)(2,1)}, bf16[448,896]{1,0:T(8,128)(2,1)}, f32[3,896]{1,0:T(4,128)}, f32[8,2,896]{2,1,0:T(2,128)}) custom-call(s32[1]{0:T(128)S(6)} %select_n.12.length_ref, f32[448,640]{1,0:T(8,128)} %get-tuple-element.128.q_ref, f32[448,512]{1,0:T(8,128)} %get-tuple-element.133.e_ref, ...), custom_call_target="tpu_custom_call" | custom-call | bytes 15000000 | tf_op jit(solution)/shard_map/pallas_call | solution.py:66
  184.2 3.3 all-to-all-start.5
  187.6 4.9 %all-to-all-done.5.sums_in_ref = f32[8,2,896]{2,1,0:T(2,128)S(1)} async-done(((f32[8,2,896]{2,1,0:T(2,128)}), f32[8,2,896]{2,1,0:T(2,128)S(1)}, u32[]{:S(2)}, u32[]{:S(2)}) %all-to-all-start.5) | async-done | bytes 57376 | tf_op jit(solution)/shard_map/all_to_all | solution.py:1659
  193.1 5.3 %shard_map.145 = (bf16[2,736,512]{2,1,0:T(8,128)(2,1)}, f32[2,896]{1,0:T(2,128)}, bf16[8,384,128]{2,1,0:T(8,128)(2,1)}) custom-call(s32[1]{0:T(128)S(6)} %select_n.12.length_ref, s32[1]{0:T(128)S(6)} %mul.25.first_ref, bf16[448,896]{1,0:T(8,128)(2,1)} %get-tuple-element.139.h_far, f32[3,896]{1,0:T(4,128)} %get-tuple-element.140.outer_ref, ...), custom_call_target="tpu_custom_call" | custom-call | bytes 24000000 | tf_op jit(solution)/shard_map/pallas_call | solution.py:66
  198.5 3.6 all-to-all-start.6
  202.1 6.3 %shard_map.146 = (bf16[448,256]{1,0:T(8,128)(2,1)}, f32[8,2,256]{2,1,0:T(2,128)}) custom-call(s32[1]{0:T(128)S(6)} %select_n.12.length_ref, bf16[2,736,512]{2,1,0:T(8,128)(2,1)} %get-tuple-element.147.d_ref, bf16[448,256]{1,0:T(8,128)(2,1)} %get-tuple-element.146.reduced_ref.reduced_far, f32[2,256]{1,0:T(2,128)} %get-tuple-element.110.refs_8_.gain_ref.reduced_gain_ref, ...), custom_call_target="tpu_custom_call" | custom-call | bytes 24000000 | tf_op jit(solution)/shard_map/pallas_call | solution.py:66
  208.3 6.2 %all-to-all-done.6 = bf16[8,384,128]{2,1,0:T(8,128)(2,1)S(1)} async-done(((bf16[8,384,128]{2,1,0:T(8,128)(2,1)}), bf16[8,384,128]{2,1,0:T(8,128)(2,1)S(1)}, u32[]{:S(2)}, u32[]{:S(2)}) %all-to-all-start.6) | async-done | bytes 786464 | tf_op jit(solution)/shard_map/all_to_all | solution.py:1659
  215.3 8.5 %all_to_all.68.sums_in_ref = f32[8,2,256]{2,1,0:T(2,128)} all-to-all(f32[8,2,256]{2,1,0:T(2,128)} %get-tuple-element.152), channel_id=1, replica_groups=mesh['dp'=8,'branch'=4] {'dp'}, dimensions={0} | all-to-all | bytes 32768 | tf_op jit(solution)/shard_map/all_to_all | solution.py:1659
  223.8 7.8 %shard_map.147 = (bf16[448,896]{1,0:T(8,128)(2,1)}, bf16[8,144,128]{2,1,0:T(8,128)(2,1)}, f32[2,256]{1,0:T(2,128)}, f32[8,2,896]{2,1,0:T(2,128)}) custom-call(s32[1]{0:T(128)S(6)} %select_n.12.length_ref, s32[1]{0:T(128)} %bitcast.place_ref, bf16[448,896]{1,0:T(8,128)(2,1)} %get-tuple-element.139.h_far, f32[3,896]{1,0:T(4,128)} %get-tuple-element.140.outer_ref, ...), custom_call_target="tpu_custom_call" | custom-call | bytes 30000000 | tf_op jit(solution)/shard_map/pallas_call | solution.py:66
  231.6 8.9 %all_to_all.69.sums_in_ref = f32[8,2,896]{2,1,0:T(2,128)} all-to-all(f32[8,2,896]{2,1,0:T(2,128)} %get-tuple-element.158), channel_id=1, replica_groups=mesh['dp'=8,'branch'=4] {'dp'}, dimensions={0} | all-to-all | bytes 114688 | tf_op jit(solution)/shard_map/all_to_all | solution.py:1659
  240.6 16.2 %shard_map.148 = (bf16[1,3872,512]{2,1,0:T(8,128)(2,1)}, f32[2,896]{1,0:T(2,128)}, bf16[8,528,128]{2,1,0:T(8,128)(2,1)}) custom-call(s32[1]{0:T(128)S(6)} %copy.27.length_ref, s32[1]{0:T(128)S(6)} %mul.25.first_ref, bf16[3136,640]{1,0:T(8,128)(2,1)} %get-tuple-element.137.h_far, f32[3,896]{1,0:T(4,128)} %get-tuple-element.138.outer_ref, ...), custom_call_target="tpu_custom_call" | custom-call | bytes 54000000 | tf_op jit(solution)/shard_map/pallas_call | solution.py:66
  256.8 3.6 all-to-all-start.9
  260.6 8.2 %shard_map.149 = (bf16[3136,384]{1,0:T(8,128)(2,1)}, f32[8,6,32,128]{3,2,1,0:T(8,128)}) custom-call(s32[1]{0:T(128)S(6)} %copy.27.length_ref, f32[3,896]{1,0:T(4,128)} %get-tuple-element.138.outer_ref, f32[2,896]{1,0:T(2,128)} %get-tuple-element.167.total_ref.refs_0_, f32[2,896]{1,0:T(2,128)} %get-tuple-element.118.gain_ref, ...), custom_call_target="tpu_custom_call" | custom-call | bytes 24000000 | tf_op jit(solution)/shard_map/pallas_call | solution.py:66
  268.8 7.3 %all-to-all-done.9 = bf16[8,528,128]{2,1,0:T(8,128)(2,1)S(1)} async-done(((bf16[8,528,128]{2,1,0:T(8,128)(2,1)}), bf16[8,528,128]{2,1,0:T(8,128)(2,1)S(1)}, u32[]{:S(2)}, u32[]{:S(2)}) %all-to-all-start.9) | async-done | bytes 1081376 | tf_op jit(solution)/shard_map/all_to_all | solution.py:1659
  276.9 3.6 all-to-all-start.11
  280.5 22.0 %shard_map.150 = (bf16[3136,256]{1,0:T(8,128)(2,1)}, f32[8,2,256]{2,1,0:T(2,128)}, f32[8,2,32,128]{3,2,1,0:T(8,128)}) custom-call(s32[1]{0:T(128)S(6)} %copy.27.length_ref, bf16[1,3872,512]{2,1,0:T(8,128)(2,1)} %get-tuple-element.171.d_ref, bf16[3136,256]{1,0:T(8,128)(2,1)} %get-tuple-element.168.reduced_far.reduced_ref.h_far, ...), custom_call_target="tpu_custom_call" | custom-call | bytes 66000000 | tf_op jit(solution)/shard_map/pallas_call | solution.py:66
  302.6 9.1 %all_to_all.70.sums_in_ref = f32[8,2,256]{2,1,0:T(2,128)} all-to-all(f32[8,2,256]{2,1,0:T(2,128)} %get-tuple-element.175), channel_id=1, replica_groups=mesh['dp'=8,'branch'=4] {'dp'}, dimensions={0} | all-to-all | bytes 32768 | tf_op jit(solution)/shard_map/all_to_all | solution.py:1659
  311.6 3.4 all-to-all-start.10
  315.1 7.4 %shard_map.151 = (bf16[3136,208]{1,0:T(8,128)(2,1)}, f32[2,256]{1,0:T(2,128)}) custom-call(s32[1]{0:T(128)S(6)} %copy.27.length_ref, s32[1]{0:T(128)} %bitcast.place_ref, f32[3,512]{1,0:T(4,128)} %get-tuple-element.124.moment_ref, f32[8,2,256]{2,1,0:T(2,128)} %all_to_all.70.sums_in_ref, f32[2,256]{1,0:T(2,128)} %get-tuple-element.110.refs_8_.gain_ref.reduced_gain_ref, ...), custom_call_target="tpu_custom_call" | custom-call | bytes 24000000 | tf_op jit(solution)/shard_map/pallas_call | solution.py:66
  324.0 2.4 collective-permute-start.13
  328.0 4.1 %shard_map.153 = (f32[2,27,160,320]{3,2,1,0:T(8,128)}, f32[2,27,32,128]{3,2,1,0:T(8,128)}) custom-call(bf16[32,384,128]{2,1,0:T(8,128)(2,1)} %bitcast.32), custom_call_target="tpu_custom_call" | custom-call | bytes 15000000 | tf_op jit(solution)/shard_map/pallas_call | solution.py:66
  332.4 2.0 collective-permute-start.15
  336.0 6.9 %all-gather.11.cloned.1.call-done = bf16[16896,128]{1,0:T(8,128)(2,1)} async-done(((bf16[528,128]{1,0:T(8,128)(2,1)}), bf16[16896,128]{1,0:T(8,128)(2,1)}) %all-gather.11.cloned.1.call-update) | async-done | bytes 4325392 | tf_op jit(solution)/shard_map/all_gather | solution.py:2011
  342.9 6.2 %shard_map.154 = (f32[2,27,160,320]{3,2,1,0:T(8,128)}, f32[2,27,32,128]{3,2,1,0:T(8,128)}, f32[2,576,832]{2,1,0:T(8,128)}, f32[2,1024]{1,0:T(2,128)}, f32[2,1024]{1,0:T(2,128)}) custom-call(bf16[32,528,128]{2,1,0:T(8,128)(2,1)} %bitcast.30, f32[2,896]{1,0:T(2,128)} %get-tuple-element.167.total_ref.refs_0_, ...), custom_call_target="tpu_custom_call", output_to_operand_aliasing={{0}: (5, {}), {1}: (6, {})} | custom-call | bytes 18000000 | tf_op jit(solution)/shard_map/pallas_call | solution.py:66
  349.6 1.8 collective-permute-done.18.other_ref
  351.4 1.8 shard_map.155
  (95 shorter events, 17.0 us)
Async XLA Ops:
  10.4 41.5 %all-to-all-start = ((bf16[4,208,896]{2,1,0:T(8,128)(2,1)}), bf16[4,208,896]{2,1,0:T(8,128)(2,1)S(1)}, u32[]{:S(2)}, u32[]{:S(2)}) async-start(bf16[4,208,896]{2,1,0:T(8,128)(2,1)} %shard_map.135.x_far.refs_3_), calls=%async_computation | async-start | bytes 2981888 | tf_op jit(solution)/shard_map/all_to_all | solution.py:1693
  51.9 1.3 copy-start
  55.7 0.9 copy-start.1
  56.7 38.8 %copy-start.2 = (bf16[1376,128]{1,0:T(8,128)(2,1)}, bf16[1376,128]{1,0:T(8,128)(2,1)S(1)}, u32[]{:S(2)}) copy-start(bf16[1376,128]{1,0:T(8,128)(2,1)S(1)} %get-tuple-element.107.refs_0_) | copy-start | bytes 1056772
  56.7 64.0 %copy-start.3 = (bf16[912,128]{1,0:T(8,128)(2,1)}, bf16[912,128]{1,0:T(8,128)(2,1)S(1)}, u32[]{:S(2)}) copy-start(bf16[912,128]{1,0:T(8,128)(2,1)S(1)} %get-tuple-element.109.refs_0_) | copy-start | bytes 700420
  56.7 33.4 %collective-permute-start = (bf16[1376,128]{1,0:T(8,128)(2,1)S(1)}, bf16[1376,128]{1,0:T(8,128)(2,1)S(1)}, u32[]{:S(2)}, u32[]{:S(2)}) collective-permute-start(bf16[1376,128]{1,0:T(8,128)(2,1)S(1)} %get-tuple-element.107.refs_0_), channel_id=1, source_target_pairs={{0,1},{1,2},{2,3},{3,0},{4,5},{5,6},{6,7},{7,4},{8,9},{9,10},{10,1... | collective-permute-start | bytes 1056776 | tf_op jit(solution)/shard_map/ppermute | solution.py:1650
  56.7 33.4 %collective-permute-start.1 = (bf16[1376,128]{1,0:T(8,128)(2,1)S(1)}, bf16[1376,128]{1,0:T(8,128)(2,1)S(1)}, u32[]{:S(2)}, u32[]{:S(2)}) collective-permute-start(bf16[1376,128]{1,0:T(8,128)(2,1)S(1)} %get-tuple-element.107.refs_0_), channel_id=1, source_target_pairs={{0,2},{1,3},{2,0},{3,1},{4,6},{5,7},{6,4},{7,5},{8,10},{9,11},{10,... | collective-permute-start | bytes 1056776 | tf_op jit(solution)/shard_map/ppermute | solution.py:1650
  58.7 31.4 %collective-permute-start.2 = (bf16[1376,128]{1,0:T(8,128)(2,1)S(1)}, bf16[1376,128]{1,0:T(8,128)(2,1)S(1)}, u32[]{:S(2)}, u32[]{:S(2)}) collective-permute-start(bf16[1376,128]{1,0:T(8,128)(2,1)S(1)} %get-tuple-element.107.refs_0_), channel_id=1, source_target_pairs={{0,3},{1,0},{2,1},{3,2},{4,7},{5,4},{6,5},{7,6},{8,11},{9,8},{10,9... | collective-permute-start | bytes 1056776 | tf_op jit(solution)/shard_map/ppermute | solution.py:1650
  69.1 26.4 %copy-start.15 = (f32[3,512]{1,0:T(4,128)}, f32[3,512]{1,0:T(4,128)S(1)}, u32[]{:S(2)}) copy-start(f32[3,512]{1,0:T(4,128)S(1)} %reduce_sum.33.refs_4_.refs_0_) | copy-start | bytes 18436
  69.1 14.2 %collective-permute-start.3 = (f32[3,512]{1,0:T(4,128)S(1)}, f32[3,512]{1,0:T(4,128)S(1)}, u32[]{:S(2)}, u32[]{:S(2)}) collective-permute-start(f32[3,512]{1,0:T(4,128)S(1)} %reduce_sum.33.refs_4_.refs_0_), channel_id=1, source_target_pairs={{0,1},{1,2},{2,3},{3,0},{4,5},{5,6},{6,7},{7,4},{8,9},{9,10},{10,1... | collective-permute-start | bytes 18440 | tf_op jit(solution)/shard_map/ppermute | solution.py:1650
  69.7 20.4 %collective-permute-start.4 = (f32[3,512]{1,0:T(4,128)S(1)}, f32[3,512]{1,0:T(4,128)S(1)}, u32[]{:S(2)}, u32[]{:S(2)}) collective-permute-start(f32[3,512]{1,0:T(4,128)S(1)} %reduce_sum.33.refs_4_.refs_0_), channel_id=1, source_target_pairs={{0,2},{1,3},{2,0},{3,1},{4,6},{5,7},{6,4},{7,5},{8,10},{9,11},{10,... | collective-permute-start | bytes 18440 | tf_op jit(solution)/shard_map/ppermute | solution.py:1650
  83.2 12.2 %copy-start.19 = (f32[3,512]{1,0:T(4,128)}, f32[3,512]{1,0:T(4,128)S(1)}, u32[]{:S(2)}) copy-start(f32[3,512]{1,0:T(4,128)S(1)} %collective-permute-done.3.refs_5_.refs_1_) | copy-start | bytes 18436
  83.2 6.9 %collective-permute-start.5 = (f32[3,512]{1,0:T(4,128)S(1)}, f32[3,512]{1,0:T(4,128)S(1)}, u32[]{:S(2)}, u32[]{:S(2)}) collective-permute-start(f32[3,512]{1,0:T(4,128)S(1)} %reduce_sum.33.refs_4_.refs_0_), channel_id=1, source_target_pairs={{0,3},{1,0},{2,1},{3,2},{4,7},{5,4},{6,5},{7,6},{8,11},{9,8},{10,9... | collective-permute-start | bytes 18440 | tf_op jit(solution)/shard_map/ppermute | solution.py:1650
  90.1 5.4 %copy-start.20 = (f32[3,512]{1,0:T(4,128)}, f32[3,512]{1,0:T(4,128)S(1)}, u32[]{:S(2)}) copy-start(f32[3,512]{1,0:T(4,128)S(1)} %collective-permute-done.4.refs_6_.refs_2_) | copy-start | bytes 18436
  90.1 5.4 %copy-start.21 = (f32[3,512]{1,0:T(4,128)}, f32[3,512]{1,0:T(4,128)S(1)}, u32[]{:S(2)}) copy-start(f32[3,512]{1,0:T(4,128)S(1)} %collective-permute-done.5.refs_7_.refs_3_) | copy-start | bytes 18436
  90.1 5.4 %copy-start.7 = (bf16[1376,128]{1,0:T(8,128)(2,1)}, bf16[1376,128]{1,0:T(8,128)(2,1)S(1)}, u32[]{:S(2)}) copy-start(bf16[1376,128]{1,0:T(8,128)(2,1)S(1)} %collective-permute-done.refs_1_) | copy-start | bytes 1056772
  90.1 5.4 %copy-start.8 = (bf16[1376,128]{1,0:T(8,128)(2,1)}, bf16[1376,128]{1,0:T(8,128)(2,1)S(1)}, u32[]{:S(2)}) copy-start(bf16[1376,128]{1,0:T(8,128)(2,1)S(1)} %collective-permute-done.1.refs_2_) | copy-start | bytes 1056772
  90.1 5.4 %copy-start.9 = (bf16[1376,128]{1,0:T(8,128)(2,1)}, bf16[1376,128]{1,0:T(8,128)(2,1)S(1)}, u32[]{:S(2)}) copy-start(bf16[1376,128]{1,0:T(8,128)(2,1)S(1)} %collective-permute-done.2.refs_3_) | copy-start | bytes 1056772
  90.2 30.5 %collective-permute-start.6 = (bf16[912,128]{1,0:T(8,128)(2,1)S(1)}, bf16[912,128]{1,0:T(8,128)(2,1)S(1)}, u32[]{:S(2)}, u32[]{:S(2)}) collective-permute-start(bf16[912,128]{1,0:T(8,128)(2,1)S(1)} %get-tuple-element.109.refs_0_), channel_id=1, source_target_pairs={{0,1},{1,2},{2,3},{3,0},{4,5},{5,6},{6,7},{7,4},{8,9},{9,10},{10,1... | collective-permute-start | bytes 700424 | tf_op jit(solution)/shard_map/ppermute | solution.py:1650
  91.1 29.6 %collective-permute-start.7 = (bf16[912,128]{1,0:T(8,128)(2,1)S(1)}, bf16[912,128]{1,0:T(8,128)(2,1)S(1)}, u32[]{:S(2)}, u32[]{:S(2)}) collective-permute-start(bf16[912,128]{1,0:T(8,128)(2,1)S(1)} %get-tuple-element.109.refs_0_), channel_id=1, source_target_pairs={{0,2},{1,3},{2,0},{3,1},{4,6},{5,7},{6,4},{7,5},{8,10},{9,11},{10,... | collective-permute-start | bytes 700424 | tf_op jit(solution)/shard_map/ppermute | solution.py:1650
  92.6 28.1 %collective-permute-start.8 = (bf16[912,128]{1,0:T(8,128)(2,1)S(1)}, bf16[912,128]{1,0:T(8,128)(2,1)S(1)}, u32[]{:S(2)}, u32[]{:S(2)}) collective-permute-start(bf16[912,128]{1,0:T(8,128)(2,1)S(1)} %get-tuple-element.109.refs_0_), channel_id=1, source_target_pairs={{0,3},{1,0},{2,1},{3,2},{4,7},{5,4},{6,5},{7,6},{8,11},{9,8},{10,9... | collective-permute-start | bytes 700424 | tf_op jit(solution)/shard_map/ppermute | solution.py:1650
  120.7 0.7 copy-start.10
  120.7 0.7 copy-start.11
  120.7 0.8 copy-start.12
  125.4 8.6 %all-to-all-start.2 = ((f32[8,2,640]{2,1,0:T(2,128)}), f32[8,2,640]{2,1,0:T(2,128)S(1)}, u32[]{:S(2)}, u32[]{:S(2)}) async-start(f32[8,2,640]{2,1,0:T(2,128)} %get-tuple-element.116), calls=%async_computation.2 | async-start | bytes 81920 | tf_op jit(solution)/shard_map/all_to_all | solution.py:1659
  129.1 94.7 %all-gather.7.cloned.1.call-start = ((), (), s32[]{:S(2)}) async-start(), calls=%async_computation.13 | async-start | bytes 5242880 | tf_op jit(solution)/shard_map/all_gather | solution.py:1763
  134.0 3.9 %copy-start.14 = (f32[8,2,640]{2,1,0:T(2,128)}, f32[8,2,640]{2,1,0:T(2,128)S(1)}, u32[]{:S(2)}) copy-start(f32[8,2,640]{2,1,0:T(2,128)S(1)} %all-to-all-done.2.sums_in_ref) | copy-start | bytes 122884
  134.0 15.8 %collective-permute-start.9 = (bf16[128,256]{1,0:T(8,128)(2,1)}, bf16[128,256]{1,0:T(8,128)(2,1)S(1)}, u32[]{:S(2)}, u32[]{:S(2)}) collective-permute-start(bf16[128,256]{1,0:T(8,128)(2,1)} %get-tuple-element.121.refs_0_), channel_id=1, source_target_pairs={{0,1},{1,2},{2,3},{3,0},{4,5},{5,6},{6,7},{7,4},{8,9},{9,10},{10,1... | collective-permute-start | bytes 196616 | tf_op jit(solution)/shard_map/ppermute | solution.py:1650
  134.1 15.8 %collective-permute-start.10 = (bf16[128,256]{1,0:T(8,128)(2,1)}, bf16[128,256]{1,0:T(8,128)(2,1)S(1)}, u32[]{:S(2)}, u32[]{:S(2)}) collective-permute-start(bf16[128,256]{1,0:T(8,128)(2,1)} %get-tuple-element.121.refs_0_), channel_id=1, source_target_pairs={{0,2},{1,3},{2,0},{3,1},{4,6},{5,7},{6,4},{7,5},{8,10},{9,11},{10,... | collective-permute-start | bytes 196616 | tf_op jit(solution)/shard_map/ppermute | solution.py:1650
  134.7 15.1 %collective-permute-start.11 = (bf16[128,256]{1,0:T(8,128)(2,1)}, bf16[128,256]{1,0:T(8,128)(2,1)S(1)}, u32[]{:S(2)}, u32[]{:S(2)}) collective-permute-start(bf16[128,256]{1,0:T(8,128)(2,1)} %get-tuple-element.121.refs_0_), channel_id=1, source_target_pairs={{0,3},{1,0},{2,1},{3,2},{4,7},{5,4},{6,5},{7,6},{8,11},{9,8},{10,9... | collective-permute-start | bytes 196616 | tf_op jit(solution)/shard_map/ppermute | solution.py:1650
  149.9 0.6 copy-start.18
  184.2 8.3 %all-to-all-start.5 = ((f32[8,2,896]{2,1,0:T(2,128)}), f32[8,2,896]{2,1,0:T(2,128)S(1)}, u32[]{:S(2)}, u32[]{:S(2)}) async-start(f32[8,2,896]{2,1,0:T(2,128)} %get-tuple-element.141), calls=%async_computation.5 | async-start | bytes 114688 | tf_op jit(solution)/shard_map/all_to_all | solution.py:1659
  198.5 16.1 %all-to-all-start.6 = ((bf16[8,384,128]{2,1,0:T(8,128)(2,1)}), bf16[8,384,128]{2,1,0:T(8,128)(2,1)S(1)}, u32[]{:S(2)}, u32[]{:S(2)}) async-start(bf16[8,384,128]{2,1,0:T(8,128)(2,1)} %get-tuple-element.151), calls=%async_computation.6 | async-start | bytes 1572864 | tf_op jit(solution)/shard_map/all_to_all | solution.py:1659
  202.0 126.0 %all-gather.9.cloned.1.call-start = ((), (), s32[]{:S(2)}) async-start(), calls=%async_computation.14 | async-start | bytes 3244032 | tf_op jit(solution)/shard_map/all_gather | solution.py:1942
  256.8 19.3 %all-to-all-start.9 = ((bf16[8,528,128]{2,1,0:T(8,128)(2,1)}), bf16[8,528,128]{2,1,0:T(8,128)(2,1)S(1)}, u32[]{:S(2)}, u32[]{:S(2)}) async-start(bf16[8,528,128]{2,1,0:T(8,128)(2,1)} %get-tuple-element.166), calls=%async_computation.9 | async-start | bytes 2162688 | tf_op jit(solution)/shard_map/all_to_all | solution.py:1659
  260.4 82.5 %all-gather.11.cloned.1.call-start = ((), (), s32[]{:S(2)}) async-start(), calls=%async_computation.15 | async-start | bytes 4460544 | tf_op jit(solution)/shard_map/all_gather | solution.py:2011
  276.9 25.6 %all-to-all-start.11 = ((f32[8,6,32,128]{3,2,1,0:T(8,128)}), f32[8,6,32,128]{3,2,1,0:T(8,128)S(1)}, u32[]{:S(2)}, u32[]{:S(2)}) async-start(f32[8,6,32,128]{3,2,1,0:T(8,128)} %get-tuple-element.169), calls=%async_computation.11 | async-start | bytes 1572864 | tf_op jit(solution)/shard_map/all_to_all | solution.py:1659
  311.6 10.9 %all-to-all-start.10 = ((f32[8,2,32,128]{3,2,1,0:T(8,128)}), f32[8,2,32,128]{3,2,1,0:T(8,128)S(1)}, u32[]{:S(2)}, u32[]{:S(2)}) async-start(f32[8,2,32,128]{3,2,1,0:T(8,128)} %get-tuple-element.173), calls=%async_computation.10 | async-start | bytes 524288 | tf_op jit(solution)/shard_map/all_to_all | solution.py:1659
  315.0 7.4 %copy-start.4 = (f32[8,2,256]{2,1,0:T(2,128)S(1)}, f32[8,2,256]{2,1,0:T(2,128)}, u32[]{:S(2)}) copy-start(f32[8,2,256]{2,1,0:T(2,128)} %all_to_all.70.sums_in_ref) | copy-start | bytes 49156
  315.0 7.4 %copy-start.5 = (f32[2,256]{1,0:T(2,128)S(1)}, f32[2,256]{1,0:T(2,128)}, u32[]{:S(2)}) copy-start(f32[2,256]{1,0:T(2,128)} %get-tuple-element.110.refs_8_.gain_ref.reduced_gain_ref) | copy-start | bytes 6148
  315.1 7.4 %copy-start.6 = (f32[3,512]{1,0:T(4,128)S(1)}, f32[3,512]{1,0:T(4,128)}, u32[]{:S(2)}) copy-start(f32[3,512]{1,0:T(4,128)} %get-tuple-element.124.moment_ref) | copy-start | bytes 18436
  322.6 9.6 %collective-permute-start.12 = (bf16[160,128]{1,0:T(8,128)(2,1)S(1)}, bf16[160,128]{1,0:T(8,128)(2,1)S(1)}, u32[]{:S(2)}, u32[]{:S(2)}) collective-permute-start(bf16[160,128]{1,0:T(8,128)(2,1)S(1)} %shard_map.152), channel_id=1, source_target_pairs={{0,1},{1,2},{2,3},{3,0},{4,5},{5,6},{6,7},{7,4},{8,9},{9,10},{10,1... | collective-permute-start | bytes 122888 | tf_op jit(solution)/shard_map/ppermute | solution.py:1650
  324.0 8.3 %collective-permute-start.13 = (bf16[160,128]{1,0:T(8,128)(2,1)S(1)}, bf16[160,128]{1,0:T(8,128)(2,1)S(1)}, u32[]{:S(2)}, u32[]{:S(2)}) collective-permute-start(bf16[160,128]{1,0:T(8,128)(2,1)S(1)} %shard_map.152), channel_id=1, source_target_pairs={{0,2},{1,3},{2,0},{3,1},{4,6},{5,7},{6,4},{7,5},{8,10},{9,11},{10,... | collective-permute-start | bytes 122888 | tf_op jit(solution)/shard_map/ppermute | solution.py:1650
  326.4 6.0 %collective-permute-start.14 = (bf16[160,128]{1,0:T(8,128)(2,1)S(1)}, bf16[160,128]{1,0:T(8,128)(2,1)S(1)}, u32[]{:S(2)}, u32[]{:S(2)}) collective-permute-start(bf16[160,128]{1,0:T(8,128)(2,1)S(1)} %shard_map.152), channel_id=1, source_target_pairs={{0,3},{1,0},{2,1},{3,2},{4,7},{5,4},{6,5},{7,6},{8,11},{9,8},{10,9... | collective-permute-start | bytes 122888 | tf_op jit(solution)/shard_map/ppermute | solution.py:1650
  332.4 16.7 %collective-permute-start.15 = (bf16[640,128]{1,0:T(8,128)(2,1)S(1)}, bf16[640,128]{1,0:T(8,128)(2,1)S(1)}, u32[]{:S(2)}, u32[]{:S(2)}) collective-permute-start(bf16[640,128]{1,0:T(8,128)(2,1)S(1)} %constant_dynamic-update-slice_fusion), channel_id=1, source_target_pairs={{0,8},{4,12},{8,0},{12,4},{16,24},{20,28},{24,16},{28,20},{1,9},{5... | collective-permute-start | bytes 491528 | tf_op jit(solution)/shard_map/ppermute | solution.py:1670
  334.5 14.7 %collective-permute-start.16 = (bf16[640,128]{1,0:T(8,128)(2,1)S(1)}, bf16[640,128]{1,0:T(8,128)(2,1)S(1)}, u32[]{:S(2)}, u32[]{:S(2)}) collective-permute-start(bf16[640,128]{1,0:T(8,128)(2,1)S(1)} %constant_dynamic-update-slice_fusion), channel_id=1, source_target_pairs={{0,16},{4,20},{8,24},{12,28},{16,0},{20,4},{24,8},{28,12},{1,17},{... | collective-permute-start | bytes 491528 | tf_op jit(solution)/shard_map/ppermute | solution.py:1670
  335.9 13.2 %collective-permute-start.17 = (bf16[640,128]{1,0:T(8,128)(2,1)S(1)}, bf16[640,128]{1,0:T(8,128)(2,1)S(1)}, u32[]{:S(2)}, u32[]{:S(2)}) collective-permute-start(bf16[640,128]{1,0:T(8,128)(2,1)S(1)} %constant_dynamic-update-slice_fusion), channel_id=1, source_target_pairs={{0,24},{4,28},{8,16},{12,20},{16,8},{20,12},{24,0},{28,4},{1,25},{... | collective-permute-start | bytes 491528 | tf_op jit(solution)/shard_map/ppermute | solution.py:1670
  349.3 2.2 collective-permute-start.18
  (3 other events, 1.9 us)
Sparse Core Ops, SparseCore 0:
  134.1 77.8 all-gather.6
  215.4 57.2 all-gather.8
  277.0 65.7 all-gather.10

commit v5 on v4

--- a/solution.py
+++ b/solution.py
@@ -633,16 +633,15 @@
         for line in range(2):
             at = rows_at(number * slots.pair_rows + line * rows, rows)
             scaled, act, slope = normalize(u_ref[at, :], center, inverse, gain, shift, mask)
-            kept_ref[at, 0:DIRECT] = scaled.astype(BF16)
-            kept_ref[at, DIRECT : 2 * DIRECT] = slope.astype(BF16)
+            kept_ref[at, :] = scaled.astype(BF16)
             acts.append(act.astype(BF16))
             slopes.append(slope.astype(BF16))
             products.append((slope * scaled).astype(BF16))
         size = small.line_rows
         pooled_ref[rows_at(number * size, size), :] = pool_pieces(matrix, acts)
-        at = rows_at(slots.rows + number * size, size)
-        kept_ref[at, 0:DIRECT] = pool_pieces(matrix, slopes)
-        kept_ref[at, DIRECT : 2 * DIRECT] = pool_pieces(matrix, products)
+        at = slots.rows + number * size
+        kept_ref[rows_at(at, size), :] = pool_pieces(matrix, slopes)
+        kept_ref[rows_at(at + slots.each * size, size), :] = pool_pieces(matrix, products)
 
 
 def outer_moments(center, inverse, count, outer_ref):
@@ -1268,9 +1267,9 @@
         slot = pair + (slots.empty if pair >= slots.gap else 0)
         at = slice(pair * rows, (pair + 1) * rows)
         start = slot % slots.each * rows
-        values = kept_ref[slot // slots.each, start : start + rows, :]
-        pooled_slope_ref[at, 0:DIRECT] = values[:, :DIRECT]
-        pooled_product_ref[at, 0:DIRECT] = values[:, DIRECT:]
+        other = start + slots.each * rows
+        pooled_slope_ref[at, 0:DIRECT] = kept_ref[slot // slots.each, start : start + rows, :]
+        pooled_product_ref[at, 0:DIRECT] = kept_ref[slot // slots.each, other : other + rows, :]
 
     @pl.loop(0, grid.side)
     def _(line):
@@ -1304,7 +1303,7 @@
         used = used + size - at
 
 
-def rest_back(grid, small, slots, block, length_ref, outer_ref, total_ref, gain_ref, grad_ref, h_far, slope_far, kept_far, x_far, reduced_far, du_far, product_out, *refs):
+def rest_back(grid, small, slots, block, length_ref, outer_ref, total_ref, gain_ref, shift_ref, grad_ref, h_far, slope_far, kept_far, x_far, reduced_far, du_far, product_out, *refs):
     h_ref, slope_ref, x_ref, reduced_ref, du_ref, plane_ref, across_ref, scale_ref, product_ref, sem_ref, in_sem, du_sem = refs
     rows = grid.line_rows
     pool = OUTER - POOLED
@@ -1319,10 +1318,9 @@
         (
             (direct, 0, DIRECT),
             (h_far, SECOND, FIRST),
-            (direct, DIRECT, 2 * DIRECT),
             (slope_far, SECOND, FIRST),
         ),
-        ((h_ref, 0), (h_ref, DIRECT), (slope_ref, 0), (slope_ref, DIRECT)),
+        ((h_ref, 0), (h_ref, DIRECT), (slope_ref, 0)),
         sem_ref,
     )
     lines.first()
@@ -1333,6 +1331,8 @@
     matrix = spread_matrix(grid, small)
     a, b, c = rest_constants(outer_ref, total_ref, gain_ref, block)
     mask = grid.mask(rows, length, DIRECT + POOLED)
+    gain = gain_ref[block : block + 1, 0:DIRECT]
+    shift = shift_ref[block : block + 1, 0:DIRECT]
     spread = Spread(grid, plane_ref, across_ref, scale_ref, length)
 
     def visit(step):
@@ -1345,7 +1345,10 @@
                 jnp.concatenate([coarse[:, :DIRECT], coarse[:, pool:]], axis=1),
                 preferred_element_type=F32,
             )
-            back = a * (grad * slope_ref[at, :].astype(F32)) - b - c * h_ref[at, :].astype(F32)
+            scaled = h_ref[at, :].astype(F32)
+            slope = silu_slope(gain * scaled[:, :DIRECT] + shift)
+            slope = jnp.concatenate([slope, slope_ref[at, :].astype(F32)], axis=1)
+            back = a * (grad * slope) - b - c * scaled
             back = back * mask
             du_ref[at, 0:DIRECT] = back[:, :DIRECT].astype(BF16)
             spread.put(line, back[:, DIRECT:])
@@ -1752,7 +1755,7 @@
         functools.partial(first_direct, grid, small, slots, 0),
         (
             shape((slots.each * small.line_rows, DIRECT), BF16),
-            shape((slots.rows + slots.each * small.line_rows, 2 * DIRECT), BF16),
+            shape((slots.rows + 2 * slots.each * small.line_rows, DIRECT), BF16),
             shape((3, SECOND), F32),
         ),
         scalars=1,
@@ -1913,7 +1916,7 @@
             pltpu.VMEM((16, OUTER), F32),
             pltpu.VMEM((small.rows, OUTER), BF16),
             pltpu.VMEM((small.rows, OUTER), BF16),
-            pltpu.VMEM((parts, coarse_rows, 2 * DIRECT), BF16),
+            pltpu.VMEM((parts, 2 * coarse_rows, DIRECT), BF16),
             Lines.semaphores(small, 6),
             pltpu.SemaphoreType.DMA((3,)),
         ],
@@ -1964,21 +1967,21 @@
         ),
         [
             pltpu.VMEM((grid.rows, DIRECT + POOLED), BF16),
-            pltpu.VMEM((grid.rows, DIRECT + POOLED), BF16),
+            pltpu.VMEM((grid.rows, POOLED), BF16),
             pltpu.VMEM(turned.shape, BF16),
             pltpu.VMEM((grid.rows, REDUCED), BF16),
             pltpu.VMEM((grid.rows, DIRECT + POOLED), BF16),
             *Spread.scratch(grid),
             pltpu.VMEM((product_rows, 768), F32),
-            Lines.semaphores(grid, 4),
+            Lines.semaphores(grid, 3),
             pltpu.SemaphoreType.DMA((2,)),
             pltpu.SemaphoreType.DMA((1,)),
         ],
         scalars=1,
         cost=8,
-        far=(5, 6, 7, 8, 9),
+        far=(6, 7, 8, 9, 10),
         far_out=(0,),
-    )(length, outer, after(total, packed), outer_gain, dx_small, h_outer, slope, kept_direct, turned, h_reduced)
+    )(length, outer, after(total, packed), outer_gain, outer_shift, dx_small, h_outer, slope, kept_direct, turned, h_reduced)
     share = add_up(exchange(packed))
     rest_pieces = exchange(rest_product)
     d_low, share = lax.optimization_barrier((after(d_low, rest_product), share))

time: 362 us -> 360 us (level)
  waiting for transfers between devices: 72.3 us -> 63.9 us
  starting transfers between devices: 52.3 us -> 58.7 us
    ppermute x15, starting transfers between devices: 20.6 us -> 27 us  [spread_over(): received.append(lax.ppermute(values, axis, perm))]
    ppermute x15, waiting for transfers between devices: 19.1 us -> 13.8 us  [spread_over(): received.append(lax.ppermute(values, axis, perm))]
  transfers between devices with their start and end apart: 29 -> 29, of which waited for: 11 -> 10; matrix products, arithmetic and copies ran while one was open for 0% -> 0% of each run, Pallas kernels for 42% -> 42%
where the time goes in v5:
time: 360 us; the launch traced here: 358 us
  Pallas kernels  161 us (45%)
  waiting for transfers between devices  63.9 us (18%)
  starting transfers between devices  58.7 us (16%)
  blocking collectives  53 us (15%)
  between operations  14.9 us (4%)
  local copies, waits for them, and re-layouts  4.47 us (1%)
    pallas_call x21, Pallas kernels, run(): pl.pallas_call(body, out_shape=jax.tree.map(placed, out_shape), in_specs=...  161 us
    all_to_all x6, blocking collectives, exchange(): return lax.all_to_all(values, 'dp', 0, 0, tiled=True)  53 us
    ppermute x15, starting transfers between devices, spread_over(): received.append(lax.ppermute(values, axis, perm))  27 us
    all_to_all x1, waiting for transfers between devices, on_device(): by_pairs = lax.all_to_all(turned, 'branch', 0, 0, tiled=True)  24.4 us
    all_to_all x6, starting transfers between devices, exchange(): return lax.all_to_all(values, 'dp', 0, 0, tiled=True)  21.2 us
    all_to_all x6, waiting for transfers between devices, exchange(): return lax.all_to_all(values, 'dp', 0, 0, tiled=True)  20.3 us
    ppermute x15, waiting for transfers between devices, spread_over(): received.append(lax.ppermute(values, axis, perm))  13.8 us
  transfers between devices with their start and end apart: 29, of which 10 were waited for; matrix products, arithmetic and copies ran while one was open for 0% of the time, Pallas kernels for 42%

profile of v5, /device:TPU:0, one launch (start us, length us, event | category | flops | bytes accessed | tf_op | source)
XLA Modules:
  0.0 358.0 jit_solution(12877705614284358989)
XLA Ops:
  7.2 3.2 shard_map.135.x_far.refs_3_
  10.4 6.3 %all-to-all-start = ((bf16[4,208,896]{2,1,0:T(8,128)(2,1)}), bf16[4,208,896]{2,1,0:T(8,128)(2,1)S(1)}, u32[]{:S(2)}, u32[]{:S(2)}) async-start(bf16[4,208,896]{2,1,0:T(8,128)(2,1)} %shard_map.135.x_far.refs_3_), calls=%async_computation | async-start | bytes 2981888 | tf_op jit(solution)/shard_map/all_to_all | solution.py:1696
  17.4 10.1 %shard_map.136 = (bf16[9,512,256]{2,1,0:T(8,128)(2,1)}, bf16[3,512,256]{2,1,0:T(8,128)(2,1)}, bf16[1152,128]{1,0:T(8,128)(2,1)}, bf16[1152,128]{1,0:T(8,128)(2,1...) custom-call(bf16[2,27,160,320]{3,2,1,0:T(8,128)(2,1)} %mid_in.1, ...), custom_call_target="tpu_custom_call" | custom-call | bytes 15000000 | tf_op jit(solution)/shard_map/pallas_call | solution.py:66
  27.5 24.4 %all-to-all-done.x_ref = bf16[4,208,896]{2,1,0:T(8,128)(2,1)S(1)} async-done(((bf16[4,208,896]{2,1,0:T(8,128)(2,1)}), bf16[4,208,896]{2,1,0:T(8,128)(2,1)S(1)}, u32[]{:S(2)}, u32[]{:S(2)}) %all-to-all-start) | async-done | bytes 1490976 | tf_op jit(solution)/shard_map/all_to_all | solution.py:1696
  53.2 2.5 shard_map.137
  58.7 8.5 %all_to_all.65 = f32[8,3,512]{2,1,0:T(4,128)S(1)} all-to-all(f32[8,3,512]{2,1,0:T(4,128)S(1)} %get-tuple-element.108), channel_id=1, replica_groups=mesh['dp'=8,'branch'=4] {'dp'}, dimensions={0} | all-to-all | bytes 98304 | tf_op jit(solution)/shard_map/all_to_all | solution.py:1662
  67.3 3.3 collective-permute-start.5
  71.7 8.2 %collective-permute-done.5.refs_7_.refs_3_ = f32[3,512]{1,0:T(4,128)S(1)} collective-permute-done((f32[3,512]{1,0:T(4,128)S(1)}, f32[3,512]{1,0:T(4,128)S(1)}, u32[]{:S(2)}, u32[]{:S(2)}) %collective-permute-start.5) | collective-permute-done | bytes 6176 | tf_op jit(solution)/shard_map/ppermute | solution.py:1653
  79.9 7.7 %collective-permute-start.3 = (f32[3,512]{1,0:T(4,128)S(1)}, f32[3,512]{1,0:T(4,128)S(1)}, u32[]{:S(2)}, u32[]{:S(2)}) collective-permute-start(f32[3,512]{1,0:T(4,128)S(1)} %reduce_sum.33.refs_4_.refs_0_), channel_id=1, source_target_pairs={{0,1},{1,2},{2,3},{3,0},{4,5},{5,6},{6,7},{7,4},{8,9},{9,10},{10,1... | collective-permute-start | bytes 18440 | tf_op jit(solution)/shard_map/ppermute | solution.py:1653
  89.0 2.6 collective-permute-start.8
  92.9 25.1 %shard_map.138 = (bf16[3136,256]{1,0:T(8,128)(2,1)}, bf16[1,3872,512]{2,1,0:T(8,128)(2,1)}, bf16[1,3872,128]{2,1,0:T(8,128)(2,1)}, f32[3136,512]{1,0:T(8,128)}, f32[2,512]{1,0:T(2,128)}) custom-call(s32[1]{0:T(128)S(6)} %copy.27.length_ref, s32[1]{0:T(128)} %bitcast.place_ref, bf16[1376,128]{1,0:T(8,128)(2,1)} %copy-done.2, bf16[1376,128]{1,0:T(8,128)(2,1)} %copy-done.9, ...), custom_call_target="tpu_custom_call" | custom-call | bytes 120000000 | tf_op jit(solution)/shard_map/pallas_call | solution.py:66
  118.9 3.9 %shard_map.139 = (f32[3136,128]{1,0:T(8,128)}, f32[8,2,640]{2,1,0:T(2,128)}) custom-call(s32[1]{0:T(128)S(6)} %copy.27.length_ref, s32[1]{0:T(128)} %bitcast.place_ref, bf16[912,128]{1,0:T(8,128)(2,1)} %copy-done.3, bf16[912,128]{1,0:T(8,128)(2,1)} %copy-done.12, bf16[912,128]{1,0:T(8,128)(2,1)} %copy-done.11, bf16[912,128]{1,0:T(8,128)(2,1)} %copy-done.10, ...), custom_call_target="tpu_custom_call" | custom-call | bytes 15000000 | tf_op jit(solution)/shard_map/pallas_call | solution.py:66
  122.8 3.7 %all-to-all-start.2 = ((f32[8,2,640]{2,1,0:T(2,128)}), f32[8,2,640]{2,1,0:T(2,128)S(1)}, u32[]{:S(2)}, u32[]{:S(2)}) async-start(f32[8,2,640]{2,1,0:T(2,128)} %get-tuple-element.116), calls=%async_computation.2 | async-start | bytes 81920 | tf_op jit(solution)/shard_map/all_to_all | solution.py:1662
  126.5 3.0 shard_map.140
  129.5 1.8 all-to-all-done.2.sums_in_ref
  131.4 3.9 %collective-permute-start.11 = (bf16[128,256]{1,0:T(8,128)(2,1)}, bf16[128,256]{1,0:T(8,128)(2,1)S(1)}, u32[]{:S(2)}, u32[]{:S(2)}) collective-permute-start(bf16[128,256]{1,0:T(8,128)(2,1)} %get-tuple-element.121.refs_0_), channel_id=1, source_target_pairs={{0,3},{1,0},{2,1},{3,2},{4,7},{5,4},{6,5},{7,6},{8,11},{9,8},{10,9... | collective-permute-start | bytes 196616 | tf_op jit(solution)/shard_map/ppermute | solution.py:1653
  135.9 11.7 %shard_map.141 = (bf16[448,640]{1,0:T(8,128)(2,1)}, bf16[3136,640]{1,0:T(8,128)(2,1)}, bf16[3136,640]{1,0:T(8,128)(2,1)}, f32[3,896]{1,0:T(4,128)}, bf16[448,640]{1,0:T(8,128)(2,1)}, /*index=5*/bf16[448,640]{1,0:T(8,128)(2,1)}) custom-call(s32[1]{0:T(128)S(6)} %copy.27.length_ref, f32[3136,128]{1,0:T(8,128)} %get-tuple-element.122.q_far, ...), custom_call_target="tpu_custom_call" | custom-call | bytes 15000000 | tf_op jit(solution)/shard_map/pallas_call | solution.py:66
  148.3 4.3 %shard_map.142 = (f32[448,640]{1,0:T(8,128)}, f32[8,3,640]{2,1,0:T(4,128)}, bf16[448,896]{1,0:T(8,128)(2,1)}) custom-call(s32[1]{0:T(128)S(6)} %select_n.12.length_ref, s32[1]{0:T(128)} %bitcast.place_ref, f32[1]{0:T(128)S(6)} %mul.20.count_ref, bf16[128,256]{1,0:T(8,128)(2,1)} %get-tuple-element.121.refs_0_, bf16[128,256]{1,0:T(8,128)(2,1)} %copy-done.18, ...), custom_call_target="tpu_custom_call" | custom-call | bytes 15000000 | tf_op jit(solution)/shard_map/pallas_call | solution.py:66
  152.7 9.1 %all_to_all.66.sums_in_ref = f32[8,3,640]{2,1,0:T(4,128)} all-to-all(f32[8,3,640]{2,1,0:T(4,128)} %get-tuple-element.129), channel_id=1, replica_groups=mesh['dp'=8,'branch'=4] {'dp'}, dimensions={0} | all-to-all | bytes 122880 | tf_op jit(solution)/shard_map/all_to_all | solution.py:1662
  161.7 6.8 %shard_map.143 = (bf16[448,256]{1,0:T(8,128)(2,1)}, bf16[2,736,512]{2,1,0:T(8,128)(2,1)}, bf16[2,736,128]{2,1,0:T(8,128)(2,1)}, f32[448,512]{1,0:T(8,128)}, f32[8,2,512]{2,1,0:T(2,128)}, /*index=5*/f32[3,640]{1,0:T(4,128)}) custom-call(s32[1]{0:T(128)S(6)} %select_n.12.length_ref, f32[448,640]{1,0:T(8,128)} %get-tuple-element.128.q_ref, ...), custom_call_target="tpu_custom_call" | custom-call | bytes 15000000 | tf_op jit(solution)/shard_map/pallas_call | solution.py:66
  168.5 8.8 %all_to_all.67.sums_in_ref = f32[8,2,512]{2,1,0:T(2,128)} all-to-all(f32[8,2,512]{2,1,0:T(2,128)} %get-tuple-element.135), channel_id=1, replica_groups=mesh['dp'=8,'branch'=4] {'dp'}, dimensions={0} | all-to-all | bytes 65536 | tf_op jit(solution)/shard_map/all_to_all | solution.py:1662
  177.3 4.7 %shard_map.144 = (bf16[49,8,832]{2,1,0:T(8,128)(2,1)}, bf16[448,896]{1,0:T(8,128)(2,1)}, bf16[448,896]{1,0:T(8,128)(2,1)}, f32[3,896]{1,0:T(4,128)}, f32[8,2,896]{2,1,0:T(2,128)}) custom-call(s32[1]{0:T(128)S(6)} %select_n.12.length_ref, f32[448,640]{1,0:T(8,128)} %get-tuple-element.128.q_ref, f32[448,512]{1,0:T(8,128)} %get-tuple-element.133.e_ref, ...), custom_call_target="tpu_custom_call" | custom-call | bytes 15000000 | tf_op jit(solution)/shard_map/pallas_call | solution.py:66
  182.1 3.3 all-to-all-start.5
  185.4 4.9 %all-to-all-done.5.sums_in_ref = f32[8,2,896]{2,1,0:T(2,128)S(1)} async-done(((f32[8,2,896]{2,1,0:T(2,128)}), f32[8,2,896]{2,1,0:T(2,128)S(1)}, u32[]{:S(2)}, u32[]{:S(2)}) %all-to-all-start.5) | async-done | bytes 57376 | tf_op jit(solution)/shard_map/all_to_all | solution.py:1662
  190.9 5.3 %shard_map.145 = (bf16[2,736,512]{2,1,0:T(8,128)(2,1)}, f32[2,896]{1,0:T(2,128)}, bf16[8,384,128]{2,1,0:T(8,128)(2,1)}) custom-call(s32[1]{0:T(128)S(6)} %select_n.12.length_ref, s32[1]{0:T(128)S(6)} %mul.25.first_ref, bf16[448,896]{1,0:T(8,128)(2,1)} %get-tuple-element.139.h_far, f32[3,896]{1,0:T(4,128)} %get-tuple-element.140.outer_ref, ...), custom_call_target="tpu_custom_call" | custom-call | bytes 24000000 | tf_op jit(solution)/shard_map/pallas_call | solution.py:66
  196.3 3.6 all-to-all-start.6
  199.9 6.3 %shard_map.146 = (bf16[448,256]{1,0:T(8,128)(2,1)}, f32[8,2,256]{2,1,0:T(2,128)}) custom-call(s32[1]{0:T(128)S(6)} %select_n.12.length_ref, bf16[2,736,512]{2,1,0:T(8,128)(2,1)} %get-tuple-element.147.d_ref, bf16[448,256]{1,0:T(8,128)(2,1)} %get-tuple-element.146.reduced_ref.reduced_far, f32[2,256]{1,0:T(2,128)} %get-tuple-element.110.refs_8_.gain_ref.reduced_gain_ref, ...), custom_call_target="tpu_custom_call" | custom-call | bytes 24000000 | tf_op jit(solution)/shard_map/pallas_call | solution.py:66
  206.2 6.2 %all-to-all-done.6 = bf16[8,384,128]{2,1,0:T(8,128)(2,1)S(1)} async-done(((bf16[8,384,128]{2,1,0:T(8,128)(2,1)}), bf16[8,384,128]{2,1,0:T(8,128)(2,1)S(1)}, u32[]{:S(2)}, u32[]{:S(2)}) %all-to-all-start.6) | async-done | bytes 786464 | tf_op jit(solution)/shard_map/all_to_all | solution.py:1662
  213.2 8.7 %all_to_all.68.sums_in_ref = f32[8,2,256]{2,1,0:T(2,128)} all-to-all(f32[8,2,256]{2,1,0:T(2,128)} %get-tuple-element.152), channel_id=1, replica_groups=mesh['dp'=8,'branch'=4] {'dp'}, dimensions={0} | all-to-all | bytes 32768 | tf_op jit(solution)/shard_map/all_to_all | solution.py:1662
  221.8 7.8 %shard_map.147 = (bf16[448,896]{1,0:T(8,128)(2,1)}, bf16[8,144,128]{2,1,0:T(8,128)(2,1)}, f32[2,256]{1,0:T(2,128)}, f32[8,2,896]{2,1,0:T(2,128)}) custom-call(s32[1]{0:T(128)S(6)} %select_n.12.length_ref, s32[1]{0:T(128)} %bitcast.place_ref, bf16[448,896]{1,0:T(8,128)(2,1)} %get-tuple-element.139.h_far, f32[3,896]{1,0:T(4,128)} %get-tuple-element.140.outer_ref, ...), custom_call_target="tpu_custom_call" | custom-call | bytes 30000000 | tf_op jit(solution)/shard_map/pallas_call | solution.py:66
  229.7 8.9 %all_to_all.69.sums_in_ref = f32[8,2,896]{2,1,0:T(2,128)} all-to-all(f32[8,2,896]{2,1,0:T(2,128)} %get-tuple-element.158), channel_id=1, replica_groups=mesh['dp'=8,'branch'=4] {'dp'}, dimensions={0} | all-to-all | bytes 114688 | tf_op jit(solution)/shard_map/all_to_all | solution.py:1662
  238.6 16.2 %shard_map.148 = (bf16[1,3872,512]{2,1,0:T(8,128)(2,1)}, f32[2,896]{1,0:T(2,128)}, bf16[8,528,128]{2,1,0:T(8,128)(2,1)}) custom-call(s32[1]{0:T(128)S(6)} %copy.27.length_ref, s32[1]{0:T(128)S(6)} %mul.25.first_ref, bf16[3136,640]{1,0:T(8,128)(2,1)} %get-tuple-element.137.h_far, f32[3,896]{1,0:T(4,128)} %get-tuple-element.138.outer_ref, ...), custom_call_target="tpu_custom_call" | custom-call | bytes 54000000 | tf_op jit(solution)/shard_map/pallas_call | solution.py:66
  254.8 3.6 all-to-all-start.9
  258.6 8.7 %shard_map.149 = (bf16[3136,384]{1,0:T(8,128)(2,1)}, f32[8,6,32,128]{3,2,1,0:T(8,128)}) custom-call(s32[1]{0:T(128)S(6)} %copy.27.length_ref, f32[3,896]{1,0:T(4,128)} %get-tuple-element.138.outer_ref, f32[2,896]{1,0:T(2,128)} %get-tuple-element.167.total_ref.refs_0_, f32[2,896]{1,0:T(2,128)} %get-tuple-element.118.gain_ref, ...), custom_call_target="tpu_custom_call" | custom-call | bytes 24000000 | tf_op jit(solution)/shard_map/pallas_call | solution.py:66
  267.4 7.4 %all-to-all-done.9 = bf16[8,528,128]{2,1,0:T(8,128)(2,1)S(1)} async-done(((bf16[8,528,128]{2,1,0:T(8,128)(2,1)}), bf16[8,528,128]{2,1,0:T(8,128)(2,1)S(1)}, u32[]{:S(2)}, u32[]{:S(2)}) %all-to-all-start.9) | async-done | bytes 1081376 | tf_op jit(solution)/shard_map/all_to_all | solution.py:1662
  275.6 3.6 all-to-all-start.11
  279.2 22.1 %shard_map.150 = (bf16[3136,256]{1,0:T(8,128)(2,1)}, f32[8,2,256]{2,1,0:T(2,128)}, f32[8,2,32,128]{3,2,1,0:T(8,128)}) custom-call(s32[1]{0:T(128)S(6)} %copy.27.length_ref, bf16[1,3872,512]{2,1,0:T(8,128)(2,1)} %get-tuple-element.171.d_ref, bf16[3136,256]{1,0:T(8,128)(2,1)} %get-tuple-element.168.reduced_far.reduced_ref.h_far, ...), custom_call_target="tpu_custom_call" | custom-call | bytes 66000000 | tf_op jit(solution)/shard_map/pallas_call | solution.py:66
  301.3 9.0 %all_to_all.70.sums_in_ref = f32[8,2,256]{2,1,0:T(2,128)} all-to-all(f32[8,2,256]{2,1,0:T(2,128)} %get-tuple-element.175), channel_id=1, replica_groups=mesh['dp'=8,'branch'=4] {'dp'}, dimensions={0} | all-to-all | bytes 32768 | tf_op jit(solution)/shard_map/all_to_all | solution.py:1662
  310.3 3.4 all-to-all-start.10
  313.7 7.4 %shard_map.151 = (bf16[3136,208]{1,0:T(8,128)(2,1)}, f32[2,256]{1,0:T(2,128)}) custom-call(s32[1]{0:T(128)S(6)} %copy.27.length_ref, s32[1]{0:T(128)} %bitcast.place_ref, f32[3,512]{1,0:T(4,128)} %get-tuple-element.124.moment_ref, f32[8,2,256]{2,1,0:T(2,128)} %all_to_all.70.sums_in_ref, f32[2,256]{1,0:T(2,128)} %get-tuple-element.110.refs_8_.gain_ref.reduced_gain_ref, ...), custom_call_target="tpu_custom_call" | custom-call | bytes 24000000 | tf_op jit(solution)/shard_map/pallas_call | solution.py:66
  321.3 3.4 collective-permute-start.14
  325.8 4.1 %shard_map.153 = (f32[2,27,160,320]{3,2,1,0:T(8,128)}, f32[2,27,32,128]{3,2,1,0:T(8,128)}) custom-call(bf16[32,384,128]{2,1,0:T(8,128)(2,1)} %bitcast.32), custom_call_target="tpu_custom_call" | custom-call | bytes 15000000 | tf_op jit(solution)/shard_map/pallas_call | solution.py:66
  329.9 4.3 %collective-permute-done.13 = bf16[160,128]{1,0:T(8,128)(2,1)S(1)} collective-permute-done((bf16[160,128]{1,0:T(8,128)(2,1)S(1)}, bf16[160,128]{1,0:T(8,128)(2,1)S(1)}, u32[]{:S(2)}, u32[]{:S(2)}) %collective-permute-start.13) | collective-permute-done | bytes 40992 | tf_op jit(solution)/shard_map/ppermute | solution.py:1653
  334.2 2.9 collective-permute-start.17
  337.8 3.4 all-gather.11.cloned.1.call-done
  341.1 6.2 %shard_map.154 = (f32[2,27,160,320]{3,2,1,0:T(8,128)}, f32[2,27,32,128]{3,2,1,0:T(8,128)}, f32[2,576,832]{2,1,0:T(8,128)}, f32[2,1024]{1,0:T(2,128)}, f32[2,1024]{1,0:T(2,128)}) custom-call(bf16[32,528,128]{2,1,0:T(8,128)(2,1)} %bitcast.30, f32[2,896]{1,0:T(2,128)} %get-tuple-element.167.total_ref.refs_0_, ...), custom_call_target="tpu_custom_call", output_to_operand_aliasing={{0}: (5, {}), {1}: (6, {})} | custom-call | bytes 18000000 | tf_op jit(solution)/shard_map/pallas_call | solution.py:66
  347.9 1.8 collective-permute-done.18.other_ref
  349.7 1.8 shard_map.155
  (95 shorter events, 15.0 us)
Async XLA Ops:
  10.4 41.5 %all-to-all-start = ((bf16[4,208,896]{2,1,0:T(8,128)(2,1)}), bf16[4,208,896]{2,1,0:T(8,128)(2,1)S(1)}, u32[]{:S(2)}, u32[]{:S(2)}) async-start(bf16[4,208,896]{2,1,0:T(8,128)(2,1)} %shard_map.135.x_far.refs_3_), calls=%async_computation | async-start | bytes 2981888 | tf_op jit(solution)/shard_map/all_to_all | solution.py:1696
  51.9 1.3 copy-start
  55.7 0.9 copy-start.1
  56.7 36.2 %copy-start.2 = (bf16[1376,128]{1,0:T(8,128)(2,1)}, bf16[1376,128]{1,0:T(8,128)(2,1)S(1)}, u32[]{:S(2)}) copy-start(bf16[1376,128]{1,0:T(8,128)(2,1)S(1)} %get-tuple-element.107.refs_0_) | copy-start | bytes 1056772
  56.7 61.4 %copy-start.3 = (bf16[912,128]{1,0:T(8,128)(2,1)}, bf16[912,128]{1,0:T(8,128)(2,1)S(1)}, u32[]{:S(2)}) copy-start(bf16[912,128]{1,0:T(8,128)(2,1)S(1)} %get-tuple-element.109.refs_0_) | copy-start | bytes 700420
  56.7 32.3 %collective-permute-start.2 = (bf16[1376,128]{1,0:T(8,128)(2,1)S(1)}, bf16[1376,128]{1,0:T(8,128)(2,1)S(1)}, u32[]{:S(2)}, u32[]{:S(2)}) collective-permute-start(bf16[1376,128]{1,0:T(8,128)(2,1)S(1)} %get-tuple-element.107.refs_0_), channel_id=1, source_target_pairs={{0,3},{1,0},{2,1},{3,2},{4,7},{5,4},{6,5},{7,6},{8,11},{9,8},{10,9... | collective-permute-start | bytes 1056776 | tf_op jit(solution)/shard_map/ppermute | solution.py:1653
  58.1 30.9 %collective-permute-start.1 = (bf16[1376,128]{1,0:T(8,128)(2,1)S(1)}, bf16[1376,128]{1,0:T(8,128)(2,1)S(1)}, u32[]{:S(2)}, u32[]{:S(2)}) collective-permute-start(bf16[1376,128]{1,0:T(8,128)(2,1)S(1)} %get-tuple-element.107.refs_0_), channel_id=1, source_target_pairs={{0,2},{1,3},{2,0},{3,1},{4,6},{5,7},{6,4},{7,5},{8,10},{9,11},{10,... | collective-permute-start | bytes 1056776 | tf_op jit(solution)/shard_map/ppermute | solution.py:1653
  58.1 30.9 %collective-permute-start = (bf16[1376,128]{1,0:T(8,128)(2,1)S(1)}, bf16[1376,128]{1,0:T(8,128)(2,1)S(1)}, u32[]{:S(2)}, u32[]{:S(2)}) collective-permute-start(bf16[1376,128]{1,0:T(8,128)(2,1)S(1)} %get-tuple-element.107.refs_0_), channel_id=1, source_target_pairs={{0,1},{1,2},{2,3},{3,0},{4,5},{5,6},{6,7},{7,4},{8,9},{9,10},{10,1... | collective-permute-start | bytes 1056776 | tf_op jit(solution)/shard_map/ppermute | solution.py:1653
  67.2 25.6 %copy-start.15 = (f32[3,512]{1,0:T(4,128)}, f32[3,512]{1,0:T(4,128)S(1)}, u32[]{:S(2)}) copy-start(f32[3,512]{1,0:T(4,128)S(1)} %reduce_sum.33.refs_4_.refs_0_) | copy-start | bytes 18436
  67.3 12.6 %collective-permute-start.5 = (f32[3,512]{1,0:T(4,128)S(1)}, f32[3,512]{1,0:T(4,128)S(1)}, u32[]{:S(2)}, u32[]{:S(2)}) collective-permute-start(f32[3,512]{1,0:T(4,128)S(1)} %reduce_sum.33.refs_4_.refs_0_), channel_id=1, source_target_pairs={{0,3},{1,0},{2,1},{3,2},{4,7},{5,4},{6,5},{7,6},{8,11},{9,8},{10,9... | collective-permute-start | bytes 18440 | tf_op jit(solution)/shard_map/ppermute | solution.py:1653
  70.6 17.0 %collective-permute-start.4 = (f32[3,512]{1,0:T(4,128)S(1)}, f32[3,512]{1,0:T(4,128)S(1)}, u32[]{:S(2)}, u32[]{:S(2)}) collective-permute-start(f32[3,512]{1,0:T(4,128)S(1)} %reduce_sum.33.refs_4_.refs_0_), channel_id=1, source_target_pairs={{0,2},{1,3},{2,0},{3,1},{4,6},{5,7},{6,4},{7,5},{8,10},{9,11},{10,... | collective-permute-start | bytes 18440 | tf_op jit(solution)/shard_map/ppermute | solution.py:1653
  79.9 13.0 %copy-start.19 = (f32[3,512]{1,0:T(4,128)}, f32[3,512]{1,0:T(4,128)S(1)}, u32[]{:S(2)}) copy-start(f32[3,512]{1,0:T(4,128)S(1)} %collective-permute-done.5.refs_7_.refs_3_) | copy-start | bytes 18436
  79.9 9.1 %collective-permute-start.3 = (f32[3,512]{1,0:T(4,128)S(1)}, f32[3,512]{1,0:T(4,128)S(1)}, u32[]{:S(2)}, u32[]{:S(2)}) collective-permute-start(f32[3,512]{1,0:T(4,128)S(1)} %reduce_sum.33.refs_4_.refs_0_), channel_id=1, source_target_pairs={{0,1},{1,2},{2,3},{3,0},{4,5},{5,6},{6,7},{7,4},{8,9},{9,10},{10,1... | collective-permute-start | bytes 18440 | tf_op jit(solution)/shard_map/ppermute | solution.py:1653
  87.6 5.3 %copy-start.20 = (f32[3,512]{1,0:T(4,128)}, f32[3,512]{1,0:T(4,128)S(1)}, u32[]{:S(2)}) copy-start(f32[3,512]{1,0:T(4,128)S(1)} %collective-permute-done.4.refs_6_.refs_2_) | copy-start | bytes 18436
  89.0 3.9 %copy-start.21 = (f32[3,512]{1,0:T(4,128)}, f32[3,512]{1,0:T(4,128)S(1)}, u32[]{:S(2)}) copy-start(f32[3,512]{1,0:T(4,128)S(1)} %collective-permute-done.3.refs_5_.refs_1_) | copy-start | bytes 18436
  89.0 3.9 %copy-start.7 = (bf16[1376,128]{1,0:T(8,128)(2,1)}, bf16[1376,128]{1,0:T(8,128)(2,1)S(1)}, u32[]{:S(2)}) copy-start(bf16[1376,128]{1,0:T(8,128)(2,1)S(1)} %collective-permute-done.2.refs_3_) | copy-start | bytes 1056772
  89.0 3.9 %copy-start.8 = (bf16[1376,128]{1,0:T(8,128)(2,1)}, bf16[1376,128]{1,0:T(8,128)(2,1)S(1)}, u32[]{:S(2)}) copy-start(bf16[1376,128]{1,0:T(8,128)(2,1)S(1)} %collective-permute-done.1.refs_2_) | copy-start | bytes 1056772
  89.0 3.9 %copy-start.9 = (bf16[1376,128]{1,0:T(8,128)(2,1)}, bf16[1376,128]{1,0:T(8,128)(2,1)S(1)}, u32[]{:S(2)}) copy-start(bf16[1376,128]{1,0:T(8,128)(2,1)S(1)} %collective-permute-done.refs_1_) | copy-start | bytes 1056772
  89.0 29.0 %collective-permute-start.8 = (bf16[912,128]{1,0:T(8,128)(2,1)S(1)}, bf16[912,128]{1,0:T(8,128)(2,1)S(1)}, u32[]{:S(2)}, u32[]{:S(2)}) collective-permute-start(bf16[912,128]{1,0:T(8,128)(2,1)S(1)} %get-tuple-element.109.refs_0_), channel_id=1, source_target_pairs={{0,3},{1,0},{2,1},{3,2},{4,7},{5,4},{6,5},{7,6},{8,11},{9,8},{10,9... | collective-permute-start | bytes 700424 | tf_op jit(solution)/shard_map/ppermute | solution.py:1653
  91.7 26.4 %collective-permute-start.7 = (bf16[912,128]{1,0:T(8,128)(2,1)S(1)}, bf16[912,128]{1,0:T(8,128)(2,1)S(1)}, u32[]{:S(2)}, u32[]{:S(2)}) collective-permute-start(bf16[912,128]{1,0:T(8,128)(2,1)S(1)} %get-tuple-element.109.refs_0_), channel_id=1, source_target_pairs={{0,2},{1,3},{2,0},{3,1},{4,6},{5,7},{6,4},{7,5},{8,10},{9,11},{10,... | collective-permute-start | bytes 700424 | tf_op jit(solution)/shard_map/ppermute | solution.py:1653
  92.8 25.3 %collective-permute-start.6 = (bf16[912,128]{1,0:T(8,128)(2,1)S(1)}, bf16[912,128]{1,0:T(8,128)(2,1)S(1)}, u32[]{:S(2)}, u32[]{:S(2)}) collective-permute-start(bf16[912,128]{1,0:T(8,128)(2,1)S(1)} %get-tuple-element.109.refs_0_), channel_id=1, source_target_pairs={{0,1},{1,2},{2,3},{3,0},{4,5},{5,6},{6,7},{7,4},{8,9},{9,10},{10,1... | collective-permute-start | bytes 700424 | tf_op jit(solution)/shard_map/ppermute | solution.py:1653
  118.1 0.7 copy-start.10
  118.1 0.7 copy-start.11
  118.1 0.8 copy-start.12
  122.8 8.6 %all-to-all-start.2 = ((f32[8,2,640]{2,1,0:T(2,128)}), f32[8,2,640]{2,1,0:T(2,128)S(1)}, u32[]{:S(2)}, u32[]{:S(2)}) async-start(f32[8,2,640]{2,1,0:T(2,128)} %get-tuple-element.116), calls=%async_computation.2 | async-start | bytes 81920 | tf_op jit(solution)/shard_map/all_to_all | solution.py:1662
  126.5 95.4 %all-gather.7.cloned.1.call-start = ((), (), s32[]{:S(2)}) async-start(), calls=%async_computation.13 | async-start | bytes 2949120 | tf_op jit(solution)/shard_map/all_gather | solution.py:1766
  131.4 4.5 %copy-start.14 = (f32[8,2,640]{2,1,0:T(2,128)}, f32[8,2,640]{2,1,0:T(2,128)S(1)}, u32[]{:S(2)}) copy-start(f32[8,2,640]{2,1,0:T(2,128)S(1)} %all-to-all-done.2.sums_in_ref) | copy-start | bytes 122884
  131.4 16.2 %collective-permute-start.11 = (bf16[128,256]{1,0:T(8,128)(2,1)}, bf16[128,256]{1,0:T(8,128)(2,1)S(1)}, u32[]{:S(2)}, u32[]{:S(2)}) collective-permute-start(bf16[128,256]{1,0:T(8,128)(2,1)} %get-tuple-element.121.refs_0_), channel_id=1, source_target_pairs={{0,3},{1,0},{2,1},{3,2},{4,7},{5,4},{6,5},{7,6},{8,11},{9,8},{10,9... | collective-permute-start | bytes 196616 | tf_op jit(solution)/shard_map/ppermute | solution.py:1653
  135.2 12.4 %collective-permute-start.10 = (bf16[128,256]{1,0:T(8,128)(2,1)}, bf16[128,256]{1,0:T(8,128)(2,1)S(1)}, u32[]{:S(2)}, u32[]{:S(2)}) collective-permute-start(bf16[128,256]{1,0:T(8,128)(2,1)} %get-tuple-element.121.refs_0_), channel_id=1, source_target_pairs={{0,2},{1,3},{2,0},{3,1},{4,6},{5,7},{6,4},{7,5},{8,10},{9,11},{10,... | collective-permute-start | bytes 196616 | tf_op jit(solution)/shard_map/ppermute | solution.py:1653
  135.2 12.4 %collective-permute-start.9 = (bf16[128,256]{1,0:T(8,128)(2,1)}, bf16[128,256]{1,0:T(8,128)(2,1)S(1)}, u32[]{:S(2)}, u32[]{:S(2)}) collective-permute-start(bf16[128,256]{1,0:T(8,128)(2,1)} %get-tuple-element.121.refs_0_), channel_id=1, source_target_pairs={{0,1},{1,2},{2,3},{3,0},{4,5},{5,6},{6,7},{7,4},{8,9},{9,10},{10,1... | collective-permute-start | bytes 196616 | tf_op jit(solution)/shard_map/ppermute | solution.py:1653
  147.7 0.6 copy-start.18
  182.1 8.3 %all-to-all-start.5 = ((f32[8,2,896]{2,1,0:T(2,128)}), f32[8,2,896]{2,1,0:T(2,128)S(1)}, u32[]{:S(2)}, u32[]{:S(2)}) async-start(f32[8,2,896]{2,1,0:T(2,128)} %get-tuple-element.141), calls=%async_computation.5 | async-start | bytes 114688 | tf_op jit(solution)/shard_map/all_to_all | solution.py:1662
  196.3 16.1 %all-to-all-start.6 = ((bf16[8,384,128]{2,1,0:T(8,128)(2,1)}), bf16[8,384,128]{2,1,0:T(8,128)(2,1)S(1)}, u32[]{:S(2)}, u32[]{:S(2)}) async-start(bf16[8,384,128]{2,1,0:T(8,128)(2,1)} %get-tuple-element.151), calls=%async_computation.6 | async-start | bytes 1572864 | tf_op jit(solution)/shard_map/all_to_all | solution.py:1662
  199.9 125.9 %all-gather.9.cloned.1.call-start = ((), (), s32[]{:S(2)}) async-start(), calls=%async_computation.14 | async-start | bytes 3244032 | tf_op jit(solution)/shard_map/all_gather | solution.py:1945
  254.8 20.0 %all-to-all-start.9 = ((bf16[8,528,128]{2,1,0:T(8,128)(2,1)}), bf16[8,528,128]{2,1,0:T(8,128)(2,1)S(1)}, u32[]{:S(2)}, u32[]{:S(2)}) async-start(bf16[8,528,128]{2,1,0:T(8,128)(2,1)} %get-tuple-element.166), calls=%async_computation.9 | async-start | bytes 2162688 | tf_op jit(solution)/shard_map/all_to_all | solution.py:1662
  258.4 82.8 %all-gather.11.cloned.1.call-start = ((), (), s32[]{:S(2)}) async-start(), calls=%async_computation.15 | async-start | bytes 4460544 | tf_op jit(solution)/shard_map/all_gather | solution.py:2014
  275.6 25.7 %all-to-all-start.11 = ((f32[8,6,32,128]{3,2,1,0:T(8,128)}), f32[8,6,32,128]{3,2,1,0:T(8,128)S(1)}, u32[]{:S(2)}, u32[]{:S(2)}) async-start(f32[8,6,32,128]{3,2,1,0:T(8,128)} %get-tuple-element.169), calls=%async_computation.11 | async-start | bytes 1572864 | tf_op jit(solution)/shard_map/all_to_all | solution.py:1662
  310.3 10.9 %all-to-all-start.10 = ((f32[8,2,32,128]{3,2,1,0:T(8,128)}), f32[8,2,32,128]{3,2,1,0:T(8,128)S(1)}, u32[]{:S(2)}, u32[]{:S(2)}) async-start(f32[8,2,32,128]{3,2,1,0:T(8,128)} %get-tuple-element.173), calls=%async_computation.10 | async-start | bytes 524288 | tf_op jit(solution)/shard_map/all_to_all | solution.py:1662
  313.7 7.4 %copy-start.4 = (f32[8,2,256]{2,1,0:T(2,128)S(1)}, f32[8,2,256]{2,1,0:T(2,128)}, u32[]{:S(2)}) copy-start(f32[8,2,256]{2,1,0:T(2,128)} %all_to_all.70.sums_in_ref) | copy-start | bytes 49156
  313.7 7.4 %copy-start.5 = (f32[2,256]{1,0:T(2,128)S(1)}, f32[2,256]{1,0:T(2,128)}, u32[]{:S(2)}) copy-start(f32[2,256]{1,0:T(2,128)} %get-tuple-element.110.refs_8_.gain_ref.reduced_gain_ref) | copy-start | bytes 6148
  313.7 7.4 %copy-start.6 = (f32[3,512]{1,0:T(4,128)S(1)}, f32[3,512]{1,0:T(4,128)}, u32[]{:S(2)}) copy-start(f32[3,512]{1,0:T(4,128)} %get-tuple-element.124.moment_ref) | copy-start | bytes 18436
  321.3 8.6 %collective-permute-start.14 = (bf16[160,128]{1,0:T(8,128)(2,1)S(1)}, bf16[160,128]{1,0:T(8,128)(2,1)S(1)}, u32[]{:S(2)}, u32[]{:S(2)}) collective-permute-start(bf16[160,128]{1,0:T(8,128)(2,1)S(1)} %shard_map.152), channel_id=1, source_target_pairs={{0,3},{1,0},{2,1},{3,2},{4,7},{5,4},{6,5},{7,6},{8,11},{9,8},{10,9... | collective-permute-start | bytes 122888 | tf_op jit(solution)/shard_map/ppermute | solution.py:1653
  324.7 9.5 %collective-permute-start.13 = (bf16[160,128]{1,0:T(8,128)(2,1)S(1)}, bf16[160,128]{1,0:T(8,128)(2,1)S(1)}, u32[]{:S(2)}, u32[]{:S(2)}) collective-permute-start(bf16[160,128]{1,0:T(8,128)(2,1)S(1)} %shard_map.152), channel_id=1, source_target_pairs={{0,2},{1,3},{2,0},{3,1},{4,6},{5,7},{6,4},{7,5},{8,10},{9,11},{10,... | collective-permute-start | bytes 122888 | tf_op jit(solution)/shard_map/ppermute | solution.py:1653
  325.1 9.1 %collective-permute-start.12 = (bf16[160,128]{1,0:T(8,128)(2,1)S(1)}, bf16[160,128]{1,0:T(8,128)(2,1)S(1)}, u32[]{:S(2)}, u32[]{:S(2)}) collective-permute-start(bf16[160,128]{1,0:T(8,128)(2,1)S(1)} %shard_map.152), channel_id=1, source_target_pairs={{0,1},{1,2},{2,3},{3,0},{4,5},{5,6},{6,7},{7,4},{8,9},{9,10},{10,1... | collective-permute-start | bytes 122888 | tf_op jit(solution)/shard_map/ppermute | solution.py:1653
  334.2 13.2 %collective-permute-start.17 = (bf16[640,128]{1,0:T(8,128)(2,1)S(1)}, bf16[640,128]{1,0:T(8,128)(2,1)S(1)}, u32[]{:S(2)}, u32[]{:S(2)}) collective-permute-start(bf16[640,128]{1,0:T(8,128)(2,1)S(1)} %constant_dynamic-update-slice_fusion), channel_id=1, source_target_pairs={{0,24},{4,28},{8,16},{12,20},{16,8},{20,12},{24,0},{28,4},{1,25},{... | collective-permute-start | bytes 491528 | tf_op jit(solution)/shard_map/ppermute | solution.py:1673
  337.1 10.3 %collective-permute-start.16 = (bf16[640,128]{1,0:T(8,128)(2,1)S(1)}, bf16[640,128]{1,0:T(8,128)(2,1)S(1)}, u32[]{:S(2)}, u32[]{:S(2)}) collective-permute-start(bf16[640,128]{1,0:T(8,128)(2,1)S(1)} %constant_dynamic-update-slice_fusion), channel_id=1, source_target_pairs={{0,16},{4,20},{8,24},{12,28},{16,0},{20,4},{24,8},{28,12},{1,17},{... | collective-permute-start | bytes 491528 | tf_op jit(solution)/shard_map/ppermute | solution.py:1673
  337.6 9.8 %collective-permute-start.15 = (bf16[640,128]{1,0:T(8,128)(2,1)S(1)}, bf16[640,128]{1,0:T(8,128)(2,1)S(1)}, u32[]{:S(2)}, u32[]{:S(2)}) collective-permute-start(bf16[640,128]{1,0:T(8,128)(2,1)S(1)} %constant_dynamic-update-slice_fusion), channel_id=1, source_target_pairs={{0,8},{4,12},{8,0},{12,4},{16,24},{20,28},{24,16},{28,20},{1,9},{5... | collective-permute-start | bytes 491528 | tf_op jit(solution)/shard_map/ppermute | solution.py:1673
  347.5 2.2 collective-permute-start.18
  (3 other events, 1.9 us)
Sparse Core Ops, SparseCore 0:
  131.5 50.5 all-gather.6
  213.3 57.8 all-gather.8
  275.8 65.3 all-gather.10
